TPU v7x, 32 devices: a whole 2x2x4 slice. The times are simulated.
32 devices in a mesh: dp: 16 (over z, y, x), seq: 2 (over core).
Axes of the slice: x: 2, y: 2, z: 4, core: 2. Of those that a mesh axis runs over, the one named last changes fastest.
Arguments:
- latents: bfloat16 [16, 1024, 1024], P('dp', 'seq'), may hold values from -6 to 6
- condition: bfloat16 [16, 1024], P('dp'), may hold values from -6 to 6
- adapter_choice: int32 [16, 5], P('dp'), may hold values from 0 to 7
- cotangent: bfloat16 [16, 1024, 1024], P('dp', 'seq'), may hold values from -6 to 6
- modulate_weight: bfloat16 [1024, 6144], P(('dp', 'seq')), may hold values from -0.1875 to 0.1875
- attend_weight: bfloat16 [1024, 3072], P(('dp', 'seq')), may hold values from -0.1875 to 0.1875
- project_weight: bfloat16 [1024, 1024], P(('dp', 'seq')), may hold values from -3 to 3
- expand_weight: bfloat16 [1024, 4096], P(('dp', 'seq')), may hold values from -0.1875 to 0.1875
- contract_weight: bfloat16 [4096, 1024], P(('dp', 'seq')), may hold values from -0.09375 to 0.09375
- modulate_down: bfloat16 [8, 1024, 16], P(None, ('dp', 'seq')), may hold values from -0.1875 to 0.1875
- modulate_up: bfloat16 [8, 16, 6144], P(None, None, ('dp', 'seq')), may hold values from -0.75 to 0.75
- attend_down: bfloat16 [8, 1024, 16], P(None, ('dp', 'seq')), may hold values from -0.1875 to 0.1875
- attend_up: bfloat16 [8, 16, 3072], P(None, None, ('dp', 'seq')), may hold values from -0.75 to 0.75
- project_down: bfloat16 [8, 1024, 16], P(None, ('dp', 'seq')), may hold values from -0.1875 to 0.1875
- project_up: bfloat16 [8, 16, 1024], P(None, None, ('dp', 'seq')), may hold values from -6 to 6
- expand_down: bfloat16 [8, 1024, 16], P(None, ('dp', 'seq')), may hold values from -0.1875 to 0.1875
- expand_up: bfloat16 [8, 16, 4096], P(None, None, ('dp', 'seq')), may hold values from -0.75 to 0.75
- contract_down: bfloat16 [8, 4096, 16], P(None, ('dp', 'seq')), may hold values from -0.09375 to 0.09375
- contract_up: bfloat16 [8, 16, 1024], P(None, None, ('dp', 'seq')), may hold values from -0.75 to 0.75
Outputs:
- block_output: bfloat16 [16, 1024, 1024], P('dp', 'seq')
- input_grad: float32 [16, 1024, 1024], P('dp', 'seq')
- condition_grad: float32 [16, 1024], P('dp')
- modulate_down_grad: float32 [8, 1024, 16], P(None, ('dp', 'seq'))
- modulate_up_grad: float32 [8, 16, 6144], P(None, None, ('dp', 'seq'))
- attend_down_grad: float32 [8, 1024, 16], P(None, ('dp', 'seq'))
- attend_up_grad: float32 [8, 16, 3072], P(None, None, ('dp', 'seq'))
- project_down_grad: float32 [8, 1024, 16], P(None, ('dp', 'seq'))
- project_up_grad: float32 [8, 16, 1024], P(None, None, ('dp', 'seq'))
- expand_down_grad: float32 [8, 1024, 16], P(None, ('dp', 'seq'))
- expand_up_grad: float32 [8, 16, 4096], P(None, None, ('dp', 'seq'))
- contract_down_grad: float32 [8, 4096, 16], P(None, ('dp', 'seq'))
- contract_up_grad: float32 [8, 16, 1024], P(None, None, ('dp', 'seq'))
All inputs are finite; a program needn't handle non-finite values.
Results may differ from a plain program's by a relative error of at most 0.01195.
The roundings to bfloat16 on the way count: a program that leaves them out, or rounds other values in their place, can miss the bound.
Values may be sent and summed in bfloat16 or wider, within the bound.
No kernel may reach another device: no remote copies, remote signals or barrier semaphores. Data moves between devices by JAX's collectives and lax.ppermute only.
A program may use at most 256 MiB of HBM per device.

v0:
```python
import jax
import jax.numpy as jnp
from jax import lax
from jax.sharding import PartitionSpec as P

D = 1024
HEADS = 16
HEAD_DIM = 64
NADAPT = 8


heads_together = 4


def normalize(values):
    centred = values - jnp.mean(values, axis=-1, keepdims=True)
    variance = jnp.mean(centred * centred, axis=-1, keepdims=True)
    return centred * lax.rsqrt(variance + 1e-06)


def gelu_tanh(values):
    return jax.nn.gelu(values, approximate=True)


def product(left, right):
    return jnp.dot(left, right, preferred_element_type=jnp.float32)


def product_back(grads, right):
    return lax.dot_general(
        grads, right, (((grads.ndim - 1,), (1,)), ((), ())), preferred_element_type=jnp.float32
    )


def adapter_middle(inputs, down):
    return jnp.einsum("ltd,ldr->ltr", inputs, down, preferred_element_type=jnp.float32).astype(
        jnp.bfloat16
    )


def adapter_out(middle, upward):
    return jnp.einsum("ltr,lrc->ltc", middle, upward, preferred_element_type=jnp.float32)


def adapter_back(inputs, middle, grads, down, upward):
    grad_middle = jnp.einsum(
        "ltc,lrc->ltr", grads, upward, preferred_element_type=jnp.float32
    ).astype(jnp.bfloat16)
    grad_inputs = jnp.einsum("ltr,ldr->ltd", grad_middle, down, preferred_element_type=jnp.float32)
    grad_upward = jnp.einsum("ltr,ltc->lrc", middle, grads, preferred_element_type=jnp.float32)
    grad_down = jnp.einsum("ltd,ltr->ldr", inputs, grad_middle, preferred_element_type=jnp.float32)
    return (grad_inputs, grad_down, grad_upward)


def select_tables(tables, adapter_choice):
    return [
        jnp.take(tables[member], adapter_choice[:, member // 2], axis=0) for member in range(10)
    ]


def head_block(array, latent, column, span_width):
    picked = lax.dynamic_index_in_dim(array, latent, 0, keepdims=False)
    return lax.dynamic_slice_in_dim(picked, column, span_width, 1)


def heads_back(stacked, latent_count, groups):
    item_rows = stacked.shape[1]
    item_span = stacked.shape[2]
    return (
        stacked.reshape(latent_count, groups, item_rows, item_span)
        .transpose(0, 2, 1, 3)
        .reshape(latent_count, item_rows, groups * item_span)
    )


def attention_forward(queries, keys_all, values_all):
    latent_count = queries.shape[0]
    query_rows = queries.shape[1]
    key_rows = keys_all.shape[1]
    groups = HEADS // heads_together
    span_width = heads_together * HEAD_DIM
    score_scale = HEAD_DIM ** (-0.5)

    def one_group(position):
        latent = position // groups
        column = position % groups * span_width
        query_heads = head_block(queries, latent, column, span_width).reshape(
            query_rows, heads_together, HEAD_DIM
        )
        key_heads = head_block(keys_all, latent, column, span_width).reshape(
            key_rows, heads_together, HEAD_DIM
        )
        value_heads = head_block(values_all, latent, column, span_width).reshape(
            key_rows, heads_together, HEAD_DIM
        )
        scores = (
            jnp.einsum("qhd,khd->hqk", query_heads, key_heads, preferred_element_type=jnp.float32)
            * score_scale
        )
        highest = jnp.max(scores, axis=-1, keepdims=True)
        powered = jnp.exp(scores - highest)
        totals = jnp.sum(powered, axis=-1, keepdims=True)
        probs = (powered / totals).astype(jnp.bfloat16)
        attended = jnp.einsum(
            "hqk,khd->qhd", probs, value_heads, preferred_element_type=jnp.float32
        )
        return (
            attended.reshape(query_rows, span_width).astype(jnp.bfloat16),
            (highest + jnp.log(totals))[..., 0],
        )

    attended, logsum = lax.map(one_group, jnp.arange(latent_count * groups))
    return (heads_back(attended, latent_count, groups), logsum)


def attention_backward(queries, keys_all, values_all, logsum, grad_attended):
    latent_count = queries.shape[0]
    query_rows = queries.shape[1]
    key_rows = keys_all.shape[1]
    groups = HEADS // heads_together
    span_width = heads_together * HEAD_DIM
    score_scale = HEAD_DIM ** (-0.5)

    def one_group(position):
        latent = position // groups
        column = position % groups * span_width
        query_heads = head_block(queries, latent, column, span_width).reshape(
            query_rows, heads_together, HEAD_DIM
        )
        key_heads = head_block(keys_all, latent, column, span_width).reshape(
            key_rows, heads_together, HEAD_DIM
        )
        value_heads = head_block(values_all, latent, column, span_width).reshape(
            key_rows, heads_together, HEAD_DIM
        )
        grad_heads = head_block(grad_attended, latent, column, span_width).reshape(
            query_rows, heads_together, HEAD_DIM
        )
        scores = (
            jnp.einsum("qhd,khd->hqk", query_heads, key_heads, preferred_element_type=jnp.float32)
            * score_scale
        )
        probs = jnp.exp(
            scores - lax.dynamic_index_in_dim(logsum, position, 0, keepdims=False)[..., None]
        )
        grad_probs = jnp.einsum(
            "qhd,khd->hqk", grad_heads, value_heads, preferred_element_type=jnp.float32
        )
        grad_values = jnp.einsum(
            "hqk,qhd->khd",
            probs.astype(jnp.bfloat16),
            grad_heads,
            preferred_element_type=jnp.float32,
        )
        inner = jnp.sum(probs * grad_probs, axis=-1, keepdims=True)
        grad_scores = (probs * (grad_probs - inner)).astype(jnp.bfloat16)
        grad_queries = (
            jnp.einsum("hqk,khd->qhd", grad_scores, key_heads, preferred_element_type=jnp.float32)
            * score_scale
        )
        grad_keys = (
            jnp.einsum("hqk,qhd->khd", grad_scores, query_heads, preferred_element_type=jnp.float32)
            * score_scale
        )
        return (
            grad_queries.reshape(query_rows, span_width),
            grad_keys.reshape(key_rows, span_width),
            grad_values.reshape(key_rows, span_width),
        )

    grad_queries, grad_keys, grad_values = lax.map(one_group, jnp.arange(latent_count * groups))
    grad_queries = heads_back(grad_queries, latent_count, groups)
    grad_keys = heads_back(grad_keys, latent_count, groups)
    grad_values = heads_back(grad_values, latent_count, groups)
    return (grad_queries, jnp.concatenate([grad_keys, grad_values], axis=2))


def local(
    latents,
    condition,
    adapter_choice,
    cotangent,
    modulate_weight,
    attend_weight,
    project_weight,
    expand_weight,
    contract_weight,
    modulate_down,
    modulate_up,
    attend_down,
    attend_up,
    project_down,
    project_up,
    expand_down,
    expand_up,
    contract_down,
    contract_up,
):
    gathered = (
        lax.all_gather(modulate_weight, ("dp", "seq"), axis=0, tiled=True),
        lax.all_gather(attend_weight, ("dp", "seq"), axis=0, tiled=True),
        lax.all_gather(project_weight, ("dp", "seq"), axis=0, tiled=True),
        lax.all_gather(expand_weight, ("dp", "seq"), axis=0, tiled=True),
        lax.all_gather(contract_weight, ("dp", "seq"), axis=0, tiled=True),
        lax.all_gather(modulate_down, ("dp", "seq"), axis=1, tiled=True),
        lax.all_gather(modulate_up, ("dp", "seq"), axis=2, tiled=True),
        lax.all_gather(attend_down, ("dp", "seq"), axis=1, tiled=True),
        lax.all_gather(attend_up, ("dp", "seq"), axis=2, tiled=True),
        lax.all_gather(project_down, ("dp", "seq"), axis=1, tiled=True),
        lax.all_gather(project_up, ("dp", "seq"), axis=2, tiled=True),
        lax.all_gather(expand_down, ("dp", "seq"), axis=1, tiled=True),
        lax.all_gather(expand_up, ("dp", "seq"), axis=2, tiled=True),
        lax.all_gather(contract_down, ("dp", "seq"), axis=1, tiled=True),
        lax.all_gather(contract_up, ("dp", "seq"), axis=2, tiled=True),
    )
    matrices = gathered[:5]
    chosen = select_tables(gathered[5:], adapter_choice)
    tokens = latents.astype(jnp.float32)
    lifted_float, silu_pull = jax.vjp(jax.nn.silu, condition.astype(jnp.float32))
    lifted = lifted_float.astype(jnp.bfloat16)[:, None, :]
    middle_modulate = adapter_middle(lifted, chosen[0])
    modulation = product(lifted, matrices[0]) + adapter_out(middle_modulate, chosen[1])
    shift_attend, scale_attend, gate_attend, shift_expand, scale_expand, gate_expand = jnp.split(
        modulation, 6, axis=2
    )
    normed, norm_pull = jax.vjp(normalize, tokens)
    entering = (normed * (1.0 + scale_attend) + shift_attend).astype(jnp.bfloat16)
    middle_attend = adapter_middle(entering, chosen[2])
    projected = (product(entering, matrices[1]) + adapter_out(middle_attend, chosen[3])).astype(
        jnp.bfloat16
    )
    queries = projected[:, :, :D]
    keys_values = lax.all_gather(projected[:, :, D:], "seq", axis=1, tiled=True)
    keys_all = keys_values[:, :, :D]
    values_all = keys_values[:, :, D:]
    attended, logsum = attention_forward(queries, keys_all, values_all)
    middle_project = adapter_middle(attended, chosen[4])
    branch_attend = product(attended, matrices[2]) + adapter_out(middle_project, chosen[5])
    middle_tokens = tokens + gate_attend * branch_attend
    normed_mlp, norm_pull_mlp = jax.vjp(normalize, middle_tokens)
    entering_mlp = (normed_mlp * (1.0 + scale_expand) + shift_expand).astype(jnp.bfloat16)
    middle_expand = adapter_middle(entering_mlp, chosen[6])
    hidden = product(entering_mlp, matrices[3]) + adapter_out(middle_expand, chosen[7])
    activated_float, gelu_pull = jax.vjp(gelu_tanh, hidden)
    activated = activated_float.astype(jnp.bfloat16)
    middle_contract = adapter_middle(activated, chosen[8])
    branch_mlp = product(activated, matrices[4]) + adapter_out(middle_contract, chosen[9])
    block_output = (middle_tokens + gate_expand * branch_mlp).astype(jnp.bfloat16)
    regathered = (
        lax.all_gather(modulate_weight, ("dp", "seq"), axis=0, tiled=True),
        lax.all_gather(attend_weight, ("dp", "seq"), axis=0, tiled=True),
        lax.all_gather(project_weight, ("dp", "seq"), axis=0, tiled=True),
        lax.all_gather(expand_weight, ("dp", "seq"), axis=0, tiled=True),
        lax.all_gather(contract_weight, ("dp", "seq"), axis=0, tiled=True),
        lax.all_gather(modulate_down, ("dp", "seq"), axis=1, tiled=True),
        lax.all_gather(modulate_up, ("dp", "seq"), axis=2, tiled=True),
        lax.all_gather(attend_down, ("dp", "seq"), axis=1, tiled=True),
        lax.all_gather(attend_up, ("dp", "seq"), axis=2, tiled=True),
        lax.all_gather(project_down, ("dp", "seq"), axis=1, tiled=True),
        lax.all_gather(project_up, ("dp", "seq"), axis=2, tiled=True),
        lax.all_gather(expand_down, ("dp", "seq"), axis=1, tiled=True),
        lax.all_gather(expand_up, ("dp", "seq"), axis=2, tiled=True),
        lax.all_gather(contract_down, ("dp", "seq"), axis=1, tiled=True),
        lax.all_gather(contract_up, ("dp", "seq"), axis=2, tiled=True),
    )
    matrices_back = regathered[:5]
    chosen_back = select_tables(regathered[5:], adapter_choice)
    grad_output = cotangent.astype(jnp.float32)
    grad_gate_expand = jnp.sum(grad_output * branch_mlp, axis=1, keepdims=True)
    grad_branch_mlp = (grad_output * gate_expand).astype(jnp.bfloat16)
    grad_act_inner, grad_contract_down, grad_contract_up = adapter_back(
        activated, middle_contract, grad_branch_mlp, chosen_back[8], chosen_back[9]
    )
    grad_activated = product_back(grad_branch_mlp, matrices_back[4]) + grad_act_inner
    grad_hidden = gelu_pull(grad_activated)[0].astype(jnp.bfloat16)
    grad_mlp_inner, grad_expand_down, grad_expand_up = adapter_back(
        entering_mlp, middle_expand, grad_hidden, chosen_back[6], chosen_back[7]
    )
    grad_entering_mlp = product_back(grad_hidden, matrices_back[3]) + grad_mlp_inner
    grad_shift_expand = jnp.sum(grad_entering_mlp, axis=1, keepdims=True)
    grad_scale_expand = jnp.sum(grad_entering_mlp * normed_mlp, axis=1, keepdims=True)
    grad_middle = grad_output + norm_pull_mlp(grad_entering_mlp * (1.0 + scale_expand))[0]
    grad_gate_attend = jnp.sum(grad_middle * branch_attend, axis=1, keepdims=True)
    grad_branch_attend = (grad_middle * gate_attend).astype(jnp.bfloat16)
    grad_att_inner, grad_project_down, grad_project_up = adapter_back(
        attended, middle_project, grad_branch_attend, chosen_back[4], chosen_back[5]
    )
    grad_attended = (product_back(grad_branch_attend, matrices_back[2]) + grad_att_inner).astype(
        jnp.bfloat16
    )
    grad_queries, grad_key_value_part = attention_backward(
        queries, keys_all, values_all, logsum, grad_attended
    )
    grad_key_value = lax.psum_scatter(grad_key_value_part, "seq", scatter_dimension=1, tiled=True)
    grad_projected = jnp.concatenate([grad_queries, grad_key_value], axis=2).astype(jnp.bfloat16)
    grad_enter_inner, grad_attend_down, grad_attend_up = adapter_back(
        entering, middle_attend, grad_projected, chosen_back[2], chosen_back[3]
    )
    grad_entering = product_back(grad_projected, matrices_back[1]) + grad_enter_inner
    grad_shift_attend = jnp.sum(grad_entering, axis=1, keepdims=True)
    grad_scale_attend = jnp.sum(grad_entering * normed, axis=1, keepdims=True)
    input_grad = grad_middle + norm_pull(grad_entering * (1.0 + scale_attend))[0]
    partial_modulation = jnp.concatenate(
        [
            grad_shift_attend,
            grad_scale_attend,
            grad_gate_attend,
            grad_shift_expand,
            grad_scale_expand,
            grad_gate_expand,
        ],
        axis=2,
    )
    grad_modulation = lax.psum(partial_modulation, "seq").astype(jnp.bfloat16)
    grad_lift_inner, grad_modulate_down, grad_modulate_up = adapter_back(
        lifted, middle_modulate, grad_modulation, chosen_back[0], chosen_back[1]
    )
    grad_lifted = product_back(grad_modulation, matrices_back[0]) + grad_lift_inner
    condition_grad = silu_pull(grad_lifted[:, 0, :])[0]
    keep_share = (lax.axis_index("seq") == 0).astype(jnp.float32)
    grad_modulate_down = grad_modulate_down * keep_share
    grad_modulate_up = grad_modulate_up * keep_share

    def to_table(member, per_latent):
        picked = (
            adapter_choice[:, member // 2][:, None] == jnp.arange(NADAPT, dtype=jnp.int32)[None, :]
        ).astype(jnp.float32)
        return jnp.einsum("la,lxy->axy", picked, per_latent, precision=lax.Precision.HIGHEST)

    table_grads = [
        to_table(member, grad)
        for member, grad in enumerate(
            [
                grad_modulate_down,
                grad_modulate_up,
                grad_attend_down,
                grad_attend_up,
                grad_project_down,
                grad_project_up,
                grad_expand_down,
                grad_expand_up,
                grad_contract_down,
                grad_contract_up,
            ]
        )
    ]
    owned = (
        lax.psum_scatter(table_grads[0], ("dp", "seq"), scatter_dimension=1, tiled=True),
        lax.psum_scatter(table_grads[1], ("dp", "seq"), scatter_dimension=2, tiled=True),
        lax.psum_scatter(table_grads[2], ("dp", "seq"), scatter_dimension=1, tiled=True),
        lax.psum_scatter(table_grads[3], ("dp", "seq"), scatter_dimension=2, tiled=True),
        lax.psum_scatter(table_grads[4], ("dp", "seq"), scatter_dimension=1, tiled=True),
        lax.psum_scatter(table_grads[5], ("dp", "seq"), scatter_dimension=2, tiled=True),
        lax.psum_scatter(table_grads[6], ("dp", "seq"), scatter_dimension=1, tiled=True),
        lax.psum_scatter(table_grads[7], ("dp", "seq"), scatter_dimension=2, tiled=True),
        lax.psum_scatter(table_grads[8], ("dp", "seq"), scatter_dimension=1, tiled=True),
        lax.psum_scatter(table_grads[9], ("dp", "seq"), scatter_dimension=2, tiled=True),
    )
    return (
        block_output,
        input_grad,
        condition_grad,
        owned[0],
        owned[1],
        owned[2],
        owned[3],
        owned[4],
        owned[5],
        owned[6],
        owned[7],
        owned[8],
        owned[9],
    )


def solution(mesh):
    placed = (
        P("dp", "seq", None),
        P("dp", None),
        P("dp", None),
        P("dp", "seq", None),
        P(("dp", "seq"), None),
        P(("dp", "seq"), None),
        P(("dp", "seq"), None),
        P(("dp", "seq"), None),
        P(("dp", "seq"), None),
        P(None, ("dp", "seq"), None),
        P(None, None, ("dp", "seq")),
        P(None, ("dp", "seq"), None),
        P(None, None, ("dp", "seq")),
        P(None, ("dp", "seq"), None),
        P(None, None, ("dp", "seq")),
        P(None, ("dp", "seq"), None),
        P(None, None, ("dp", "seq")),
        P(None, ("dp", "seq"), None),
        P(None, None, ("dp", "seq")),
    )
    return jax.shard_map(
        local,
        mesh=mesh,
        in_specs=placed,
        out_specs=(
            P("dp", "seq", None),
            P("dp", "seq", None),
            P("dp", None),
            P(None, ("dp", "seq"), None),
            P(None, None, ("dp", "seq")),
            P(None, ("dp", "seq"), None),
            P(None, None, ("dp", "seq")),
            P(None, ("dp", "seq"), None),
            P(None, None, ("dp", "seq")),
            P(None, ("dp", "seq"), None),
            P(None, None, ("dp", "seq")),
            P(None, ("dp", "seq"), None),
            P(None, None, ("dp", "seq")),
        ),
        check_vma=False,
    )
```

profile of v0, /device:TPU:0, one launch (start us, length us, event | category | flops | bytes accessed | tf_op | source)
XLA Modules:
  0.0 2101.9 jit_solution(3389181017574580662)
XLA Ops:
  18.8 56.4 %all_gather.67 = bf16[8,1024,16]{2,0,1:T(8,128)(2,1)S(1)} all-gather(bf16[8,32,16]{2,0,1:T(8,128)(2,1)S(1)} %copy.58), channel_id=1, replica_groups=mesh['dp'=16,'seq'=2] {'dp','seq'}, dimensions={1}, use_global_device_ids=true | all-gather | bytes 270336 | tf_op jit(solution)/shard_map/all_gather | solution.py:207
  76.0 55.5 %all_gather.64 = bf16[8,1024,16]{2,0,1:T(8,128)(2,1)S(1)} all-gather(bf16[8,32,16]{2,0,1:T(8,128)(2,1)S(1)} %copy.54), channel_id=1, replica_groups=mesh['dp'=16,'seq'=2] {'dp','seq'}, dimensions={1}, use_global_device_ids=true | all-gather | bytes 270336 | tf_op jit(solution)/shard_map/all_gather | solution.py:205
  132.4 95.7 %all_gather.68 = bf16[8,16,3072]{1,0,2:T(8,128)(2,1)S(1)} all-gather(bf16[8,16,96]{1,0,2:T(8,128)(2,1)S(1)} %copy.60), channel_id=1, replica_groups=mesh['dp'=16,'seq'=2] {'dp','seq'}, dimensions={2}, use_global_device_ids=true | all-gather | bytes 811008 | tf_op jit(solution)/shard_map/all_gather | solution.py:208
  233.6 8.7 constant_dynamic-slice_fusion.13
  242.3 5.8 copy.95
  248.3 11.5 all-gather.10.cloned.1.call-done
  259.8 6.3 fusion.99
  267.1 66.8 %all-gather.14.cloned.1.call-done = bf16[1024,3072]{1,0:T(8,128)(2,1)} async-done(((bf16[32,3072]{1,0:T(8,128)(2,1)}), bf16[1024,3072]{1,0:T(8,128)(2,1)}) %all-gather.14.cloned.1.call-update) | async-done | bytes 6291472 | tf_op jit(solution)/shard_map/all_gather | solution.py:201
  333.9 5.5 fusion.143
  352.6 50.6 %all_gather.78 = bf16[8,16,1024]{1,0,2:T(8,128)(2,1)S(1)} all-gather(bf16[8,16,32]{1,0,2:T(8,128)(2,1)S(1)} %copy.71), channel_id=1, replica_groups=mesh['dp'=16,'seq'=2] {'dp','seq'}, dimensions={2}, use_global_device_ids=true | all-gather | bytes 270336 | tf_op jit(solution)/shard_map/all_gather | solution.py:214
  404.0 47.3 %all_gather.74 = bf16[8,1024,16]{2,0,1:T(8,128)(2,1)S(1)} all-gather(bf16[8,32,16]{2,0,1:T(8,128)(2,1)S(1)} %copy.69), channel_id=1, replica_groups=mesh['dp'=16,'seq'=2] {'dp','seq'}, dimensions={1}, use_global_device_ids=true | all-gather | bytes 270336 | tf_op jit(solution)/shard_map/all_gather | solution.py:211
  452.1 45.6 %all_gather.72 = bf16[8,16,1024]{1,0,2:T(8,128)(2,1)S(1)} all-gather(bf16[8,16,32]{1,0,2:T(8,128)(2,1)S(1)} %copy.67), channel_id=1, replica_groups=mesh['dp'=16,'seq'=2] {'dp','seq'}, dimensions={2}, use_global_device_ids=true | all-gather | bytes 270336 | tf_op jit(solution)/shard_map/all_gather | solution.py:210
  498.5 49.2 %all_gather.71 = bf16[8,1024,16]{2,0,1:T(8,128)(2,1)S(1)} all-gather(bf16[8,32,16]{2,0,1:T(8,128)(2,1)S(1)} %copy.65), channel_id=1, replica_groups=mesh['dp'=16,'seq'=2] {'dp','seq'}, dimensions={1}, use_global_device_ids=true | all-gather | bytes 270336 | tf_op jit(solution)/shard_map/all_gather | solution.py:209
  552.0 10.1 fusion.47
  562.1 4.7 fusion.137
  566.9 2.9 copy.64
  569.7 4.0 copy.62
  573.7 43.8 %while.36 = (s32[]{:T(128)}, bf16[4,512,256]{1,2,0:T(8,128)(2,1)}, f32[4,4,512]{2,1,0:T(4,128)S(1)}, s32[4]{0:T(128)S(1)}, bf16[1,1024,1024]{1,2,0:T(8,128)(2,1)...) while((s32[]{:T(128)}, bf16[4,512,256]{1,2,0:T(8,128)(2,1)}, ...), condition=%wide.region_5.9_spmd, body=%wide.region_2.8_spmd.sunk | while | flops 555874304 | bytes 29950268 | solution.py:112
  619.7 3.2 fusion.144
  626.0 10.2 fusion.145
  636.2 8.7 multiply_convert_fusion.1
  645.0 41.7 %all-gather.26.cloned.1.call-done = bf16[8,4096,16]{1,2,0:T(8,128)(2,1)} async-done(((bf16[8,128,16]{1,2,0:T(8,128)(2,1)}), bf16[8,4096,16]{1,2,0:T(8,128)(2,1)}) %all-gather.26.cloned.1.call-update) | async-done | bytes 1048592 | tf_op jit(solution)/shard_map/all_gather | solution.py:213
  686.7 9.9 fusion.16
  696.6 8.5 fusion.147
  714.2 79.1 %while.37 = (s32[]{:T(128)}, bf16[4,512,256]{1,2,0:T(8,128)(2,1)}, f32[4,1024,256]{1,2,0:T(8,128)}, f32[4,1024,256]{1,2,0:T(8,128)}, s32[4]{0:T(128)S(1)}, /*ind...) while((s32[]{:T(128)}, bf16[4,512,256]{1,2,0:T(8,128)(2,1)}, ...), condition=%wide.region_12.19_spmd, body=%wide.region_10.18_spmd.sunk | while | flops 1367865344 | bytes 76341624 | solution.py:171
  724.8 2.9 multiply_reduce_fusion.6
  744.5 2.9 multiply_reduce_fusion.6
  764.2 2.9 multiply_reduce_fusion.6
  783.9 2.9 multiply_reduce_fusion.6
  793.3 8.4 pad_maximum_fusion
  803.5 2.7 copy.85
  806.2 4.4 reshape.944
  811.0 3.1 copy.87
  814.2 4.5 reshape.946
  819.4 3.4 convolution_convert_fusion.7
  823.2 2.7 copy.91
  825.9 4.1 reshape.950
  832.9 2.7 copy.89
  835.6 4.0 reshape.948
  839.6 10.5 fusion.146
  855.0 5.7 fusion.43
  863.6 3.6 copy.81
  867.2 4.1 reshape.940
  871.4 5.9 fusion.30
  877.4 4.2 psum.7
  882.0 2.7 copy.77
  884.7 4.1 reshape.936
  891.3 6.8 copy.83
  898.2 8.9 reshape.942
  907.7 12.2 copy.79
  919.9 16.3 reshape.938
  936.9 2.8 fusion.154
  941.4 2.8 fusion.151
  945.9 10.0 reduce-scatter.42.cloned.1.call-done
  957.4 130.5 %reduce-scatter.44.cloned.1.call-done = f32[32,128]{1,0:T(8,128)} async-done(((f32[1024,128]{1,0:T(8,128)}), f32[32,128]{1,0:T(8,128)}) %reduce-scatter.44.cloned.1.call-update) | async-done | bytes 16400
  1089.5 130.5 %reduce-scatter.48.cloned.1.call-done = f32[32,128]{1,0:T(8,128)} async-done(((f32[1024,128]{1,0:T(8,128)}), f32[32,128]{1,0:T(8,128)}) %reduce-scatter.48.cloned.1.call-update) | async-done | bytes 16400
  1221.5 130.5 %reduce-scatter.46.cloned.1.call-done = f32[32,128]{1,0:T(8,128)} async-done(((f32[1024,128]{1,0:T(8,128)}), f32[32,128]{1,0:T(8,128)}) %reduce-scatter.46.cloned.1.call-update) | async-done | bytes 16400
  1353.7 8.0 fusion.80
  1362.3 121.7 %reduce-scatter.38.cloned.1.call-done = f32[32,128]{1,0:T(8,128)} async-done(((f32[1024,128]{1,0:T(8,128)}), f32[32,128]{1,0:T(8,128)}) %reduce-scatter.38.cloned.1.call-update) | async-done | bytes 16400
  1485.6 130.5 %reduce-scatter.34.cloned.1.call-done = f32[32,128]{1,0:T(8,128)} async-done(((f32[1024,128]{1,0:T(8,128)}), f32[32,128]{1,0:T(8,128)}) %reduce-scatter.34.cloned.1.call-update) | async-done | bytes 16400
  1617.6 97.4 %reduce-scatter.40.cloned.1.call-done = f32[96,128]{1,0:T(8,128)} async-done(((f32[3072,128]{1,0:T(8,128)}), f32[96,128]{1,0:T(8,128)}) %reduce-scatter.40.cloned.1.call-update) | async-done | bytes 49168
  1716.8 105.0 %reduce-scatter.36.cloned.1.call-done = f32[192,128]{1,0:T(8,128)} async-done(((f32[6144,128]{1,0:T(8,128)}), f32[192,128]{1,0:T(8,128)}) %reduce-scatter.36.cloned.1.call-update) | async-done | bytes 98320
  1823.9 136.0 %reduce-scatter.32.cloned.1.call-done = f32[8,128,16]{1,2,0:T(8,128)} async-done(((f32[8,4096,16]{1,2,0:T(8,128)}), f32[8,128,16]{1,2,0:T(8,128)}) %reduce-scatter.32.cloned.1.call-update) | async-done | bytes 65552 | tf_op jit(solution)/shard_map/reduce_scatter | solution.py:356
  1960.0 134.9 %reduce-scatter.30.cloned.1.call-done = f32[8,16,128]{2,1,0:T(8,128)} async-done(((f32[8,16,4096]{2,1,0:T(8,128)}), f32[8,16,128]{2,1,0:T(8,128)}) %reduce-scatter.30.cloned.1.call-update) | async-done | bytes 65552 | tf_op jit(solution)/shard_map/reduce_scatter | solution.py:355
  (386 shorter events, 170.0 us)
Async XLA Ops:
  7.2 226.4 %all-gather.12.cloned.1.call-start = ((), (), s32[]{:S(2)}) async-start(), calls=%async_computation.12 | async-start | bytes 12976128 | tf_op jit(solution)/shard_map/all_gather | solution.py:206
  9.1 250.8 %all-gather.10.cloned.1.call-start = ((), (), s32[]{:S(2)}) async-start(), calls=%async_computation.11 | async-start | bytes 12976128 | tf_op jit(solution)/shard_map/all_gather | solution.py:200
  9.8 324.1 %all-gather.14.cloned.1.call-start = ((), (), s32[]{:S(2)}) async-start(), calls=%async_computation.13 | async-start | bytes 6488064 | tf_op jit(solution)/shard_map/all_gather | solution.py:201
  10.5 541.4 %all-gather.24.cloned.1.call-start = ((), (), s32[]{:S(2)}) async-start(), calls=%async_computation.18 | async-start | bytes 8650752 | tf_op jit(solution)/shard_map/all_gather | solution.py:204
  11.1 551.0 %all-gather.16.cloned.1.call-start = ((), (), s32[]{:S(2)}) async-start(), calls=%async_computation.14 | async-start | bytes 6291456 | tf_op jit(solution)/shard_map/all_gather | solution.py:233
  76.0 190.7 %copy-start.24 = (bf16[1,1024,16]{1,2,0:T(8,128)(2,1)}, bf16[1,1024,16]{1,2,0:T(8,128)(2,1)S(1)}, u32[]{:S(2)}) copy-start(bf16[1,1024,16]{1,2,0:T(8,128)(2,1)S(1)} %copy.96) | copy-start | bytes 98308
  132.4 100.6 %copy-start.52 = (bf16[1,1024,16]{1,2,0:T(8,128)(2,1)}, bf16[1,1024,16]{1,2,0:T(8,128)(2,1)S(1)}, u32[]{:S(2)}) copy-start(bf16[1,1024,16]{1,2,0:T(8,128)(2,1)S(1)} %copy.94) | copy-start | bytes 98308
  228.1 4.2 copy-start.42
  231.1 108.4 %copy-start.22 = (bf16[1,16,3072]{2,1,0:T(8,128)(2,1)}, bf16[1,16,3072]{2,1,0:T(8,128)(2,1)S(1)}, u32[]{:S(2)}) copy-start(bf16[1,16,3072]{2,1,0:T(8,128)(2,1)S(1)} %copy.97) | copy-start | bytes 294916
  231.3 34.9 %copy-start.34 = (f32[512]{0:T(512)}, f32[512]{0:T(512)S(1)}, u32[]{:S(2)}) copy-start(f32[512]{0:T(512)S(1)} %broadcast_multiply_fusion.11) | copy-start | bytes 6148
  232.3 33.9 %copy-start.40 = (f32[512]{0:T(512)}, f32[512]{0:T(512)S(1)}, u32[]{:S(2)}) copy-start(f32[512]{0:T(512)S(1)} %fusion.107) | copy-start | bytes 6148
  232.9 26.9 %copy-start.44 = (f32[1,1024]{1,0:T(1,128)}, f32[1,1024]{1,0:T(1,128)S(1)}, u32[]{:S(2)}) copy-start(f32[1,1024]{1,0:T(1,128)S(1)} %get-tuple-element.401) | copy-start | bytes 12292
  248.1 18.0 copy-start.26
  266.2 73.2 %copy-start.32 = (f32[1,1,1024]{2,1,0:T(1,128)}, f32[1,1,1024]{2,1,0:T(1,128)S(1)}, u32[]{:S(2)}) copy-start(f32[1,1,1024]{2,1,0:T(1,128)S(1)} %get-tuple-element.422) | copy-start | bytes 12292
  266.2 285.8 %copy-start.46 = (f32[1,1,1024]{2,1,0:T(1,128)}, f32[1,1,1024]{2,1,0:T(1,128)S(1)}, u32[]{:S(2)}) copy-start(f32[1,1,1024]{2,1,0:T(1,128)S(1)} %get-tuple-element.418) | copy-start | bytes 12292
  266.7 72.8 %copy-start.15 = (bf16[512,1024]{1,0:T(8,128)(2,1)}, bf16[512,1024]{1,0:T(8,128)(2,1)S(1)}, u32[]{:S(2)}) copy-start(bf16[512,1024]{1,0:T(8,128)(2,1)S(1)} %fusion.41) | copy-start | bytes 3145732
  267.1 72.4 %copy-start.36 = (bf16[512,16]{0,1:T(8,128)(2,1)}, bf16[512,16]{0,1:T(8,128)(2,1)S(1)}, u32[]{:S(2)}) copy-start(bf16[512,16]{0,1:T(8,128)(2,1)S(1)} %convolution_convert_fusion.5) | copy-start | bytes 49156
  342.2 9.9 copy-start.48
  342.2 10.0 copy-start.49
  342.2 10.1 copy-start.50
  342.2 10.3 copy-start.51
  343.7 276.0 %all-gather.18.cloned.1.call-start = ((), (), s32[]{:S(2)}) async-start(), calls=%async_computation.15 | async-start | bytes 2162688 | tf_op jit(solution)/shard_map/all_gather | solution.py:202
  344.3 281.7 %all-gather.20.cloned.1.call-start = ((), (), s32[]{:S(2)}) async-start(), calls=%async_computation.16 | async-start | bytes 8650752 | tf_op jit(solution)/shard_map/all_gather | solution.py:203
  345.0 291.2 %all-gather.22.cloned.1.call-start = ((), (), s32[]{:S(2)}) async-start(), calls=%async_computation.17 | async-start | bytes 1081344 | tf_op jit(solution)/shard_map/all_gather | solution.py:212
  345.8 340.9 %all-gather.26.cloned.1.call-start = ((), (), s32[]{:S(2)}) async-start(), calls=%async_computation.19 | async-start | bytes 1081344 | tf_op jit(solution)/shard_map/all_gather | solution.py:213
  346.5 503.6 %reduce-scatter.28.cloned.1.call-start = ((), (), s32[]{:S(2)}) async-start(), calls=%async_computation.20 | async-start | bytes 12582912 | tf_op jit(solution)/shard_map/reduce_scatter | solution.py:294
  403.9 147.6 %copy-start.30 = (bf16[1,16,1024]{2,1,0:T(8,128)(2,1)}, bf16[1,16,1024]{2,1,0:T(8,128)(2,1)S(1)}, u32[]{:S(2)}) copy-start(bf16[1,16,1024]{2,1,0:T(8,128)(2,1)S(1)} %copy.101) | copy-start | bytes 98308
  498.2 52.0 %slice-start = ((bf16[1,512,3072]{2,1,0:T(8,128)(2,1)}), bf16[1,512,1024]{2,1,0:T(8,128)(2,1)S(1)}, s32[]{:S(2)}) async-start(bf16[1,512,3072]{2,1,0:T(8,128)(2,1)} %copy-done.10), calls=%async_computation.31 | async-start | bytes 2097152 | tf_op jit(solution)/shard_map/slice | solution.py:232
  552.0 134.7 %copy-start.58 = (bf16[512,16]{0,1:T(8,128)(2,1)}, bf16[512,16]{0,1:T(8,128)(2,1)S(1)}, u32[]{:S(2)}) copy-start(bf16[512,16]{0,1:T(8,128)(2,1)S(1)} %convolution_convert_fusion.3) | copy-start | bytes 49156
  617.5 5.4 copy-start.5
  619.7 5.1 copy-start.28
  624.9 83.8 %copy-start = (f32[1,512,1024]{2,1,0:T(8,128)}, f32[1,512,1024]{2,1,0:T(8,128)S(1)}, u32[]{:S(2)}) copy-start(f32[1,512,1024]{2,1,0:T(8,128)S(1)} %get-tuple-element.405) | copy-start | bytes 6291460
  625.6 10.6 copy-start.17
  626.0 10.2 copy-start.38
  696.6 8.5 copy-start.9
  801.8 154.1 %reduce-scatter.42.cloned.1.call-start = ((), (), s32[]{:S(2)}) async-start(), calls=%async_computation.27 | async-start | bytes 540672
  806.2 4.5 copy-start.29
  810.6 277.4 %reduce-scatter.44.cloned.1.call-start = ((), (), s32[]{:S(2)}) async-start(), calls=%async_computation.28 | async-start | bytes 540672
  818.7 4.1 copy-start.13
  818.7 4.2 copy-start.47
  818.7 401.3 %reduce-scatter.48.cloned.1.call-start = ((), (), s32[]{:S(2)}) async-start(), calls=%async_computation.30 | async-start | bytes 540672
  825.9 4.6 copy-start.61
  825.9 6.4 copy-start.8
  825.9 6.6 copy-start.18
  830.1 522.0 %reduce-scatter.46.cloned.1.call-start = ((), (), s32[]{:S(2)}) async-start(), calls=%async_computation.29 | async-start | bytes 540672
  839.6 644.4 %reduce-scatter.38.cloned.1.call-start = ((), (), s32[]{:S(2)}) async-start(), calls=%async_computation.25 | async-start | bytes 540672
  852.7 8.0 copy-start.19
  855.0 5.7 copy-start.3
  855.0 5.8 copy-start.25
  855.0 5.8 copy-start.33
  855.0 5.8 copy-start.35
  871.3 6.0 copy-start.60
  871.4 10.3 copy-start.27
  877.3 738.7 %reduce-scatter.34.cloned.1.call-start = ((), (), s32[]{:S(2)}) async-start(), calls=%async_computation.23 | async-start | bytes 540672
  884.7 4.3 copy-start.20
  884.7 4.3 copy-start.37
  888.8 826.2 %reduce-scatter.40.cloned.1.call-start = ((), (), s32[]{:S(2)}) async-start(), calls=%async_computation.26 | async-start | bytes 1622016
  898.2 9.0 copy-start.62
  907.2 914.6 %reduce-scatter.36.cloned.1.call-start = ((), (), s32[]{:S(2)}) async-start(), calls=%async_computation.24 | async-start | bytes 3244032
  936.2 1023.7 %reduce-scatter.32.cloned.1.call-start = ((), (), s32[]{:S(2)}) async-start(), calls=%async_computation.22 | async-start | bytes 2162688 | tf_op jit(solution)/shard_map/reduce_scatter | solution.py:356
  941.4 1153.5 %reduce-scatter.30.cloned.1.call-start = ((), (), s32[]{:S(2)}) async-start(), calls=%async_computation.21 | async-start | bytes 2162688 | tf_op jit(solution)/shard_map/reduce_scatter | solution.py:355
  944.3 409.3 %copy-start.53 = (bf16[1,1024,16]{1,2,0:T(8,128)(2,1)S(1)}, bf16[1,1024,16]{1,2,0:T(8,128)(2,1)}, u32[]{:S(2)}) copy-start(bf16[1,1024,16]{1,2,0:T(8,128)(2,1)} %copy-done.52) | copy-start | bytes 98308
  1353.7 8.0 copy-start.43
  1353.7 8.0 copy-start.45
  (21 other events, 49.3 us)
Sparse Core Ops, SparseCore 0:
  11.4 124.0 all-gather.11
  138.4 121.3 all-gather.9
  262.7 71.1 all-gather.13
  336.6 88.6 all-gather.23
  427.3 13.6 all-gather.15
  443.8 60.0 all-gather.17
  506.7 78.5 all-gather.19
  588.1 47.4 all-gather.21
  638.5 48.1 all-gather.25
  801.9 16.3 reduce-scatter.27
  820.6 135.2 reduce-scatter.41
  958.0 129.9 reduce-scatter.43
  1090.3 129.6 reduce-scatter.47
  1222.1 129.8 reduce-scatter.45
  1354.2 129.7 reduce-scatter.37
  1486.1 129.8 reduce-scatter.33
  1622.0 92.9 reduce-scatter.39
  1721.2 100.5 reduce-scatter.35
  1824.7 135.1 reduce-scatter.31
  1962.6 132.2 reduce-scatter.29
where the time goes:
time: 2120 us; the launch traced here: 2100 us
  waiting for transfers between devices  1250 us (59%)
  blocking collectives  405 us (19%)
  local copies, waits for them, and re-layouts  191 us (9%)
  matrix products  167 us (8%)
  other arithmetic  40.5 us (2%)
  between operations  24.5 us (1%)
  loops' own time  21.2 us (1%)
    unnamed x28, waiting for transfers between devices  861 us
    reduce_scatter x1, waiting for transfers between devices, local(): lax.psum_scatter(table_grads[8], ('dp', 'seq'), scatter_dimension=1, tile...  136 us
    reduce_scatter x1, waiting for transfers between devices, local(): lax.psum_scatter(table_grads[7], ('dp', 'seq'), scatter_dimension=2, tile...  135 us
    unnamed x181, local copies, waits for them, and re-layouts  122 us
    all_gather x1, blocking collectives, local(): lax.all_gather(attend_up, ('dp', 'seq'), axis=2, tiled=True)  95.7 us
    all_gather x1, waiting for transfers between devices, local(): lax.all_gather(attend_weight, ('dp', 'seq'), axis=0, tiled=True)  66.8 us
    all_gather x1, blocking collectives, local(): lax.all_gather(attend_down, ('dp', 'seq'), axis=1, tiled=True)  56.4 us
    all_gather x1, blocking collectives, local(): lax.all_gather(modulate_down, ('dp', 'seq'), axis=1, tiled=True)  55.5 us
  transfers between devices with their start and end apart: 20, of which 13 were waited for; matrix products, arithmetic and copies ran while one was open for 14% of the time, Pallas kernels for 0%

commit v1 on v0

v1 whole, which is shorter than its diff:
```python
import jax
import jax.numpy as jnp
from jax import lax
from jax.experimental import pallas as pl
from jax.experimental.pallas import tpu as pltpu
from jax.sharding import PartitionSpec as P

D = 1024
HEADS = 16
HEAD_DIM = 64
FF = 4096
RANK = 16
bf16 = jnp.bfloat16
f32 = jnp.float32
EPSILON = 1e-06
LOG2E = 1.4426950408889634
GROUP = 256
TILE = 512
GROUPS = 32
NADAPT = 8
CHUNK = 128
VMEM_LIMIT = 56 * 1024 * 1024
SHIFT_ATTEND, SCALE_ATTEND, GATE_ATTEND, SHIFT_EXPAND, SCALE_EXPAND, GATE_EXPAND = range(6)


def product(left, right):
    return lax.dot_general(left, right, (((1,), (0,)), ((), ())), preferred_element_type=f32)


def product_back(grads, right):
    return lax.dot_general(grads, right, (((1,), (1,)), ((), ())), preferred_element_type=f32)


def product_rows(left, right):
    return lax.dot_general(left, right, (((0,), (0,)), ((), ())), preferred_element_type=f32)


def normalize(values):
    centred = values - jnp.mean(values, axis=-1, keepdims=True)
    variance = jnp.mean(centred * centred, axis=-1, keepdims=True)
    inverse = lax.rsqrt(variance + EPSILON)
    return centred * inverse, inverse


def normalize_back(grads, normed, inverse):
    mean = jnp.mean(grads, axis=-1, keepdims=True)
    along = jnp.mean(grads * normed, axis=-1, keepdims=True)
    return (grads - mean - normed * along) * inverse


def each_chunk(rows, step):
    def body(position, carry):
        step(pl.ds(pl.multiple_of(position * CHUNK, CHUNK), CHUNK))
        return carry

    lax.fori_loop(0, rows // CHUNK, body, 0)


def whole(shape):
    return pl.BlockSpec(shape, lambda *_: (0,) * len(shape))


def params():
    return pltpu.CompilerParams(vmem_limit_bytes=VMEM_LIMIT)


def enter_kernel(latents, modulation, weight, down, up, projected, entering, middle):
    @pl.when(pl.program_id(0) == 0)
    def _():
        def step(rows):
            normed, _ = normalize(latents[rows].astype(f32))
            values = normed * (1.0 + modulation[SCALE_ATTEND : SCALE_ATTEND + 1]) + modulation[
                SHIFT_ATTEND : SHIFT_ATTEND + 1
            ]
            values = values.astype(bf16)
            entering[rows] = values
            middle[rows] = product_back(values, down[...]).astype(bf16)

        each_chunk(latents.shape[0], step)

    projected[...] = (
        product(entering[...], weight[...].reshape(D, TILE)) + product(middle[...], up[...])
    ).astype(bf16)


def enter(latents, modulation, weight, down, up):
    rows = latents.shape[0]
    groups, deep, columns = weight.shape
    return pl.pallas_call(
        enter_kernel,
        grid=(columns // TILE,),
        in_specs=[
            whole((rows, D)),
            whole(modulation.shape),
            pl.BlockSpec((groups, deep, TILE), lambda j: (0, 0, j)),
            whole(down.shape),
            pl.BlockSpec((RANK, TILE), lambda j: (0, j)),
        ],
        out_specs=[
            pl.BlockSpec((rows, TILE), lambda j: (0, j)),
            whole((rows, D)),
            whole((rows, RANK)),
        ],
        out_shape=[
            jax.ShapeDtypeStruct((rows, columns), bf16),
            jax.ShapeDtypeStruct((rows, D), bf16),
            jax.ShapeDtypeStruct((rows, RANK), bf16),
        ],
        compiler_params=params(),
        name="enter",
    )(latents, modulation, weight, down, up)


def head_mask(head, dtype=jnp.bool_):
    lane = lax.broadcasted_iota(jnp.int32, (1, GROUP), 1)
    return jnp.logical_and(lane >= head * HEAD_DIM, lane < (head + 1) * HEAD_DIM)


def attend_kernel(queries, keys_near, values_near, keys_far, values_far, attended, logsum):
    rows = queries.shape[0]
    block = 256
    scale = HEAD_DIM ** (-0.5)
    lane = lax.broadcasted_iota(jnp.int32, (1, 128), 1)

    for start in range(0, rows, block):
        here = pl.ds(start, block)
        q = queries[here] * jnp.asarray(scale, bf16)
        total = jnp.zeros((block, GROUP), f32)
        sums = jnp.zeros((block, 128), f32)
        for head in range(GROUP // HEAD_DIM):
            mask = head_mask(head)
            mine = jnp.where(mask, q, jnp.zeros_like(q))
            near = product_back(mine, keys_near[...])
            far = product_back(mine, keys_far[...])
            highest = jnp.maximum(
                jnp.max(near, axis=1, keepdims=True), jnp.max(far, axis=1, keepdims=True)
            )
            near = jnp.exp2((near - highest) * LOG2E)
            far = jnp.exp2((far - highest) * LOG2E)
            denominator = jnp.sum(near, axis=1, keepdims=True) + jnp.sum(
                far, axis=1, keepdims=True
            )
            share = 1.0 / denominator
            out = product((near * share).astype(bf16), values_near[...]) + product(
                (far * share).astype(bf16), values_far[...]
            )
            total = jnp.where(mask, out, total)
            sums = jnp.where(lane == head, highest + jnp.log(denominator), sums)
        attended[here] = total.astype(bf16)
        logsum[0, here] = sums


def attend(projected, other):
    rows = projected.shape[0]
    groups = D // GROUP

    def at(first):
        return pl.BlockSpec((rows, GROUP), lambda g: (0, first + g))

    return pl.pallas_call(
        attend_kernel,
        grid=(groups,),
        in_specs=[at(0), at(groups), at(2 * groups), at(0), at(groups)],
        out_specs=[at(0), pl.BlockSpec((1, rows, 128), lambda g: (g, 0, 0))],
        out_shape=[
            jax.ShapeDtypeStruct((rows, D), bf16),
            jax.ShapeDtypeStruct((groups, rows, 128), f32),
        ],
        compiler_params=params(),
        name="attend",
    )(projected, projected, projected, other, other)


def attend_back_kernel(
    queries, keys_near, values_near, keys_far, values_far, grads, logsum,
    grad_queries, grad_near, grad_far, keys_sum, values_sum
):
    rows = queries.shape[0]
    block = 256
    scale = HEAD_DIM ** (-0.5)
    scaled = queries[...] * jnp.asarray(scale, bf16)
    scaled_t = scaled.T
    grads_t = grads[...].T
    for start in range(0, rows, block):
        here = slice(start, start + block)
        q = scaled[here]
        g = grads[here]
        total = jnp.zeros((block, GROUP), f32)
        for head in range(GROUP // HEAD_DIM):
            mask = head_mask(head)
            part = slice(head * HEAD_DIM, (head + 1) * HEAD_DIM)
            mine = jnp.where(mask, q, jnp.zeros_like(q))
            mine_g = jnp.where(mask, g, jnp.zeros_like(g))
            shift = logsum[0, here, head : head + 1]
            pn = jnp.exp2((product_back(mine, keys_near[...]) - shift) * LOG2E)
            pf = jnp.exp2((product_back(mine, keys_far[...]) - shift) * LOG2E)
            gn = product_back(mine_g, values_near[...])
            gf = product_back(mine_g, values_far[...])
            inner = jnp.sum(pn * gn, axis=1, keepdims=True) + jnp.sum(
                pf * gf, axis=1, keepdims=True
            )
            sn = (pn * (gn - inner)).astype(bf16)
            sf = (pf * (gf - inner)).astype(bf16)
            out = product(sn, keys_near[...]) + product(sf, keys_far[...])
            total = jnp.where(mask, out * scale, total)
            vn = product(grads_t[part, here], pn.astype(bf16))
            vf = product(grads_t[part, here], pf.astype(bf16))
            kn = product(scaled_t[part, here], sn)
            kf = product(scaled_t[part, here], sf)
            if start == 0:
                values_sum[part, :rows] = vn
                values_sum[part, rows:] = vf
                keys_sum[part, :rows] = kn
                keys_sum[part, rows:] = kf
            else:
                values_sum[part, :rows] += vn
                values_sum[part, rows:] += vf
                keys_sum[part, :rows] += kn
                keys_sum[part, rows:] += kf
        grad_queries[here] = total.astype(bf16)
    grad_near[0] = keys_sum[:, :rows].T
    grad_near[1] = values_sum[:, :rows].T
    grad_far[0] = keys_sum[:, rows:].T
    grad_far[1] = values_sum[:, rows:].T


def attend_back(projected, other, grads, logsum):
    rows = projected.shape[0]
    groups = D // GROUP

    def at(first):
        return pl.BlockSpec((rows, GROUP), lambda g: (0, first + g))

    pair = pl.BlockSpec((2, rows, GROUP), lambda g: (0, 0, g))
    return pl.pallas_call(
        attend_back_kernel,
        grid=(groups,),
        in_specs=[at(0), at(groups), at(2 * groups), at(0), at(groups), at(0),
                  pl.BlockSpec((1, rows, 128), lambda g: (g, 0, 0))],
        out_specs=[at(0), pair, pair],
        out_shape=[
            jax.ShapeDtypeStruct((rows, D), bf16),
            jax.ShapeDtypeStruct((2, rows, D), f32),
            jax.ShapeDtypeStruct((2, rows, D), f32),
        ],
        scratch_shapes=[pltpu.VMEM((GROUP, 2 * rows), f32), pltpu.VMEM((GROUP, 2 * rows), f32)],
        compiler_params=params(),
        name="attend_back",
    )(projected, projected, projected, other, other, grads, logsum)


def gelu_both(values):
    root = 0.7978845608028654
    square = values * values
    inner = jnp.tanh(values * (root + (root * 0.044715) * square))
    half = 0.5 + 0.5 * inner
    slope = half + (0.5 * values) * (1.0 - inner * inner) * (root + (3.0 * root * 0.044715) * square)
    return values * half, slope


def feed_kernel(
    latents, attended, cotangent, modulation, project, expand, contract,
    project_down, project_up, expand_down, expand_up, contract_down, contract_up,
    block_output, grad_middle, grad_attended, sums,
    grad_project_down, grad_project_up, grad_expand_down, grad_expand_up,
    grad_contract_down, grad_contract_up,
    branch_attend, middle_tokens, entering, grad_branch, branch, grad_entering,
    middle_project, middle_expand, middle_contract, back_contract, back_expand, grad_branch_attend,
    back_project,
):
    step_at = pl.program_id(0)
    rows_all = latents.shape[0]

    def row(which):
        return modulation[which : which + 1]

    @pl.when(step_at == 0)
    def _():
        def step(rows):
            middle = product_back(attended[rows], project_down[...]).astype(bf16)
            middle_project[rows] = middle
            out = product(attended[rows], project[...].reshape(D, D)) + product(
                middle, project_up[...]
            )
            branch_attend[rows] = out
            tokens = latents[rows].astype(f32) + row(GATE_ATTEND) * out
            middle_tokens[rows] = tokens
            normed, _ = normalize(tokens)
            values = (normed * (1.0 + row(SCALE_EXPAND)) + row(SHIFT_EXPAND)).astype(bf16)
            entering[rows] = values
            middle_expand[rows] = product_back(values, expand_down[...]).astype(bf16)
            grads = (cotangent[rows].astype(f32) * row(GATE_EXPAND)).astype(bf16)
            grad_branch[rows] = grads
            back_contract[rows] = product_back(grads, contract_up[...]).astype(bf16)
            branch[rows] = jnp.zeros((CHUNK, D), f32)
            grad_entering[rows] = jnp.zeros((CHUNK, D), f32)
            middle_contract[rows] = jnp.zeros((CHUNK, RANK), f32)
            back_expand[rows] = jnp.zeros((CHUNK, RANK), f32)

        each_chunk(rows_all, step)

    wide = expand[...].reshape(D, TILE)
    deep = contract[...].reshape(TILE, D)
    hidden = product(entering[...], wide) + product(middle_expand[...], expand_up[...])
    activated, slope = gelu_both(hidden)
    activated = activated.astype(bf16)
    branch[...] += product(activated, deep)
    middle_contract[...] += product_back(activated, contract_down[...])
    grads = product_back(grad_branch[...], deep) + product(back_contract[...], contract_down[...])
    grads = (grads * slope).astype(bf16)
    grad_entering[...] += product_back(grads, wide)
    back_expand[...] += product_back(grads, expand_up[...])
    grad_contract_down[...] = product_rows(back_contract[...], activated)
    grad_expand_up[...] = product_rows(middle_expand[...], grads)

    @pl.when(step_at == pl.num_programs(0) - 1)
    def _():
        sums[...] = jnp.zeros_like(sums)
        last_middle = middle_contract[...].astype(bf16)
        last_back = back_expand[...].astype(bf16)
        grad_contract_up[...] = product_rows(last_middle, grad_branch[...])
        grad_expand_down[...] = product_rows(last_back, entering[...])

        def add(which, values):
            sums[which : which + 1] += jnp.sum(values, axis=0, keepdims=True)

        def step(rows):
            out = branch[rows] + product(middle_contract[rows].astype(bf16), contract_up[...])
            tokens = middle_tokens[rows]
            block_output[rows] = (tokens + row(GATE_EXPAND) * out).astype(bf16)
            cotangents = cotangent[rows].astype(f32)
            add(GATE_EXPAND, cotangents * out)
            grad = grad_entering[rows] + product(back_expand[rows].astype(bf16), expand_down[...])
            normed, inverse = normalize(tokens)
            add(SHIFT_EXPAND, grad)
            add(SCALE_EXPAND, grad * normed)
            grad = cotangents + normalize_back(grad * (1.0 + row(SCALE_EXPAND)), normed, inverse)
            grad_middle[rows] = grad
            add(GATE_ATTEND, grad * branch_attend[rows])
            grad = (grad * row(GATE_ATTEND)).astype(bf16)
            grad_branch_attend[rows] = grad
            back = product_back(grad, project_up[...]).astype(bf16)
            back_project[rows] = back
            grad_attended[rows] = (
                product_back(grad, project[...].reshape(D, D)) + product(back, project_down[...])
            ).astype(bf16)

        each_chunk(rows_all, step)
        grad_project_up[...] = product_rows(middle_project[...], grad_branch_attend[...])
        grad_project_down[...] = product_rows(back_project[...], attended[...])


def feed(latents, attended, cotangent, modulation, packed, chosen):
    rows = latents.shape[0]
    groups, nine, _ = packed.shape
    deep = nine // 9
    together = TILE // (4 * deep)
    project_down, project_up, expand_down, expand_up, contract_down, contract_up = chosen
    tile = pl.BlockSpec((RANK, TILE), lambda j: (0, j))
    narrow = whole((RANK, D))

    def buffer(columns, dtype):
        return pltpu.VMEM((rows, columns), dtype)

    return pl.pallas_call(
        feed_kernel,
        grid=(FF // TILE,),
        in_specs=[
            whole((rows, D)),
            whole((rows, D)),
            whole((rows, D)),
            whole(modulation.shape),
            pl.BlockSpec((groups, deep, D), lambda j: (0, 4, 0)),
            pl.BlockSpec((groups, deep, TILE), lambda j: (0, 5 + j // 2, j % 2)),
            pl.BlockSpec((together, 4 * deep, D), lambda j: (j, 0, 0)),
            narrow,
            narrow,
            narrow,
            tile,
            tile,
            narrow,
        ],
        out_specs=[
            whole((rows, D)),
            whole((rows, D)),
            whole((rows, D)),
            whole((8, D)),
            narrow,
            narrow,
            narrow,
            tile,
            tile,
            narrow,
        ],
        out_shape=[
            jax.ShapeDtypeStruct((rows, D), bf16),
            jax.ShapeDtypeStruct((rows, D), f32),
            jax.ShapeDtypeStruct((rows, D), bf16),
            jax.ShapeDtypeStruct((8, D), f32),
            jax.ShapeDtypeStruct((RANK, D), f32),
            jax.ShapeDtypeStruct((RANK, D), f32),
            jax.ShapeDtypeStruct((RANK, D), f32),
            jax.ShapeDtypeStruct((RANK, FF), f32),
            jax.ShapeDtypeStruct((RANK, FF), f32),
            jax.ShapeDtypeStruct((RANK, D), f32),
        ],
        scratch_shapes=[
            buffer(D, f32),
            buffer(D, f32),
            buffer(D, bf16),
            buffer(D, bf16),
            buffer(D, f32),
            buffer(D, f32),
            buffer(RANK, bf16),
            buffer(RANK, bf16),
            buffer(RANK, f32),
            buffer(RANK, bf16),
            buffer(RANK, f32),
            buffer(D, bf16),
            buffer(RANK, bf16),
        ],
        compiler_params=params(),
        name="feed",
    )(latents, attended, cotangent, modulation, packed, packed, packed,
      project_down, project_up, expand_down, expand_up, contract_down, contract_up)


def leave_kernel(
    grad_queries, grad_own, grad_other, weight, down, up, entering, middle, latents, modulation,
    grad_middle, input_grad, sums, grad_down, grad_up, back
):
    step_at = pl.program_id(0)
    rows_all = latents.shape[0]

    def accumulate(grads):
        grad_up[...] = product_rows(middle[...], grads)
        first = product_back(grads, weight[...].reshape(D, TILE))
        second = product_back(grads, up[...])

        @pl.when(step_at == 0)
        def _():
            input_grad[...] = first
            back[...] = second

        @pl.when(step_at > 0)
        def _():
            input_grad[...] += first
            back[...] += second

    @pl.when(step_at < D // TILE)
    def _():
        accumulate(grad_queries[...])

    @pl.when(step_at >= D // TILE)
    def _():
        accumulate((grad_own[0] + grad_other[0]).astype(bf16))

    @pl.when(step_at == pl.num_programs(0) - 1)
    def _():
        sums[...] = jnp.zeros_like(sums)
        grad_down[...] = product_rows(back[...].astype(bf16), entering[...])

        def step(rows):
            grad = input_grad[rows] + product(back[rows].astype(bf16), down[...])
            normed, inverse = normalize(latents[rows].astype(f32))
            sums[0:1] += jnp.sum(grad, axis=0, keepdims=True)
            sums[1:2] += jnp.sum(grad * normed, axis=0, keepdims=True)
            grad = grad * (1.0 + modulation[SCALE_ATTEND : SCALE_ATTEND + 1])
            input_grad[rows] = grad_middle[rows] + normalize_back(grad, normed, inverse)

        each_chunk(rows_all, step)


def leave(grad_queries, grad_own, grad_other, weight, down, up, entering, middle, latents,
          modulation, grad_middle):
    rows = latents.shape[0]
    groups, deep, columns = weight.shape
    each = D // TILE

    def pair(j):
        later = jnp.maximum(j - each, 0)
        return later // each, 0, later % each

    tile = pl.BlockSpec((RANK, TILE), lambda j: (0, j))
    return pl.pallas_call(
        leave_kernel,
        grid=(columns // TILE,),
        in_specs=[
            pl.BlockSpec((rows, TILE), lambda j: (0, jnp.minimum(j, each - 1))),
            pl.BlockSpec((1, rows, TILE), pair),
            pl.BlockSpec((1, rows, TILE), pair),
            pl.BlockSpec((groups, deep, TILE), lambda j: (0, 0, j)),
            whole(down.shape),
            tile,
            whole((rows, D)),
            whole((rows, RANK)),
            whole((rows, D)),
            whole(modulation.shape),
            whole((rows, D)),
        ],
        out_specs=[whole((rows, D)), whole((8, D)), whole((RANK, D)), tile],
        out_shape=[
            jax.ShapeDtypeStruct((rows, D), f32),
            jax.ShapeDtypeStruct((8, D), f32),
            jax.ShapeDtypeStruct((RANK, D), f32),
            jax.ShapeDtypeStruct((RANK, columns), f32),
        ],
        scratch_shapes=[pltpu.VMEM((rows, RANK), f32)],
        compiler_params=params(),
        name="leave",
    )(grad_queries, grad_own, grad_other, weight, down, up, entering, middle, latents, modulation,
      grad_middle)


WIDTHS = (D, 6 * D, D, 3 * D, D, D, D, FF, FF, D)


def swap_cores(values):
    return lax.ppermute(values, "seq", [(0, 1), (1, 0)])


def pick_kernel(starts, choice_ref, tables_ref, out_ref):
    lanes = lax.broadcasted_iota(jnp.int32, tables_ref.shape[1:], 1)
    for latent in range(out_ref.shape[0]):
        picked = tables_ref[choice_ref[latent, 0]]
        for member in range(1, 5):
            picked = jnp.where(lanes >= starts[member], tables_ref[choice_ref[latent, member]], picked)
        out_ref[latent] = picked


def pick_tables(starts, choice, tables):
    return pl.pallas_call(
        lambda *refs: pick_kernel(starts, *refs),
        out_shape=jax.ShapeDtypeStruct((choice.shape[0],) + tables.shape[1:], tables.dtype),
        in_specs=[pl.BlockSpec(memory_space=pltpu.SMEM), pl.BlockSpec(memory_space=pltpu.VMEM)],
        out_specs=pl.BlockSpec(memory_space=pltpu.VMEM),
        name="pick_tables",
    )(choice, tables)


def table_sum_kernel(starts, choice_ref, grads_ref, out_ref):
    lanes = lax.broadcasted_iota(jnp.int32, grads_ref.shape[1:], 1)
    out_ref[...] = jnp.zeros_like(out_ref)
    for latent in range(grads_ref.shape[0]):
        grads = grads_ref[latent]
        for member in range(5):
            inside = jnp.logical_and(lanes >= starts[member], lanes < starts[member + 1])
            out_ref[choice_ref[latent, member]] += jnp.where(inside, grads, 0.0)


def table_sums(starts, choice, grads):
    return pl.pallas_call(
        lambda *refs: table_sum_kernel(starts, *refs),
        out_shape=jax.ShapeDtypeStruct((NADAPT,) + grads.shape[1:], f32),
        in_specs=[pl.BlockSpec(memory_space=pltpu.SMEM), pl.BlockSpec(memory_space=pltpu.VMEM)],
        out_specs=pl.BlockSpec(memory_space=pltpu.VMEM),
        name="table_sums",
    )(choice, grads)


def regroup(gathered, devices):
    if devices <= GROUPS:
        return gathered
    deep = D // devices
    pieces = [gathered[:, : 4 * deep].reshape(GROUPS, -1, D)]
    for part in range(4, 9):
        pieces.append(gathered[:, part * deep : (part + 1) * deep].reshape(GROUPS, -1, D))
    return jnp.concatenate(pieces, axis=1)


def make_local(chips):
    devices = 2 * chips
    own = tuple(width // devices for width in WIDTHS)
    span = sum(own)
    padded = -(-span // 128) * 128
    offsets = [sum(own[:member]) for member in range(11)]
    starts = tuple(offsets[0:11:2])
    chip_rows = D // chips

    def local(
        latents,
        condition,
        adapter_choice,
        cotangent,
        modulate_weight,
        attend_weight,
        project_weight,
        expand_weight,
        contract_weight,
        *tables,
    ):
        chip = lax.axis_index("dp")
        core = lax.axis_index("seq")

        def half(array, which, axis):
            size = array.shape[axis] // 2
            return lax.dynamic_slice_in_dim(array, which * size, size, axis)

        def to_chips(values):
            return lax.all_to_all(values, "dp", split_axis=0, concat_axis=0, tiled=True)

        packed = jnp.concatenate(
            [contract_weight, project_weight]
            + [expand_weight[:, part * D : (part + 1) * D] for part in range(4)],
            axis=0,
        )
        attend_all = lax.all_gather(attend_weight, ("dp", "seq"), axis=0, tiled=True)
        attend_all = attend_all.reshape(GROUPS, D // GROUPS, 3 * D)
        gathered = regroup(
            lax.all_gather(packed, ("dp", "seq"), axis=0, tiled=False), devices
        )
        wide = D // devices
        modulate_mine = half(modulate_weight, core, 1)
        modulate_other = swap_cores(half(modulate_weight, 1 - core, 1))

        note = jnp.concatenate(
            [condition, jnp.pad(adapter_choice.astype(bf16), ((0, 0), (0, 123)))], axis=1
        )
        notes = to_chips(jnp.broadcast_to(note, (chips, note.shape[1])))
        choice = notes[:, D : D + 5].astype(jnp.int32)
        lifted_all = jax.nn.silu(notes[:, :D].astype(f32)).astype(bf16)

        lifted_mine = lax.dynamic_slice_in_dim(lifted_all, (2 * chip + core) * wide, wide, 1)
        lifted_other = lax.dynamic_slice_in_dim(lifted_all, (2 * chip + 1 - core) * wide, wide, 1)
        partial = product(lifted_mine, modulate_mine) + product(lifted_other, modulate_other)
        partial_high = lax.reduce_precision(partial, 8, 7)
        partial_low = (partial - partial_high).astype(bf16)
        partial_high = partial_high.astype(bf16)

        mine = [
            table.transpose(0, 2, 1) if member % 2 == 0 else table
            for member, table in enumerate(tables)
        ]
        mine = jnp.pad(jnp.concatenate(mine, axis=2), ((0, 0), (0, 0), (0, padded - span)))
        picked = pick_tables(starts, choice, mine)
        block = jnp.concatenate([picked.reshape(chips, RANK * padded), partial_high, partial_low], axis=1)
        block = to_chips(block)
        summed = jnp.sum(
            block[:, RANK * padded : RANK * padded + 3 * D].astype(f32)
            + block[:, RANK * padded + 3 * D :].astype(f32),
            axis=0,
        )
        both = jnp.concatenate([summed, swap_cores(summed)])
        modulation = jnp.where(core == 0, both, jnp.roll(both, 3 * D))[None]
        near = block[:, : RANK * padded].reshape(chips, 1, RANK, padded)
        far = swap_cores(near)
        pair = jnp.concatenate(
            [jnp.where(core == 0, near, far), jnp.where(core == 0, far, near)], axis=1
        )
        pair = pair.transpose(2, 0, 1, 3)
        chosen = [
            pair[..., offsets[member] : offsets[member + 1]].reshape(RANK, WIDTHS[member])
            for member in range(10)
        ]

        lifted_float, silu_pull = jax.vjp(jax.nn.silu, condition.astype(f32))
        lifted = lifted_float.astype(bf16)
        middle_modulate = product_back(lifted, chosen[0]).astype(bf16)
        modulation = modulation + product(middle_modulate, chosen[1])
        shift_attend, scale_attend, gate_attend, shift_expand, scale_expand, gate_expand = jnp.split(
            modulation, 6, axis=1
        )

        modulation = jnp.pad(modulation.reshape(6, D), ((0, 2), (0, 0)))

        tokens = latents[0]
        projected, entering, middle_attend = enter(
            tokens, modulation, attend_all, chosen[2], chosen[3]
        )
        other = swap_cores(projected[:, D:])
        attended, logsum = attend(projected, other)
        (
            block_output,
            grad_middle,
            grad_attended,
            sums_feed,
            grad_project_down,
            grad_project_up,
            grad_expand_down,
            grad_expand_up,
            grad_contract_down,
            grad_contract_up,
        ) = feed(tokens, attended, cotangent[0], modulation, gathered, chosen[4:])
        grad_queries, grad_near, grad_far = attend_back(projected, other, grad_attended, logsum)
        input_grad, sums_attend, grad_attend_down, grad_attend_up = leave(
            grad_queries,
            grad_near,
            swap_cores(grad_far),
            attend_all,
            chosen[2],
            chosen[3],
            entering,
            middle_attend,
            tokens,
            modulation,
            grad_middle,
        )

        partial_modulation = (sums_attend + sums_feed)[:6].reshape(1, 6 * D)
        grad_modulation = (partial_modulation + swap_cores(partial_modulation)).astype(bf16)
        grad_middle_modulate = product_back(grad_modulation, chosen[1]).astype(bf16)
        keep = (core == 0).astype(f32)
        grad_modulate_down = product_rows(grad_middle_modulate, lifted) * keep
        grad_modulate_up = product_rows(middle_modulate, grad_modulation) * keep

        table_grads = [
            grad_modulate_down,
            grad_modulate_up,
            grad_attend_down,
            grad_attend_up,
            grad_project_down,
            grad_project_up,
            grad_expand_down,
            grad_expand_up,
            grad_contract_down,
            grad_contract_up,
        ]
        sent = jnp.concatenate(
            [grad.reshape(RANK, chips, 2, width) for grad, width in zip(table_grads, own)], axis=3
        )
        sent = jnp.pad(sent, ((0, 0), (0, 0), (0, 0), (0, padded - span))).transpose(2, 1, 0, 3)
        near = lax.dynamic_index_in_dim(sent, core, 0, keepdims=False)
        far = lax.dynamic_index_in_dim(sent, 1 - core, 0, keepdims=False)
        arrived = to_chips(near + swap_cores(far))
        owned = table_sums(starts, choice, arrived)
        owned = [owned[:, :, offsets[member] : offsets[member + 1]] for member in range(10)]
        owned = [
            grad.transpose(0, 2, 1) if member % 2 == 0 else grad for member, grad in enumerate(owned)
        ]

        modulations = to_chips(jnp.broadcast_to(grad_modulation, (chips, 6 * D)))
        grad_lifted = product_back(modulations, modulate_weight)
        grad_lifted = to_chips(grad_lifted)
        near, far = grad_lifted[:, None], swap_cores(grad_lifted)[:, None]
        grad_lifted = jnp.concatenate(
            [jnp.where(core == 0, near, far), jnp.where(core == 0, far, near)], axis=1
        ).reshape(1, D)
        grad_lifted = grad_lifted + product(grad_middle_modulate, chosen[0])
        condition_grad = silu_pull(grad_lifted)[0]
        return (block_output[None], input_grad[None], condition_grad, *owned)

    return local


def solution(mesh):
    rows = P(("dp", "seq"), None)
    down = P(None, ("dp", "seq"), None)
    up = P(None, None, ("dp", "seq"))
    tokens = P("dp", "seq", None)
    return jax.shard_map(
        make_local(mesh.shape["dp"]),
        mesh=mesh,
        in_specs=(tokens, P("dp", None), P("dp", None), tokens) + (rows,) * 5 + (down, up) * 5,
        out_specs=(tokens, tokens, P("dp", None)) + (down, up) * 5,
        check_vma=False,
    )
```

time: 2120 us -> 399 us (0.19)
  waiting for transfers between devices: 1250 us -> 148 us
  blocking collectives: 405 us -> 27.2 us
  matrix products: 167 us -> 2.95 us
  local copies, waits for them, and re-layouts: 191 us -> 54.3 us
  Pallas kernels: 0 us -> 120 us
  other arithmetic: 40.5 us -> 8.59 us
  loops' own time: 21.2 us -> 0 us
    unnamed x28 -> x2, waiting for transfers between devices: 861 us -> 0.7 us
    all_gather x7 -> x0, blocking collectives: 400 us -> none  [the longest x1 95.7 us: local(): lax.all_gather(attend_up, ('dp', 'seq'), axis=2, tiled=True)]
    reduce_scatter x3 -> x0, waiting for transfers between devices: 271 us -> none  [the longest x1 136 us: local(): lax.psum_scatter(table_grads[8], ('dp', 'seq'), scatter_dimension=1, tile...]
    dot_general x66 -> x7, matrix products: 167 us -> 2.95 us  [the longest x3 2.22 us: product_back(): lax.dot_general(grads, right, (((1,), (1,)), ((), ())), preferred_element...]
    pallas_call x0 -> x7, Pallas kernels: none -> 120 us  [the longest x1 44.4 us: feed(): pl.pallas_call(feed_kernel, grid=(FF // TILE,), in_specs=[whole((rows, D)...]
    unnamed x181 -> x86, local copies, waits for them, and re-layouts: 122 us -> 13.8 us
    all_gather x1, waiting for transfers between devices: 66.8 us -> 16.4 us  [local(): lax.all_gather(attend_weight, ('dp', 'seq'), axis=0, tiled=True)]
    all_to_all x0 -> x4, waiting for transfers between devices: none -> 37.1 us  [to_chips(): return lax.all_to_all(values, 'dp', split_axis=0, concat_axis=0, tiled=True)]
  transfers between devices with their start and end apart: 20 -> 14, of which waited for: 13 -> 9; matrix products, arithmetic and copies ran while one was open for 14% -> 12% of each run, Pallas kernels for 0% -> 7%
where the time goes in v1:
time: 399 us; the launch traced here: 398 us
  waiting for transfers between devices  148 us (37%)
  Pallas kernels  120 us (30%)
  local copies, waits for them, and re-layouts  54.3 us (14%)
  blocking collectives  27.2 us (7%)
  starting transfers between devices  21.1 us (5%)
  between operations  14.9 us (4%)
  other arithmetic  8.59 us (2%)
    all_gather x1, waiting for transfers between devices, local(): lax.all_gather(packed, ('dp', 'seq'), axis=0, tiled=False)  84.2 us
    pallas_call x1, Pallas kernels, feed(): pl.pallas_call(feed_kernel, grid=(FF // TILE,), in_specs=[whole((rows, D)...  44.4 us
    all_to_all x4, waiting for transfers between devices, to_chips(): return lax.all_to_all(values, 'dp', split_axis=0, concat_axis=0, tiled=True)  37.1 us
    pallas_call x1, Pallas kernels, attend_back(): pl.pallas_call(attend_back_kernel, grid=(groups,), in_specs=[at(0), at(gr...  29.4 us
    all_to_all x1, blocking collectives, to_chips(): return lax.all_to_all(values, 'dp', split_axis=0, concat_axis=0, tiled=True)  27.2 us
    all_to_all x4, starting transfers between devices, to_chips(): return lax.all_to_all(values, 'dp', split_axis=0, concat_axis=0, tiled=True)  19.2 us
    all_gather x1, waiting for transfers between devices, local(): lax.all_gather(attend_weight, ('dp', 'seq'), axis=0, tiled=True)  16.4 us
    pallas_call x1, Pallas kernels, leave(): pl.pallas_call(leave_kernel, grid=(columns // TILE,), in_specs=[pl.BlockS...  16.2 us
  transfers between devices with their start and end apart: 14, of which 9 were waited for; matrix products, arithmetic and copies ran while one was open for 12% of the time, Pallas kernels for 7%

profile of v1, /device:TPU:0, one launch (start us, length us, event | category | flops | bytes accessed | tf_op | source)
XLA Modules:
  0.0 397.7 jit_solution(5585905817574300018)
XLA Ops:
  8.1 1.0 constant_dynamic-update-slice_fusion.1
  9.1 0.8 constant_dynamic-update-slice_fusion
  9.9 0.8 slice_dynamic-update-slice_fusion.3
  10.8 0.8 slice_dynamic-update-slice_fusion.2
  11.6 0.8 slice_dynamic-update-slice_fusion.1
  12.5 0.8 slice_dynamic-update-slice_fusion
  13.3 0.8 copy-done.4
  14.8 0.9 reduce.6
  15.7 0.7 reshape.187
  16.5 8.3 %all-to-all-start = ((bf16[16,2,576]{2,1,0:T(2,128)(2,1)}), bf16[16,2,576]{2,1,0:T(2,128)(2,1)S(1)}, u32[]{:S(2)}, u32[]{:S(2)}) async-start(bf16[16,2,576]{2,1,0:T(2,128)(2,1)} %reshape.187), calls=%async_computation | async-start | bytes 81920 | tf_op jit(solution)/shard_map/all_to_all | solution.py:600
  25.9 6.5 %all-to-all-done = bf16[16,2,576]{2,1,0:T(2,128)(2,1)S(1)} async-done(((bf16[16,2,576]{2,1,0:T(2,128)(2,1)}), bf16[16,2,576]{2,1,0:T(2,128)(2,1)S(1)}, u32[]{:S(2)}, u32[]{:S(2)}) %all-to-all-start) | async-done | bytes 36896 | tf_op jit(solution)/shard_map/all_to_all | solution.py:600
  33.2 1.8 pick_tables.1
  35.0 1.1 copy.120
  36.6 1.1 reduce.7
  38.2 27.2 %all_to_all.47 = bf16[16,2,9216]{2,1,0:T(2,128)(2,1)S(1)} all-to-all(bf16[16,2,9216]{2,1,0:T(2,128)(2,1)S(1)} %reshape.189), channel_id=1, replica_groups=mesh['dp'=16,'seq'=2] {'dp'}, dimensions={0} | all-to-all | bytes 1179648 | tf_op jit(solution)/shard_map/all_to_all | solution.py:600
  67.1 1.6 collective-permute-done.2
  69.0 0.9 fusion.34
  71.7 0.8 reshape.153.down
  72.7 0.8 reshape.154.up
  74.1 16.4 %all-gather.4.cloned.1.call-done = bf16[1024,3072]{1,0:T(8,128)(2,1)} async-done(((bf16[32,3072]{1,0:T(8,128)(2,1)}), bf16[1024,3072]{1,0:T(8,128)(2,1)}) %all-gather.4.cloned.1.call-update) | async-done | bytes 6291472 | tf_op jit(solution)/shard_map/all_gather | solution.py:607
  90.5 10.5 %enter.1 = (bf16[512,3072]{1,0:T(8,128)(2,1)}, bf16[512,1024]{1,0:T(8,128)(2,1)}, bf16[512,16]{1,0:T(8,128)(2,1)}) custom-call(bf16[512,1024]{1,0:T(8,128)(2,1)} %bitcast.102, f32[8,1024]{1,0:T(8,128)} %pad.18.modulation, bf16[32,32,3072]{2,1,0:T(8,128)(2,1)} %bitcast.100, bf16[16,1024]{1,0:T(8,128)(2,1)} %reshape.153.down, bf16[16,3072]{1,0:T(8,128)(2,1)} %reshape.154.up), custom_call_target="tpu_custom_call" | custom-call | tf_op jit(solution)/shard_map/enter/pallas_call | solution.py:89
  101.0 3.3 slice.106
  104.6 0.8 copy.99
  105.4 1.7 reshape.155.project_down
  107.0 1.7 copy.100
  108.7 1.7 reshape.156.project_up
  110.4 0.8 copy.101
  111.2 1.7 reshape.157.expand_down
  113.1 0.8 reshape.160.contract_up
  114.1 0.7 reshape.158.expand_up
  115.0 0.7 reshape.159.contract_down
  115.7 1.3 copy-done.1
  117.0 15.9 %attend.1 = (bf16[512,1024]{1,0:T(8,128)(2,1)}, f32[4,512,128]{2,1,0:T(8,128)}) custom-call(bf16[512,3072]{1,0:T(8,128)(2,1)} %get-tuple-element.35.queries.keys_near.values_near, bf16[512,3072]{1,0:T(8,128)(2,1)} %get-tuple-element.35.queries.keys_near.values_near, bf16[512,3072]{1,0:T(8,128)(2,1)} %get-tuple-element.35.queries.keys_near.values_near, ...), custom_call_target="tpu_custom_call" | custom-call | tf_op jit(solution)/shard_map/attend/pallas_call | solution.py:160
  133.0 84.2 %all-gather.6.cloned.1.call-done = bf16[9216,1024]{1,0:T(8,128)(2,1)} async-done(((bf16[288,1024]{1,0:T(8,128)(2,1)}), bf16[9216,1024]{1,0:T(8,128)(2,1)}) %all-gather.6.cloned.1.call-update) | async-done | bytes 18874384 | tf_op jit(solution)/shard_map/all_gather | solution.py:610
  217.2 44.4 %feed.1 = (bf16[512,1024]{1,0:T(8,128)(2,1)}, f32[512,1024]{1,0:T(8,128)}, bf16[512,1024]{1,0:T(8,128)(2,1)}, f32[8,1024]{1,0:T(8,128)}, f32[16,1024]{1,0:T(8,12...) custom-call(bf16[512,1024]{1,0:T(8,128)(2,1)} %bitcast.103, ...), custom_call_target="tpu_custom_call" | custom-call | tf_op jit(solution)/shard_map/feed/pallas_call | solution.py:365
  261.6 29.4 %attend_back.1 = (bf16[512,1024]{1,0:T(8,128)(2,1)}, f32[2,512,1024]{2,1,0:T(8,128)}, f32[2,512,1024]{2,1,0:T(8,128)}) custom-call(bf16[512,3072]{1,0:T(8,128)(2,1)} %get-tuple-element.35.queries.keys_near.values_near, bf16[512,3072]{1,0:T(8,128)(2,1)} %get-tuple-element.35.queries.keys_near.values_near, ...), custom_call_target="tpu_custom_call" | custom-call | tf_op jit(solution)/shard_map/attend_back/pallas_call | solution.py:235
  291.3 7.1 %collective-permute-done.4.grad_other = f32[2,512,1024]{2,1,0:T(8,128)S(1)} collective-permute-done((f32[2,512,1024]{2,1,0:T(8,128)}, f32[2,512,1024]{2,1,0:T(8,128)S(1)}, u32[]{:S(2)}, u32[]{:S(2)}) %collective-permute-start.4) | collective-permute-done | bytes 4194336 | tf_op jit(solution)/shard_map/ppermute | solution.py:519
  298.4 2.0 copy-done.2
  300.4 16.2 %leave.1 = (f32[512,1024]{1,0:T(8,128)}, f32[8,1024]{1,0:T(8,128)}, f32[16,1024]{1,0:T(8,128)}, f32[16,3072]{1,0:T(8,128)}) custom-call(bf16[512,1024]{1,0:T(8,128)(2,1)} %get-tuple-element.40.grad_queries, f32[2,512,1024]{2,1,0:T(8,128)} %get-tuple-element.41.grad_own, f32[2,512,1024]{2,1,0:T(8,128)} %copy-done.2, bf16[32,32,3072]{2,1,0:T(8,128)(2,1)} %bitcast.101, ...), custom_call_target="tpu_custom_call" | custom-call | tf_op jit(solution)/shard_map/leave/pallas_call | solution.py:485
  316.7 0.8 fusion.15
  319.8 0.9 copy.115
  320.9 0.9 copy.116
  322.0 0.9 copy.109
  323.2 0.9 copy.110
  326.1 0.9 copy.107
  327.0 3.3 concatenate.39
  330.3 1.0 fusion.4
  331.8 1.8 reduce.8
  333.6 0.8 reshape.191
  334.4 3.8 all-to-all-start.2
  338.2 9.1 %all-to-all-done.2 = bf16[16,2,3072]{2,1,0:T(2,128)(2,1)S(1)} async-done(((bf16[16,2,3072]{2,1,0:T(2,128)(2,1)}), bf16[16,2,3072]{2,1,0:T(2,128)(2,1)S(1)}, u32[]{:S(2)}, u32[]{:S(2)}) %all-to-all-start.2) | async-done | bytes 196640 | tf_op jit(solution)/shard_map/all_to_all | solution.py:600
  347.4 0.9 fusion.6
  348.3 3.5 all-to-all-start.3
  351.8 2.1 fusion.3
  353.9 5.0 %all-to-all-done.3 = f32[16,1,32]{2,1,0:T(1,128)S(1)} async-done(((f32[16,1,32]{2,1,0:T(1,128)}), f32[16,1,32]{2,1,0:T(1,128)S(1)}, u32[]{:S(2)}, u32[]{:S(2)}) %all-to-all-start.3) | async-done | bytes 2080 | tf_op jit(solution)/shard_map/all_to_all | solution.py:600
  358.9 3.6 all-to-all-start.4
  362.8 1.0 collective-permute-done.6
  364.5 16.5 %all-to-all-done.4.refs_1_ = f32[16,16,768]{2,1,0:T(8,128)S(1)} async-done(((f32[16,16,768]{2,1,0:T(8,128)}), f32[16,16,768]{2,1,0:T(8,128)S(1)}, u32[]{:S(2)}, u32[]{:S(2)}) %all-to-all-start.4) | async-done | bytes 786464 | tf_op jit(solution)/shard_map/all_to_all | solution.py:600
  381.0 0.9 copy-done.3
  381.9 2.2 table_sums.1
  384.1 1.8 fusion.36
  386.0 1.7 slice_bitcast_fusion
  387.7 1.7 slice.146
  389.4 1.5 slice.148
  (154 shorter events, 16.3 us)
Async XLA Ops:
  7.2 17.6 %copy-start = (bf16[32,6144]{1,0:T(8,128)(2,1)S(1)}, bf16[32,6144]{1,0:T(8,128)(2,1)}, u32[]{:S(2)}) copy-start(bf16[32,6144]{1,0:T(8,128)(2,1)} %param.23) | copy-start | bytes 1179652
  7.2 6.9 %copy-start.34 = (s32[1,5]{1,0:T(1,128)S(1)}, s32[1,5]{1,0:T(1,128)}, u32[]{:S(2)}) copy-start(s32[1,5]{1,0:T(1,128)} %param.21) | copy-start | bytes 64
  7.2 6.9 %copy-start.19 = (bf16[1,1024]{1,0:T(2,128)(2,1)S(1)}, bf16[1,1024]{1,0:T(2,128)(2,1)}, u32[]{:S(2)}) copy-start(bf16[1,1024]{1,0:T(2,128)(2,1)} %param.20) | copy-start | bytes 6148
  7.2 17.7 %copy-start.20 = (bf16[8,32,16]{1,2,0:T(8,128)(2,1)S(1)}, bf16[8,32,16]{1,2,0:T(8,128)(2,1)}, u32[]{:S(2)}) copy-start(bf16[8,32,16]{1,2,0:T(8,128)(2,1)} %param.28) | copy-start | bytes 24580
  7.2 17.7 %copy-start.21 = (bf16[8,32,16]{1,2,0:T(8,128)(2,1)S(1)}, bf16[8,32,16]{1,2,0:T(8,128)(2,1)}, u32[]{:S(2)}) copy-start(bf16[8,32,16]{1,2,0:T(8,128)(2,1)} %param.30) | copy-start | bytes 24580
  7.2 17.7 %copy-start.23 = (bf16[8,32,16]{1,2,0:T(8,128)(2,1)S(1)}, bf16[8,32,16]{1,2,0:T(8,128)(2,1)}, u32[]{:S(2)}) copy-start(bf16[8,32,16]{1,2,0:T(8,128)(2,1)} %param.32) | copy-start | bytes 24580
  7.2 17.7 %copy-start.25 = (bf16[8,32,16]{1,2,0:T(8,128)(2,1)S(1)}, bf16[8,32,16]{1,2,0:T(8,128)(2,1)}, u32[]{:S(2)}) copy-start(bf16[8,32,16]{1,2,0:T(8,128)(2,1)} %param.34) | copy-start | bytes 24580
  7.3 17.7 %copy-start.27 = (bf16[8,128,16]{1,2,0:T(8,128)(2,1)S(1)}, bf16[8,128,16]{1,2,0:T(8,128)(2,1)}, u32[]{:S(2)}) copy-start(bf16[8,128,16]{1,2,0:T(8,128)(2,1)} %param.36) | copy-start | bytes 98308
  7.3 17.7 %copy-start.13 = (bf16[8,16,192]{2,1,0:T(8,128)(2,1)S(1)}, bf16[8,16,192]{2,1,0:T(8,128)(2,1)}, u32[]{:S(2)}) copy-start(bf16[8,16,192]{2,1,0:T(8,128)(2,1)} %param.29) | copy-start | bytes 147460
  7.3 17.7 %copy-start.22 = (bf16[8,16,96]{2,1,0:T(8,128)(2,1)S(1)}, bf16[8,16,96]{2,1,0:T(8,128)(2,1)}, u32[]{:S(2)}) copy-start(bf16[8,16,96]{2,1,0:T(8,128)(2,1)} %param.31) | copy-start | bytes 73732
  7.3 17.7 %copy-start.24 = (bf16[8,16,32]{2,1,0:T(8,128)(2,1)S(1)}, bf16[8,16,32]{2,1,0:T(8,128)(2,1)}, u32[]{:S(2)}) copy-start(bf16[8,16,32]{2,1,0:T(8,128)(2,1)} %param.33) | copy-start | bytes 24580
  7.3 17.7 %copy-start.26 = (bf16[8,16,128]{2,1,0:T(8,128)(2,1)S(1)}, bf16[8,16,128]{2,1,0:T(8,128)(2,1)}, u32[]{:S(2)}) copy-start(bf16[8,16,128]{2,1,0:T(8,128)(2,1)} %param.35) | copy-start | bytes 98308
  7.3 17.7 %copy-start.28 = (bf16[8,16,32]{2,1,0:T(8,128)(2,1)S(1)}, bf16[8,16,32]{2,1,0:T(8,128)(2,1)}, u32[]{:S(2)}) copy-start(bf16[8,16,32]{2,1,0:T(8,128)(2,1)} %param.37) | copy-start | bytes 24580
  7.3 83.2 %all-gather.4.cloned.1.call-start = ((), (), s32[]{:S(2)}) async-start(), calls=%async_computation.5 | async-start | bytes 6488064 | tf_op jit(solution)/shard_map/all_gather | solution.py:607
  8.1 209.2 %all-gather.6.cloned.1.call-start = ((), (), s32[]{:S(2)}) async-start(), calls=%async_computation.6 | async-start | bytes 19464192 | tf_op jit(solution)/shard_map/all_gather | solution.py:610
  13.3 0.8 copy-start.4
  16.5 15.9 %all-to-all-start = ((bf16[16,2,576]{2,1,0:T(2,128)(2,1)}), bf16[16,2,576]{2,1,0:T(2,128)(2,1)S(1)}, u32[]{:S(2)}, u32[]{:S(2)}) async-start(bf16[16,2,576]{2,1,0:T(2,128)(2,1)} %reshape.187), calls=%async_computation | async-start | bytes 81920 | tf_op jit(solution)/shard_map/all_to_all | solution.py:600
  24.8 11.5 %collective-permute-start = (bf16[32,3072]{1,0:T(8,128)(2,1)S(1)}, bf16[32,3072]{1,0:T(8,128)(2,1)S(1)}, u32[]{:S(2)}, u32[]{:S(2)}) collective-permute-start(bf16[32,3072]{1,0:T(8,128)(2,1)S(1)} %constant_dynamic-slice_fusion), channel_id=1, source_target_pairs={{0,1},{1,0},{2,3},{3,2},{4,5},{5,4},{6,7},{7,6},{8,9},{9,8},{10,11... | collective-permute-start | bytes 589832 | tf_op jit(solution)/shard_map/ppermute | solution.py:519
  66.3 2.4 collective-permute-start.2
  66.4 4.3 %copy-start.30 = (f32[1,1024]{1,0:T(1,128)}, f32[1,1024]{1,0:T(1,128)S(1)}, u32[]{:S(2)}) copy-start(f32[1,1024]{1,0:T(1,128)S(1)} %get-tuple-element.58) | copy-start | bytes 12292
  66.5 5.1 %collective-permute-start.1 = (f32[3072]{0:T(1024)S(1)}, f32[3072]{0:T(1024)S(1)}, u32[]{:S(2)}, u32[]{:S(2)}) collective-permute-start(f32[3072]{0:T(1024)S(1)} %add_reduce_fusion), channel_id=1, source_target_pairs={{0,1},{1,0},{2,3},{3,2},{4,5},{5,4},{6,7},{7,6},{8,9},{9,8},{10,11... | collective-permute-start | bytes 36872 | tf_op jit(solution)/shard_map/ppermute | solution.py:519
  70.2 30.8 %copy-start.11 = (bf16[16,1024]{1,0:T(8,128)(2,1)}, bf16[16,1024]{1,0:T(8,128)(2,1)S(1)}, u32[]{:S(2)}) copy-start(bf16[16,1024]{1,0:T(8,128)(2,1)S(1)} %reshape.149) | copy-start | bytes 98308
  70.7 30.3 %copy-start.5 = (bf16[16,6144]{1,0:T(8,128)(2,1)}, bf16[16,6144]{1,0:T(8,128)(2,1)S(1)}, u32[]{:S(2)}) copy-start(bf16[16,6144]{1,0:T(8,128)(2,1)S(1)} %reshape.150) | copy-start | bytes 589828
  101.0 3.6 copy-start.7
  104.3 11.4 %collective-permute-start.3 = (bf16[512,2048]{1,0:T(8,128)(2,1)}, bf16[512,2048]{1,0:T(8,128)(2,1)S(1)}, u32[]{:S(2)}, u32[]{:S(2)}) collective-permute-start(bf16[512,2048]{1,0:T(8,128)(2,1)} %slice.106), channel_id=1, source_target_pairs={{0,1},{1,0},{2,3},{3,2},{4,5},{5,4},{6,7},{7,6},{8,9},{9,8},{10,11... | collective-permute-start | bytes 6291464 | tf_op jit(solution)/shard_map/ppermute | solution.py:519
  115.7 1.3 copy-start.1
  291.0 7.4 %collective-permute-start.4 = (f32[2,512,1024]{2,1,0:T(8,128)}, f32[2,512,1024]{2,1,0:T(8,128)S(1)}, u32[]{:S(2)}, u32[]{:S(2)}) collective-permute-start(f32[2,512,1024]{2,1,0:T(8,128)} %get-tuple-element.42), channel_id=1, source_target_pairs={{0,1},{1,0},{2,3},{3,2},{4,5},{5,4},{6,7},{7,6},{8,9},{9,8},{10,11... | collective-permute-start | bytes 12582920 | tf_op jit(solution)/shard_map/ppermute | solution.py:519
  298.4 2.0 copy-start.2
  300.4 16.3 %copy-start.29 = (f32[8,1024]{1,0:T(8,128)S(1)}, f32[8,1024]{1,0:T(8,128)}, u32[]{:S(2)}) copy-start(f32[8,1024]{1,0:T(8,128)} %get-tuple-element.48) | copy-start | bytes 98308
  300.4 17.4 %copy-start.17 = (f32[16,1024]{1,0:T(8,128)S(1)}, f32[16,1024]{1,0:T(8,128)}, u32[]{:S(2)}) copy-start(f32[16,1024]{1,0:T(8,128)} %get-tuple-element.51) | copy-start | bytes 196612
  300.4 17.9 %copy-start.16 = (f32[16,1024]{1,0:T(8,128)S(1)}, f32[16,1024]{1,0:T(8,128)}, u32[]{:S(2)}) copy-start(f32[16,1024]{1,0:T(8,128)} %get-tuple-element.52) | copy-start | bytes 196612
  316.6 2.1 copy-start.15
  316.6 2.5 copy-start.9
  317.5 6.6 %collective-permute-start.5 = (f32[1,6144]{1,0:T(1,128)S(1)}, f32[1,6144]{1,0:T(1,128)S(1)}, u32[]{:S(2)}, u32[]{:S(2)}) collective-permute-start(f32[1,6144]{1,0:T(1,128)S(1)} %bitcast.114), channel_id=1, source_target_pairs={{0,1},{1,0},{2,3},{3,2},{4,5},{5,4},{6,7},{7,6},{8,9},{9,8},{10,11... | collective-permute-start | bytes 73736 | tf_op jit(solution)/shard_map/ppermute | solution.py:519
  318.1 1.5 copy-start.8
  318.7 2.0 copy-start.14
  319.1 2.7 copy-start.18
  319.4 3.5 copy-start.10
  319.8 4.4 %copy-start.32 = (f32[16]{0:T(128)S(1)}, f32[16]{0:T(128)}, u32[]{:S(2)}) copy-start(f32[16]{0:T(128)} %get-tuple-element.83) | copy-start | bytes 196
  323.2 1.9 copy-start.6
  331.3 20.4 %collective-permute-start.7 = (f32[16,16,768]{2,1,0:T(8,128)}, f32[16,16,768]{2,1,0:T(8,128)}, u32[]{:S(2)}, u32[]{:S(2)}) collective-permute-start(f32[16,16,768]{2,1,0:T(8,128)} %fusion.4), channel_id=1, source_target_pairs={{0,1},{1,0},{2,3},{3,2},{4,5},{5,4},{6,7},{7,6},{8,9},{9,8},{10,11... | collective-permute-start | bytes 2359304 | tf_op jit(solution)/shard_map/ppermute | solution.py:519
  334.4 12.9 %all-to-all-start.2 = ((bf16[16,2,3072]{2,1,0:T(2,128)(2,1)}), bf16[16,2,3072]{2,1,0:T(2,128)(2,1)S(1)}, u32[]{:S(2)}, u32[]{:S(2)}) async-start(bf16[16,2,3072]{2,1,0:T(2,128)(2,1)} %reshape.191), calls=%async_computation.2 | async-start | bytes 393216 | tf_op jit(solution)/shard_map/all_to_all | solution.py:600
  348.3 10.6 %all-to-all-start.3 = ((f32[16,1,32]{2,1,0:T(1,128)}), f32[16,1,32]{2,1,0:T(1,128)S(1)}, u32[]{:S(2)}, u32[]{:S(2)}) async-start(f32[16,1,32]{2,1,0:T(1,128)} %bitcast.17), calls=%async_computation.3 | async-start | bytes 16384 | tf_op jit(solution)/shard_map/all_to_all | solution.py:600
  353.9 8.7 %copy-start.12 = (bf16[16,1024]{1,0:T(8,128)(2,1)S(1)}, bf16[16,1024]{1,0:T(8,128)(2,1)}, u32[]{:S(2)}) copy-start(bf16[16,1024]{1,0:T(8,128)(2,1)} %copy-done.11) | copy-start | bytes 98308
  353.9 8.7 %copy-start.33 = (bf16[16]{0:T(256)(128)(2,1)S(1)}, bf16[16]{0:T(256)(128)(2,1)}, u32[]{:S(2)}) copy-start(bf16[16]{0:T(256)(128)(2,1)} %get-tuple-element.82) | copy-start | bytes 100
  353.9 10.0 %copy-start.31 = (f32[1,1024]{1,0:T(1,128)S(1)}, f32[1,1024]{1,0:T(1,128)}, u32[]{:S(2)}) copy-start(f32[1,1024]{1,0:T(1,128)} %copy-done.30) | copy-start | bytes 12292
  358.9 22.1 %all-to-all-start.4 = ((f32[16,16,768]{2,1,0:T(8,128)}), f32[16,16,768]{2,1,0:T(8,128)S(1)}, u32[]{:S(2)}, u32[]{:S(2)}) async-start(f32[16,16,768]{2,1,0:T(8,128)} %fusion.3), calls=%async_computation.4 | async-start | bytes 1572864 | tf_op jit(solution)/shard_map/all_to_all | solution.py:600
  362.5 1.2 collective-permute-start.6
  381.0 0.9 copy-start.3
Sparse Core Ops, SparseCore 0:
  11.0 79.4 all-gather.3
  94.0 123.1 all-gather.5

commit v2 on v1

v2 whole, which is shorter than its diff:
```python
import jax
import jax.numpy as jnp
from jax import lax
from jax.experimental import pallas as pl
from jax.experimental.pallas import tpu as pltpu
from jax.sharding import PartitionSpec as P

D = 1024
HEADS = 16
HEAD_DIM = 64
FF = 4096
RANK = 16
bf16 = jnp.bfloat16
f32 = jnp.float32
EPSILON = 1e-06
TINY = pl.CostEstimate(flops=1, bytes_accessed=1, transcendentals=0)
LOG2E = 1.4426950408889634
GROUP = 256
TILE = 512
NADAPT = 8
CHUNK = 128
VMEM_LIMIT = 56 * 1024 * 1024
FIRST_ROWS = 48
SHIFT_ATTEND, SCALE_ATTEND, GATE_ATTEND, SHIFT_EXPAND, SCALE_EXPAND, GATE_EXPAND = range(6)


def product(left, right):
    return lax.dot_general(left, right, (((1,), (0,)), ((), ())), preferred_element_type=f32)


def product_back(grads, right):
    return lax.dot_general(grads, right, (((1,), (1,)), ((), ())), preferred_element_type=f32)


def product_rows(left, right):
    return lax.dot_general(left, right, (((0,), (0,)), ((), ())), preferred_element_type=f32)


def normalize(values):
    centred = values - jnp.mean(values, axis=-1, keepdims=True)
    variance = jnp.mean(centred * centred, axis=-1, keepdims=True)
    inverse = lax.rsqrt(variance + EPSILON)
    return centred * inverse, inverse


def normalize_back(grads, normed, inverse):
    mean = jnp.mean(grads, axis=-1, keepdims=True)
    along = jnp.mean(grads * normed, axis=-1, keepdims=True)
    return (grads - mean - normed * along) * inverse


def each_chunk(rows, step):
    def body(position, carry):
        step(pl.ds(pl.multiple_of(position * CHUNK, CHUNK), CHUNK))
        return carry

    lax.fori_loop(0, rows // CHUNK, body, 0)


def whole(shape):
    return pl.BlockSpec(shape, lambda *_: (0,) * len(shape))


def params():
    return pltpu.CompilerParams(vmem_limit_bytes=VMEM_LIMIT)


def piece_places(place, far, relative):
    chip_z, chip_y, chip_x, core = (place[axis] for axis in range(4))
    for dz in range(4):
        z = lax.rem(chip_z + 4 - dz, 4) if relative else dz
        for dy in range(2):
            for dx in range(2):
                chip = z * 4 + (chip_y ^ dy) * 2 + (chip_x ^ dx)
                yield dz, dy, dx, chip * 2 + (core ^ far)


def crossed(refs, half, dz, dy, dx):
    if half == 0:
        return refs[2 * dy].at[dx, dz % 2]
    return refs[1 + 2 * dx].at[dy, dz % 2]


def wait_for(target, semaphore):
    pltpu.make_async_copy(target, target, semaphore).wait()


def fetch_attend(place, refs, weight, semaphores):
    if len(refs) == 1:
        for half in range(2):
            columns = pl.ds(half * (3 * D // 2), 3 * D // 2)
            pltpu.make_async_copy(
                refs[0].at[:, columns], weight.at[:, columns], semaphores.at[half]
            ).start()
        return
    for half in range(2):
        columns = pl.ds(half * (3 * D // 2), 3 * D // 2)
        for far in range(2):
            for dz, dy, dx, device in piece_places(place, far, True):
                rows = pl.ds(pl.multiple_of(device * 32, 32), 32)
                pltpu.make_async_copy(
                    crossed(refs[4 * far : 4 * far + 4], dz // 2, dz, dy, dx).at[:, columns],
                    weight.at[rows, columns],
                    semaphores.at[half],
                ).start()


def wait_attend(weight, semaphores, half):
    columns = pl.ds(half * (3 * D // 2), 3 * D // 2)
    wait_for(weight.at[:, columns], semaphores.at[half])


def fetch_feed(place, refs, project, expand, contract, semaphores):
    if len(refs) == 3:
        pltpu.make_async_copy(refs[0], project, semaphores.at[0]).start()
        for tile in range(FF // TILE):
            pltpu.make_async_copy(
                refs[1].at[:, pl.ds(tile * TILE, TILE)],
                expand.at[tile // 2, tile % 2],
                semaphores.at[1],
            ).start()
        pltpu.make_async_copy(refs[2], contract, semaphores.at[2]).start()
        return

    def each(step):
        for far in range(2):
            for dz, dy, dx, device in piece_places(place, far, False):
                step(far, dz, dy, dx, device)

    def rows_of(device, deep, first, count):
        return pl.ds(pl.multiple_of(device * deep + first, 16), count)

    def main_rows(first, count, far, dz, dy, dx):
        held = refs[7 * far : 7 * far + 7]
        block = (
            held[0].at[dz] if dy + dx == 0 else held[2 * (dx + 2 * dy) - 1 + dz // 2].at[dz % 2]
        )
        return block.at[pl.ds(first, count)]

    def from_project(far, dz, dy, dx, device):
        pltpu.make_async_copy(
            main_rows(0, 32, far, dz, dy, dx),
            project.at[rows_of(device, 32, 0, 32)],
            semaphores.at[0],
        ).start()

    def from_expand(far, dz, dy, dx, device):
        for part in range(4):
            for half in range(2):
                pltpu.make_async_copy(
                    main_rows(32 * (1 + part), 32, far, dz, dy, dx).at[:, pl.ds(half * TILE, TILE)],
                    expand.at[part, half, rows_of(device, 32, 0, 32)],
                    semaphores.at[1],
                ).start()

    def from_contract(far, dz, dy, dx, device):
        pltpu.make_async_copy(
            main_rows(160, FIRST_ROWS, far, dz, dy, dx),
            contract.at[rows_of(device, 128, 0, FIRST_ROWS)],
            semaphores.at[2],
        ).start()
        pltpu.make_async_copy(
            refs[14 + far].at[dz, 2 * dy + dx],
            contract.at[rows_of(device, 128, FIRST_ROWS, 128 - FIRST_ROWS)],
            semaphores.at[2],
        ).start()

    each(from_project)
    each(from_expand)
    each(from_contract)


def smem():
    return pl.BlockSpec(memory_space=pltpu.SMEM)


def anywhere(arrays):
    return [pl.BlockSpec(memory_space=pltpu.HBM)] * len(arrays)


def enter_kernel(count, place, latents, modulation, down, up, *refs):
    weights = refs[:count]
    queries, keys_values, entering, middle, weight, semaphores = refs[count:]
    step_at = pl.program_id(0)

    @pl.when(step_at == 0)
    def _():
        fetch_attend(place, weights, weight, semaphores)

        def step(rows):
            normed, _ = normalize(latents[rows].astype(f32))
            values = normed * (1.0 + modulation[SCALE_ATTEND : SCALE_ATTEND + 1]) + modulation[
                SHIFT_ATTEND : SHIFT_ATTEND + 1
            ]
            values = values.astype(bf16)
            entering[rows] = values
            middle[rows] = product_back(values, down[...]).astype(bf16)

        each_chunk(latents.shape[0], step)
        wait_attend(weight, semaphores, 0)
        wait_attend(weight, semaphores, 1)

    here = pl.ds(pl.multiple_of(step_at * TILE, TILE), TILE)
    projected = (
        product(entering[...], weight[:, here]) + product(middle[...], up[...])
    ).astype(bf16)

    @pl.when(step_at < D // TILE)
    def _():
        queries[...] = projected

    @pl.when(step_at >= D // TILE)
    def _():
        keys_values[...] = projected


def enter(place, latents, modulation, weights, down, up):
    rows = latents.shape[0]
    columns = up.shape[1]
    return pl.pallas_call(
        lambda *refs: enter_kernel(len(weights), *refs),
        grid=(columns // TILE,),
        in_specs=[
            smem(),
            whole((rows, D)),
            whole(modulation.shape),
            whole(down.shape),
            pl.BlockSpec((RANK, TILE), lambda j: (0, j)),
        ]
        + anywhere(weights),
        out_specs=[
            pl.BlockSpec((rows, TILE), lambda j: (0, jnp.minimum(j, D // TILE - 1))),
            pl.BlockSpec((rows, TILE), lambda j: (0, jnp.maximum(j - D // TILE, 0))),
            whole((rows, D)),
            whole((rows, RANK)),
        ],
        out_shape=[
            jax.ShapeDtypeStruct((rows, D), bf16),
            jax.ShapeDtypeStruct((rows, columns - D), bf16),
            jax.ShapeDtypeStruct((rows, D), bf16),
            jax.ShapeDtypeStruct((rows, RANK), bf16),
        ],
        scratch_shapes=[pltpu.VMEM((D, columns), bf16), pltpu.SemaphoreType.DMA((2,))],
        compiler_params=params(),
        cost_estimate=TINY,
        name="enter",
    )(place, latents, modulation, down, up, *weights)


def head_mask(head, dtype=jnp.bool_):
    lane = lax.broadcasted_iota(jnp.int32, (1, GROUP), 1)
    return jnp.logical_and(lane >= head * HEAD_DIM, lane < (head + 1) * HEAD_DIM)


def attend_kernel(queries, keys_near, values_near, keys_far, values_far, attended, logsum):
    rows = queries.shape[0]
    block = 256
    scale = HEAD_DIM ** (-0.5)
    lane = lax.broadcasted_iota(jnp.int32, (1, 128), 1)

    for start in range(0, rows, block):
        here = pl.ds(start, block)
        q = queries[here] * jnp.asarray(scale, bf16)
        total = jnp.zeros((block, GROUP), f32)
        sums = jnp.zeros((block, 128), f32)
        for head in range(GROUP // HEAD_DIM):
            mask = head_mask(head)
            mine = jnp.where(mask, q, jnp.zeros_like(q))
            near = product_back(mine, keys_near[...])
            far = product_back(mine, keys_far[...])
            highest = jnp.maximum(
                jnp.max(near, axis=1, keepdims=True), jnp.max(far, axis=1, keepdims=True)
            )
            near = jnp.exp2((near - highest) * LOG2E)
            far = jnp.exp2((far - highest) * LOG2E)
            denominator = jnp.sum(near, axis=1, keepdims=True) + jnp.sum(
                far, axis=1, keepdims=True
            )
            share = 1.0 / denominator
            out = product((near * share).astype(bf16), values_near[...]) + product(
                (far * share).astype(bf16), values_far[...]
            )
            total = jnp.where(mask, out, total)
            sums = jnp.where(lane == head, highest + jnp.log(denominator), sums)
        attended[here] = total.astype(bf16)
        logsum[0, here] = sums


def attend(queries, near, far, first, groups, earlier=None):
    rows = queries.shape[0]
    every = D // GROUP

    def at(start):
        return pl.BlockSpec((rows, GROUP), lambda g: (0, start + first + g))

    given = [] if earlier is None else [earlier]
    return pl.pallas_call(
        lambda *refs: attend_kernel(*refs[:5], *refs[5 + len(given) :]),
        grid=(groups,),
        in_specs=[at(0), at(0), at(every), at(0), at(every)] + anywhere(given),
        out_specs=[at(0), pl.BlockSpec((1, rows, 128), lambda g: (g, 0, 0))],
        out_shape=[
            jax.ShapeDtypeStruct((rows, D), bf16),
            jax.ShapeDtypeStruct((groups, rows, 128), f32),
        ],
        input_output_aliases={5: 0} if given else {},
        compiler_params=params(),
        cost_estimate=TINY,
        name="attend",
    )(queries, near, near, far, far, *given)


def attend_back_kernel(
    queries, keys_near, values_near, keys_far, values_far, grads, logsum,
    grad_queries, grad_near, grad_far, keys_sum, values_sum
):
    rows = queries.shape[0]
    block = 256
    scale = HEAD_DIM ** (-0.5)
    scaled = queries[...] * jnp.asarray(scale, bf16)
    scaled_t = scaled.T
    grads_t = grads[...].T
    for start in range(0, rows, block):
        here = slice(start, start + block)
        q = scaled[here]
        g = grads[here]
        total = jnp.zeros((block, GROUP), f32)
        for head in range(GROUP // HEAD_DIM):
            mask = head_mask(head)
            part = slice(head * HEAD_DIM, (head + 1) * HEAD_DIM)
            mine = jnp.where(mask, q, jnp.zeros_like(q))
            mine_g = jnp.where(mask, g, jnp.zeros_like(g))
            shift = logsum[0, here, head : head + 1]
            pn = jnp.exp2((product_back(mine, keys_near[...]) - shift) * LOG2E)
            pf = jnp.exp2((product_back(mine, keys_far[...]) - shift) * LOG2E)
            gn = product_back(mine_g, values_near[...])
            gf = product_back(mine_g, values_far[...])
            inner = jnp.sum(pn * gn, axis=1, keepdims=True) + jnp.sum(
                pf * gf, axis=1, keepdims=True
            )
            sn = (pn * (gn - inner)).astype(bf16)
            sf = (pf * (gf - inner)).astype(bf16)
            out = product(sn, keys_near[...]) + product(sf, keys_far[...])
            total = jnp.where(mask, out * scale, total)
            vn = product(grads_t[part, here], pn.astype(bf16))
            vf = product(grads_t[part, here], pf.astype(bf16))
            kn = product(scaled_t[part, here], sn)
            kf = product(scaled_t[part, here], sf)
            if start == 0:
                values_sum[part, :rows] = vn
                values_sum[part, rows:] = vf
                keys_sum[part, :rows] = kn
                keys_sum[part, rows:] = kf
            else:
                values_sum[part, :rows] += vn
                values_sum[part, rows:] += vf
                keys_sum[part, :rows] += kn
                keys_sum[part, rows:] += kf
        grad_queries[here] = total.astype(bf16)
    grad_near[0] = keys_sum[:, :rows].T
    grad_near[1] = values_sum[:, :rows].T
    grad_far[0] = keys_sum[:, rows:].T
    grad_far[1] = values_sum[:, rows:].T


def attend_back(queries, near, far, grads, logsum, first):
    rows = queries.shape[0]
    every = D // GROUP
    groups = logsum.shape[0]

    def at(start):
        return pl.BlockSpec((rows, GROUP), lambda g: (0, start + first + g))

    pair = pl.BlockSpec((2, rows, GROUP), lambda g: (0, 0, g))
    return pl.pallas_call(
        attend_back_kernel,
        grid=(groups,),
        in_specs=[at(0), at(0), at(every), at(0), at(every), at(0),
                  pl.BlockSpec((1, rows, 128), lambda g: (g, 0, 0))],
        out_specs=[pl.BlockSpec((rows, GROUP), lambda g: (0, g)), pair, pair],
        out_shape=[
            jax.ShapeDtypeStruct((rows, groups * GROUP), bf16),
            jax.ShapeDtypeStruct((2, rows, groups * GROUP), f32),
            jax.ShapeDtypeStruct((2, rows, groups * GROUP), f32),
        ],
        scratch_shapes=[pltpu.VMEM((GROUP, 2 * rows), f32), pltpu.VMEM((GROUP, 2 * rows), f32)],
        compiler_params=params(),
        cost_estimate=TINY,
        name="attend_back",
    )(queries, near, near, far, far, grads, logsum)


def gelu_both(values):
    root = 0.7978845608028654
    square = values * values
    inner = jnp.tanh(values * (root + (root * 0.044715) * square))
    half = 0.5 + 0.5 * inner
    slope = half + (0.5 * values) * (1.0 - inner * inner) * (root + (3.0 * root * 0.044715) * square)
    return values * half, slope


def feed_kernel(
    count, place, latents, attended, cotangent, modulation,
    project_down, project_up, expand_down, expand_up, contract_down, contract_up,
    *refs,
):
    weights = refs[:count]
    (
        block_output, grad_middle, grad_attended, sums,
        grad_project_down, grad_project_up, grad_expand_down, grad_expand_up,
        grad_contract_down, grad_contract_up,
        branch_attend, middle_tokens, entering, grad_branch, branch, grad_entering,
        middle_project, middle_expand, middle_contract, back_contract, back_expand,
        grad_branch_attend, back_project, project, expand, contract, semaphores,
    ) = refs[count:]
    step_at = pl.program_id(0)
    rows_all = latents.shape[0]

    def row(which):
        return modulation[which : which + 1]

    @pl.when(step_at == 0)
    def _():
        fetch_feed(place, weights, project, expand, contract, semaphores)
        wait_for(project, semaphores.at[0])

        def step(rows):
            middle = product_back(attended[rows], project_down[...]).astype(bf16)
            middle_project[rows] = middle
            out = product(attended[rows], project[...]) + product(
                middle, project_up[...]
            )
            branch_attend[rows] = out
            tokens = latents[rows].astype(f32) + row(GATE_ATTEND) * out
            middle_tokens[rows] = tokens
            normed, _ = normalize(tokens)
            values = (normed * (1.0 + row(SCALE_EXPAND)) + row(SHIFT_EXPAND)).astype(bf16)
            entering[rows] = values
            middle_expand[rows] = product_back(values, expand_down[...]).astype(bf16)
            grads = (cotangent[rows].astype(f32) * row(GATE_EXPAND)).astype(bf16)
            grad_branch[rows] = grads
            back_contract[rows] = product_back(grads, contract_up[...]).astype(bf16)
            branch[rows] = jnp.zeros((CHUNK, D), f32)
            grad_entering[rows] = jnp.zeros((CHUNK, D), f32)
            middle_contract[rows] = jnp.zeros((CHUNK, RANK), f32)
            back_expand[rows] = jnp.zeros((CHUNK, RANK), f32)

        each_chunk(rows_all, step)
        wait_for(expand, semaphores.at[1])
        wait_for(contract, semaphores.at[2])

    wide = expand[step_at // 2, step_at % 2]
    deep = contract[pl.ds(pl.multiple_of(step_at * TILE, TILE), TILE)]
    hidden = product(entering[...], wide) + product(middle_expand[...], expand_up[...])
    activated, slope = gelu_both(hidden)
    activated = activated.astype(bf16)
    branch[...] += product(activated, deep)
    middle_contract[...] += product_back(activated, contract_down[...])
    grads = product_back(grad_branch[...], deep) + product(back_contract[...], contract_down[...])
    grads = (grads * slope).astype(bf16)
    grad_entering[...] += product_back(grads, wide)
    back_expand[...] += product_back(grads, expand_up[...])
    grad_contract_down[...] = product_rows(back_contract[...], activated)
    grad_expand_up[...] = product_rows(middle_expand[...], grads)

    @pl.when(step_at == pl.num_programs(0) - 1)
    def _():
        sums[...] = jnp.zeros_like(sums)
        last_middle = middle_contract[...].astype(bf16)
        last_back = back_expand[...].astype(bf16)
        grad_contract_up[...] = product_rows(last_middle, grad_branch[...])
        grad_expand_down[...] = product_rows(last_back, entering[...])

        def add(which, values):
            sums[which : which + 1] += jnp.sum(values, axis=0, keepdims=True)

        def step(rows):
            out = branch[rows] + product(middle_contract[rows].astype(bf16), contract_up[...])
            tokens = middle_tokens[rows]
            block_output[rows] = (tokens + row(GATE_EXPAND) * out).astype(bf16)
            cotangents = cotangent[rows].astype(f32)
            add(GATE_EXPAND, cotangents * out)
            grad = grad_entering[rows] + product(back_expand[rows].astype(bf16), expand_down[...])
            normed, inverse = normalize(tokens)
            add(SHIFT_EXPAND, grad)
            add(SCALE_EXPAND, grad * normed)
            grad = cotangents + normalize_back(grad * (1.0 + row(SCALE_EXPAND)), normed, inverse)
            grad_middle[rows] = grad
            add(GATE_ATTEND, grad * branch_attend[rows])
            grad = (grad * row(GATE_ATTEND)).astype(bf16)
            grad_branch_attend[rows] = grad
            back = product_back(grad, project_up[...]).astype(bf16)
            back_project[rows] = back
            grad_attended[rows] = (
                product_back(grad, project[...]) + product(back, project_down[...])
            ).astype(bf16)

        each_chunk(rows_all, step)
        grad_project_up[...] = product_rows(middle_project[...], grad_branch_attend[...])
        grad_project_down[...] = product_rows(back_project[...], attended[...])


def feed(place, latents, attended, cotangent, modulation, weights, chosen):
    rows = latents.shape[0]
    project_down, project_up, expand_down, expand_up, contract_down, contract_up = chosen
    tile = pl.BlockSpec((RANK, TILE), lambda j: (0, j))
    narrow = whole((RANK, D))

    def buffer(columns, dtype):
        return pltpu.VMEM((rows, columns), dtype)

    return pl.pallas_call(
        lambda *refs: feed_kernel(len(weights), *refs),
        grid=(FF // TILE,),
        in_specs=[
            smem(),
            whole((rows, D)),
            whole((rows, D)),
            whole((rows, D)),
            whole(modulation.shape),
            narrow,
            narrow,
            narrow,
            tile,
            tile,
            narrow,
        ]
        + anywhere(weights),
        out_specs=[
            whole((rows, D)),
            whole((rows, D)),
            whole((rows, D)),
            whole((8, D)),
            narrow,
            narrow,
            narrow,
            tile,
            tile,
            narrow,
        ],
        out_shape=[
            jax.ShapeDtypeStruct((rows, D), bf16),
            jax.ShapeDtypeStruct((rows, D), f32),
            jax.ShapeDtypeStruct((rows, D), bf16),
            jax.ShapeDtypeStruct((8, D), f32),
            jax.ShapeDtypeStruct((RANK, D), f32),
            jax.ShapeDtypeStruct((RANK, D), f32),
            jax.ShapeDtypeStruct((RANK, D), f32),
            jax.ShapeDtypeStruct((RANK, FF), f32),
            jax.ShapeDtypeStruct((RANK, FF), f32),
            jax.ShapeDtypeStruct((RANK, D), f32),
        ],
        scratch_shapes=[
            buffer(D, f32),
            buffer(D, f32),
            buffer(D, bf16),
            buffer(D, bf16),
            buffer(D, f32),
            buffer(D, f32),
            buffer(RANK, bf16),
            buffer(RANK, bf16),
            buffer(RANK, f32),
            buffer(RANK, bf16),
            buffer(RANK, f32),
            buffer(D, bf16),
            buffer(RANK, bf16),
            pltpu.VMEM((D, D), bf16),
            pltpu.VMEM((4, 2, D, TILE), bf16),
            pltpu.VMEM((FF, D), bf16),
            pltpu.SemaphoreType.DMA((3,)),
        ],
        compiler_params=params(),
        cost_estimate=TINY,
        name="feed",
    )(place, latents, attended, cotangent, modulation,
      project_down, project_up, expand_down, expand_up, contract_down, contract_up, *weights)


def leave_kernel(
    count, place, queries_0, queries_1, own_0, own_1, other_0, other_1, down, up, entering, middle,
    latents, modulation, grad_middle, *refs,
):
    weights = refs[:count]
    input_grad, sums, grad_down, grad_up, back, weight, semaphores = refs[count:]
    step_at = pl.program_id(0)
    rows_all = latents.shape[0]

    @pl.when(step_at == 0)
    def _():
        fetch_attend(place, weights, weight, semaphores)
        wait_attend(weight, semaphores, 0)

    @pl.when(step_at == 3)
    def _():
        wait_attend(weight, semaphores, 1)

    here = pl.ds(pl.multiple_of(leave_tile(step_at) * TILE, TILE), TILE)

    def accumulate(grads):
        grad_up[...] = product_rows(middle[...], grads)
        first = product_back(grads, weight[:, here])
        second = product_back(grads, up[...])

        @pl.when(step_at == 0)
        def _():
            input_grad[...] = first
            back[...] = second

        @pl.when(step_at > 0)
        def _():
            input_grad[...] += first
            back[...] += second

    @pl.when(step_at == 0)
    def _():
        accumulate(queries_0[...])

    @pl.when(step_at == 1)
    def _():
        accumulate(queries_1[...])

    @pl.when(jnp.logical_or(step_at == 2, step_at == 4))
    def _():
        accumulate((own_0[0] + other_0[0]).astype(bf16))

    @pl.when(jnp.logical_or(step_at == 3, step_at == 5))
    def _():
        accumulate((own_1[0] + other_1[0]).astype(bf16))

    @pl.when(step_at == pl.num_programs(0) - 1)
    def _():
        sums[...] = jnp.zeros_like(sums)
        grad_down[...] = product_rows(back[...].astype(bf16), entering[...])

        def step(rows):
            grad = input_grad[rows] + product(back[rows].astype(bf16), down[...])
            normed, inverse = normalize(latents[rows].astype(f32))
            sums[0:1] += jnp.sum(grad, axis=0, keepdims=True)
            sums[1:2] += jnp.sum(grad * normed, axis=0, keepdims=True)
            grad = grad * (1.0 + modulation[SCALE_ATTEND : SCALE_ATTEND + 1])
            input_grad[rows] = grad_middle[rows] + normalize_back(grad, normed, inverse)

        each_chunk(rows_all, step)


def leave_tile(step_at):
    return step_at


def leave(place, queries, own, other, weights, down, up, entering, middle, latents, modulation,
          grad_middle):
    rows = latents.shape[0]
    columns = up.shape[1]
    tile = pl.BlockSpec((RANK, TILE), lambda j: (0, leave_tile(j)))
    pair = pl.BlockSpec((1, rows, TILE), lambda j: (j // 4, 0, 0))
    return pl.pallas_call(
        lambda *refs: leave_kernel(len(weights), *refs),
        grid=(columns // TILE,),
        in_specs=[smem()]
        + [whole((rows, TILE))] * 2
        + [pair] * 4
        + [
            whole(down.shape),
            tile,
            whole((rows, D)),
            whole((rows, RANK)),
            whole((rows, D)),
            whole(modulation.shape),
            whole((rows, D)),
        ]
        + anywhere(weights),
        out_specs=[whole((rows, D)), whole((8, D)), whole((RANK, D)), tile],
        out_shape=[
            jax.ShapeDtypeStruct((rows, D), f32),
            jax.ShapeDtypeStruct((8, D), f32),
            jax.ShapeDtypeStruct((RANK, D), f32),
            jax.ShapeDtypeStruct((RANK, columns), f32),
        ],
        scratch_shapes=[
            pltpu.VMEM((rows, RANK), f32),
            pltpu.VMEM((D, columns), bf16),
            pltpu.SemaphoreType.DMA((2,)),
        ],
        compiler_params=params(),
        cost_estimate=TINY,
        name="leave",
    )(place, *queries, *own, *other, down, up, entering, middle, latents, modulation, grad_middle,
      *weights)


PARTS_OF_HALVES = (
    (SHIFT_ATTEND, GATE_ATTEND, SHIFT_EXPAND),
    (SCALE_ATTEND, SCALE_EXPAND, GATE_EXPAND),
)
WIDTHS = (D, 6 * D, D, 3 * D, D, D, D, FF, FF, D)


def swap_cores(values):
    return lax.ppermute(values, "seq", [(0, 1), (1, 0)])


def vmem(count):
    return [pl.BlockSpec(memory_space=pltpu.VMEM)] * count


def rounded_up(span):
    return -(-span // 128) * 128


def note_kernel(condition, choice, out):
    values = condition[...].astype(f32)
    lanes = lax.broadcasted_iota(jnp.int32, (1, 128), 1)
    last = jnp.zeros((1, 128), f32)
    for member in range(5):
        last = jnp.where(lanes == member, choice[0, member].astype(f32), last)
    rows = [values[:, 128 * at : 128 * (at + 1)] for at in range(D // 128)]
    note = jnp.concatenate(rows + [last] + [jnp.zeros((7, 128), f32)], axis=0).astype(bf16)
    for chip in range(out.shape[0]):
        out[chip] = note


def write_notes(chips, condition, choice):
    return pl.pallas_call(
        note_kernel,
        in_specs=vmem(1) + [smem()],
        out_specs=vmem(1)[0],
        out_shape=jax.ShapeDtypeStruct((chips, 16, 128), bf16),
        cost_estimate=TINY,
        name="write_notes",
    )(condition, choice)


def prepare_kernel(early, late, choice, at, lifted, mine, other, tables, out, weight, parts):
    weight[...] = jnp.zeros_like(weight)
    rows = 2 * mine.shape[0]
    m = mine[...].astype(f32)
    o = other[...].astype(f32)
    both = jnp.where(at[1] == 0, jnp.concatenate([m, o]), jnp.concatenate([o, m]))
    weight[pl.ds(pl.multiple_of(at[0], rows), rows)] = both.astype(bf16)
    partial = product(lifted[...], weight[...])
    high = partial.astype(bf16).astype(f32)
    span = parts.shape[2]
    for row in range(8):
        part = slice(row * span, (row + 1) * span)
        parts[:, row] = high[:, part]
        parts[:, 8 + row] = partial[:, part] - high[:, part]
    size = tables.shape[2]
    lanes = lax.broadcasted_iota(jnp.int32, (RANK, size), 1)
    starts = [0, early[0] + early[1], rounded_up(sum(early))]
    starts += [starts[2] + late[0] + late[1], starts[2] + sum(late[:4])]
    for latent in range(out.shape[0]):
        picked = tables[choice[latent, 0]]
        for member in range(1, 5):
            picked = jnp.where(lanes >= starts[member], tables[choice[latent, member]], picked)
        out[latent, :, :size] = picked
        out[latent, :, size:] = parts[latent].astype(bf16)


def prepare(early, late, choice, at, lifted, mine, other, tables):
    chips = choice.shape[0]
    size = tables.shape[2]
    span = mine.shape[1] // 8
    return pl.pallas_call(
        lambda *refs: prepare_kernel(early, late, *refs),
        in_specs=[smem()] * 2 + vmem(4),
        out_specs=vmem(1)[0],
        out_shape=jax.ShapeDtypeStruct((chips, RANK, size + span), bf16),
        scratch_shapes=[
            pltpu.VMEM((128, mine.shape[1]), bf16),
            pltpu.VMEM((chips, 16, span), f32),
        ],
        cost_estimate=TINY,
        name="prepare",
    )(choice, at, lifted, mine, other, tables)


def put_together(own, blocks, first, outs):
    for width, out in zip(own, outs):
        for start in range(0, out.shape[1], 128):
            pieces = []
            for device in range(start // width, (start + 127) // width + 1):
                low = max(start - device * width, 0)
                high = min(start + 128 - device * width, width)
                pieces.append(blocks[device][:, first + low : first + high])
            out[:, start : start + 128] = joined(pieces).astype(bf16)
        first += width


def open_kernel(early, late, core, condition, near, far, *outs):
    tables, (modulation, middle, lifted) = outs[:10], outs[10:]
    size = rounded_up(sum(early)) + rounded_up(sum(late))
    on_first = core[0] == 0
    blocks = []
    near_sum = jnp.zeros((16, near.shape[2] - size), f32)
    far_sum = near_sum
    for chip in range(near.shape[0]):
        n = near[chip].astype(f32)
        f = far[chip].astype(f32)
        near_sum += n[:, size:]
        far_sum += f[:, size:]
        n, f = n[:, :size], f[:, :size]
        blocks += [jnp.where(on_first, n, f), jnp.where(on_first, f, n)]
    put_together(early, blocks, 0, tables[:4])
    put_together(late, blocks, rounded_up(sum(early)), tables[4:])
    near_sum = near_sum[:8] + near_sum[8:]
    far_sum = far_sum[:8] + far_sum[8:]
    values = condition[...].astype(f32)
    lifted[...] = (values * (1.0 / (1.0 + jnp.exp(-values)))).astype(bf16)
    middle[...] = product_back(lifted[...], tables[0][...]).astype(bf16)
    adapted = product(middle[...], tables[1][...])
    halves = (jnp.where(on_first, near_sum, far_sum), jnp.where(on_first, far_sum, near_sum))
    modulation[...] = jnp.zeros_like(modulation)
    for half, targets in zip(halves, PARTS_OF_HALVES):
        for place in range(3 * D // 128):
            row, lane = targets[place // 8], place % 8 * 128
            modulation[row : row + 1, lane : lane + 128] = (
                half[place // 3 : place // 3 + 1, place % 3 * 128 : (place % 3 + 1) * 128]
                + adapted[:, row * D + lane : row * D + lane + 128]
            )


def open_block(early, late, core, condition, near, far):
    chips = near.shape[0]
    shapes = [((RANK, 2 * chips * width), bf16) for width in early + late]
    shapes += [((8, D), f32), ((1, RANK), bf16), ((1, D), bf16)]
    return pl.pallas_call(
        lambda *refs: open_kernel(early, late, *refs),
        in_specs=[smem()] + vmem(3),
        out_specs=vmem(len(shapes)),
        out_shape=[jax.ShapeDtypeStruct(*shape) for shape in shapes],
        compiler_params=params(),
        cost_estimate=TINY,
        name="open_block",
    )(core, condition, near, far)


def joined(pieces):
    return pieces[0] if len(pieces) == 1 else jnp.concatenate(pieces, axis=1)

def pack_into(own, core, grads, out):
    chips, span = out.shape[1], out.shape[3]
    for chip in range(chips):
        for k in range(2):
            device = 2 * chip + k
            pieces = [grad[:, device * width : (device + 1) * width] for width, grad in zip(own, grads)]
            if span > sum(own):
                pieces.append(jnp.zeros((RANK, span - sum(own)), f32))
            out[core[0] ^ k, chip] = joined(pieces)


def pack_late(own, core, grads):
    chips = grads[0].shape[1] // own[0] // 2
    return pl.pallas_call(
        lambda core, *refs: pack_into(own, core, refs[:-1], refs[-1]),
        out_shape=jax.ShapeDtypeStruct((2, chips, RANK, rounded_up(sum(own))), f32),
        in_specs=[smem()] + vmem(len(grads)),
        out_specs=vmem(1)[0],
        cost_estimate=TINY,
        name="pack_late",
    )(core, *grads)


def pack_early_kernel(
    own, core, attend, attend_there, feed, feed_there, middle, lifted, up, down_grad, up_grad,
    out, grad_modulation, grad_middle, modulate_down, modulate_up
):
    early = attend[...] + attend_there[...]
    late = feed[...] + feed_there[...]
    rows = [early[row : row + 1] if row < 2 else late[row : row + 1] for row in range(6)]
    grads = jnp.concatenate(rows, axis=1).astype(bf16)
    grad_modulation[...] = grads
    back = product_back(grads, up[...]).astype(bf16)
    grad_middle[...] = back
    keep = jnp.where(core[0] == 0, 1.0, 0.0)
    modulate_down[...] = product_rows(back, lifted[...]) * keep
    modulate_up[...] = product_rows(middle[...], grads) * keep
    pack_into(own, core, (modulate_down, modulate_up, down_grad, up_grad), out)


def pack_early(own, core, sums, middle, lifted, up, grads):
    chips = grads[0].shape[1] // own[2] // 2
    return pl.pallas_call(
        lambda *refs: pack_early_kernel(own, *refs),
        out_shape=[
            jax.ShapeDtypeStruct((2, chips, RANK, rounded_up(sum(own))), f32),
            jax.ShapeDtypeStruct((1, 6 * D), bf16),
            jax.ShapeDtypeStruct((1, RANK), bf16),
        ],
        in_specs=[smem()] + vmem(9),
        out_specs=vmem(3),
        scratch_shapes=[pltpu.VMEM((RANK, D), f32), pltpu.VMEM((RANK, 6 * D), f32)],
        cost_estimate=TINY,
        name="pack_early",
    )(core, *sums, middle, lifted, up, *grads)


def sums_kernel(own, members, choice, grads, *refs):
    outs, total = refs[:-1], refs[-1]
    lanes = lax.broadcasted_iota(jnp.int32, grads.shape[1:], 1)
    total[...] = jnp.zeros_like(total)
    for latent in range(grads.shape[0]):
        offset = 0
        for pair, member in enumerate(members):
            width = own[2 * pair] + own[2 * pair + 1]
            inside = jnp.logical_and(lanes >= offset, lanes < offset + width)
            total[choice[latent, member]] += jnp.where(inside, grads[latent], 0.0)
            offset += width
    for entry in range(NADAPT):
        values = total[entry]
        offset = 0
        for width, out in zip(own, outs):
            out[entry] = values[:, offset : offset + width]
            offset += width

def table_sums(own, members, choice, grads):
    sums = pl.pallas_call(
        lambda *refs: sums_kernel(own, members, *refs),
        out_shape=[jax.ShapeDtypeStruct((NADAPT, RANK, width), f32) for width in own],
        in_specs=[smem()] + vmem(1),
        out_specs=vmem(len(own)),
        scratch_shapes=[pltpu.VMEM((NADAPT,) + grads.shape[1:], f32)],
        cost_estimate=TINY,
        name="table_sums")(choice, grads)
    return [array.transpose(0, 2, 1) if which % 2 == 0 else array for which, array in enumerate(sums)]


def swap_all(arrays):
    return list(arrays) + [swap_cores(array) for array in arrays]


def after(values, *others):
    return lax.optimization_barrier((values, *others))[0]


def cut_kernel(project, expand, contract, main, last):
    deep = project.shape[0]
    main[:deep] = project[...]
    for part in range(4):
        main[(1 + part) * deep : (2 + part) * deep] = expand[:, part * D : (part + 1) * D]
    main[5 * deep :] = contract[: FIRST_ROWS]
    last[...] = contract[FIRST_ROWS:]


def cut_weights(project_weight, expand_weight, contract_weight):
    rows = contract_weight.shape[0] - FIRST_ROWS
    return pl.pallas_call(
        cut_kernel,
        in_specs=vmem(3),
        out_specs=vmem(2),
        out_shape=[
            jax.ShapeDtypeStruct((5 * project_weight.shape[0] + FIRST_ROWS, D), bf16),
            jax.ShapeDtypeStruct((rows, D), bf16),
        ],
        cost_estimate=TINY,
        name="cut_weights",
    )(project_weight, expand_weight, contract_weight)


class PermutedGather:
    chips = 16

    def exchange(self, values, over):
        return lax.ppermute(values, "dp", [(chip, chip ^ over) for chip in range(self.chips)])

    def along(self, values, step=1):
        return lax.ppermute(
            values, "dp", [(chip, (chip + 4 * step) % self.chips) for chip in range(self.chips)]
        )

    def begin(self, attend_weight, project_weight, expand_weight, contract_weight):
        main, last = cut_weights(project_weight, expand_weight, contract_weight)
        self.attend = [attend_weight] + [self.along(attend_weight, step) for step in (1, 2, 3)]
        self.main = self.lines(main)
        self.last = last
        self.attend_crossed = self.cross(jnp.stack(self.attend[:2]), jnp.stack(self.attend[2:]))
        return [self.attend_crossed[1], self.attend_crossed[3]]

    def cross_last(self):
        self.plane = [self.last] + [self.exchange(self.last, over) for over in (1, 2, 3)]
        return self.plane[1:]

    def lines(self, values):
        groups = [[z * 4 + line for z in range(self.chips // 4)] for line in range(4)]
        return lax.all_gather(values, "dp", axis=0, tiled=False, axis_index_groups=groups)

    def cross(self, first, second):
        return first, self.exchange(first, 1), second, self.exchange(second, 2)

    def cross_again(self, first, first_there, second, second_there):
        first = jnp.stack([first, first_there])
        second = jnp.stack([second, second_there])
        return [first, second, self.exchange(first, 2), self.exchange(second, 1)]

    def attend_all(self):
        return swap_all(self.cross_again(*self.attend_crossed))

    def cross_main(self):
        self.planes = self.lines(jnp.stack(self.plane))
        first, second = self.main[:2], self.main[2:]
        self.crossed = [
            self.exchange(first, 1), self.exchange(second, 1),
            self.exchange(first, 2), self.exchange(second, 2),
        ]

    def join(self, held, before):
        joined = lax.optimization_barrier((*before, *held))
        return joined[: len(before)], list(joined[len(before) :])

    def early_main(self, *before):
        before, joined = self.join([self.crossed[0], self.crossed[3]], before)
        self.crossed[0], self.crossed[3] = joined
        return before

    def more_main(self, *before):
        self.far_main = swap_cores(self.main)
        before, joined = self.join([self.crossed[1], self.crossed[2], self.far_main], before)
        self.crossed[1], self.crossed[2], self.far_main = joined
        first, second = after(self.crossed[0], before[0]), after(self.crossed[3], before[0])
        self.diagonal = [self.exchange(first, 2), self.exchange(second, 1)]
        return before

    def feed_all(self, *before):
        far = [swap_cores(self.crossed[0]), swap_cores(self.crossed[3])]
        before, joined = self.join([*far, *self.diagonal, self.planes], before)
        far, diagonal, planes = joined[:2], joined[2:4], joined[4:]
        main = [self.main, *self.crossed, *diagonal]
        other = [self.far_main, far[0], swap_cores(self.crossed[1]), swap_cores(self.crossed[2]), far[1]]
        return before, main + other + [swap_cores(array) for array in diagonal] + swap_all(planes)


class WholeGather:
    def begin(self, *matrices):
        self.all = [
            lax.all_gather(array, ("dp", "seq"), axis=0, tiled=True) for array in matrices
        ]
        return []

    def attend_all(self):
        return self.all[:1]

    def cross_last(self):
        return []

    def cross_main(self):
        pass

    def early_main(self, *before):
        return before

    def more_main(self, *before):
        return before

    def feed_all(self, *before):
        return before, self.all[1:]


def make_local(chips):
    devices = 2 * chips
    own = tuple(width // devices for width in WIDTHS)
    early, late = own[:4], own[4:]
    wide = D // devices

    def local(
        latents,
        condition,
        adapter_choice,
        cotangent,
        modulate_weight,
        attend_weight,
        project_weight,
        expand_weight,
        contract_weight,
        *tables,
    ):
        chip = lax.axis_index("dp")
        core = lax.axis_index("seq")
        place = jnp.stack([chip // 4, chip // 2 % 2, chip % 2, core]).astype(jnp.int32)
        core_at = place[3:]
        tokens = latents[0]

        def to_chips(values):
            return lax.all_to_all(values, "dp", split_axis=0, concat_axis=0, tiled=True)

        gather = PermutedGather() if chips == PermutedGather.chips else WholeGather()
        begun = gather.begin(attend_weight, project_weight, expand_weight, contract_weight)

        notes = to_chips(write_notes(chips, condition, adapter_choice))
        notes = after(notes, *gather.cross_last())
        choice = notes[:, 8, :5].astype(jnp.int32)
        row = 2 * wide * chip // 128
        lifted_all = lax.dynamic_index_in_dim(notes, row, 1, keepdims=False)
        lifted_all = jax.nn.silu(lifted_all.astype(f32)).astype(bf16)

        def columns_of(which):
            return jnp.concatenate(
                [
                    lax.dynamic_slice_in_dim(modulate_weight, which * D, D, 1),
                    lax.dynamic_slice_in_dim(modulate_weight, 2 * D + which * 2 * D, 2 * D, 1),
                ],
                axis=1,
            )

        def laid_out(own, tables):
            values = jnp.concatenate(
                [table.transpose(0, 2, 1) if which % 2 == 0 else table for which, table in enumerate(tables)],
                axis=2,
            )
            span = values.shape[2]
            return jnp.pad(values, ((0, 0), (0, 0), (0, rounded_up(span) - span)))

        at = jnp.stack([2 * wide * chip % 128, core])
        block = prepare(
            early,
            late,
            choice,
            at.astype(jnp.int32),
            lifted_all,
            columns_of(core),
            swap_cores(columns_of(1 - core)),
            jnp.concatenate([laid_out(early, tables[:4]), laid_out(late, tables[4:])], axis=2),
        )
        block = to_chips(after(block, *begun))
        *chosen, modulation, middle_modulate, lifted = open_block(
            early, late, core_at, condition, block, swap_cores(block)
        )
        modulate_down, modulate_up, attend_down, attend_up, *chosen_late = chosen

        attend_all = gather.attend_all()
        gather.cross_main()
        queries, near, entering, middle_attend = enter(
            place, tokens, modulation, attend_all, attend_down, attend_up
        )
        queries, near = gather.early_main(queries, near)
        far = swap_cores(near)
        attended, logsum_0 = attend(queries, near, far, 0, 2)
        logsum_0, far = gather.more_main(logsum_0, far)
        attended, logsum_1 = attend(queries, near, far, 2, 2, attended)
        (attended, logsum_1), feed_all = gather.feed_all(attended, logsum_1)
        modulate_all = lax.all_gather(
            after(modulate_weight, *feed_all), ("dp", "seq"), axis=0, tiled=True
        )
        block_output, grad_middle, grad_attended, sums_feed, *grads_late = feed(
            place, tokens, attended, cotangent[0], modulation, feed_all, chosen_late
        )
        grads_attended = [
            attend_back(queries, near, far, grad_attended, logsum, 2 * half)
            for half, logsum in enumerate((logsum_0, logsum_1))
        ]
        grad_queries, grad_near, grad_far = zip(*grads_attended)
        input_grad, sums_attend, *grads_attend = leave(
            place,
            grad_queries,
            grad_near,
            [swap_cores(grad) for grad in grad_far],
            attend_all,
            attend_down,
            attend_up,
            entering,
            middle_attend,
            tokens,
            modulation,
            grad_middle,
        )

        packed = pack_late(late, core_at, [after(grads_late[0], grad_far[1]), *grads_late[1:]])
        arrived_late = to_chips(packed[0] + swap_cores(packed[1]))
        packed, grad_modulation, grad_middle_modulate = pack_early(
            early,
            core_at,
            (sums_attend, swap_cores(sums_attend), sums_feed, swap_cores(sums_feed)),
            middle_modulate,
            lifted,
            modulate_up,
            grads_attend,
        )
        arrived_early = to_chips(packed[0] + swap_cores(packed[1]))
        grad_lifted = product_back(grad_modulation, modulate_all) + product(
            grad_middle_modulate, modulate_down
        )
        condition_grad = jax.vjp(jax.nn.silu, condition.astype(f32))[1](grad_lifted)[0]
        arrived_early, arrived_late, condition_grad = lax.optimization_barrier(
            (arrived_early, arrived_late, condition_grad)
        )
        owned_early = table_sums(early, (0, 1), choice, arrived_early)
        owned_late = table_sums(late, (2, 3, 4), choice, arrived_late)
        return (block_output[None], input_grad[None], condition_grad, *owned_early, *owned_late)

    return local


def solution(mesh):
    rows = P(("dp", "seq"), None)
    down = P(None, ("dp", "seq"), None)
    up = P(None, None, ("dp", "seq"))
    tokens = P("dp", "seq", None)
    return jax.shard_map(
        make_local(mesh.shape["dp"]),
        mesh=mesh,
        in_specs=(tokens, P("dp", None), P("dp", None), tokens) + (rows,) * 5 + (down, up) * 5,
        out_specs=(tokens, tokens, P("dp", None)) + (down, up) * 5,
        check_vma=False,
    )
```

time: 399 us -> 321 us (0.80)
  waiting for transfers between devices: 148 us -> 74.6 us
  local copies, waits for them, and re-layouts: 54.3 us -> 16.1 us
  starting transfers between devices: 21.1 us -> 52.7 us
  blocking collectives: 27.2 us -> 0 us
  Pallas kernels: 120 us -> 142 us
  matrix products: 2.95 us -> 8.69 us
    all_gather x2 -> x3, waiting for transfers between devices: 101 us -> 0.04 us  [the longest x1 0.02 us: local(): lax.all_gather(after(modulate_weight, *feed_all), ('dp', 'seq'), axis=0,...]
    ppermute x0 -> x16, waiting for transfers between devices: none -> 27.8 us  [the longest x13 22.1 us: exchange(): lax.ppermute(values, 'dp', [(chip, chip ^ over) for chip in range(self.ch...]
    all_to_all x1 -> x0, blocking collectives: 27.2 us -> none  [to_chips(): return lax.all_to_all(values, 'dp', split_axis=0, concat_axis=0, tiled=True)]
    ppermute x0 -> x16, starting transfers between devices: none -> 24.6 us  [the longest x13 17.7 us: exchange(): lax.ppermute(values, 'dp', [(chip, chip ^ over) for chip in range(self.ch...]
    pallas_call x7 -> x15, Pallas kernels: 120 us -> 142 us  [the longest x1 44.6 us: feed(): pl.pallas_call(lambda *refs: feed_kernel(len(weights), *refs), grid=(FF /...]
    reshape x32 -> x0, local copies, waits for them, and re-layouts: 17.4 us -> none  [the longest x10 9.33 us: local(): pair[..., offsets[member]:offsets[member + 1]].reshape(RANK, WIDTHS[member])]
    slice x19 -> x1, local copies, waits for them, and re-layouts: 13.8 us -> 2.74 us  [cross_main(): first, second = (self.main[:2], self.main[2:])]
    all_to_all x4, waiting for transfers between devices: 37.1 us -> 26.4 us  [to_chips(): return lax.all_to_all(values, 'dp', split_axis=0, concat_axis=0, tiled=True)]
  transfers between devices with their start and end apart: 14 -> 44, of which waited for: 9 -> 21; matrix products, arithmetic and copies ran while one was open for 12% -> 8% of each run, Pallas kernels for 7% -> 43%
where the time goes in v2:
time: 321 us; the launch traced here: 317 us
  Pallas kernels  142 us (44%)
  waiting for transfers between devices  74.6 us (23%)
  starting transfers between devices  52.7 us (16%)
  local copies, waits for them, and re-layouts  16.1 us (5%)
  between operations  14.5 us (5%)
  matrix products  8.69 us (3%)
  other arithmetic  8.16 us (3%)
    pallas_call x1, Pallas kernels, feed(): pl.pallas_call(lambda *refs: feed_kernel(len(weights), *refs), grid=(FF /...  44.6 us
    pallas_call x2, Pallas kernels, attend_back(): pl.pallas_call(attend_back_kernel, grid=(groups,), in_specs=[at(0), at(0)...  32.5 us
    all_to_all x4, waiting for transfers between devices, to_chips(): return lax.all_to_all(values, 'dp', split_axis=0, concat_axis=0, tiled=True)  26.4 us
    all_to_all x4, starting transfers between devices, to_chips(): return lax.all_to_all(values, 'dp', split_axis=0, concat_axis=0, tiled=True)  23.7 us
    ppermute x13, waiting for transfers between devices, exchange(): lax.ppermute(values, 'dp', [(chip, chip ^ over) for chip in range(self.ch...  22.1 us
    ppermute x21, waiting for transfers between devices, swap_cores(): return lax.ppermute(values, 'seq', [(0, 1), (1, 0)])  19.6 us
    pallas_call x1, Pallas kernels, leave(): pl.pallas_call(lambda *refs: leave_kernel(len(weights), *refs), grid=(col...  18.2 us
    pallas_call x2, Pallas kernels, attend(): pl.pallas_call(lambda *refs: attend_kernel(*refs[:5], *refs[5 + len(given...  17.9 us
  transfers between devices with their start and end apart: 44, of which 21 were waited for; matrix products, arithmetic and copies ran while one was open for 8% of the time, Pallas kernels for 43%

profile of v2, /device:TPU:0, one launch (start us, length us, event | category | flops | bytes accessed | tf_op | source)
XLA Modules:
  0.0 317.0 jit_solution(11140435783863968448)
XLA Ops:
  7.3 2.0 cut_weights.1
  9.3 2.9 collective-permute-start
  12.2 1.5 collective-permute-start.1
  13.8 2.1 collective-permute-start.4
  15.8 2.0 collective-permute-start.7
  17.8 1.4 write_notes.1
  19.3 5.3 %all-to-all-start = ((bf16[16,16,128]{2,1,0:T(8,128)(2,1)}), bf16[16,16,128]{2,1,0:T(8,128)(2,1)S(1)}, u32[]{:S(2)}, u32[]{:S(2)}) async-start(bf16[16,16,128]{2,1,0:T(8,128)(2,1)} %write_notes.1), calls=%async_computation | async-start | bytes 131072 | tf_op jit(solution)/shard_map/all_to_all | solution.py:1082
  25.3 1.0 constant_dynamic-slice_fusion
  26.3 0.9 constant_dynamic-slice_fusion.1
  28.2 0.8 concatenate.17.refs_5_
  29.0 2.8 collective-permute-start.6
  31.9 1.5 collective-permute-start.5
  33.4 5.7 %collective-permute-done.6 = bf16[32,3072]{1,0:T(8,128)(2,1)S(1)} collective-permute-done((bf16[32,3072]{1,0:T(8,128)(2,1)S(1)}, bf16[32,3072]{1,0:T(8,128)(2,1)S(1)}, u32[]{:S(2)}, u32[]{:S(2)}) %collective-permute-start.6) | collective-permute-done | bytes 196640 | tf_op jit(solution)/shard_map/ppermute | solution.py:966
  39.1 1.7 collective-permute-start.8
  43.8 2.6 prepare.1
  46.3 2.8 collective-permute-done.8
  49.2 9.6 %all-to-all-start.1 = ((bf16[16,16,1152]{2,1,0:T(8,128)(2,1)}), bf16[16,16,1152]{2,1,0:T(8,128)(2,1)}, u32[]{:S(2)}, u32[]{:S(2)}) async-start(bf16[16,16,1152]{2,1,0:T(8,128)(2,1)} %prepare.1), calls=%async_computation.1 | async-start | bytes 1179648 | tf_op jit(solution)/shard_map/all_to_all | solution.py:1082
  58.9 1.9 collective-permute-start.10
  60.9 1.5 collective-permute-start.11
  62.5 17.8 %all-to-all-done.1.refs_2_ = bf16[16,16,1152]{2,1,0:T(8,128)(2,1)} async-done(((bf16[16,16,1152]{2,1,0:T(8,128)(2,1)}), bf16[16,16,1152]{2,1,0:T(8,128)(2,1)}, u32[]{:S(2)}, u32[]{:S(2)}) %all-to-all-start.1) | async-done | bytes 589856 | tf_op jit(solution)/shard_map/all_to_all | solution.py:1082
  80.3 2.1 pad_maximum_fusion.2
  82.6 2.7 fusion.21
  86.0 1.3 collective-permute-start.17
  88.5 2.5 open_block.1
  92.6 11.4 %enter.1 = (bf16[512,1024]{1,0:T(8,128)(2,1)}, bf16[512,2048]{1,0:T(8,128)(2,1)}, bf16[512,1024]{1,0:T(8,128)(2,1)}, bf16[512,16]{1,0:T(8,128)(2,1)}) custom-call(s32[4]{0:T(128)} %pad_add_fusion.refs_0_, bf16[512,1024]{1,0:T(8,128)(2,1)} %bitcast.67, f32[8,1024]{1,0:T(8,128)} %get-tuple-element.97.refs_2_.refs_4_.refs_12_, ...), custom_call_target="tpu_custom_call" | custom-call | flops 1 | bytes 1 | tf_op jit(solution)/shard_map/enter/pallas_call | solution.py:220
  104.0 3.1 collective-permute-done.16.refs_12_
  107.9 1.5 collective-permute-start.19
  109.3 1.3 collective-permute-start.20
  110.6 3.5 %collective-permute-done.18.refs_3_.refs_4_.keys_far.values_far = bf16[512,2048]{1,0:T(8,128)(2,1)S(1)} collective-permute-done((bf16[512,2048]{1,0:T(8,128)(2,1)}, bf16[512,2048]{1,0:T(8,128)(2,1)S(1)}, u32[]{:S(2)}, u32[]{:S(2)}) %collective-permute-start.18) | collective-permute-done | bytes 2097184 | tf_op jit(solution)/shard_map/ppermute | solution.py:699
  114.3 1.3 copy-done
  115.5 8.9 %attend.2 = (bf16[512,1024]{1,0:T(8,128)(2,1)}, f32[2,512,128]{2,1,0:T(8,128)}) custom-call(bf16[512,1024]{1,0:T(8,128)(2,1)} %get-tuple-element.103.refs_0_.queries, bf16[512,2048]{1,0:T(8,128)(2,1)} %get-tuple-element.104.refs_1_.refs_2_.keys_near.values_near, bf16[512,2048]{1,0:T(8,128)(2,1)} %get-tuple-element.104.refs_1_.refs_2_.keys_near.values_near, ...), custom_call_target="tpu_custom_call" | custom-call | flops 1 | bytes 1 | tf_op jit(solution)/shard_map/attend/pallas_call | solution.py:297
  124.5 4.4 %collective-permute-done.19.refs_13_ = bf16[2,208,1024]{2,1,0:T(8,128)(2,1)S(1)} collective-permute-done((bf16[2,208,1024]{2,1,0:T(8,128)(2,1)}, bf16[2,208,1024]{2,1,0:T(8,128)(2,1)S(1)}, u32[]{:S(2)}, u32[]{:S(2)}) %collective-permute-start.19) | collective-permute-done | bytes 852000 | tf_op jit(solution)/shard_map/ppermute | solution.py:963
  128.9 1.2 collective-permute-done.20.refs_14_
  130.1 1.2 copy-done.10
  131.3 1.3 collective-permute-start.24
  133.2 8.9 %attend.3 = (bf16[512,1024]{1,0:T(8,128)(2,1)}, f32[2,512,128]{2,1,0:T(8,128)}) custom-call(bf16[512,1024]{1,0:T(8,128)(2,1)} %get-tuple-element.103.refs_0_.queries, bf16[512,2048]{1,0:T(8,128)(2,1)} %get-tuple-element.104.refs_1_.refs_2_.keys_near.values_near, ...), custom_call_target="tpu_custom_call", output_to_operand_aliasing={{0}: (5, {})} | custom-call | flops 1 | bytes 1 | tf_op jit(solution)/shard_map/attend/pallas_call | solution.py:297
  142.2 9.3 %collective-permute-done.24.refs_16_ = bf16[2,208,1024]{2,1,0:T(8,128)(2,1)} collective-permute-done((bf16[2,208,1024]{2,1,0:T(8,128)(2,1)}, bf16[2,208,1024]{2,1,0:T(8,128)(2,1)}, u32[]{:S(2)}, u32[]{:S(2)}) %collective-permute-start.24) | collective-permute-done | bytes 852000 | tf_op jit(solution)/shard_map/ppermute | solution.py:963
  151.5 1.0 collective-permute-done.25.refs_17_
  153.6 5.9 %collective-permute-done.26.refs_20_ = bf16[2,208,1024]{2,1,0:T(8,128)(2,1)S(1)} collective-permute-done((bf16[2,208,1024]{2,1,0:T(8,128)(2,1)S(1)}, bf16[2,208,1024]{2,1,0:T(8,128)(2,1)S(1)}, u32[]{:S(2)}, u32[]{:S(2)}) %collective-permute-start.26) | collective-permute-done | bytes 852000 | tf_op jit(solution)/shard_map/ppermute | solution.py:699
  160.1 1.2 collective-permute-done.28.refs_23_
  161.3 1.2 collective-permute-done.29.refs_24_
  162.5 0.9 copy-done.19
  163.5 1.4 copy-done.8
  164.9 44.6 %feed.1 = (bf16[512,1024]{1,0:T(8,128)(2,1)}, f32[512,1024]{1,0:T(8,128)}, bf16[512,1024]{1,0:T(8,128)(2,1)}, f32[8,1024]{1,0:T(8,128)}, f32[16,1024]{1,0:T(8,12...) custom-call(s32[4]{0:T(128)} %pad_add_fusion.refs_0_, ...), custom_call_target="tpu_custom_call" | custom-call | flops 1 | bytes 1 | tf_op jit(solution)/shard_map/feed/pallas_call | solution.py:512
  209.5 16.0 %attend_back.2 = (bf16[512,512]{1,0:T(8,128)(2,1)}, f32[2,512,512]{2,1,0:T(8,128)}, f32[2,512,512]{2,1,0:T(8,128)}) custom-call(bf16[512,1024]{1,0:T(8,128)(2,1)} %get-tuple-element.103.refs_0_.queries, bf16[512,2048]{1,0:T(8,128)(2,1)} %get-tuple-element.104.refs_1_.refs_2_.keys_near.values_near, ...), custom_call_target="tpu_custom_call" | custom-call | flops 1 | bytes 1 | tf_op jit(solution)/shard_map/attend_back/pallas_call | solution.py:375
  225.5 16.5 %attend_back.3 = (bf16[512,512]{1,0:T(8,128)(2,1)}, f32[2,512,512]{2,1,0:T(8,128)}, f32[2,512,512]{2,1,0:T(8,128)}) custom-call(bf16[512,1024]{1,0:T(8,128)(2,1)} %get-tuple-element.103.refs_0_.queries, bf16[512,2048]{1,0:T(8,128)(2,1)} %get-tuple-element.104.refs_1_.refs_2_.keys_near.values_near, ...), custom_call_target="tpu_custom_call" | custom-call | flops 1 | bytes 1 | tf_op jit(solution)/shard_map/attend_back/pallas_call | solution.py:375
  242.6 2.5 pack_late.1
  245.0 1.0 slice_bitcast_fusion
  246.6 3.4 %collective-permute-done.31.refs_5_ = f32[2,512,512]{2,1,0:T(8,128)S(1)} collective-permute-done((f32[2,512,512]{2,1,0:T(8,128)}, f32[2,512,512]{2,1,0:T(8,128)S(1)}, u32[]{:S(2)}, u32[]{:S(2)}) %collective-permute-start.31) | collective-permute-done | bytes 2097184 | tf_op jit(solution)/shard_map/ppermute | solution.py:699
  250.0 2.1 collective-permute-done.32.refs_6_
  252.1 18.2 %leave.1 = (f32[512,1024]{1,0:T(8,128)}, f32[8,1024]{1,0:T(8,128)}, f32[16,1024]{1,0:T(8,128)}, f32[16,3072]{1,0:T(8,128)}) custom-call(s32[4]{0:T(128)} %pad_add_fusion.refs_0_, bf16[512,512]{1,0:T(8,128)(2,1)} %get-tuple-element.132.refs_1_, bf16[512,512]{1,0:T(8,128)(2,1)} %get-tuple-element.134.refs_2_, f32[2,512,512]{2,1,0:T(8,128)} %get-tuple-element.135.refs_3_, ...), custom_call_target="tpu_custom_call" | custom-call | flops 1 | bytes 1 | tf_op jit(solution)/shard_map/leave/pallas_call | solution.py:656
  270.6 0.8 fusion
  271.4 5.2 %all-to-all-start.3 = ((f32[16,16,384]{2,1,0:T(8,128)}), f32[16,16,384]{2,1,0:T(8,128)S(1)}, u32[]{:S(2)}, u32[]{:S(2)}) async-start(f32[16,16,384]{2,1,0:T(8,128)} %fusion), calls=%async_computation.3 | async-start | bytes 786432 | tf_op jit(solution)/shard_map/all_to_all | solution.py:1082
  277.3 2.7 pack_early.1
  280.0 1.0 slice_bitcast_fusion.2
  281.3 0.8 fusion.17
  282.1 0.8 collective-permute-done.35
  282.8 1.8 bitcast_add_fusion
  284.6 5.2 %all-to-all-done.3.refs_1_ = f32[16,16,384]{2,1,0:T(8,128)S(1)} async-done(((f32[16,16,384]{2,1,0:T(8,128)}), f32[16,16,384]{2,1,0:T(8,128)S(1)}, u32[]{:S(2)}, u32[]{:S(2)}) %all-to-all-start.3) | async-done | bytes 393248 | tf_op jit(solution)/shard_map/all_to_all | solution.py:1082
  289.8 3.7 %all-to-all-start.2 = ((f32[16,16,384]{2,1,0:T(8,128)}), f32[16,16,384]{2,1,0:T(8,128)S(1)}, u32[]{:S(2)}, u32[]{:S(2)}) async-start(f32[16,16,384]{2,1,0:T(8,128)} %bitcast_add_fusion), calls=%async_computation.2 | async-start | bytes 786432 | tf_op jit(solution)/shard_map/all_to_all | solution.py:1082
  293.5 7.9 %fusion.8 = f32[1,1024]{1,0:T(1,128)S(1)} fusion(bf16[1024,6144]{1,0:T(8,128)(2,1)} %all-gather.6.cloned.1.call-done, bf16[1,6144]{1,0:T(2,128)(2,1)S(1)} %copy-done.37), kind=kOutput, calls=%fused_computation.20 | convolution fusion | flops 12582912 | bytes 12599296 | tf_op jit(solution)/shard_map/dot_general | solution.py:32
  302.1 3.4 %all-to-all-done.2.refs_1_ = f32[16,16,384]{2,1,0:T(8,128)S(1)} async-done(((f32[16,16,384]{2,1,0:T(8,128)}), f32[16,16,384]{2,1,0:T(8,128)S(1)}, u32[]{:S(2)}, u32[]{:S(2)}) %all-to-all-start.2) | async-done | bytes 393248 | tf_op jit(solution)/shard_map/all_to_all | solution.py:1082
  306.3 1.9 table_sums.2
  308.2 2.1 table_sums.3
  (145 shorter events, 15.3 us)
Async XLA Ops:
  7.2 21.8 %copy-start.20 = (bf16[32,3072]{1,0:T(8,128)(2,1)S(1)}, bf16[32,3072]{1,0:T(8,128)(2,1)}, u32[]{:S(2)}) copy-start(bf16[32,3072]{1,0:T(8,128)(2,1)} %param.24) | copy-start | bytes 589828
  7.2 20.8 %copy-start.28 = (bf16[8,16,96]{2,1,0:T(8,128)(2,1)S(1)}, bf16[8,16,96]{2,1,0:T(8,128)(2,1)}, u32[]{:S(2)}) copy-start(bf16[8,16,96]{2,1,0:T(8,128)(2,1)} %param.31) | copy-start | bytes 73732
  7.2 20.8 %copy-start.29 = (bf16[8,32,16]{1,2,0:T(8,128)(2,1)S(1)}, bf16[8,32,16]{1,2,0:T(8,128)(2,1)}, u32[]{:S(2)}) copy-start(bf16[8,32,16]{1,2,0:T(8,128)(2,1)} %param.30) | copy-start | bytes 24580
  7.2 20.8 %copy-start.22 = (bf16[8,16,192]{2,1,0:T(8,128)(2,1)S(1)}, bf16[8,16,192]{2,1,0:T(8,128)(2,1)}, u32[]{:S(2)}) copy-start(bf16[8,16,192]{2,1,0:T(8,128)(2,1)} %param.29) | copy-start | bytes 147460
  7.2 20.8 %copy-start.30 = (bf16[8,32,16]{1,2,0:T(8,128)(2,1)S(1)}, bf16[8,32,16]{1,2,0:T(8,128)(2,1)}, u32[]{:S(2)}) copy-start(bf16[8,32,16]{1,2,0:T(8,128)(2,1)} %param.28) | copy-start | bytes 24580
  7.2 20.9 %copy-start.31 = (bf16[8,32,16]{1,2,0:T(8,128)(2,1)S(1)}, bf16[8,32,16]{1,2,0:T(8,128)(2,1)}, u32[]{:S(2)}) copy-start(bf16[8,32,16]{1,2,0:T(8,128)(2,1)} %param.32) | copy-start | bytes 24580
  7.2 20.9 %copy-start.32 = (bf16[8,16,32]{2,1,0:T(8,128)(2,1)S(1)}, bf16[8,16,32]{2,1,0:T(8,128)(2,1)}, u32[]{:S(2)}) copy-start(bf16[8,16,32]{2,1,0:T(8,128)(2,1)} %param.33) | copy-start | bytes 24580
  7.3 20.9 %copy-start.33 = (bf16[8,32,16]{1,2,0:T(8,128)(2,1)S(1)}, bf16[8,32,16]{1,2,0:T(8,128)(2,1)}, u32[]{:S(2)}) copy-start(bf16[8,32,16]{1,2,0:T(8,128)(2,1)} %param.34) | copy-start | bytes 24580
  7.3 20.9 %copy-start.34 = (bf16[8,16,128]{2,1,0:T(8,128)(2,1)S(1)}, bf16[8,16,128]{2,1,0:T(8,128)(2,1)}, u32[]{:S(2)}) copy-start(bf16[8,16,128]{2,1,0:T(8,128)(2,1)} %param.35) | copy-start | bytes 98308
  7.3 20.9 %copy-start.35 = (bf16[8,128,16]{1,2,0:T(8,128)(2,1)S(1)}, bf16[8,128,16]{1,2,0:T(8,128)(2,1)}, u32[]{:S(2)}) copy-start(bf16[8,128,16]{1,2,0:T(8,128)(2,1)} %param.36) | copy-start | bytes 98308
  7.3 20.9 %copy-start.36 = (bf16[8,16,32]{2,1,0:T(8,128)(2,1)S(1)}, bf16[8,16,32]{2,1,0:T(8,128)(2,1)}, u32[]{:S(2)}) copy-start(bf16[8,16,32]{2,1,0:T(8,128)(2,1)} %param.37) | copy-start | bytes 24580
  9.3 32.1 %collective-permute-start = (bf16[80,1024]{1,0:T(8,128)(2,1)}, bf16[80,1024]{1,0:T(8,128)(2,1)}, u32[]{:S(2)}, u32[]{:S(2)}) collective-permute-start(bf16[80,1024]{1,0:T(8,128)(2,1)} %get-tuple-element.94), channel_id=1, source_target_pairs={{0,2},{2,0},{4,6},{6,4},{8,10},{10,8},{12,14},{14,12},{16,18},{18,... | collective-permute-start | bytes 491528 | tf_op jit(solution)/shard_map/ppermute | solution.py:963
  12.2 29.2 %collective-permute-start.1 = (bf16[80,1024]{1,0:T(8,128)(2,1)}, bf16[80,1024]{1,0:T(8,128)(2,1)}, u32[]{:S(2)}, u32[]{:S(2)}) collective-permute-start(bf16[80,1024]{1,0:T(8,128)(2,1)} %get-tuple-element.94), channel_id=1, source_target_pairs={{0,4},{2,6},{4,0},{6,2},{8,12},{10,14},{12,8},{14,10},{16,20},{18,... | collective-permute-start | bytes 491528 | tf_op jit(solution)/shard_map/ppermute | solution.py:963
  13.8 27.7 %collective-permute-start.2 = (bf16[80,1024]{1,0:T(8,128)(2,1)}, bf16[80,1024]{1,0:T(8,128)(2,1)}, u32[]{:S(2)}, u32[]{:S(2)}) collective-permute-start(bf16[80,1024]{1,0:T(8,128)(2,1)} %get-tuple-element.94), channel_id=1, source_target_pairs={{0,6},{2,4},{4,2},{6,0},{8,14},{10,12},{12,10},{14,8},{16,22},{18,... | collective-permute-start | bytes 491528 | tf_op jit(solution)/shard_map/ppermute | solution.py:963
  13.8 15.2 %collective-permute-start.4 = (bf16[32,3072]{1,0:T(8,128)(2,1)}, bf16[32,3072]{1,0:T(8,128)(2,1)S(1)}, u32[]{:S(2)}, u32[]{:S(2)}) collective-permute-start(bf16[32,3072]{1,0:T(8,128)(2,1)} %param.24), channel_id=1, source_target_pairs={{0,8},{2,10},{4,12},{6,14},{8,16},{10,18},{12,20},{14,22},{16,24},... | collective-permute-start | bytes 589832 | tf_op jit(solution)/shard_map/ppermute | solution.py:966
  15.8 16.1 %collective-permute-start.7 = (bf16[32,3072]{1,0:T(8,128)(2,1)}, bf16[32,3072]{1,0:T(8,128)(2,1)S(1)}, u32[]{:S(2)}, u32[]{:S(2)}) collective-permute-start(bf16[32,3072]{1,0:T(8,128)(2,1)} %param.24), channel_id=1, source_target_pairs={{0,24},{2,26},{4,28},{6,30},{8,0},{10,2},{12,4},{14,6},{16,8},{18,... | collective-permute-start | bytes 589832 | tf_op jit(solution)/shard_map/ppermute | solution.py:966
  19.3 22.2 %all-to-all-start = ((bf16[16,16,128]{2,1,0:T(8,128)(2,1)}), bf16[16,16,128]{2,1,0:T(8,128)(2,1)S(1)}, u32[]{:S(2)}, u32[]{:S(2)}) async-start(bf16[16,16,128]{2,1,0:T(8,128)(2,1)} %write_notes.1), calls=%async_computation | async-start | bytes 131072 | tf_op jit(solution)/shard_map/all_to_all | solution.py:1082
  24.6 58.1 %all-gather.8.cloned.1.call-start = ((), (), s32[]{:S(2)}) async-start(), calls=%async_computation.5 | async-start | bytes 2129920 | tf_op jit(solution)/shard_map/all_gather | solution.py:984
  29.0 10.1 %collective-permute-start.6 = (bf16[32,3072]{1,0:T(8,128)(2,1)S(1)}, bf16[32,3072]{1,0:T(8,128)(2,1)S(1)}, u32[]{:S(2)}, u32[]{:S(2)}) collective-permute-start(bf16[32,3072]{1,0:T(8,128)(2,1)S(1)} %copy-done.20), channel_id=1, source_target_pairs={{0,16},{2,18},{4,20},{6,22},{8,24},{10,26},{12,28},{14,30},{16,0},... | collective-permute-start | bytes 589832 | tf_op jit(solution)/shard_map/ppermute | solution.py:966
  31.9 14.4 %collective-permute-start.5 = (bf16[2,32,3072]{2,1,0:T(8,128)(2,1)S(1)}, bf16[2,32,3072]{2,1,0:T(8,128)(2,1)S(1)}, u32[]{:S(2)}, u32[]{:S(2)}) collective-permute-start(bf16[2,32,3072]{2,1,0:T(8,128)(2,1)S(1)} %get-tuple-element.180), channel_id=1, source_target_pairs={{0,2},{2,0},{4,6},{6,4},{8,10},{10,8},{12,14},{14,12},{16,18},{18,... | collective-permute-start | bytes 1179656 | tf_op jit(solution)/shard_map/ppermute | solution.py:963
  39.1 10.0 %collective-permute-start.8 = (bf16[2,32,3072]{2,1,0:T(8,128)(2,1)S(1)}, bf16[2,32,3072]{2,1,0:T(8,128)(2,1)S(1)}, u32[]{:S(2)}, u32[]{:S(2)}) collective-permute-start(bf16[2,32,3072]{2,1,0:T(8,128)(2,1)S(1)} %get-tuple-element.178), channel_id=1, source_target_pairs={{0,4},{2,6},{4,0},{6,2},{8,12},{10,14},{12,8},{14,10},{16,20},{18,... | collective-permute-start | bytes 1179656 | tf_op jit(solution)/shard_map/ppermute | solution.py:963
  41.4 1.7 collective-permute-start.3
  49.2 31.1 %all-to-all-start.1 = ((bf16[16,16,1152]{2,1,0:T(8,128)(2,1)}), bf16[16,16,1152]{2,1,0:T(8,128)(2,1)}, u32[]{:S(2)}, u32[]{:S(2)}) async-start(bf16[16,16,1152]{2,1,0:T(8,128)(2,1)} %prepare.1), calls=%async_computation.1 | async-start | bytes 1179648 | tf_op jit(solution)/shard_map/all_to_all | solution.py:1082
  58.8 83.4 %all-gather.10.cloned.1.call-start = ((), (), s32[]{:S(2)}) async-start(), calls=%async_computation.6 | async-start | bytes 3276800 | tf_op jit(solution)/shard_map/all_gather | solution.py:984
  58.9 26.5 %copy-start.1 = (bf16[2,2,32,3072]{3,2,1,0:T(8,128)(2,1)}, bf16[2,2,32,3072]{3,2,1,0:T(8,128)(2,1)S(1)}, u32[]{:S(2)}) copy-start(bf16[2,2,32,3072]{3,2,1,0:T(8,128)(2,1)S(1)} %pad_maximum_fusion.refs_5_.refs_14_) | copy-start | bytes 2359300
  58.9 27.0 %collective-permute-start.10 = (bf16[2,2,32,3072]{3,2,1,0:T(8,128)(2,1)S(1)}, bf16[2,2,32,3072]{3,2,1,0:T(8,128)(2,1)S(1)}, u32[]{:S(2)}, u32[]{:S(2)}) collective-permute-start(bf16[2,2,32,3072]{3,2,1,0:T(8,128)(2,1)S(1)} %pad_maximum_fusion.refs_5_.refs_14_), channel_id=1, source_target_pairs={{0,4},{2,6},{4,0},{6,2},{8,12},{10,14},{12,8},{14,10},{16,20},{18,... | collective-permute-start | bytes 2359304 | tf_op jit(solution)/shard_map/ppermute | solution.py:963
  60.9 26.4 %copy-start.2 = (bf16[2,2,32,3072]{3,2,1,0:T(8,128)(2,1)}, bf16[2,2,32,3072]{3,2,1,0:T(8,128)(2,1)S(1)}, u32[]{:S(2)}) copy-start(bf16[2,2,32,3072]{3,2,1,0:T(8,128)(2,1)S(1)} %pad_maximum_fusion.1.refs_6_.refs_15_) | copy-start | bytes 2359300
  60.9 26.3 %collective-permute-start.11 = (bf16[2,2,32,3072]{3,2,1,0:T(8,128)(2,1)S(1)}, bf16[2,2,32,3072]{3,2,1,0:T(8,128)(2,1)S(1)}, u32[]{:S(2)}, u32[]{:S(2)}) collective-permute-start(bf16[2,2,32,3072]{3,2,1,0:T(8,128)(2,1)S(1)} %pad_maximum_fusion.1.refs_6_.refs_15_), channel_id=1, source_target_pairs={{0,2},{2,0},{4,6},{6,4},{8,10},{10,8},{12,14},{14,12},{16,18},{18,... | collective-permute-start | bytes 2359304 | tf_op jit(solution)/shard_map/ppermute | solution.py:963
  62.5 24.9 %collective-permute-start.12 = (bf16[2,2,32,3072]{3,2,1,0:T(8,128)(2,1)S(1)}, bf16[2,2,32,3072]{3,2,1,0:T(8,128)(2,1)}, u32[]{:S(2)}, u32[]{:S(2)}) collective-permute-start(bf16[2,2,32,3072]{3,2,1,0:T(8,128)(2,1)S(1)} %pad_maximum_fusion.refs_5_.refs_14_), channel_id=1, source_target_pairs={{0,1},{1,0},{2,3},{3,2},{4,5},{5,4},{6,7},{7,6},{8,9},{9,8},{10,11... | collective-permute-start | bytes 2359304 | tf_op jit(solution)/shard_map/ppermute | solution.py:699
  80.3 7.6 %collective-permute-start.9 = (bf16[16,16,1152]{2,1,0:T(8,128)(2,1)}, bf16[16,16,1152]{2,1,0:T(8,128)(2,1)}, u32[]{:S(2)}, u32[]{:S(2)}) collective-permute-start(bf16[16,16,1152]{2,1,0:T(8,128)(2,1)} %all-to-all-done.1.refs_2_), channel_id=1, source_target_pairs={{0,1},{1,0},{2,3},{3,2},{4,5},{5,4},{6,7},{7,6},{8,9},{9,8},{10,11... | collective-permute-start | bytes 1769480 | tf_op jit(solution)/shard_map/ppermute | solution.py:699
  82.4 211.1 %all-gather.6.cloned.1.call-start = ((), (), s32[]{:S(2)}) async-start(), calls=%async_computation.4 | async-start | bytes 12976128 | tf_op jit(solution)/shard_map/all_gather | solution.py:1139
  85.4 21.7 %collective-permute-start.16 = (bf16[2,208,1024]{2,1,0:T(8,128)(2,1)}, bf16[2,208,1024]{2,1,0:T(8,128)(2,1)}, u32[]{:S(2)}, u32[]{:S(2)}) collective-permute-start(bf16[2,208,1024]{2,1,0:T(8,128)(2,1)} %bitcast.22), channel_id=1, source_target_pairs={{0,2},{2,0},{4,6},{6,4},{8,10},{10,8},{12,14},{14,12},{16,18},{18,... | collective-permute-start | bytes 2555912 | tf_op jit(solution)/shard_map/ppermute | solution.py:963
  86.0 21.4 %collective-permute-start.17 = (bf16[2,208,1024]{2,1,0:T(8,128)(2,1)}, bf16[2,208,1024]{2,1,0:T(8,128)(2,1)}, u32[]{:S(2)}, u32[]{:S(2)}) collective-permute-start(bf16[2,208,1024]{2,1,0:T(8,128)(2,1)} %bitcast.23), channel_id=1, source_target_pairs={{0,4},{2,6},{4,0},{6,2},{8,12},{10,14},{12,8},{14,10},{16,20},{18,... | collective-permute-start | bytes 2555912 | tf_op jit(solution)/shard_map/ppermute | solution.py:963
  87.3 3.8 %collective-permute-start.13 = (bf16[2,2,32,3072]{3,2,1,0:T(8,128)(2,1)S(1)}, bf16[2,2,32,3072]{3,2,1,0:T(8,128)(2,1)}, u32[]{:S(2)}, u32[]{:S(2)}) collective-permute-start(bf16[2,2,32,3072]{3,2,1,0:T(8,128)(2,1)S(1)} %pad_maximum_fusion.1.refs_6_.refs_15_), channel_id=1, source_target_pairs={{0,1},{1,0},{2,3},{3,2},{4,5},{5,4},{6,7},{7,6},{8,9},{9,8},{10,11... | collective-permute-start | bytes 2359304 | tf_op jit(solution)/shard_map/ppermute | solution.py:699
  87.4 4.3 %collective-permute-start.14 = (bf16[2,2,32,3072]{3,2,1,0:T(8,128)(2,1)S(1)}, bf16[2,2,32,3072]{3,2,1,0:T(8,128)(2,1)S(1)}, u32[]{:S(2)}, u32[]{:S(2)}) collective-permute-start(bf16[2,2,32,3072]{3,2,1,0:T(8,128)(2,1)S(1)} %collective-permute-done.10.refs_7_.refs_16_), channel_id=1, source_target_pairs={{0,1},{1,0},{2,3},{3,2},{4,5},{5,4},{6,7},{7,6},{8,9},{9,8},{10,11... | collective-permute-start | bytes 2359304 | tf_op jit(solution)/shard_map/ppermute | solution.py:699
  87.9 4.1 %collective-permute-start.15 = (bf16[2,2,32,3072]{3,2,1,0:T(8,128)(2,1)S(1)}, bf16[2,2,32,3072]{3,2,1,0:T(8,128)(2,1)}, u32[]{:S(2)}, u32[]{:S(2)}) collective-permute-start(bf16[2,2,32,3072]{3,2,1,0:T(8,128)(2,1)S(1)} %collective-permute-done.11.refs_8_.refs_17_), channel_id=1, source_target_pairs={{0,1},{1,0},{2,3},{3,2},{4,5},{5,4},{6,7},{7,6},{8,9},{9,8},{10,11... | collective-permute-start | bytes 2359304 | tf_op jit(solution)/shard_map/ppermute | solution.py:699
  92.6 14.8 %copy-start.3 = (bf16[832,1024]{1,0:T(8,128)(2,1)S(1)}, bf16[832,1024]{1,0:T(8,128)(2,1)}, u32[]{:S(2)}) copy-start(bf16[832,1024]{1,0:T(8,128)(2,1)} %all-gather.8.cloned.1.call-done) | copy-start | bytes 5111812
  107.3 6.8 %collective-permute-start.18 = (bf16[512,2048]{1,0:T(8,128)(2,1)}, bf16[512,2048]{1,0:T(8,128)(2,1)S(1)}, u32[]{:S(2)}, u32[]{:S(2)}) collective-permute-start(bf16[512,2048]{1,0:T(8,128)(2,1)} %get-tuple-element.104.refs_1_.refs_2_.keys_near.values_near), channel_id=1, source_target_pairs={{0,1},{1,0},{2,3},{3,2},{4,5},{5,4},{6,7},{7,6},{8,9},{9,8},{10,11... | collective-permute-start | bytes 6291464 | tf_op jit(solution)/shard_map/ppermute | solution.py:699
  107.4 22.8 %collective-permute-start.21 = (bf16[4,208,1024]{2,1,0:T(8,128)(2,1)S(1)}, bf16[4,208,1024]{2,1,0:T(8,128)(2,1)S(1)}, u32[]{:S(2)}, u32[]{:S(2)}) collective-permute-start(bf16[4,208,1024]{2,1,0:T(8,128)(2,1)S(1)} %bitcast.71), channel_id=1, source_target_pairs={{0,1},{1,0},{2,3},{3,2},{4,5},{5,4},{6,7},{7,6},{8,9},{9,8},{10,11... | collective-permute-start | bytes 5111816 | tf_op jit(solution)/shard_map/ppermute | solution.py:699
  107.9 21.1 %collective-permute-start.19 = (bf16[2,208,1024]{2,1,0:T(8,128)(2,1)}, bf16[2,208,1024]{2,1,0:T(8,128)(2,1)S(1)}, u32[]{:S(2)}, u32[]{:S(2)}) collective-permute-start(bf16[2,208,1024]{2,1,0:T(8,128)(2,1)} %bitcast.23), channel_id=1, source_target_pairs={{0,2},{2,0},{4,6},{6,4},{8,10},{10,8},{12,14},{14,12},{16,18},{18,... | collective-permute-start | bytes 2555912 | tf_op jit(solution)/shard_map/ppermute | solution.py:963
  109.3 20.8 %collective-permute-start.20 = (bf16[2,208,1024]{2,1,0:T(8,128)(2,1)}, bf16[2,208,1024]{2,1,0:T(8,128)(2,1)S(1)}, u32[]{:S(2)}, u32[]{:S(2)}) collective-permute-start(bf16[2,208,1024]{2,1,0:T(8,128)(2,1)} %bitcast.22), channel_id=1, source_target_pairs={{0,4},{2,6},{4,0},{6,2},{8,12},{10,14},{12,8},{14,10},{16,20},{18,... | collective-permute-start | bytes 2555912 | tf_op jit(solution)/shard_map/ppermute | solution.py:963
  110.6 31.5 %collective-permute-start.22 = (bf16[2,208,1024]{2,1,0:T(8,128)(2,1)}, bf16[2,208,1024]{2,1,0:T(8,128)(2,1)S(1)}, u32[]{:S(2)}, u32[]{:S(2)}) collective-permute-start(bf16[2,208,1024]{2,1,0:T(8,128)(2,1)} %collective-permute-done.16.refs_12_), channel_id=1, source_target_pairs={{0,1},{1,0},{2,3},{3,2},{4,5},{5,4},{6,7},{7,6},{8,9},{9,8},{10,11... | collective-permute-start | bytes 2555912 | tf_op jit(solution)/shard_map/ppermute | solution.py:699
  114.2 28.0 %collective-permute-start.23 = (bf16[2,208,1024]{2,1,0:T(8,128)(2,1)}, bf16[2,208,1024]{2,1,0:T(8,128)(2,1)}, u32[]{:S(2)}, u32[]{:S(2)}) collective-permute-start(bf16[2,208,1024]{2,1,0:T(8,128)(2,1)} %collective-permute-done.17.refs_15_), channel_id=1, source_target_pairs={{0,1},{1,0},{2,3},{3,2},{4,5},{5,4},{6,7},{7,6},{8,9},{9,8},{10,11... | collective-permute-start | bytes 2555912 | tf_op jit(solution)/shard_map/ppermute | solution.py:699
  128.9 34.5 %copy-start.13 = (bf16[2,208,1024]{2,1,0:T(8,128)(2,1)}, bf16[2,208,1024]{2,1,0:T(8,128)(2,1)S(1)}, u32[]{:S(2)}) copy-start(bf16[2,208,1024]{2,1,0:T(8,128)(2,1)S(1)} %collective-permute-done.19.refs_13_) | copy-start | bytes 2555908
  130.1 22.4 %copy-start.14 = (bf16[2,208,1024]{2,1,0:T(8,128)(2,1)}, bf16[2,208,1024]{2,1,0:T(8,128)(2,1)S(1)}, u32[]{:S(2)}) copy-start(bf16[2,208,1024]{2,1,0:T(8,128)(2,1)S(1)} %collective-permute-done.20.refs_14_) | copy-start | bytes 2555908
  131.3 20.1 %collective-permute-start.24 = (bf16[2,208,1024]{2,1,0:T(8,128)(2,1)}, bf16[2,208,1024]{2,1,0:T(8,128)(2,1)}, u32[]{:S(2)}, u32[]{:S(2)}) collective-permute-start(bf16[2,208,1024]{2,1,0:T(8,128)(2,1)} %collective-permute-done.16.refs_12_), channel_id=1, source_target_pairs={{0,4},{2,6},{4,0},{6,2},{8,12},{10,14},{12,8},{14,10},{16,20},{18,... | collective-permute-start | bytes 2555912 | tf_op jit(solution)/shard_map/ppermute | solution.py:963
  132.7 19.8 %collective-permute-start.25 = (bf16[2,208,1024]{2,1,0:T(8,128)(2,1)}, bf16[2,208,1024]{2,1,0:T(8,128)(2,1)}, u32[]{:S(2)}, u32[]{:S(2)}) collective-permute-start(bf16[2,208,1024]{2,1,0:T(8,128)(2,1)} %collective-permute-done.17.refs_15_), channel_id=1, source_target_pairs={{0,2},{2,0},{4,6},{6,4},{8,10},{10,8},{12,14},{14,12},{16,18},{18,... | collective-permute-start | bytes 2555912 | tf_op jit(solution)/shard_map/ppermute | solution.py:963
  152.5 10.9 %collective-permute-start.30 = (bf16[4,4,80,1024]{3,2,1,0:T(8,128)(2,1)}, bf16[4,4,80,1024]{3,2,1,0:T(8,128)(2,1)S(1)}, u32[]{:S(2)}, u32[]{:S(2)}) collective-permute-start(bf16[4,4,80,1024]{3,2,1,0:T(8,128)(2,1)} %bitcast.72), channel_id=1, source_target_pairs={{0,1},{1,0},{2,3},{3,2},{4,5},{5,4},{6,7},{7,6},{8,9},{9,8},{10,11... | collective-permute-start | bytes 7864328 | tf_op jit(solution)/shard_map/ppermute | solution.py:699
  152.5 7.0 %collective-permute-start.26 = (bf16[2,208,1024]{2,1,0:T(8,128)(2,1)S(1)}, bf16[2,208,1024]{2,1,0:T(8,128)(2,1)S(1)}, u32[]{:S(2)}, u32[]{:S(2)}) collective-permute-start(bf16[2,208,1024]{2,1,0:T(8,128)(2,1)S(1)} %collective-permute-done.19.refs_13_), channel_id=1, source_target_pairs={{0,1},{1,0},{2,3},{3,2},{4,5},{5,4},{6,7},{7,6},{8,9},{9,8},{10,11... | collective-permute-start | bytes 2555912 | tf_op jit(solution)/shard_map/ppermute | solution.py:699
  153.0 7.0 %collective-permute-start.27 = (bf16[2,208,1024]{2,1,0:T(8,128)(2,1)}, bf16[2,208,1024]{2,1,0:T(8,128)(2,1)S(1)}, u32[]{:S(2)}, u32[]{:S(2)}) collective-permute-start(bf16[2,208,1024]{2,1,0:T(8,128)(2,1)} %copy-done.14), channel_id=1, source_target_pairs={{0,1},{1,0},{2,3},{3,2},{4,5},{5,4},{6,7},{7,6},{8,9},{9,8},{10,11... | collective-permute-start | bytes 2555912 | tf_op jit(solution)/shard_map/ppermute | solution.py:699
  153.1 8.2 %collective-permute-start.28 = (bf16[2,208,1024]{2,1,0:T(8,128)(2,1)}, bf16[2,208,1024]{2,1,0:T(8,128)(2,1)S(1)}, u32[]{:S(2)}, u32[]{:S(2)}) collective-permute-start(bf16[2,208,1024]{2,1,0:T(8,128)(2,1)} %collective-permute-done.24.refs_16_), channel_id=1, source_target_pairs={{0,1},{1,0},{2,3},{3,2},{4,5},{5,4},{6,7},{7,6},{8,9},{9,8},{10,11... | collective-permute-start | bytes 2555912 | tf_op jit(solution)/shard_map/ppermute | solution.py:699
  153.5 9.0 %collective-permute-start.29 = (bf16[2,208,1024]{2,1,0:T(8,128)(2,1)}, bf16[2,208,1024]{2,1,0:T(8,128)(2,1)S(1)}, u32[]{:S(2)}, u32[]{:S(2)}) collective-permute-start(bf16[2,208,1024]{2,1,0:T(8,128)(2,1)} %collective-permute-done.25.refs_17_), channel_id=1, source_target_pairs={{0,1},{1,0},{2,3},{3,2},{4,5},{5,4},{6,7},{7,6},{8,9},{9,8},{10,11... | collective-permute-start | bytes 2555912 | tf_op jit(solution)/shard_map/ppermute | solution.py:699
  242.0 8.0 %collective-permute-start.31 = (f32[2,512,512]{2,1,0:T(8,128)}, f32[2,512,512]{2,1,0:T(8,128)S(1)}, u32[]{:S(2)}, u32[]{:S(2)}) collective-permute-start(f32[2,512,512]{2,1,0:T(8,128)} %get-tuple-element.137), channel_id=1, source_target_pairs={{0,1},{1,0},{2,3},{3,2},{4,5},{5,4},{6,7},{7,6},{8,9},{9,8},{10,11... | collective-permute-start | bytes 6291464 | tf_op jit(solution)/shard_map/ppermute | solution.py:699
  242.2 10.0 %collective-permute-start.32 = (f32[2,512,512]{2,1,0:T(8,128)}, f32[2,512,512]{2,1,0:T(8,128)}, u32[]{:S(2)}, u32[]{:S(2)}) collective-permute-start(f32[2,512,512]{2,1,0:T(8,128)} %get-tuple-element.138), channel_id=1, source_target_pairs={{0,1},{1,0},{2,3},{3,2},{4,5},{5,4},{6,7},{7,6},{8,9},{9,8},{10,11... | collective-permute-start | bytes 6291464 | tf_op jit(solution)/shard_map/ppermute | solution.py:699
  246.1 24.6 %collective-permute-start.36 = (f32[16,16,384]{2,1,0:T(8,128)S(1)}, f32[16,16,384]{2,1,0:T(8,128)S(1)}, u32[]{:S(2)}, u32[]{:S(2)}) collective-permute-start(f32[16,16,384]{2,1,0:T(8,128)S(1)} %slice_bitcast_fusion), channel_id=1, source_target_pairs={{0,1},{1,0},{2,3},{3,2},{4,5},{5,4},{6,7},{7,6},{8,9},{9,8},{10,11... | collective-permute-start | bytes 1179656 | tf_op jit(solution)/shard_map/ppermute | solution.py:699
  246.3 30.4 %collective-permute-start.34 = (f32[8,1024]{1,0:T(8,128)S(1)}, f32[8,1024]{1,0:T(8,128)S(1)}, u32[]{:S(2)}, u32[]{:S(2)}) collective-permute-start(f32[8,1024]{1,0:T(8,128)S(1)} %copy-done.24), channel_id=1, source_target_pairs={{0,1},{1,0},{2,3},{3,2},{4,5},{5,4},{6,7},{7,6},{8,9},{9,8},{10,11... | collective-permute-start | bytes 98312 | tf_op jit(solution)/shard_map/ppermute | solution.py:699
  252.1 18.5 %copy-start.7 = (f32[2,16,16,384]{3,2,1,0:T(8,128)S(1)}, f32[2,16,16,384]{3,2,1,0:T(8,128)}, u32[]{:S(2)}) copy-start(f32[2,16,16,384]{3,2,1,0:T(8,128)} %pack_late.1) | copy-start | bytes 2359300
  270.3 11.0 %copy-start.27 = (bf16[16,1024]{1,0:T(8,128)(2,1)S(1)}, bf16[16,1024]{1,0:T(8,128)(2,1)}, u32[]{:S(2)}) copy-start(bf16[16,1024]{1,0:T(8,128)(2,1)} %get-tuple-element.161) | copy-start | bytes 98308
  270.4 6.3 %collective-permute-start.33 = (f32[8,1024]{1,0:T(8,128)}, f32[8,1024]{1,0:T(8,128)S(1)}, u32[]{:S(2)}, u32[]{:S(2)}) collective-permute-start(f32[8,1024]{1,0:T(8,128)} %get-tuple-element.143.refs_1_), channel_id=1, source_target_pairs={{0,1},{1,0},{2,3},{3,2},{4,5},{5,4},{6,7},{7,6},{8,9},{9,8},{10,11... | collective-permute-start | bytes 98312 | tf_op jit(solution)/shard_map/ppermute | solution.py:699
  271.4 18.4 %all-to-all-start.3 = ((f32[16,16,384]{2,1,0:T(8,128)}), f32[16,16,384]{2,1,0:T(8,128)S(1)}, u32[]{:S(2)}, u32[]{:S(2)}) async-start(f32[16,16,384]{2,1,0:T(8,128)} %fusion), calls=%async_computation.3 | async-start | bytes 786432 | tf_op jit(solution)/shard_map/all_to_all | solution.py:1082
  280.0 13.5 %copy-start.37 = (bf16[1,6144]{1,0:T(2,128)(2,1)S(1)}, bf16[1,6144]{1,0:T(2,128)(2,1)}, u32[]{:S(2)}) copy-start(bf16[1,6144]{1,0:T(2,128)(2,1)} %get-tuple-element.158) | copy-start | bytes 36868
  281.1 1.8 collective-permute-start.35
  289.8 11.7 %copy-start.11 = (f32[16,16,384]{2,1,0:T(8,128)}, f32[16,16,384]{2,1,0:T(8,128)S(1)}, u32[]{:S(2)}) copy-start(f32[16,16,384]{2,1,0:T(8,128)S(1)} %all-to-all-done.3.refs_1_) | copy-start | bytes 1179652
  289.8 15.7 %all-to-all-start.2 = ((f32[16,16,384]{2,1,0:T(8,128)}), f32[16,16,384]{2,1,0:T(8,128)S(1)}, u32[]{:S(2)}, u32[]{:S(2)}) async-start(f32[16,16,384]{2,1,0:T(8,128)} %bitcast_add_fusion), calls=%async_computation.2 | async-start | bytes 786432 | tf_op jit(solution)/shard_map/all_to_all | solution.py:1082
  (18 other events, 50.6 us)
Sparse Core Ops, SparseCore 0:
  27.6 50.2 all-gather.7
  82.5 55.5 all-gather.9
  163.6 95.9 all-gather.5

commit v3 on v2

--- a/solution.py
+++ b/solution.py
@@ -17,10 +17,11 @@
 LOG2E = 1.4426950408889634
 GROUP = 256
 TILE = 512
+WIDE = D + 128
 NADAPT = 8
 CHUNK = 128
-VMEM_LIMIT = 56 * 1024 * 1024
-FIRST_ROWS = 48
+VMEM_LIMIT = 62 * 1024 * 1024
+FIRST_ROWS = 32
 SHIFT_ATTEND, SCALE_ATTEND, GATE_ATTEND, SHIFT_EXPAND, SCALE_EXPAND, GATE_EXPAND = range(6)
 
 
@@ -86,46 +87,54 @@
 
 
 def fetch_attend(place, refs, weight, semaphores):
-    if len(refs) == 1:
-        for half in range(2):
-            columns = pl.ds(half * (3 * D // 2), 3 * D // 2)
+    for part in range(3):
+        columns = pl.ds(part * D, D)
+        if len(refs) == 1:
             pltpu.make_async_copy(
-                refs[0].at[:, columns], weight.at[:, columns], semaphores.at[half]
+                refs[0].at[:, columns], weight.at[pl.ds(0, D), columns], semaphores.at[part]
             ).start()
-        return
-    for half in range(2):
-        columns = pl.ds(half * (3 * D // 2), 3 * D // 2)
+            continue
         for far in range(2):
             for dz, dy, dx, device in piece_places(place, far, True):
                 rows = pl.ds(pl.multiple_of(device * 32, 32), 32)
                 pltpu.make_async_copy(
                     crossed(refs[4 * far : 4 * far + 4], dz // 2, dz, dy, dx).at[:, columns],
                     weight.at[rows, columns],
-                    semaphores.at[half],
+                    semaphores.at[part],
                 ).start()
 
 
-def wait_attend(weight, semaphores, half):
-    columns = pl.ds(half * (3 * D // 2), 3 * D // 2)
-    wait_for(weight.at[:, columns], semaphores.at[half])
+def wait_attend(weight, semaphores, part):
+    columns = pl.ds(pl.multiple_of(part * D, D), D)
+    wait_for(weight.at[pl.ds(0, D), columns], semaphores.at[part])
+
+
+def padded_rows(values):
+    values = values.astype(f32)
+    rest = jnp.zeros((WIDE - D - RANK, values.shape[1]), f32)
+    return jnp.concatenate([values, rest])
+
+
+def widen(target, middle):
+    rest = jnp.zeros((middle.shape[0], WIDE - D - RANK), f32)
+    target[:, D:] = jnp.concatenate([middle, rest], axis=1).astype(bf16)
 
 
 def fetch_feed(place, refs, project, expand, contract, semaphores):
     if len(refs) == 3:
         pltpu.make_async_copy(refs[0], project, semaphores.at[0]).start()
-        for tile in range(FF // TILE):
+        for part in range(4):
             pltpu.make_async_copy(
-                refs[1].at[:, pl.ds(tile * TILE, TILE)],
-                expand.at[tile // 2, tile % 2],
-                semaphores.at[1],
+                refs[1].at[:, pl.ds(part * D, D)],
+                expand.at[part, pl.ds(0, D)],
+                semaphores.at[1 + part],
             ).start()
-        pltpu.make_async_copy(refs[2], contract, semaphores.at[2]).start()
+            pltpu.make_async_copy(
+                refs[2].at[pl.ds(part * D, D)],
+                contract.at[pl.ds(part * D, D), pl.ds(0, D)],
+                semaphores.at[5 + part],
+            ).start()
         return
-
-    def each(step):
-        for far in range(2):
-            for dz, dy, dx, device in piece_places(place, far, False):
-                step(far, dz, dy, dx, device)
 
     def rows_of(device, deep, first, count):
         return pl.ds(pl.multiple_of(device * deep + first, 16), count)
@@ -137,37 +146,36 @@
         )
         return block.at[pl.ds(first, count)]
 
-    def from_project(far, dz, dy, dx, device):
+    every = [
+        (far, dz, dy, dx, device)
+        for far in range(2)
+        for dz, dy, dx, device in piece_places(place, far, False)
+    ]
+    for *at, device in every:
         pltpu.make_async_copy(
-            main_rows(0, 32, far, dz, dy, dx),
-            project.at[rows_of(device, 32, 0, 32)],
-            semaphores.at[0],
+            main_rows(0, 32, *at), project.at[rows_of(device, 32, 0, 32)], semaphores.at[0]
         ).start()
-
-    def from_expand(far, dz, dy, dx, device):
-        for part in range(4):
-            for half in range(2):
-                pltpu.make_async_copy(
-                    main_rows(32 * (1 + part), 32, far, dz, dy, dx).at[:, pl.ds(half * TILE, TILE)],
-                    expand.at[part, half, rows_of(device, 32, 0, 32)],
-                    semaphores.at[1],
-                ).start()
-
-    def from_contract(far, dz, dy, dx, device):
-        pltpu.make_async_copy(
-            main_rows(160, FIRST_ROWS, far, dz, dy, dx),
-            contract.at[rows_of(device, 128, 0, FIRST_ROWS)],
-            semaphores.at[2],
-        ).start()
-        pltpu.make_async_copy(
-            refs[14 + far].at[dz, 2 * dy + dx],
-            contract.at[rows_of(device, 128, FIRST_ROWS, 128 - FIRST_ROWS)],
-            semaphores.at[2],
-        ).start()
-
-    each(from_project)
-    each(from_expand)
-    each(from_contract)
+    for part in range(4):
+        for *at, device in every:
+            pltpu.make_async_copy(
+                main_rows(32 * (1 + part), 32, *at),
+                expand.at[part, rows_of(device, 32, 0, 32)],
+                semaphores.at[1 + part],
+            ).start()
+        for far, dz, dy, dx, device in every:
+            if dz != part:
+                continue
+            columns = pl.ds(0, D)
+            pltpu.make_async_copy(
+                main_rows(160, FIRST_ROWS, far, dz, dy, dx),
+                contract.at[rows_of(device, 128, 0, FIRST_ROWS), columns],
+                semaphores.at[5 + part],
+            ).start()
+            pltpu.make_async_copy(
+                refs[14].at[dz, place[3] ^ far, 2 * dy + dx],
+                contract.at[rows_of(device, 128, FIRST_ROWS, 128 - FIRST_ROWS), columns],
+                semaphores.at[5 + part],
+            ).start()
 
 
 def smem():
@@ -180,7 +188,7 @@
 
 def enter_kernel(count, place, latents, modulation, down, up, *refs):
     weights = refs[:count]
-    queries, keys_values, entering, middle, weight, semaphores = refs[count:]
+    queries, keys_values, entering, middle, wide, weight, semaphores = refs[count:]
     step_at = pl.program_id(0)
 
     @pl.when(step_at == 0)
@@ -194,22 +202,22 @@
             ]
             values = values.astype(bf16)
             entering[rows] = values
-            middle[rows] = product_back(values, down[...]).astype(bf16)
+            wide[rows, :D] = values
 
         each_chunk(latents.shape[0], step)
-        wait_attend(weight, semaphores, 0)
-        wait_attend(weight, semaphores, 1)
-
-    here = pl.ds(pl.multiple_of(step_at * TILE, TILE), TILE)
-    projected = (
-        product(entering[...], weight[:, here]) + product(middle[...], up[...])
-    ).astype(bf16)
-
-    @pl.when(step_at < D // TILE)
+        weight[D:] = padded_rows(up[...]).astype(bf16)
+        values = product_back(entering[...], down[...]).astype(bf16)
+        middle[...] = values
+        widen(wide, values.astype(f32))
+
+    wait_attend(weight, semaphores, step_at)
+    projected = product(wide[...], weight[:, pl.ds(pl.multiple_of(step_at * D, D), D)]).astype(bf16)
+
+    @pl.when(step_at == 0)
     def _():
         queries[...] = projected
 
-    @pl.when(step_at >= D // TILE)
+    @pl.when(step_at > 0)
     def _():
         keys_values[...] = projected
 
@@ -219,18 +227,18 @@
     columns = up.shape[1]
     return pl.pallas_call(
         lambda *refs: enter_kernel(len(weights), *refs),
-        grid=(columns // TILE,),
+        grid=(columns // D,),
         in_specs=[
             smem(),
             whole((rows, D)),
             whole(modulation.shape),
             whole(down.shape),
-            pl.BlockSpec((RANK, TILE), lambda j: (0, j)),
+            whole(up.shape),
         ]
         + anywhere(weights),
         out_specs=[
-            pl.BlockSpec((rows, TILE), lambda j: (0, jnp.minimum(j, D // TILE - 1))),
-            pl.BlockSpec((rows, TILE), lambda j: (0, jnp.maximum(j - D // TILE, 0))),
+            whole((rows, D)),
+            pl.BlockSpec((rows, D), lambda j: (0, jnp.maximum(j - 1, 0))),
             whole((rows, D)),
             whole((rows, RANK)),
         ],
@@ -240,7 +248,11 @@
             jax.ShapeDtypeStruct((rows, D), bf16),
             jax.ShapeDtypeStruct((rows, RANK), bf16),
         ],
-        scratch_shapes=[pltpu.VMEM((D, columns), bf16), pltpu.SemaphoreType.DMA((2,))],
+        scratch_shapes=[
+            pltpu.VMEM((rows, WIDE), bf16),
+            pltpu.VMEM((WIDE, columns), bf16),
+            pltpu.SemaphoreType.DMA((3,)),
+        ],
         compiler_params=params(),
         cost_estimate=TINY,
         name="enter",
@@ -315,7 +327,7 @@
     grad_queries, grad_near, grad_far, keys_sum, values_sum
 ):
     rows = queries.shape[0]
-    block = 256
+    block = 512
     scale = HEAD_DIM ** (-0.5)
     scaled = queries[...] * jnp.asarray(scale, bf16)
     scaled_t = scaled.T
@@ -410,8 +422,8 @@
         grad_project_down, grad_project_up, grad_expand_down, grad_expand_up,
         grad_contract_down, grad_contract_up,
         branch_attend, middle_tokens, entering, grad_branch, branch, grad_entering,
-        middle_project, middle_expand, middle_contract, back_contract, back_expand,
-        grad_branch_attend, back_project, project, expand, contract, semaphores,
+        middle_project, middle_expand, back_contract, grad_branch_attend, back_project,
+        project, expand, contract, semaphores,
     ) = refs[count:]
     step_at = pl.program_id(0)
     rows_all = latents.shape[0]
@@ -422,80 +434,85 @@
     @pl.when(step_at == 0)
     def _():
         fetch_feed(place, weights, project, expand, contract, semaphores)
+
+        def first(rows):
+            grad_branch[rows, :D] = (cotangent[rows].astype(f32) * row(GATE_EXPAND)).astype(bf16)
+            branch[rows] = jnp.zeros((CHUNK, WIDE), f32)
+            grad_entering[rows] = jnp.zeros((CHUNK, WIDE), f32)
+
+        each_chunk(rows_all, first)
+        middle = product_back(grad_branch[:, :D], contract_up[...]).astype(bf16)
+        back_contract[...] = middle
+        widen(grad_branch, middle.astype(f32))
+        middle_project[...] = product_back(attended[...], project_down[...]).astype(bf16)
         wait_for(project, semaphores.at[0])
+        branch_attend[...] = product(attended[...], project[...]) + product(
+            middle_project[...], project_up[...]
+        )
 
         def step(rows):
-            middle = product_back(attended[rows], project_down[...]).astype(bf16)
-            middle_project[rows] = middle
-            out = product(attended[rows], project[...]) + product(
-                middle, project_up[...]
-            )
-            branch_attend[rows] = out
-            tokens = latents[rows].astype(f32) + row(GATE_ATTEND) * out
+            tokens = latents[rows].astype(f32) + row(GATE_ATTEND) * branch_attend[rows]
             middle_tokens[rows] = tokens
             normed, _ = normalize(tokens)
-            values = (normed * (1.0 + row(SCALE_EXPAND)) + row(SHIFT_EXPAND)).astype(bf16)
-            entering[rows] = values
-            middle_expand[rows] = product_back(values, expand_down[...]).astype(bf16)
-            grads = (cotangent[rows].astype(f32) * row(GATE_EXPAND)).astype(bf16)
-            grad_branch[rows] = grads
-            back_contract[rows] = product_back(grads, contract_up[...]).astype(bf16)
-            branch[rows] = jnp.zeros((CHUNK, D), f32)
-            grad_entering[rows] = jnp.zeros((CHUNK, D), f32)
-            middle_contract[rows] = jnp.zeros((CHUNK, RANK), f32)
-            back_expand[rows] = jnp.zeros((CHUNK, RANK), f32)
+            values = normed * (1.0 + row(SCALE_EXPAND)) + row(SHIFT_EXPAND)
+            entering[rows, :D] = values.astype(bf16)
 
         each_chunk(rows_all, step)
-        wait_for(expand, semaphores.at[1])
-        wait_for(contract, semaphores.at[2])
-
-    wide = expand[step_at // 2, step_at % 2]
-    deep = contract[pl.ds(pl.multiple_of(step_at * TILE, TILE), TILE)]
-    hidden = product(entering[...], wide) + product(middle_expand[...], expand_up[...])
+        middle = product_back(entering[:, :D], expand_down[...]).astype(bf16)
+        middle_expand[...] = middle
+        widen(entering, middle.astype(f32))
+
+    here = pl.ds(pl.multiple_of(step_at * D, D), D)
+    expand[step_at, D:] = padded_rows(expand_up[...]).astype(bf16)
+    contract[here, D:] = padded_rows(contract_down[...]).T.astype(bf16)
+    wait_for(expand.at[step_at, pl.ds(0, D)], semaphores.at[1 + step_at])
+    wait_for(contract.at[here, pl.ds(0, D)], semaphores.at[5 + step_at])
+    wide = expand[step_at]
+    deep = contract[here]
+    grads = product_back(grad_branch[...], deep)
+    hidden = product(entering[...], wide)
     activated, slope = gelu_both(hidden)
     activated = activated.astype(bf16)
+    grads = (grads * slope).astype(bf16)
     branch[...] += product(activated, deep)
-    middle_contract[...] += product_back(activated, contract_down[...])
-    grads = product_back(grad_branch[...], deep) + product(back_contract[...], contract_down[...])
-    grads = (grads * slope).astype(bf16)
     grad_entering[...] += product_back(grads, wide)
-    back_expand[...] += product_back(grads, expand_up[...])
     grad_contract_down[...] = product_rows(back_contract[...], activated)
     grad_expand_up[...] = product_rows(middle_expand[...], grads)
 
     @pl.when(step_at == pl.num_programs(0) - 1)
     def _():
         sums[...] = jnp.zeros_like(sums)
-        last_middle = middle_contract[...].astype(bf16)
-        last_back = back_expand[...].astype(bf16)
-        grad_contract_up[...] = product_rows(last_middle, grad_branch[...])
-        grad_expand_down[...] = product_rows(last_back, entering[...])
+        last_middle = branch[:, D : D + RANK].astype(bf16)
+        last_back = grad_entering[:, D : D + RANK].astype(bf16)
+        grad_contract_up[...] = product_rows(last_middle, grad_branch[:, :D])
+        grad_expand_down[...] = product_rows(last_back, entering[:, :D])
+        branch[:, :D] += product(last_middle, contract_up[...])
+        grad_entering[:, :D] += product(last_back, expand_down[...])
 
         def add(which, values):
             sums[which : which + 1] += jnp.sum(values, axis=0, keepdims=True)
 
         def step(rows):
-            out = branch[rows] + product(middle_contract[rows].astype(bf16), contract_up[...])
+            out = branch[rows, :D]
             tokens = middle_tokens[rows]
             block_output[rows] = (tokens + row(GATE_EXPAND) * out).astype(bf16)
             cotangents = cotangent[rows].astype(f32)
             add(GATE_EXPAND, cotangents * out)
-            grad = grad_entering[rows] + product(back_expand[rows].astype(bf16), expand_down[...])
+            grad = grad_entering[rows, :D]
             normed, inverse = normalize(tokens)
             add(SHIFT_EXPAND, grad)
             add(SCALE_EXPAND, grad * normed)
             grad = cotangents + normalize_back(grad * (1.0 + row(SCALE_EXPAND)), normed, inverse)
             grad_middle[rows] = grad
             add(GATE_ATTEND, grad * branch_attend[rows])
-            grad = (grad * row(GATE_ATTEND)).astype(bf16)
-            grad_branch_attend[rows] = grad
-            back = product_back(grad, project_up[...]).astype(bf16)
-            back_project[rows] = back
-            grad_attended[rows] = (
-                product_back(grad, project[...]) + product(back, project_down[...])
-            ).astype(bf16)
+            grad_branch_attend[rows] = (grad * row(GATE_ATTEND)).astype(bf16)
 
         each_chunk(rows_all, step)
+        back_project[...] = product_back(grad_branch_attend[...], project_up[...]).astype(bf16)
+        grad_attended[...] = (
+            product_back(grad_branch_attend[...], project[...])
+            + product(back_project[...], project_down[...])
+        ).astype(bf16)
         grad_project_up[...] = product_rows(middle_project[...], grad_branch_attend[...])
         grad_project_down[...] = product_rows(back_project[...], attended[...])
 
@@ -503,7 +520,7 @@
 def feed(place, latents, attended, cotangent, modulation, weights, chosen):
     rows = latents.shape[0]
     project_down, project_up, expand_down, expand_up, contract_down, contract_up = chosen
-    tile = pl.BlockSpec((RANK, TILE), lambda j: (0, j))
+    tile = pl.BlockSpec((RANK, D), lambda j: (0, j))
     narrow = whole((RANK, D))
 
     def buffer(columns, dtype):
@@ -511,7 +528,7 @@
 
     return pl.pallas_call(
         lambda *refs: feed_kernel(len(weights), *refs),
-        grid=(FF // TILE,),
+        grid=(FF // D,),
         in_specs=[
             smem(),
             whole((rows, D)),
@@ -553,21 +570,19 @@
         scratch_shapes=[
             buffer(D, f32),
             buffer(D, f32),
-            buffer(D, bf16),
-            buffer(D, bf16),
-            buffer(D, f32),
-            buffer(D, f32),
+            buffer(WIDE, bf16),
+            buffer(WIDE, bf16),
+            buffer(WIDE, f32),
+            buffer(WIDE, f32),
             buffer(RANK, bf16),
             buffer(RANK, bf16),
-            buffer(RANK, f32),
             buffer(RANK, bf16),
-            buffer(RANK, f32),
             buffer(D, bf16),
             buffer(RANK, bf16),
             pltpu.VMEM((D, D), bf16),
-            pltpu.VMEM((4, 2, D, TILE), bf16),
-            pltpu.VMEM((FF, D), bf16),
-            pltpu.SemaphoreType.DMA((3,)),
+            pltpu.VMEM((4, WIDE, D), bf16),
+            pltpu.VMEM((FF, WIDE), bf16),
+            pltpu.SemaphoreType.DMA((9,)),
         ],
         compiler_params=params(),
         cost_estimate=TINY,
@@ -577,63 +592,55 @@
 
 
 def leave_kernel(
-    count, place, queries_0, queries_1, own_0, own_1, other_0, other_1, down, up, entering, middle,
-    latents, modulation, grad_middle, *refs,
+    count, place, queries_0, queries_1, own_0, own_1, other_0, other_1, down, up, middle,
+    modulation, *refs,
 ):
     weights = refs[:count]
-    input_grad, sums, grad_down, grad_up, back, weight, semaphores = refs[count:]
+    (
+        entering_there, latents_there, grad_middle_there, input_grad, sums, grad_down, grad_up,
+        total, weight, entering, latents, grad_middle, semaphores, semaphore,
+    ) = refs[count:]
     step_at = pl.program_id(0)
     rows_all = latents.shape[0]
+    copies = [
+        pltpu.make_async_copy(source, target, semaphore.at[which])
+        for which, (source, target) in enumerate(
+            ((entering_there, entering), (latents_there, latents), (grad_middle_there, grad_middle))
+        )
+    ]
+
+    def through(first, second):
+        grads = jnp.concatenate([first, second], axis=1)
+        grad_up[...] = product_rows(middle[...], grads)
+        return product_back(grads, weight[:, pl.ds(pl.multiple_of(step_at * D, D), D)])
 
     @pl.when(step_at == 0)
     def _():
         fetch_attend(place, weights, weight, semaphores)
+        for copy in copies:
+            copy.start()
+        weight[D:] = padded_rows(up[...]).astype(bf16)
         wait_attend(weight, semaphores, 0)
-
-    @pl.when(step_at == 3)
+        total[...] = through(queries_0[...], queries_1[...])
+
+    @pl.when(step_at > 0)
     def _():
-        wait_attend(weight, semaphores, 1)
-
-    here = pl.ds(pl.multiple_of(leave_tile(step_at) * TILE, TILE), TILE)
-
-    def accumulate(grads):
-        grad_up[...] = product_rows(middle[...], grads)
-        first = product_back(grads, weight[:, here])
-        second = product_back(grads, up[...])
-
-        @pl.when(step_at == 0)
-        def _():
-            input_grad[...] = first
-            back[...] = second
-
-        @pl.when(step_at > 0)
-        def _():
-            input_grad[...] += first
-            back[...] += second
-
-    @pl.when(step_at == 0)
-    def _():
-        accumulate(queries_0[...])
-
-    @pl.when(step_at == 1)
-    def _():
-        accumulate(queries_1[...])
-
-    @pl.when(jnp.logical_or(step_at == 2, step_at == 4))
-    def _():
-        accumulate((own_0[0] + other_0[0]).astype(bf16))
-
-    @pl.when(jnp.logical_or(step_at == 3, step_at == 5))
-    def _():
-        accumulate((own_1[0] + other_1[0]).astype(bf16))
+        wait_attend(weight, semaphores, step_at)
+        total[...] += through(
+            (own_0[0] + other_0[0]).astype(bf16), (own_1[0] + other_1[0]).astype(bf16)
+        )
 
     @pl.when(step_at == pl.num_programs(0) - 1)
     def _():
+        for copy in copies:
+            copy.wait()
         sums[...] = jnp.zeros_like(sums)
-        grad_down[...] = product_rows(back[...].astype(bf16), entering[...])
+        last = total[:, D : D + RANK].astype(bf16)
+        grad_down[...] = product_rows(last, entering[...])
+        total[:, :D] += product(last, down[...])
 
         def step(rows):
-            grad = input_grad[rows] + product(back[rows].astype(bf16), down[...])
+            grad = total[rows, :D]
             normed, inverse = normalize(latents[rows].astype(f32))
             sums[0:1] += jnp.sum(grad, axis=0, keepdims=True)
             sums[1:2] += jnp.sum(grad * normed, axis=0, keepdims=True)
@@ -643,32 +650,21 @@
         each_chunk(rows_all, step)
 
 
-def leave_tile(step_at):
-    return step_at
-
-
 def leave(place, queries, own, other, weights, down, up, entering, middle, latents, modulation,
           grad_middle):
     rows = latents.shape[0]
     columns = up.shape[1]
-    tile = pl.BlockSpec((RANK, TILE), lambda j: (0, leave_tile(j)))
-    pair = pl.BlockSpec((1, rows, TILE), lambda j: (j // 4, 0, 0))
+    tile = pl.BlockSpec((RANK, D), lambda j: (0, j))
+    pair = pl.BlockSpec((1, rows, TILE), lambda j: (j // 2, 0, 0))
     return pl.pallas_call(
         lambda *refs: leave_kernel(len(weights), *refs),
-        grid=(columns // TILE,),
+        grid=(columns // D,),
         in_specs=[smem()]
         + [whole((rows, TILE))] * 2
         + [pair] * 4
-        + [
-            whole(down.shape),
-            tile,
-            whole((rows, D)),
-            whole((rows, RANK)),
-            whole((rows, D)),
-            whole(modulation.shape),
-            whole((rows, D)),
-        ]
-        + anywhere(weights),
+        + [whole(down.shape), whole(up.shape), whole((rows, RANK)), whole(modulation.shape)]
+        + anywhere(weights)
+        + anywhere(range(3)),
         out_specs=[whole((rows, D)), whole((8, D)), whole((RANK, D)), tile],
         out_shape=[
             jax.ShapeDtypeStruct((rows, D), f32),
@@ -677,15 +673,19 @@
             jax.ShapeDtypeStruct((RANK, columns), f32),
         ],
         scratch_shapes=[
-            pltpu.VMEM((rows, RANK), f32),
-            pltpu.VMEM((D, columns), bf16),
-            pltpu.SemaphoreType.DMA((2,)),
+            pltpu.VMEM((rows, WIDE), f32),
+            pltpu.VMEM((WIDE, columns), bf16),
+            pltpu.VMEM((rows, D), bf16),
+            pltpu.VMEM((rows, D), bf16),
+            pltpu.VMEM((rows, D), f32),
+            pltpu.SemaphoreType.DMA((3,)),
+            pltpu.SemaphoreType.DMA((3,)),
         ],
         compiler_params=params(),
         cost_estimate=TINY,
         name="leave",
-    )(place, *queries, *own, *other, down, up, entering, middle, latents, modulation, grad_middle,
-      *weights)
+    )(place, *queries, *own, *other, down, up, middle, modulation, *weights, entering, latents,
+      grad_middle)
 
 
 PARTS_OF_HALVES = (
@@ -837,24 +837,30 @@
 def joined(pieces):
     return pieces[0] if len(pieces) == 1 else jnp.concatenate(pieces, axis=1)
 
-def pack_into(own, core, grads, out):
-    chips, span = out.shape[1], out.shape[3]
+def pack_into(own, core, grads, near, far):
+    chips, span = near.shape[0], near.shape[2]
+    on_first = core[0] == 0
     for chip in range(chips):
-        for k in range(2):
-            device = 2 * chip + k
+        parts = []
+        for device in (2 * chip, 2 * chip + 1):
             pieces = [grad[:, device * width : (device + 1) * width] for width, grad in zip(own, grads)]
             if span > sum(own):
                 pieces.append(jnp.zeros((RANK, span - sum(own)), f32))
-            out[core[0] ^ k, chip] = joined(pieces)
+            parts.append(joined(pieces))
+        near[chip] = jnp.where(on_first, parts[0], parts[1])
+        far[chip] = jnp.where(on_first, parts[1], parts[0])
+
+
+def packed_shapes(own, chips):
+    return [jax.ShapeDtypeStruct((chips, RANK, rounded_up(sum(own))), f32)] * 2
 
 
 def pack_late(own, core, grads):
-    chips = grads[0].shape[1] // own[0] // 2
     return pl.pallas_call(
-        lambda core, *refs: pack_into(own, core, refs[:-1], refs[-1]),
-        out_shape=jax.ShapeDtypeStruct((2, chips, RANK, rounded_up(sum(own))), f32),
+        lambda core, *refs: pack_into(own, core, refs[:-2], *refs[-2:]),
+        out_shape=packed_shapes(own, grads[0].shape[1] // own[0] // 2),
         in_specs=[smem()] + vmem(len(grads)),
-        out_specs=vmem(1)[0],
+        out_specs=vmem(2),
         cost_estimate=TINY,
         name="pack_late",
     )(core, *grads)
@@ -862,7 +868,7 @@
 
 def pack_early_kernel(
     own, core, attend, attend_there, feed, feed_there, middle, lifted, up, down_grad, up_grad,
-    out, grad_modulation, grad_middle, modulate_down, modulate_up
+    near, far, grad_modulation, grad_middle, modulate_down, modulate_up
 ):
     early = attend[...] + attend_there[...]
     late = feed[...] + feed_there[...]
@@ -874,20 +880,16 @@
     keep = jnp.where(core[0] == 0, 1.0, 0.0)
     modulate_down[...] = product_rows(back, lifted[...]) * keep
     modulate_up[...] = product_rows(middle[...], grads) * keep
-    pack_into(own, core, (modulate_down, modulate_up, down_grad, up_grad), out)
+    pack_into(own, core, (modulate_down, modulate_up, down_grad, up_grad), near, far)
 
 
 def pack_early(own, core, sums, middle, lifted, up, grads):
-    chips = grads[0].shape[1] // own[2] // 2
     return pl.pallas_call(
         lambda *refs: pack_early_kernel(own, *refs),
-        out_shape=[
-            jax.ShapeDtypeStruct((2, chips, RANK, rounded_up(sum(own))), f32),
-            jax.ShapeDtypeStruct((1, 6 * D), bf16),
-            jax.ShapeDtypeStruct((1, RANK), bf16),
-        ],
+        out_shape=packed_shapes(own, grads[0].shape[1] // own[2] // 2)
+        + [jax.ShapeDtypeStruct((1, 6 * D), bf16), jax.ShapeDtypeStruct((1, RANK), bf16)],
         in_specs=[smem()] + vmem(9),
-        out_specs=vmem(3),
+        out_specs=vmem(4),
         scratch_shapes=[pltpu.VMEM((RANK, D), f32), pltpu.VMEM((RANK, 6 * D), f32)],
         cost_estimate=TINY,
         name="pack_early",
@@ -976,8 +978,16 @@
         return [self.attend_crossed[1], self.attend_crossed[3]]
 
     def cross_last(self):
-        self.plane = [self.last] + [self.exchange(self.last, over) for over in (1, 2, 3)]
+        self.plane = [self.last, self.exchange(self.last, 1)]
         return self.plane[1:]
+
+    def cross_last_y(self):
+        self.plane.append(self.exchange(self.last, 2))
+        return self.plane[2:]
+
+    def cross_last_again(self, *before):
+        self.plane.append(self.exchange(after(self.plane[1], *before), 2))
+        return self.plane[3:]
 
     def lines(self, values):
         groups = [[z * 4 + line for z in range(self.chips // 4)] for line in range(4)]
@@ -995,7 +1005,17 @@
         return swap_all(self.cross_again(*self.attend_crossed))
 
     def cross_main(self):
-        self.planes = self.lines(jnp.stack(self.plane))
+        planes = lax.all_gather(
+            jnp.stack(self.plane),
+            ("dp", "seq"),
+            axis=0,
+            tiled=False,
+            axis_index_groups=[
+                [2 * (z * 4 + line) + core for z in range(self.chips // 4) for core in range(2)]
+                for line in range(4)
+            ],
+        )
+        self.planes = planes.reshape(self.chips // 4, 2, *planes.shape[1:])
         first, second = self.main[:2], self.main[2:]
         self.crossed = [
             self.exchange(first, 1), self.exchange(second, 1),
@@ -1012,20 +1032,20 @@
         return before
 
     def more_main(self, *before):
-        self.far_main = swap_cores(self.main)
-        before, joined = self.join([self.crossed[1], self.crossed[2], self.far_main], before)
-        self.crossed[1], self.crossed[2], self.far_main = joined
+        far = [swap_cores(self.main), swap_cores(self.crossed[0])]
+        before, joined = self.join([self.crossed[1], self.crossed[2], *far], before)
+        self.crossed[1:3], self.far = joined[:2], joined[2:]
         first, second = after(self.crossed[0], before[0]), after(self.crossed[3], before[0])
         self.diagonal = [self.exchange(first, 2), self.exchange(second, 1)]
         return before
 
     def feed_all(self, *before):
-        far = [swap_cores(self.crossed[0]), swap_cores(self.crossed[3])]
-        before, joined = self.join([*far, *self.diagonal, self.planes], before)
-        far, diagonal, planes = joined[:2], joined[2:4], joined[4:]
+        far = [swap_cores(array) for array in self.crossed[1:]]
+        before, joined = self.join([*self.diagonal, *far, self.planes], before)
+        diagonal, far, planes = joined[:2], joined[2:-1], joined[-1]
         main = [self.main, *self.crossed, *diagonal]
-        other = [self.far_main, far[0], swap_cores(self.crossed[1]), swap_cores(self.crossed[2]), far[1]]
-        return before, main + other + [swap_cores(array) for array in diagonal] + swap_all(planes)
+        other = [*self.far, *far, *(swap_cores(array) for array in diagonal)]
+        return before, main + other + [planes]
 
 
 class WholeGather:
@@ -1039,6 +1059,12 @@
         return self.all[:1]
 
     def cross_last(self):
+        return []
+
+    def cross_last_y(self):
+        return []
+
+    def cross_last_again(self, *before):
         return []
 
     def cross_main(self):
@@ -1119,7 +1145,8 @@
             swap_cores(columns_of(1 - core)),
             jnp.concatenate([laid_out(early, tables[:4]), laid_out(late, tables[4:])], axis=2),
         )
-        block = to_chips(after(block, *begun))
+        block = after(block, *begun, *gather.cross_last_y())
+        block = after(to_chips(block), *gather.cross_last_again(block))
         *chosen, modulation, middle_modulate, lifted = open_block(
             early, late, core_at, condition, block, swap_cores(block)
         )
@@ -1142,10 +1169,13 @@
         block_output, grad_middle, grad_attended, sums_feed, *grads_late = feed(
             place, tokens, attended, cotangent[0], modulation, feed_all, chosen_late
         )
-        grads_attended = [
-            attend_back(queries, near, far, grad_attended, logsum, 2 * half)
-            for half, logsum in enumerate((logsum_0, logsum_1))
-        ]
+        packed, packed_far = pack_late(late, core_at, grads_late)
+        half_0 = attend_back(queries, near, far, grad_attended, logsum_0, 0)
+        packed_far = swap_cores(packed_far)
+        grad_attended, packed_far = lax.optimization_barrier((grad_attended, packed_far))
+        arrived_late = to_chips(packed + packed_far)
+        half_1 = attend_back(queries, near, far, grad_attended, logsum_1, 2)
+        grads_attended = [half_0, half_1]
         grad_queries, grad_near, grad_far = zip(*grads_attended)
         input_grad, sums_attend, *grads_attend = leave(
             place,
@@ -1162,9 +1192,8 @@
             grad_middle,
         )
 
-        packed = pack_late(late, core_at, [after(grads_late[0], grad_far[1]), *grads_late[1:]])
-        arrived_late = to_chips(packed[0] + swap_cores(packed[1]))
-        packed, grad_modulation, grad_middle_modulate = pack_early(
+        sums_attend, arrived_late = lax.optimization_barrier((sums_attend, arrived_late))
+        packed, packed_far, grad_modulation, grad_middle_modulate = pack_early(
             early,
             core_at,
             (sums_attend, swap_cores(sums_attend), sums_feed, swap_cores(sums_feed)),
@@ -1173,16 +1202,15 @@
             modulate_up,
             grads_attend,
         )
-        arrived_early = to_chips(packed[0] + swap_cores(packed[1]))
+        arrived_early = to_chips(packed + swap_cores(packed_far))
         grad_lifted = product_back(grad_modulation, modulate_all) + product(
             grad_middle_modulate, modulate_down
         )
         condition_grad = jax.vjp(jax.nn.silu, condition.astype(f32))[1](grad_lifted)[0]
-        arrived_early, arrived_late, condition_grad = lax.optimization_barrier(
-            (arrived_early, arrived_late, condition_grad)
-        )
+        arrived_late = after(arrived_late, condition_grad)
+        owned_late = table_sums(late, (2, 3, 4), choice, arrived_late)
+        arrived_early, *owned_late = lax.optimization_barrier((arrived_early, *owned_late))
         owned_early = table_sums(early, (0, 1), choice, arrived_early)
-        owned_late = table_sums(late, (2, 3, 4), choice, arrived_late)
         return (block_output[None], input_grad[None], condition_grad, *owned_early, *owned_late)
 
     return local

time: 321 us -> 293 us (0.913)
  waiting for transfers between devices: 74.6 us -> 65 us
  Pallas kernels: 142 us -> 133 us
  local copies, waits for them, and re-layouts: 16.1 us -> 8.52 us
  starting transfers between devices: 52.7 us -> 49.2 us
    ppermute x13, waiting for transfers between devices: 22.1 us -> 34.3 us  [exchange(): lax.ppermute(values, 'dp', [(chip, chip ^ over) for chip in range(self.ch...]
    ppermute x21 -> x20, waiting for transfers between devices: 19.6 us -> 8.43 us  [swap_cores(): return lax.ppermute(values, 'seq', [(0, 1), (1, 0)])]
    ppermute x3, waiting for transfers between devices: 5.66 us -> 0.01 us  [along(): lax.ppermute(values, 'dp', [(chip, (chip + 4 * step) % self.chips) for ch...]
    unnamed x76 -> x40, local copies, waits for them, and re-layouts: 7.57 us -> 2.33 us
    all_to_all x4, waiting for transfers between devices: 26.4 us -> 21.5 us  [to_chips(): return lax.all_to_all(values, 'dp', split_axis=0, concat_axis=0, tiled=True)]
    pallas_call x1, Pallas kernels: 18.2 us -> 13.8 us  [leave(): pl.pallas_call(lambda *refs: leave_kernel(len(weights), *refs), grid=(col...]
  transfers between devices with their start and end apart: 44 -> 43, of which waited for: 21 -> 19; matrix products, arithmetic and copies ran while one was open for 8% -> 9% of each run, Pallas kernels for 43% -> 45%
where the time goes in v3:
time: 293 us; the launch traced here: 289 us
  Pallas kernels  133 us (45%)
  waiting for transfers between devices  65 us (22%)
  starting transfers between devices  49.2 us (17%)
  between operations  14.3 us (5%)
  other arithmetic  10.7 us (4%)
  matrix products  8.71 us (3%)
  local copies, waits for them, and re-layouts  8.52 us (3%)
    pallas_call x1, Pallas kernels, feed(): pl.pallas_call(lambda *refs: feed_kernel(len(weights), *refs), grid=(FF /...  42.7 us
    ppermute x13, waiting for transfers between devices, exchange(): lax.ppermute(values, 'dp', [(chip, chip ^ over) for chip in range(self.ch...  34.3 us
    pallas_call x2, Pallas kernels, attend_back(): pl.pallas_call(attend_back_kernel, grid=(groups,), in_specs=[at(0), at(0)...  30.7 us
    all_to_all x4, starting transfers between devices, to_chips(): return lax.all_to_all(values, 'dp', split_axis=0, concat_axis=0, tiled=True)  21.5 us
    all_to_all x4, waiting for transfers between devices, to_chips(): return lax.all_to_all(values, 'dp', split_axis=0, concat_axis=0, tiled=True)  21.5 us
    ppermute x13, starting transfers between devices, exchange(): lax.ppermute(values, 'dp', [(chip, chip ^ over) for chip in range(self.ch...  19.4 us
    pallas_call x2, Pallas kernels, attend(): pl.pallas_call(lambda *refs: attend_kernel(*refs[:5], *refs[5 + len(given...  18 us
    pallas_call x1, Pallas kernels, leave(): pl.pallas_call(lambda *refs: leave_kernel(len(weights), *refs), grid=(col...  13.8 us
  transfers between devices with their start and end apart: 43, of which 19 were waited for; matrix products, arithmetic and copies ran while one was open for 9% of the time, Pallas kernels for 45%

profile of v3, /device:TPU:0, one launch (start us, length us, event | category | flops | bytes accessed | tf_op | source)
XLA Modules:
  0.0 289.2 jit_solution(15672574832028676497)
XLA Ops:
  7.2 1.9 cut_weights.1
  9.1 2.9 %collective-permute-start = (bf16[96,1024]{1,0:T(8,128)(2,1)}, bf16[96,1024]{1,0:T(8,128)(2,1)}, u32[]{:S(2)}, u32[]{:S(2)}) collective-permute-start(bf16[96,1024]{1,0:T(8,128)(2,1)} %get-tuple-element.109), channel_id=1, source_target_pairs={{0,2},{2,0},{4,6},{6,4},{8,10},{10,8},{12,14},{14,12},{16,18},{18,... | collective-permute-start | bytes 589832 | tf_op jit(solution)/shard_map/ppermute | solution.py:965
  12.1 1.5 collective-permute-start.7
  13.6 2.6 collective-permute-start.4
  16.2 1.3 collective-permute-start.5
  18.2 1.4 write_notes.1
  19.6 4.7 %all-to-all-start = ((bf16[16,16,128]{2,1,0:T(8,128)(2,1)}), bf16[16,16,128]{2,1,0:T(8,128)(2,1)S(1)}, u32[]{:S(2)}, u32[]{:S(2)}) async-start(bf16[16,16,128]{2,1,0:T(8,128)(2,1)} %write_notes.1), calls=%async_computation | async-start | bytes 131072 | tf_op jit(solution)/shard_map/all_to_all | solution.py:1108
  25.1 0.9 constant_dynamic-slice_fusion.1
  26.0 1.0 fusion.6
  27.0 1.7 concatenate.17.refs_5_
  28.7 0.7 pad_maximum_fusion.6
  30.2 2.0 collective-permute-start.6
  32.2 1.5 collective-permute-start.3
  36.3 2.6 prepare.1
  38.9 3.2 %collective-permute-done.6 = bf16[2,32,3072]{2,1,0:T(8,128)(2,1)S(1)} collective-permute-done((bf16[2,32,3072]{2,1,0:T(8,128)(2,1)S(1)}, bf16[2,32,3072]{2,1,0:T(8,128)(2,1)S(1)}, u32[]{:S(2)}, u32[]{:S(2)}) %collective-permute-start.6) | collective-permute-done | bytes 393248 | tf_op jit(solution)/shard_map/ppermute | solution.py:965
  42.0 1.5 collective-permute-done.3
  43.9 6.2 %collective-permute-done.8 = bf16[96,1024]{1,0:T(8,128)(2,1)S(1)} collective-permute-done((bf16[96,1024]{1,0:T(8,128)(2,1)}, bf16[96,1024]{1,0:T(8,128)(2,1)S(1)}, u32[]{:S(2)}, u32[]{:S(2)}) %collective-permute-start.8) | collective-permute-done | bytes 196640 | tf_op jit(solution)/shard_map/ppermute | solution.py:965
  50.0 2.0 pad_maximum_fusion.2
  52.1 5.6 %all-to-all-start.1 = ((bf16[16,16,1152]{2,1,0:T(8,128)(2,1)}), bf16[16,16,1152]{2,1,0:T(8,128)(2,1)S(1)}, u32[]{:S(2)}, u32[]{:S(2)}) async-start(bf16[16,16,1152]{2,1,0:T(8,128)(2,1)} %prepare.1), calls=%async_computation.1 | async-start | bytes 1179648 | tf_op jit(solution)/shard_map/all_to_all | solution.py:1108
  58.1 2.0 collective-permute-start.11
  60.0 1.1 pad_maximum_fusion.refs_5_.refs_11_
  61.1 1.5 collective-permute-start.10
  62.7 14.5 %all-to-all-done.1.refs_2_ = bf16[16,16,1152]{2,1,0:T(8,128)(2,1)S(1)} async-done(((bf16[16,16,1152]{2,1,0:T(8,128)(2,1)}), bf16[16,16,1152]{2,1,0:T(8,128)(2,1)S(1)}, u32[]{:S(2)}, u32[]{:S(2)}) %all-to-all-start.1) | async-done | bytes 589856 | tf_op jit(solution)/shard_map/all_to_all | solution.py:1108
  77.7 4.4 %collective-permute-done.11.refs_8_.refs_14_ = bf16[2,2,32,3072]{3,2,1,0:T(8,128)(2,1)S(1)} collective-permute-done((bf16[2,2,32,3072]{3,2,1,0:T(8,128)(2,1)S(1)}, bf16[2,2,32,3072]{3,2,1,0:T(8,128)(2,1)S(1)}, u32[]{:S(2)}, u32[]{:S(2)}) %collective-permute-start.11) | collective-permute-done | bytes 786464 | tf_op jit(solution)/shard_map/ppermute | solution.py:965
  82.1 1.4 collective-permute-done.10.refs_7_.refs_13_
  83.5 2.6 fusion.20
  86.2 1.1 collective-permute-start.16
  87.3 1.4 collective-permute-start.17
  89.3 2.5 open_block.1
  91.8 9.9 %enter.1 = (bf16[512,1024]{1,0:T(8,128)(2,1)}, bf16[512,2048]{1,0:T(8,128)(2,1)}, bf16[512,1024]{1,0:T(8,128)(2,1)}, bf16[512,16]{1,0:T(8,128)(2,1)}) custom-call(s32[4]{0:T(128)} %pad_add_fusion.refs_0_, bf16[512,1024]{1,0:T(8,128)(2,1)} %bitcast.57, f32[8,1024]{1,0:T(8,128)} %get-tuple-element.114.refs_2_.refs_4_.refs_10_, ...), custom_call_target="tpu_custom_call" | custom-call | flops 1 | bytes 1 | tf_op jit(solution)/shard_map/enter/pallas_call | solution.py:228
  101.8 4.7 %collective-permute-done.16.refs_12_ = bf16[2,192,1024]{2,1,0:T(8,128)(2,1)} collective-permute-done((bf16[2,192,1024]{2,1,0:T(8,128)(2,1)}, bf16[2,192,1024]{2,1,0:T(8,128)(2,1)}, u32[]{:S(2)}, u32[]{:S(2)}) %collective-permute-start.16) | collective-permute-done | bytes 786464 | tf_op jit(solution)/shard_map/ppermute | solution.py:965
  106.5 0.8 collective-permute-done.17.refs_15_
  107.8 1.0 collective-permute-start.19
  108.7 1.7 collective-permute-start.20
  110.4 3.9 %collective-permute-done.18.refs_3_.refs_4_.keys_far.values_far = bf16[512,2048]{1,0:T(8,128)(2,1)} collective-permute-done((bf16[512,2048]{1,0:T(8,128)(2,1)}, bf16[512,2048]{1,0:T(8,128)(2,1)}, u32[]{:S(2)}, u32[]{:S(2)}) %collective-permute-start.18) | collective-permute-done | bytes 2097184 | tf_op jit(solution)/shard_map/ppermute | solution.py:699
  114.4 9.0 %attend.2 = (bf16[512,1024]{1,0:T(8,128)(2,1)}, f32[2,512,128]{2,1,0:T(8,128)}) custom-call(bf16[512,1024]{1,0:T(8,128)(2,1)} %get-tuple-element.120.refs_0_.queries, bf16[512,2048]{1,0:T(8,128)(2,1)} %get-tuple-element.121.refs_1_.refs_2_.keys_near.values_near, bf16[512,2048]{1,0:T(8,128)(2,1)} %get-tuple-element.121.refs_1_.refs_2_.keys_near.values_near, ...), custom_call_target="tpu_custom_call" | custom-call | flops 1 | bytes 1 | tf_op jit(solution)/shard_map/attend/pallas_call | solution.py:309
  123.4 4.1 %collective-permute-done.19.refs_13_ = bf16[2,192,1024]{2,1,0:T(8,128)(2,1)} collective-permute-done((bf16[2,192,1024]{2,1,0:T(8,128)(2,1)}, bf16[2,192,1024]{2,1,0:T(8,128)(2,1)}, u32[]{:S(2)}, u32[]{:S(2)}) %collective-permute-start.19) | collective-permute-done | bytes 786464 | tf_op jit(solution)/shard_map/ppermute | solution.py:965
  127.5 0.7 collective-permute-done.20.refs_14_
  128.2 1.0 collective-permute-start.24
  129.3 1.4 collective-permute-start.23
  131.2 9.0 %attend.3 = (bf16[512,1024]{1,0:T(8,128)(2,1)}, f32[2,512,128]{2,1,0:T(8,128)}) custom-call(bf16[512,1024]{1,0:T(8,128)(2,1)} %get-tuple-element.120.refs_0_.queries, bf16[512,2048]{1,0:T(8,128)(2,1)} %get-tuple-element.121.refs_1_.refs_2_.keys_near.values_near, ...), custom_call_target="tpu_custom_call", output_to_operand_aliasing={{0}: (5, {})} | custom-call | flops 1 | bytes 1 | tf_op jit(solution)/shard_map/attend/pallas_call | solution.py:309
  140.2 6.6 %collective-permute-done.24.refs_17_ = bf16[2,192,1024]{2,1,0:T(8,128)(2,1)S(1)} collective-permute-done((bf16[2,192,1024]{2,1,0:T(8,128)(2,1)}, bf16[2,192,1024]{2,1,0:T(8,128)(2,1)S(1)}, u32[]{:S(2)}, u32[]{:S(2)}) %collective-permute-start.24) | collective-permute-done | bytes 786464 | tf_op jit(solution)/shard_map/ppermute | solution.py:965
  146.7 0.8 collective-permute-done.23.refs_16_
  148.1 2.1 collective-permute-done.28.refs_23_
  150.2 0.9 copy-done.10
  151.2 42.7 %feed.1 = (bf16[512,1024]{1,0:T(8,128)(2,1)}, f32[512,1024]{1,0:T(8,128)}, bf16[512,1024]{1,0:T(8,128)(2,1)}, f32[8,1024]{1,0:T(8,128)}, f32[16,1024]{1,0:T(8,12...) custom-call(s32[4]{0:T(128)} %pad_add_fusion.refs_0_, ...), custom_call_target="tpu_custom_call" | custom-call | flops 1 | bytes 1 | tf_op jit(solution)/shard_map/feed/pallas_call | solution.py:529
  193.9 2.4 pack_late.1
  196.5 15.6 %attend_back.2 = (bf16[512,512]{1,0:T(8,128)(2,1)}, f32[2,512,512]{2,1,0:T(8,128)}, f32[2,512,512]{2,1,0:T(8,128)}) custom-call(bf16[512,1024]{1,0:T(8,128)(2,1)} %get-tuple-element.120.refs_0_.queries, bf16[512,2048]{1,0:T(8,128)(2,1)} %get-tuple-element.121.refs_1_.refs_2_.keys_near.values_near, ...), custom_call_target="tpu_custom_call" | custom-call | flops 1 | bytes 1 | tf_op jit(solution)/shard_map/attend_back/pallas_call | solution.py:387
  212.5 15.1 %attend_back.3 = (bf16[512,512]{1,0:T(8,128)(2,1)}, f32[2,512,512]{2,1,0:T(8,128)}, f32[2,512,512]{2,1,0:T(8,128)}) custom-call(bf16[512,1024]{1,0:T(8,128)(2,1)} %get-tuple-element.120.refs_0_.queries, bf16[512,2048]{1,0:T(8,128)(2,1)} %get-tuple-element.121.refs_1_.refs_2_.keys_near.values_near, ...), custom_call_target="tpu_custom_call" | custom-call | flops 1 | bytes 1 | tf_op jit(solution)/shard_map/attend_back/pallas_call | solution.py:387
  227.7 0.8 add.72
  228.6 5.9 %all-to-all-start.2 = ((f32[16,16,384]{2,1,0:T(8,128)}), f32[16,16,384]{2,1,0:T(8,128)S(1)}, u32[]{:S(2)}, u32[]{:S(2)}) async-start(f32[16,16,384]{2,1,0:T(8,128)} %add.72), calls=%async_computation.2 | async-start | bytes 786432 | tf_op jit(solution)/shard_map/all_to_all | solution.py:1108
  234.7 13.8 %leave.1 = (f32[512,1024]{1,0:T(8,128)}, f32[8,1024]{1,0:T(8,128)}, f32[16,1024]{1,0:T(8,128)}, f32[16,3072]{1,0:T(8,128)}) custom-call(s32[4]{0:T(128)} %pad_add_fusion.refs_0_, bf16[512,512]{1,0:T(8,128)(2,1)} %get-tuple-element.151.refs_1_, bf16[512,512]{1,0:T(8,128)(2,1)} %get-tuple-element.161.refs_2_, f32[2,512,512]{2,1,0:T(8,128)} %get-tuple-element.162.refs_3_, ...), custom_call_target="tpu_custom_call" | custom-call | flops 1 | bytes 1 | tf_op jit(solution)/shard_map/leave/pallas_call | solution.py:659
  248.6 4.4 %all-to-all-done.2.refs_1_ = f32[16,16,384]{2,1,0:T(8,128)S(1)} async-done(((f32[16,16,384]{2,1,0:T(8,128)}), f32[16,16,384]{2,1,0:T(8,128)S(1)}, u32[]{:S(2)}, u32[]{:S(2)}) %all-to-all-start.2) | async-done | bytes 393248 | tf_op jit(solution)/shard_map/all_to_all | solution.py:1108
  253.1 1.4 collective-permute-done.33.refs_2_
  255.1 2.7 pack_early.1
  257.9 0.8 fusion.16
  258.7 1.0 collective-permute-done.35
  259.7 1.8 add.76
  261.5 5.3 %all-to-all-start.3 = ((f32[16,16,384]{2,1,0:T(8,128)}), f32[16,16,384]{2,1,0:T(8,128)S(1)}, u32[]{:S(2)}, u32[]{:S(2)}) async-start(f32[16,16,384]{2,1,0:T(8,128)} %add.76), calls=%async_computation.3 | async-start | bytes 786432 | tf_op jit(solution)/shard_map/all_to_all | solution.py:1108
  266.9 7.9 %fusion.7 = f32[1,1024]{1,0:T(1,128)S(1)} fusion(bf16[1024,6144]{1,0:T(8,128)(2,1)} %all-gather.6.cloned.1.call-done, bf16[1,6144]{1,0:T(2,128)(2,1)} %get-tuple-element.180), kind=kOutput, calls=%fused_computation.15 | convolution fusion | flops 12582912 | bytes 12599296 | tf_op jit(solution)/shard_map/dot_general | solution.py:33
  275.5 2.1 table_sums.2
  277.6 2.2 all-to-all-done.3.refs_1_
  279.8 0.7 copy-done.7
  280.5 1.9 table_sums.3
  (105 shorter events, 10.8 us)
Async XLA Ops:
  7.2 21.5 %copy-start.5 = (bf16[32,6144]{1,0:T(8,128)(2,1)S(1)}, bf16[32,6144]{1,0:T(8,128)(2,1)}, u32[]{:S(2)}) copy-start(bf16[32,6144]{1,0:T(8,128)(2,1)} %param.23) | copy-start | bytes 1179652
  9.1 25.5 %collective-permute-start = (bf16[96,1024]{1,0:T(8,128)(2,1)}, bf16[96,1024]{1,0:T(8,128)(2,1)}, u32[]{:S(2)}, u32[]{:S(2)}) collective-permute-start(bf16[96,1024]{1,0:T(8,128)(2,1)} %get-tuple-element.109), channel_id=1, source_target_pairs={{0,2},{2,0},{4,6},{6,4},{8,10},{10,8},{12,14},{14,12},{16,18},{18,... | collective-permute-start | bytes 589832 | tf_op jit(solution)/shard_map/ppermute | solution.py:965
  12.1 26.8 %collective-permute-start.7 = (bf16[96,1024]{1,0:T(8,128)(2,1)}, bf16[96,1024]{1,0:T(8,128)(2,1)}, u32[]{:S(2)}, u32[]{:S(2)}) collective-permute-start(bf16[96,1024]{1,0:T(8,128)(2,1)} %get-tuple-element.109), channel_id=1, source_target_pairs={{0,4},{2,6},{4,0},{6,2},{8,12},{10,14},{12,8},{14,10},{16,20},{18,... | collective-permute-start | bytes 589832 | tf_op jit(solution)/shard_map/ppermute | solution.py:965
  13.6 16.5 %collective-permute-start.4 = (bf16[32,3072]{1,0:T(8,128)(2,1)}, bf16[32,3072]{1,0:T(8,128)(2,1)S(1)}, u32[]{:S(2)}, u32[]{:S(2)}) collective-permute-start(bf16[32,3072]{1,0:T(8,128)(2,1)} %param.24), channel_id=1, source_target_pairs={{0,16},{2,18},{4,20},{6,22},{8,24},{10,26},{12,28},{14,30},{16,0},... | collective-permute-start | bytes 589832 | tf_op jit(solution)/shard_map/ppermute | solution.py:968
  16.2 13.9 %collective-permute-start.5 = (bf16[32,3072]{1,0:T(8,128)(2,1)}, bf16[32,3072]{1,0:T(8,128)(2,1)S(1)}, u32[]{:S(2)}, u32[]{:S(2)}) collective-permute-start(bf16[32,3072]{1,0:T(8,128)(2,1)} %param.24), channel_id=1, source_target_pairs={{0,24},{2,26},{4,28},{6,30},{8,0},{10,2},{12,4},{14,6},{16,8},{18,... | collective-permute-start | bytes 589832 | tf_op jit(solution)/shard_map/ppermute | solution.py:968
  17.5 14.6 %collective-permute-start.2 = (bf16[32,3072]{1,0:T(8,128)(2,1)}, bf16[32,3072]{1,0:T(8,128)(2,1)S(1)}, u32[]{:S(2)}, u32[]{:S(2)}) collective-permute-start(bf16[32,3072]{1,0:T(8,128)(2,1)} %param.24), channel_id=1, source_target_pairs={{0,8},{2,10},{4,12},{6,14},{8,16},{10,18},{12,20},{14,22},{16,24},... | collective-permute-start | bytes 589832 | tf_op jit(solution)/shard_map/ppermute | solution.py:968
  19.6 12.5 %copy-start.13 = (bf16[32,3072]{1,0:T(8,128)(2,1)S(1)}, bf16[32,3072]{1,0:T(8,128)(2,1)}, u32[]{:S(2)}) copy-start(bf16[32,3072]{1,0:T(8,128)(2,1)} %param.24) | copy-start | bytes 589828
  19.6 15.0 %all-to-all-start = ((bf16[16,16,128]{2,1,0:T(8,128)(2,1)}), bf16[16,16,128]{2,1,0:T(8,128)(2,1)S(1)}, u32[]{:S(2)}, u32[]{:S(2)}) async-start(bf16[16,16,128]{2,1,0:T(8,128)(2,1)} %write_notes.1), calls=%async_computation | async-start | bytes 131072 | tf_op jit(solution)/shard_map/all_to_all | solution.py:1108
  24.3 59.2 %all-gather.8.cloned.1.call-start = ((), (), s32[]{:S(2)}) async-start(), calls=%async_computation.5 | async-start | bytes 1966080 | tf_op jit(solution)/shard_map/all_gather | solution.py:994
  25.1 122.5 %all-gather.10.cloned.1.call-start = ((), (), s32[]{:S(2)}) async-start(), calls=%async_computation.6 | async-start | bytes 7077888 | tf_op jit(solution)/shard_map/all_gather | solution.py:1008
  30.1 6.2 %collective-permute-start.1 = (bf16[32,3072]{1,0:T(8,128)(2,1)}, bf16[32,3072]{1,0:T(8,128)(2,1)}, u32[]{:S(2)}, u32[]{:S(2)}) collective-permute-start(bf16[32,3072]{1,0:T(8,128)(2,1)} %pad_maximum_fusion.6), channel_id=1, source_target_pairs={{0,1},{1,0},{2,3},{3,2},{4,5},{5,4},{6,7},{7,6},{8,9},{9,8},{10,11... | collective-permute-start | bytes 589832 | tf_op jit(solution)/shard_map/ppermute | solution.py:699
  30.1 19.9 %copy-start.14 = (bf16[96,1024]{1,0:T(8,128)(2,1)S(1)}, bf16[96,1024]{1,0:T(8,128)(2,1)}, u32[]{:S(2)}) copy-start(bf16[96,1024]{1,0:T(8,128)(2,1)} %get-tuple-element.109) | copy-start | bytes 589828
  30.2 11.8 %collective-permute-start.6 = (bf16[2,32,3072]{2,1,0:T(8,128)(2,1)S(1)}, bf16[2,32,3072]{2,1,0:T(8,128)(2,1)S(1)}, u32[]{:S(2)}, u32[]{:S(2)}) collective-permute-start(bf16[2,32,3072]{2,1,0:T(8,128)(2,1)S(1)} %get-tuple-element.208), channel_id=1, source_target_pairs={{0,4},{2,6},{4,0},{6,2},{8,12},{10,14},{12,8},{14,10},{16,20},{18,... | collective-permute-start | bytes 1179656 | tf_op jit(solution)/shard_map/ppermute | solution.py:965
  32.2 11.3 %collective-permute-start.3 = (bf16[2,32,3072]{2,1,0:T(8,128)(2,1)S(1)}, bf16[2,32,3072]{2,1,0:T(8,128)(2,1)S(1)}, u32[]{:S(2)}, u32[]{:S(2)}) collective-permute-start(bf16[2,32,3072]{2,1,0:T(8,128)(2,1)S(1)} %get-tuple-element.210), channel_id=1, source_target_pairs={{0,2},{2,0},{4,6},{6,4},{8,10},{10,8},{12,14},{14,12},{16,18},{18,... | collective-permute-start | bytes 1179656 | tf_op jit(solution)/shard_map/ppermute | solution.py:965
  43.5 8.6 %copy-start.11 = (bf16[2,32,3072]{2,1,0:T(8,128)(2,1)}, bf16[2,32,3072]{2,1,0:T(8,128)(2,1)S(1)}, u32[]{:S(2)}) copy-start(bf16[2,32,3072]{2,1,0:T(8,128)(2,1)S(1)} %collective-permute-done.3) | copy-start | bytes 1179652
  43.5 6.5 %collective-permute-start.8 = (bf16[96,1024]{1,0:T(8,128)(2,1)}, bf16[96,1024]{1,0:T(8,128)(2,1)S(1)}, u32[]{:S(2)}, u32[]{:S(2)}) collective-permute-start(bf16[96,1024]{1,0:T(8,128)(2,1)} %collective-permute-done), channel_id=1, source_target_pairs={{0,4},{2,6},{4,0},{6,2},{8,12},{10,14},{12,8},{14,10},{16,20},{18,... | collective-permute-start | bytes 589832 | tf_op jit(solution)/shard_map/ppermute | solution.py:965
  52.1 25.1 %all-to-all-start.1 = ((bf16[16,16,1152]{2,1,0:T(8,128)(2,1)}), bf16[16,16,1152]{2,1,0:T(8,128)(2,1)S(1)}, u32[]{:S(2)}, u32[]{:S(2)}) async-start(bf16[16,16,1152]{2,1,0:T(8,128)(2,1)} %prepare.1), calls=%async_computation.1 | async-start | bytes 1179648 | tf_op jit(solution)/shard_map/all_to_all | solution.py:1108
  57.7 209.1 %all-gather.6.cloned.1.call-start = ((), (), s32[]{:S(2)}) async-start(), calls=%async_computation.4 | async-start | bytes 12976128 | tf_op jit(solution)/shard_map/all_gather | solution.py:1166
  58.0 28.1 %copy-start = (bf16[2,2,32,3072]{3,2,1,0:T(8,128)(2,1)}, bf16[2,2,32,3072]{3,2,1,0:T(8,128)(2,1)S(1)}, u32[]{:S(2)}) copy-start(bf16[2,2,32,3072]{3,2,1,0:T(8,128)(2,1)S(1)} %pad_maximum_fusion.1.refs_6_.refs_12_) | copy-start | bytes 2359300
  58.1 24.1 %collective-permute-start.11 = (bf16[2,2,32,3072]{3,2,1,0:T(8,128)(2,1)S(1)}, bf16[2,2,32,3072]{3,2,1,0:T(8,128)(2,1)S(1)}, u32[]{:S(2)}, u32[]{:S(2)}) collective-permute-start(bf16[2,2,32,3072]{3,2,1,0:T(8,128)(2,1)S(1)} %pad_maximum_fusion.1.refs_6_.refs_12_), channel_id=1, source_target_pairs={{0,2},{2,0},{4,6},{6,4},{8,10},{10,8},{12,14},{14,12},{16,18},{18,... | collective-permute-start | bytes 2359304 | tf_op jit(solution)/shard_map/ppermute | solution.py:965
  61.1 30.7 %copy-start.1 = (bf16[2,2,32,3072]{3,2,1,0:T(8,128)(2,1)}, bf16[2,2,32,3072]{3,2,1,0:T(8,128)(2,1)S(1)}, u32[]{:S(2)}) copy-start(bf16[2,2,32,3072]{3,2,1,0:T(8,128)(2,1)S(1)} %pad_maximum_fusion.refs_5_.refs_11_) | copy-start | bytes 2359300
  61.1 22.4 %collective-permute-start.10 = (bf16[2,2,32,3072]{3,2,1,0:T(8,128)(2,1)S(1)}, bf16[2,2,32,3072]{3,2,1,0:T(8,128)(2,1)}, u32[]{:S(2)}, u32[]{:S(2)}) collective-permute-start(bf16[2,2,32,3072]{3,2,1,0:T(8,128)(2,1)S(1)} %pad_maximum_fusion.refs_5_.refs_11_), channel_id=1, source_target_pairs={{0,4},{2,6},{4,0},{6,2},{8,12},{10,14},{12,8},{14,10},{16,20},{18,... | collective-permute-start | bytes 2359304 | tf_op jit(solution)/shard_map/ppermute | solution.py:965
  62.7 23.5 %collective-permute-start.13 = (bf16[2,2,32,3072]{3,2,1,0:T(8,128)(2,1)S(1)}, bf16[2,2,32,3072]{3,2,1,0:T(8,128)(2,1)}, u32[]{:S(2)}, u32[]{:S(2)}) collective-permute-start(bf16[2,2,32,3072]{3,2,1,0:T(8,128)(2,1)S(1)} %pad_maximum_fusion.1.refs_6_.refs_12_), channel_id=1, source_target_pairs={{0,1},{1,0},{2,3},{3,2},{4,5},{5,4},{6,7},{7,6},{8,9},{9,8},{10,11... | collective-permute-start | bytes 2359304 | tf_op jit(solution)/shard_map/ppermute | solution.py:699
  77.2 8.9 %copy-start.4 = (bf16[16,16,1152]{2,1,0:T(8,128)(2,1)}, bf16[16,16,1152]{2,1,0:T(8,128)(2,1)S(1)}, u32[]{:S(2)}) copy-start(bf16[16,16,1152]{2,1,0:T(8,128)(2,1)S(1)} %all-to-all-done.1.refs_2_) | copy-start | bytes 1769476
  77.2 10.1 %collective-permute-start.9 = (bf16[16,16,1152]{2,1,0:T(8,128)(2,1)S(1)}, bf16[16,16,1152]{2,1,0:T(8,128)(2,1)}, u32[]{:S(2)}, u32[]{:S(2)}) collective-permute-start(bf16[16,16,1152]{2,1,0:T(8,128)(2,1)S(1)} %all-to-all-done.1.refs_2_), channel_id=1, source_target_pairs={{0,1},{1,0},{2,3},{3,2},{4,5},{5,4},{6,7},{7,6},{8,9},{9,8},{10,11... | collective-permute-start | bytes 1769480 | tf_op jit(solution)/shard_map/ppermute | solution.py:699
  77.2 14.6 %collective-permute-start.12 = (bf16[2,2,32,3072]{3,2,1,0:T(8,128)(2,1)S(1)}, bf16[2,2,32,3072]{3,2,1,0:T(8,128)(2,1)}, u32[]{:S(2)}, u32[]{:S(2)}) collective-permute-start(bf16[2,2,32,3072]{3,2,1,0:T(8,128)(2,1)S(1)} %pad_maximum_fusion.refs_5_.refs_11_), channel_id=1, source_target_pairs={{0,1},{1,0},{2,3},{3,2},{4,5},{5,4},{6,7},{7,6},{8,9},{9,8},{10,11... | collective-permute-start | bytes 2359304 | tf_op jit(solution)/shard_map/ppermute | solution.py:699
  82.1 9.7 %copy-start.3 = (bf16[2,2,32,3072]{3,2,1,0:T(8,128)(2,1)}, bf16[2,2,32,3072]{3,2,1,0:T(8,128)(2,1)S(1)}, u32[]{:S(2)}) copy-start(bf16[2,2,32,3072]{3,2,1,0:T(8,128)(2,1)S(1)} %collective-permute-done.11.refs_8_.refs_14_) | copy-start | bytes 2359300
  82.1 9.7 %collective-permute-start.15 = (bf16[2,2,32,3072]{3,2,1,0:T(8,128)(2,1)S(1)}, bf16[2,2,32,3072]{3,2,1,0:T(8,128)(2,1)}, u32[]{:S(2)}, u32[]{:S(2)}) collective-permute-start(bf16[2,2,32,3072]{3,2,1,0:T(8,128)(2,1)S(1)} %collective-permute-done.11.refs_8_.refs_14_), channel_id=1, source_target_pairs={{0,1},{1,0},{2,3},{3,2},{4,5},{5,4},{6,7},{7,6},{8,9},{9,8},{10,11... | collective-permute-start | bytes 2359304 | tf_op jit(solution)/shard_map/ppermute | solution.py:699
  83.5 8.3 %collective-permute-start.14 = (bf16[2,2,32,3072]{3,2,1,0:T(8,128)(2,1)}, bf16[2,2,32,3072]{3,2,1,0:T(8,128)(2,1)}, u32[]{:S(2)}, u32[]{:S(2)}) collective-permute-start(bf16[2,2,32,3072]{3,2,1,0:T(8,128)(2,1)} %collective-permute-done.10.refs_7_.refs_13_), channel_id=1, source_target_pairs={{0,1},{1,0},{2,3},{3,2},{4,5},{5,4},{6,7},{7,6},{8,9},{9,8},{10,11... | collective-permute-start | bytes 2359304 | tf_op jit(solution)/shard_map/ppermute | solution.py:699
  86.2 20.3 %collective-permute-start.16 = (bf16[2,192,1024]{2,1,0:T(8,128)(2,1)}, bf16[2,192,1024]{2,1,0:T(8,128)(2,1)}, u32[]{:S(2)}, u32[]{:S(2)}) collective-permute-start(bf16[2,192,1024]{2,1,0:T(8,128)(2,1)} %bitcast.22), channel_id=1, source_target_pairs={{0,2},{2,0},{4,6},{6,4},{8,10},{10,8},{12,14},{14,12},{16,18},{18,... | collective-permute-start | bytes 2359304 | tf_op jit(solution)/shard_map/ppermute | solution.py:965
  87.3 20.0 %collective-permute-start.17 = (bf16[2,192,1024]{2,1,0:T(8,128)(2,1)}, bf16[2,192,1024]{2,1,0:T(8,128)(2,1)}, u32[]{:S(2)}, u32[]{:S(2)}) collective-permute-start(bf16[2,192,1024]{2,1,0:T(8,128)(2,1)} %bitcast.23), channel_id=1, source_target_pairs={{0,4},{2,6},{4,0},{6,2},{8,12},{10,14},{12,8},{14,10},{16,20},{18,... | collective-permute-start | bytes 2359304 | tf_op jit(solution)/shard_map/ppermute | solution.py:965
  91.8 15.4 %copy-start.2 = (bf16[768,1024]{1,0:T(8,128)(2,1)S(1)}, bf16[768,1024]{1,0:T(8,128)(2,1)}, u32[]{:S(2)}) copy-start(bf16[768,1024]{1,0:T(8,128)(2,1)} %all-gather.8.cloned.1.call-done) | copy-start | bytes 4718596
  107.2 7.0 %collective-permute-start.18 = (bf16[512,2048]{1,0:T(8,128)(2,1)}, bf16[512,2048]{1,0:T(8,128)(2,1)}, u32[]{:S(2)}, u32[]{:S(2)}) collective-permute-start(bf16[512,2048]{1,0:T(8,128)(2,1)} %get-tuple-element.121.refs_1_.refs_2_.keys_near.values_near), channel_id=1, source_target_pairs={{0,1},{1,0},{2,3},{3,2},{4,5},{5,4},{6,7},{7,6},{8,9},{9,8},{10,11... | collective-permute-start | bytes 6291464 | tf_op jit(solution)/shard_map/ppermute | solution.py:699
  107.3 21.0 %collective-permute-start.21 = (bf16[4,192,1024]{2,1,0:T(8,128)(2,1)S(1)}, bf16[4,192,1024]{2,1,0:T(8,128)(2,1)}, u32[]{:S(2)}, u32[]{:S(2)}) collective-permute-start(bf16[4,192,1024]{2,1,0:T(8,128)(2,1)S(1)} %bitcast.61), channel_id=1, source_target_pairs={{0,1},{1,0},{2,3},{3,2},{4,5},{5,4},{6,7},{7,6},{8,9},{9,8},{10,11... | collective-permute-start | bytes 4718600 | tf_op jit(solution)/shard_map/ppermute | solution.py:699
  107.8 19.8 %collective-permute-start.19 = (bf16[2,192,1024]{2,1,0:T(8,128)(2,1)}, bf16[2,192,1024]{2,1,0:T(8,128)(2,1)}, u32[]{:S(2)}, u32[]{:S(2)}) collective-permute-start(bf16[2,192,1024]{2,1,0:T(8,128)(2,1)} %bitcast.23), channel_id=1, source_target_pairs={{0,2},{2,0},{4,6},{6,4},{8,10},{10,8},{12,14},{14,12},{16,18},{18,... | collective-permute-start | bytes 2359304 | tf_op jit(solution)/shard_map/ppermute | solution.py:965
  108.7 19.5 %collective-permute-start.20 = (bf16[2,192,1024]{2,1,0:T(8,128)(2,1)}, bf16[2,192,1024]{2,1,0:T(8,128)(2,1)}, u32[]{:S(2)}, u32[]{:S(2)}) collective-permute-start(bf16[2,192,1024]{2,1,0:T(8,128)(2,1)} %bitcast.22), channel_id=1, source_target_pairs={{0,4},{2,6},{4,0},{6,2},{8,12},{10,14},{12,8},{14,10},{16,20},{18,... | collective-permute-start | bytes 2359304 | tf_op jit(solution)/shard_map/ppermute | solution.py:965
  110.4 17.8 %collective-permute-start.22 = (bf16[2,192,1024]{2,1,0:T(8,128)(2,1)}, bf16[2,192,1024]{2,1,0:T(8,128)(2,1)}, u32[]{:S(2)}, u32[]{:S(2)}) collective-permute-start(bf16[2,192,1024]{2,1,0:T(8,128)(2,1)} %collective-permute-done.16.refs_12_), channel_id=1, source_target_pairs={{0,1},{1,0},{2,3},{3,2},{4,5},{5,4},{6,7},{7,6},{8,9},{9,8},{10,11... | collective-permute-start | bytes 2359304 | tf_op jit(solution)/shard_map/ppermute | solution.py:699
  114.3 25.9 %collective-permute-start.27 = (bf16[2,192,1024]{2,1,0:T(8,128)(2,1)}, bf16[2,192,1024]{2,1,0:T(8,128)(2,1)}, u32[]{:S(2)}, u32[]{:S(2)}) collective-permute-start(bf16[2,192,1024]{2,1,0:T(8,128)(2,1)} %collective-permute-done.17.refs_15_), channel_id=1, source_target_pairs={{0,1},{1,0},{2,3},{3,2},{4,5},{5,4},{6,7},{7,6},{8,9},{9,8},{10,11... | collective-permute-start | bytes 2359304 | tf_op jit(solution)/shard_map/ppermute | solution.py:699
  128.2 18.5 %collective-permute-start.24 = (bf16[2,192,1024]{2,1,0:T(8,128)(2,1)}, bf16[2,192,1024]{2,1,0:T(8,128)(2,1)S(1)}, u32[]{:S(2)}, u32[]{:S(2)}) collective-permute-start(bf16[2,192,1024]{2,1,0:T(8,128)(2,1)} %collective-permute-done.17.refs_15_), channel_id=1, source_target_pairs={{0,2},{2,0},{4,6},{6,4},{8,10},{10,8},{12,14},{14,12},{16,18},{18,... | collective-permute-start | bytes 2359304 | tf_op jit(solution)/shard_map/ppermute | solution.py:965
  129.3 18.2 %collective-permute-start.23 = (bf16[2,192,1024]{2,1,0:T(8,128)(2,1)}, bf16[2,192,1024]{2,1,0:T(8,128)(2,1)S(1)}, u32[]{:S(2)}, u32[]{:S(2)}) collective-permute-start(bf16[2,192,1024]{2,1,0:T(8,128)(2,1)} %collective-permute-done.16.refs_12_), channel_id=1, source_target_pairs={{0,4},{2,6},{4,0},{6,2},{8,12},{10,14},{12,8},{14,10},{16,20},{18,... | collective-permute-start | bytes 2359304 | tf_op jit(solution)/shard_map/ppermute | solution.py:965
  130.7 16.8 %collective-permute-start.25 = (bf16[2,192,1024]{2,1,0:T(8,128)(2,1)}, bf16[2,192,1024]{2,1,0:T(8,128)(2,1)}, u32[]{:S(2)}, u32[]{:S(2)}) collective-permute-start(bf16[2,192,1024]{2,1,0:T(8,128)(2,1)} %collective-permute-done.19.refs_13_), channel_id=1, source_target_pairs={{0,1},{1,0},{2,3},{3,2},{4,5},{5,4},{6,7},{7,6},{8,9},{9,8},{10,11... | collective-permute-start | bytes 2359304 | tf_op jit(solution)/shard_map/ppermute | solution.py:699
  130.7 16.8 %collective-permute-start.26 = (bf16[2,192,1024]{2,1,0:T(8,128)(2,1)}, bf16[2,192,1024]{2,1,0:T(8,128)(2,1)}, u32[]{:S(2)}, u32[]{:S(2)}) collective-permute-start(bf16[2,192,1024]{2,1,0:T(8,128)(2,1)} %collective-permute-done.20.refs_14_), channel_id=1, source_target_pairs={{0,1},{1,0},{2,3},{3,2},{4,5},{5,4},{6,7},{7,6},{8,9},{9,8},{10,11... | collective-permute-start | bytes 2359304 | tf_op jit(solution)/shard_map/ppermute | solution.py:699
  146.7 4.4 %copy-start.8 = (bf16[2,192,1024]{2,1,0:T(8,128)(2,1)}, bf16[2,192,1024]{2,1,0:T(8,128)(2,1)S(1)}, u32[]{:S(2)}) copy-start(bf16[2,192,1024]{2,1,0:T(8,128)(2,1)S(1)} %collective-permute-done.24.refs_17_) | copy-start | bytes 2359300
  147.5 3.7 %copy-start.9 = (bf16[2,192,1024]{2,1,0:T(8,128)(2,1)}, bf16[2,192,1024]{2,1,0:T(8,128)(2,1)S(1)}, u32[]{:S(2)}) copy-start(bf16[2,192,1024]{2,1,0:T(8,128)(2,1)S(1)} %collective-permute-done.23.refs_16_) | copy-start | bytes 2359300
  147.5 2.7 collective-permute-start.28
  147.6 3.5 %collective-permute-start.29 = (bf16[2,192,1024]{2,1,0:T(8,128)(2,1)S(1)}, bf16[2,192,1024]{2,1,0:T(8,128)(2,1)}, u32[]{:S(2)}, u32[]{:S(2)}) collective-permute-start(bf16[2,192,1024]{2,1,0:T(8,128)(2,1)S(1)} %collective-permute-done.24.refs_17_), channel_id=1, source_target_pairs={{0,1},{1,0},{2,3},{3,2},{4,5},{5,4},{6,7},{7,6},{8,9},{9,8},{10,11... | collective-permute-start | bytes 2359304 | tf_op jit(solution)/shard_map/ppermute | solution.py:699
  150.2 0.9 copy-start.10
  196.4 16.1 %collective-permute-start.30 = (f32[16,16,384]{2,1,0:T(8,128)}, f32[16,16,384]{2,1,0:T(8,128)S(1)}, u32[]{:S(2)}, u32[]{:S(2)}) collective-permute-start(f32[16,16,384]{2,1,0:T(8,128)} %get-tuple-element.158), channel_id=1, source_target_pairs={{0,1},{1,0},{2,3},{3,2},{4,5},{5,4},{6,7},{7,6},{8,9},{9,8},{10,11... | collective-permute-start | bytes 1179656 | tf_op jit(solution)/shard_map/ppermute | solution.py:699
  212.1 15.7 %copy-start.12 = (f32[16,16,384]{2,1,0:T(8,128)S(1)}, f32[16,16,384]{2,1,0:T(8,128)}, u32[]{:S(2)}) copy-start(f32[16,16,384]{2,1,0:T(8,128)} %get-tuple-element.171) | copy-start | bytes 1179652
  212.1 22.4 %copy-start.16 = (f32[8,1024]{1,0:T(8,128)S(1)}, f32[8,1024]{1,0:T(8,128)}, u32[]{:S(2)}) copy-start(f32[8,1024]{1,0:T(8,128)} %get-tuple-element.174.refs_3_) | copy-start | bytes 98308
  212.1 22.7 %collective-permute-start.31 = (f32[2,512,512]{2,1,0:T(8,128)}, f32[2,512,512]{2,1,0:T(8,128)}, u32[]{:S(2)}, u32[]{:S(2)}) collective-permute-start(f32[2,512,512]{2,1,0:T(8,128)} %get-tuple-element.164), channel_id=1, source_target_pairs={{0,1},{1,0},{2,3},{3,2},{4,5},{5,4},{6,7},{7,6},{8,9},{9,8},{10,11... | collective-permute-start | bytes 6291464 | tf_op jit(solution)/shard_map/ppermute | solution.py:699
  227.6 7.1 %collective-permute-start.32 = (f32[2,512,512]{2,1,0:T(8,128)}, f32[2,512,512]{2,1,0:T(8,128)}, u32[]{:S(2)}, u32[]{:S(2)}) collective-permute-start(f32[2,512,512]{2,1,0:T(8,128)} %get-tuple-element.165), channel_id=1, source_target_pairs={{0,1},{1,0},{2,3},{3,2},{4,5},{5,4},{6,7},{7,6},{8,9},{9,8},{10,11... | collective-permute-start | bytes 6291464 | tf_op jit(solution)/shard_map/ppermute | solution.py:699
  228.6 24.5 %all-to-all-start.2 = ((f32[16,16,384]{2,1,0:T(8,128)}), f32[16,16,384]{2,1,0:T(8,128)S(1)}, u32[]{:S(2)}, u32[]{:S(2)}) async-start(f32[16,16,384]{2,1,0:T(8,128)} %add.72), calls=%async_computation.2 | async-start | bytes 786432 | tf_op jit(solution)/shard_map/all_to_all | solution.py:1108
  234.5 18.5 %collective-permute-start.34 = (f32[8,1024]{1,0:T(8,128)S(1)}, f32[8,1024]{1,0:T(8,128)S(1)}, u32[]{:S(2)}, u32[]{:S(2)}) collective-permute-start(f32[8,1024]{1,0:T(8,128)S(1)} %copy-done.16), channel_id=1, source_target_pairs={{0,1},{1,0},{2,3},{3,2},{4,5},{5,4},{6,7},{7,6},{8,9},{9,8},{10,11... | collective-permute-start | bytes 98312 | tf_op jit(solution)/shard_map/ppermute | solution.py:699
  234.7 23.2 %copy-start.19 = (bf16[16,1024]{1,0:T(8,128)(2,1)S(1)}, bf16[16,1024]{1,0:T(8,128)(2,1)}, u32[]{:S(2)}) copy-start(bf16[16,1024]{1,0:T(8,128)(2,1)} %get-tuple-element.183) | copy-start | bytes 98308
  253.0 21.8 %copy-start.6 = (f32[16,16,384]{2,1,0:T(8,128)}, f32[16,16,384]{2,1,0:T(8,128)S(1)}, u32[]{:S(2)}) copy-start(f32[16,16,384]{2,1,0:T(8,128)S(1)} %all-to-all-done.2.refs_1_) | copy-start | bytes 1179652
  253.0 1.4 collective-permute-start.33
  253.0 1.4 copy-start.17
  254.4 0.6 copy-start.18
  257.8 1.9 collective-permute-start.35
  261.5 18.3 %all-to-all-start.3 = ((f32[16,16,384]{2,1,0:T(8,128)}), f32[16,16,384]{2,1,0:T(8,128)S(1)}, u32[]{:S(2)}, u32[]{:S(2)}) async-start(f32[16,16,384]{2,1,0:T(8,128)} %add.76), calls=%async_computation.3 | async-start | bytes 786432 | tf_op jit(solution)/shard_map/all_to_all | solution.py:1108
  266.9 8.0 %copy-start.15 = (bf16[1,1024]{1,0:T(2,128)(2,1)S(1)}, bf16[1,1024]{1,0:T(2,128)(2,1)}, u32[]{:S(2)}) copy-start(bf16[1,1024]{1,0:T(2,128)(2,1)} %refs_1_.1) | copy-start | bytes 6148
  279.8 0.7 copy-start.7
Sparse Core Ops, SparseCore 0:
  26.7 44.6 all-gather.7
  73.0 63.4 all-gather.9
  151.3 104.5 all-gather.5

commit v4 on v3

--- a/solution.py
+++ b/solution.py
@@ -188,7 +188,7 @@
 
 def enter_kernel(count, place, latents, modulation, down, up, *refs):
     weights = refs[:count]
-    queries, keys_values, entering, middle, wide, weight, semaphores = refs[count:]
+    queries, keys_values, middle, wide, weight, semaphores = refs[count:]
     step_at = pl.program_id(0)
 
     @pl.when(step_at == 0)
@@ -200,13 +200,11 @@
             values = normed * (1.0 + modulation[SCALE_ATTEND : SCALE_ATTEND + 1]) + modulation[
                 SHIFT_ATTEND : SHIFT_ATTEND + 1
             ]
-            values = values.astype(bf16)
-            entering[rows] = values
-            wide[rows, :D] = values
+            wide[rows, :D] = values.astype(bf16)
 
         each_chunk(latents.shape[0], step)
         weight[D:] = padded_rows(up[...]).astype(bf16)
-        values = product_back(entering[...], down[...]).astype(bf16)
+        values = product_back(wide[:, :D], down[...]).astype(bf16)
         middle[...] = values
         widen(wide, values.astype(f32))
 
@@ -239,13 +237,11 @@
         out_specs=[
             whole((rows, D)),
             pl.BlockSpec((rows, D), lambda j: (0, jnp.maximum(j - 1, 0))),
-            whole((rows, D)),
             whole((rows, RANK)),
         ],
         out_shape=[
             jax.ShapeDtypeStruct((rows, D), bf16),
             jax.ShapeDtypeStruct((rows, columns - D), bf16),
-            jax.ShapeDtypeStruct((rows, D), bf16),
             jax.ShapeDtypeStruct((rows, RANK), bf16),
         ],
         scratch_shapes=[
@@ -269,33 +265,37 @@
     block = 256
     scale = HEAD_DIM ** (-0.5)
     lane = lax.broadcasted_iota(jnp.int32, (1, 128), 1)
-
-    for start in range(0, rows, block):
-        here = pl.ds(start, block)
-        q = queries[here] * jnp.asarray(scale, bf16)
-        total = jnp.zeros((block, GROUP), f32)
-        sums = jnp.zeros((block, 128), f32)
-        for head in range(GROUP // HEAD_DIM):
-            mask = head_mask(head)
-            mine = jnp.where(mask, q, jnp.zeros_like(q))
-            near = product_back(mine, keys_near[...])
-            far = product_back(mine, keys_far[...])
-            highest = jnp.maximum(
-                jnp.max(near, axis=1, keepdims=True), jnp.max(far, axis=1, keepdims=True)
-            )
-            near = jnp.exp2((near - highest) * LOG2E)
-            far = jnp.exp2((far - highest) * LOG2E)
-            denominator = jnp.sum(near, axis=1, keepdims=True) + jnp.sum(
-                far, axis=1, keepdims=True
-            )
-            share = 1.0 / denominator
-            out = product((near * share).astype(bf16), values_near[...]) + product(
-                (far * share).astype(bf16), values_far[...]
-            )
-            total = jnp.where(mask, out, total)
-            sums = jnp.where(lane == head, highest + jnp.log(denominator), sums)
-        attended[here] = total.astype(bf16)
-        logsum[0, here] = sums
+    heads = GROUP // HEAD_DIM
+    work = [(start, head) for start in range(0, rows, block) for head in range(heads)]
+
+    def scores(start, head):
+        q = queries[start : start + block] * jnp.asarray(scale, bf16)
+        mine = jnp.where(head_mask(head), q, jnp.zeros_like(q))
+        return product_back(mine, keys_near[...]), product_back(mine, keys_far[...])
+
+    ready = scores(*work[0])
+    for at, (start, head) in enumerate(work):
+        near, far = ready
+        if at + 1 < len(work):
+            ready = scores(*work[at + 1])
+        if head == 0:
+            total = jnp.zeros((block, GROUP), f32)
+            sums = jnp.zeros((block, 128), f32)
+        highest = jnp.maximum(
+            jnp.max(near, axis=1, keepdims=True), jnp.max(far, axis=1, keepdims=True)
+        )
+        near = jnp.exp2((near - highest) * LOG2E)
+        far = jnp.exp2((far - highest) * LOG2E)
+        denominator = jnp.sum(near, axis=1, keepdims=True) + jnp.sum(far, axis=1, keepdims=True)
+        share = 1.0 / denominator
+        out = product((near * share).astype(bf16), values_near[...]) + product(
+            (far * share).astype(bf16), values_far[...]
+        )
+        total = jnp.where(head_mask(head), out, total)
+        sums = jnp.where(lane == head, highest + jnp.log(denominator), sums)
+        if head == heads - 1:
+            attended[start : start + block] = total.astype(bf16)
+            logsum[0, start : start + block] = sums
 
 
 def attend(queries, near, far, first, groups, earlier=None):
@@ -332,47 +332,62 @@
     scaled = queries[...] * jnp.asarray(scale, bf16)
     scaled_t = scaled.T
     grads_t = grads[...].T
-    for start in range(0, rows, block):
+    heads = GROUP // HEAD_DIM
+    work = [(start, head) for start in range(0, rows, block) for head in range(heads)]
+
+    def scores(start, head):
         here = slice(start, start + block)
+        mask = head_mask(head)
         q = scaled[here]
         g = grads[here]
-        total = jnp.zeros((block, GROUP), f32)
-        for head in range(GROUP // HEAD_DIM):
-            mask = head_mask(head)
-            part = slice(head * HEAD_DIM, (head + 1) * HEAD_DIM)
-            mine = jnp.where(mask, q, jnp.zeros_like(q))
-            mine_g = jnp.where(mask, g, jnp.zeros_like(g))
-            shift = logsum[0, here, head : head + 1]
-            pn = jnp.exp2((product_back(mine, keys_near[...]) - shift) * LOG2E)
-            pf = jnp.exp2((product_back(mine, keys_far[...]) - shift) * LOG2E)
-            gn = product_back(mine_g, values_near[...])
-            gf = product_back(mine_g, values_far[...])
-            inner = jnp.sum(pn * gn, axis=1, keepdims=True) + jnp.sum(
-                pf * gf, axis=1, keepdims=True
-            )
-            sn = (pn * (gn - inner)).astype(bf16)
-            sf = (pf * (gf - inner)).astype(bf16)
-            out = product(sn, keys_near[...]) + product(sf, keys_far[...])
-            total = jnp.where(mask, out * scale, total)
-            vn = product(grads_t[part, here], pn.astype(bf16))
-            vf = product(grads_t[part, here], pf.astype(bf16))
-            kn = product(scaled_t[part, here], sn)
-            kf = product(scaled_t[part, here], sf)
-            if start == 0:
-                values_sum[part, :rows] = vn
-                values_sum[part, rows:] = vf
-                keys_sum[part, :rows] = kn
-                keys_sum[part, rows:] = kf
-            else:
-                values_sum[part, :rows] += vn
-                values_sum[part, rows:] += vf
-                keys_sum[part, :rows] += kn
-                keys_sum[part, rows:] += kf
-        grad_queries[here] = total.astype(bf16)
+        mine = jnp.where(mask, q, jnp.zeros_like(q))
+        mine_g = jnp.where(mask, g, jnp.zeros_like(g))
+        return (
+            product_back(mine, keys_near[...]),
+            product_back(mine, keys_far[...]),
+            product_back(mine_g, values_near[...]),
+            product_back(mine_g, values_far[...]),
+        )
+
+    ready = scores(*work[0])
+    for at, (start, head) in enumerate(work):
+        sn, sf, gn, gf = ready
+        if at + 1 < len(work):
+            ready = scores(*work[at + 1])
+        here = slice(start, start + block)
+        part = slice(head * HEAD_DIM, (head + 1) * HEAD_DIM)
+        if head == 0:
+            total = jnp.zeros((block, GROUP), f32)
+        shift = logsum[0, here, head : head + 1]
+        pn = jnp.exp2((sn - shift) * LOG2E)
+        pf = jnp.exp2((sf - shift) * LOG2E)
+        inner = jnp.sum(pn * gn, axis=1, keepdims=True) + jnp.sum(pf * gf, axis=1, keepdims=True)
+        dn = (pn * (gn - inner)).astype(bf16)
+        df = (pf * (gf - inner)).astype(bf16)
+        pn = pn.astype(bf16)
+        pf = pf.astype(bf16)
+        out = product(dn, keys_near[...]) + product(df, keys_far[...])
+        total = jnp.where(head_mask(head), out * scale, total)
+        vn = product(grads_t[part, here], pn)
+        vf = product(grads_t[part, here], pf)
+        kn = product(scaled_t[part, here], dn)
+        kf = product(scaled_t[part, here], df)
+        if start == 0:
+            values_sum[part, :rows] = vn
+            values_sum[part, rows:] = vf
+            keys_sum[part, :rows] = kn
+            keys_sum[part, rows:] = kf
+        else:
+            values_sum[part, :rows] += vn
+            values_sum[part, rows:] += vf
+            keys_sum[part, :rows] += kn
+            keys_sum[part, rows:] += kf
+        if head == heads - 1:
+            grad_queries[here] = total.astype(bf16)
     grad_near[0] = keys_sum[:, :rows].T
     grad_near[1] = values_sum[:, :rows].T
-    grad_far[0] = keys_sum[:, rows:].T
-    grad_far[1] = values_sum[:, rows:].T
+    grad_far[0] = keys_sum[:, rows:].T.astype(bf16)
+    grad_far[1] = values_sum[:, rows:].T.astype(bf16)
 
 
 def attend_back(queries, near, far, grads, logsum, first):
@@ -393,7 +408,7 @@
         out_shape=[
             jax.ShapeDtypeStruct((rows, groups * GROUP), bf16),
             jax.ShapeDtypeStruct((2, rows, groups * GROUP), f32),
-            jax.ShapeDtypeStruct((2, rows, groups * GROUP), f32),
+            jax.ShapeDtypeStruct((2, rows, groups * GROUP), bf16),
         ],
         scratch_shapes=[pltpu.VMEM((GROUP, 2 * rows), f32), pltpu.VMEM((GROUP, 2 * rows), f32)],
         compiler_params=params(),
@@ -597,7 +612,7 @@
 ):
     weights = refs[:count]
     (
-        entering_there, latents_there, grad_middle_there, input_grad, sums, grad_down, grad_up,
+        latents_there, grad_middle_there, input_grad, sums, grad_down, grad_up,
         total, weight, entering, latents, grad_middle, semaphores, semaphore,
     ) = refs[count:]
     step_at = pl.program_id(0)
@@ -605,7 +620,7 @@
     copies = [
         pltpu.make_async_copy(source, target, semaphore.at[which])
         for which, (source, target) in enumerate(
-            ((entering_there, entering), (latents_there, latents), (grad_middle_there, grad_middle))
+            ((latents_there, latents), (grad_middle_there, grad_middle))
         )
     ]
 
@@ -627,7 +642,8 @@
     def _():
         wait_attend(weight, semaphores, step_at)
         total[...] += through(
-            (own_0[0] + other_0[0]).astype(bf16), (own_1[0] + other_1[0]).astype(bf16)
+            (own_0[0] + other_0[0].astype(f32)).astype(bf16),
+            (own_1[0] + other_1[0].astype(f32)).astype(bf16),
         )
 
     @pl.when(step_at == pl.num_programs(0) - 1)
@@ -636,7 +652,6 @@
             copy.wait()
         sums[...] = jnp.zeros_like(sums)
         last = total[:, D : D + RANK].astype(bf16)
-        grad_down[...] = product_rows(last, entering[...])
         total[:, :D] += product(last, down[...])
 
         def step(rows):
@@ -644,14 +659,16 @@
             normed, inverse = normalize(latents[rows].astype(f32))
             sums[0:1] += jnp.sum(grad, axis=0, keepdims=True)
             sums[1:2] += jnp.sum(grad * normed, axis=0, keepdims=True)
-            grad = grad * (1.0 + modulation[SCALE_ATTEND : SCALE_ATTEND + 1])
-            input_grad[rows] = grad_middle[rows] + normalize_back(grad, normed, inverse)
+            scale = 1.0 + modulation[SCALE_ATTEND : SCALE_ATTEND + 1]
+            shift = modulation[SHIFT_ATTEND : SHIFT_ATTEND + 1]
+            entering[rows] = (normed * scale + shift).astype(bf16)
+            input_grad[rows] = grad_middle[rows] + normalize_back(grad * scale, normed, inverse)
 
         each_chunk(rows_all, step)
-
-
-def leave(place, queries, own, other, weights, down, up, entering, middle, latents, modulation,
-          grad_middle):
+        grad_down[...] = product_rows(last, entering[...])
+
+
+def leave(place, queries, own, other, weights, down, up, middle, latents, modulation, grad_middle):
     rows = latents.shape[0]
     columns = up.shape[1]
     tile = pl.BlockSpec((RANK, D), lambda j: (0, j))
@@ -664,7 +681,7 @@
         + [pair] * 4
         + [whole(down.shape), whole(up.shape), whole((rows, RANK)), whole(modulation.shape)]
         + anywhere(weights)
-        + anywhere(range(3)),
+        + anywhere(range(2)),
         out_specs=[whole((rows, D)), whole((8, D)), whole((RANK, D)), tile],
         out_shape=[
             jax.ShapeDtypeStruct((rows, D), f32),
@@ -679,12 +696,12 @@
             pltpu.VMEM((rows, D), bf16),
             pltpu.VMEM((rows, D), f32),
             pltpu.SemaphoreType.DMA((3,)),
-            pltpu.SemaphoreType.DMA((3,)),
+            pltpu.SemaphoreType.DMA((2,)),
         ],
         compiler_params=params(),
         cost_estimate=TINY,
         name="leave",
-    )(place, *queries, *own, *other, down, up, middle, modulation, *weights, entering, latents,
+    )(place, *queries, *own, *other, down, up, middle, modulation, *weights, latents,
       grad_middle)
 
 
@@ -896,33 +913,63 @@
     )(core, *sums, middle, lifted, up, *grads)
 
 
-def sums_kernel(own, members, choice, grads, *refs):
+def condition_kernel(grads, weight, back, down, condition, out):
+    total = jnp.zeros((weight.shape[0], 128), f32)
+    for start in range(0, weight.shape[1], 128):
+        lanes = slice(start, start + 128)
+        total += weight[:, lanes].astype(f32) * grads[:, lanes].astype(f32)
+    lifted = jnp.sum(total.T, axis=0, keepdims=True) + product(back[...], down[...])
+    values = condition[...].astype(f32)
+    gate = 1.0 / (1.0 + jnp.exp(-values))
+    out[...] = lifted * gate * (1.0 + values * (1.0 - gate))
+
+
+def condition_back(grads, weight, back, down, condition):
+    part = pl.BlockSpec((1, 128), lambda j: (0, j))
+    return pl.pallas_call(
+        condition_kernel,
+        grid=(D // 128,),
+        in_specs=[
+            whole(grads.shape),
+            pl.BlockSpec((128, weight.shape[1]), lambda j: (j, 0)),
+            whole(back.shape),
+            pl.BlockSpec((RANK, 128), lambda j: (0, j)),
+            part,
+        ],
+        out_specs=part,
+        out_shape=jax.ShapeDtypeStruct(condition.shape, f32),
+        cost_estimate=TINY,
+        compiler_params=params(),
+        name="condition_back",
+    )(grads, weight, back, down, condition)
+
+
+def sums_kernel(own, starts, choice, grads, *refs):
     outs, total = refs[:-1], refs[-1]
     lanes = lax.broadcasted_iota(jnp.int32, grads.shape[1:], 1)
     total[...] = jnp.zeros_like(total)
     for latent in range(grads.shape[0]):
-        offset = 0
-        for pair, member in enumerate(members):
-            width = own[2 * pair] + own[2 * pair + 1]
-            inside = jnp.logical_and(lanes >= offset, lanes < offset + width)
-            total[choice[latent, member]] += jnp.where(inside, grads[latent], 0.0)
-            offset += width
+        for member in range(5):
+            first = starts[2 * member]
+            last = starts[2 * member + 1] + own[2 * member + 1]
+            inside = jnp.logical_and(lanes >= first, lanes < last)
+            total[choice[latent, member]] += jnp.where(inside, grads[latent].astype(f32), 0.0)
     for entry in range(NADAPT):
         values = total[entry]
-        offset = 0
-        for width, out in zip(own, outs):
-            out[entry] = values[:, offset : offset + width]
-            offset += width
-
-def table_sums(own, members, choice, grads):
+        for start, width, out in zip(starts, own, outs):
+            out[entry] = values[:, start : start + width]
+
+
+def table_sums(own, starts, choice, grads):
     sums = pl.pallas_call(
-        lambda *refs: sums_kernel(own, members, *refs),
+        lambda *refs: sums_kernel(own, starts, *refs),
         out_shape=[jax.ShapeDtypeStruct((NADAPT, RANK, width), f32) for width in own],
         in_specs=[smem()] + vmem(1),
         out_specs=vmem(len(own)),
         scratch_shapes=[pltpu.VMEM((NADAPT,) + grads.shape[1:], f32)],
         cost_estimate=TINY,
-        name="table_sums")(choice, grads)
+        name="table_sums",
+    )(choice, grads)
     return [array.transpose(0, 2, 1) if which % 2 == 0 else array for which, array in enumerate(sums)]
 
 
@@ -978,16 +1025,16 @@
         return [self.attend_crossed[1], self.attend_crossed[3]]
 
     def cross_last(self):
-        self.plane = [self.last, self.exchange(self.last, 1)]
+        self.plane = [self.last, self.exchange(self.last, 1), self.exchange(self.last, 2)]
         return self.plane[1:]
 
-    def cross_last_y(self):
-        self.plane.append(self.exchange(self.last, 2))
-        return self.plane[2:]
-
     def cross_last_again(self, *before):
-        self.plane.append(self.exchange(after(self.plane[1], *before), 2))
-        return self.plane[3:]
+        self.attend = self.cross_again(*self.attend_crossed)
+        more = [*self.attend[2:], self.exchange(self.plane[1], 2)]
+        before, more = self.join(more, before)
+        self.attend[2:] = more[:2]
+        self.plane += more[2:]
+        return before
 
     def lines(self, values):
         groups = [[z * 4 + line for z in range(self.chips // 4)] for line in range(4)]
@@ -1002,7 +1049,7 @@
         return [first, second, self.exchange(first, 2), self.exchange(second, 1)]
 
     def attend_all(self):
-        return swap_all(self.cross_again(*self.attend_crossed))
+        return swap_all(self.attend)
 
     def cross_main(self):
         planes = lax.all_gather(
@@ -1061,11 +1108,8 @@
     def cross_last(self):
         return []
 
-    def cross_last_y(self):
-        return []
-
     def cross_last_again(self, *before):
-        return []
+        return before
 
     def cross_main(self):
         pass
@@ -1142,11 +1186,11 @@
             at.astype(jnp.int32),
             lifted_all,
             columns_of(core),
-            swap_cores(columns_of(1 - core)),
+            swap_cores(after(columns_of(1 - core), notes)),
             jnp.concatenate([laid_out(early, tables[:4]), laid_out(late, tables[4:])], axis=2),
         )
-        block = after(block, *begun, *gather.cross_last_y())
-        block = after(to_chips(block), *gather.cross_last_again(block))
+        block = after(block, *begun)
+        (block,) = gather.cross_last_again(to_chips(block))
         *chosen, modulation, middle_modulate, lifted = open_block(
             early, late, core_at, condition, block, swap_cores(block)
         )
@@ -1154,7 +1198,7 @@
 
         attend_all = gather.attend_all()
         gather.cross_main()
-        queries, near, entering, middle_attend = enter(
+        queries, near, middle_attend = enter(
             place, tokens, modulation, attend_all, attend_down, attend_up
         )
         queries, near = gather.early_main(queries, near)
@@ -1173,7 +1217,7 @@
         half_0 = attend_back(queries, near, far, grad_attended, logsum_0, 0)
         packed_far = swap_cores(packed_far)
         grad_attended, packed_far = lax.optimization_barrier((grad_attended, packed_far))
-        arrived_late = to_chips(packed + packed_far)
+        grads_late = (packed + packed_far).astype(bf16)
         half_1 = attend_back(queries, near, far, grad_attended, logsum_1, 2)
         grads_attended = [half_0, half_1]
         grad_queries, grad_near, grad_far = zip(*grads_attended)
@@ -1185,14 +1229,13 @@
             attend_all,
             attend_down,
             attend_up,
-            entering,
             middle_attend,
             tokens,
             modulation,
             grad_middle,
         )
 
-        sums_attend, arrived_late = lax.optimization_barrier((sums_attend, arrived_late))
+        sums_attend, grads_late = lax.optimization_barrier((sums_attend, grads_late))
         packed, packed_far, grad_modulation, grad_middle_modulate = pack_early(
             early,
             core_at,
@@ -1202,16 +1245,16 @@
             modulate_up,
             grads_attend,
         )
-        arrived_early = to_chips(packed + swap_cores(packed_far))
-        grad_lifted = product_back(grad_modulation, modulate_all) + product(
-            grad_middle_modulate, modulate_down
-        )
-        condition_grad = jax.vjp(jax.nn.silu, condition.astype(f32))[1](grad_lifted)[0]
-        arrived_late = after(arrived_late, condition_grad)
-        owned_late = table_sums(late, (2, 3, 4), choice, arrived_late)
-        arrived_early, *owned_late = lax.optimization_barrier((arrived_early, *owned_late))
-        owned_early = table_sums(early, (0, 1), choice, arrived_early)
-        return (block_output[None], input_grad[None], condition_grad, *owned_early, *owned_late)
+        grads_early = (packed + swap_cores(packed_far)).astype(bf16)
+        arrived = to_chips(jnp.concatenate([grads_early, grads_late], axis=2))
+        condition_grad = condition_back(
+            grad_modulation, modulate_all, grad_middle_modulate, modulate_down, condition
+        )
+        arrived = after(arrived, condition_grad)
+        starts = [sum(early[:member]) for member in range(4)]
+        starts += [rounded_up(sum(early)) + sum(late[:member]) for member in range(6)]
+        owned = table_sums(own, starts, choice, arrived)
+        return (block_output[None], input_grad[None], condition_grad, *owned)
 
     return local
 

time: 293 us -> 285 us (0.973)
  matrix products: 8.71 us -> 0 us
  Pallas kernels: 133 us -> 138 us
  waiting for transfers between devices: 65 us -> 61.3 us
    all_to_all x4 -> x3, waiting for transfers between devices: 21.5 us -> 4.98 us  [to_chips(): return lax.all_to_all(values, 'dp', split_axis=0, concat_axis=0, tiled=True)]
    ppermute x13, waiting for transfers between devices: 34.3 us -> 43.7 us  [exchange(): lax.ppermute(values, 'dp', [(chip, chip ^ over) for chip in range(self.ch...]
    dot_general x2 -> x0, matrix products: 8.71 us -> none  [the longest x1 7.93 us: product_back(): lax.dot_general(grads, right, (((1,), (1,)), ((), ())), preferred_element...]
    pallas_call x2, Pallas kernels: 4.02 us -> 11.3 us  [the longest x1 9.04 us: condition_back(): pl.pallas_call(condition_kernel, grid=(D // 128,), in_specs=[whole(grads....]
    ppermute x20, waiting for transfers between devices: 8.43 us -> 11.8 us  [swap_cores(): return lax.ppermute(values, 'seq', [(0, 1), (1, 0)])]
    all_to_all x4 -> x3, starting transfers between devices: 21.5 us -> 19.6 us  [to_chips(): return lax.all_to_all(values, 'dp', split_axis=0, concat_axis=0, tiled=True)]
  transfers between devices with their start and end apart: 43 -> 42, of which waited for: 19 -> 16; matrix products, arithmetic and copies ran while one was open for 9% -> 5% of each run, Pallas kernels for 45% -> 48%
where the time goes in v4:
time: 285 us; the launch traced here: 281 us
  Pallas kernels  138 us (48%)
  waiting for transfers between devices  61.3 us (22%)
  starting transfers between devices  48.5 us (17%)
  between operations  14.4 us (5%)
  local copies, waits for them, and re-layouts  9.36 us (3%)
  other arithmetic  9.08 us (3%)
    ppermute x13, waiting for transfers between devices, exchange(): lax.ppermute(values, 'dp', [(chip, chip ^ over) for chip in range(self.ch...  43.7 us
    pallas_call x1, Pallas kernels, feed(): pl.pallas_call(lambda *refs: feed_kernel(len(weights), *refs), grid=(FF /...  42.7 us
    pallas_call x2, Pallas kernels, attend_back(): pl.pallas_call(attend_back_kernel, grid=(groups,), in_specs=[at(0), at(0)...  29.8 us
    all_to_all x3, starting transfers between devices, to_chips(): return lax.all_to_all(values, 'dp', split_axis=0, concat_axis=0, tiled=True)  19.6 us
    ppermute x13, starting transfers between devices, exchange(): lax.ppermute(values, 'dp', [(chip, chip ^ over) for chip in range(self.ch...  19.5 us
    pallas_call x2, Pallas kernels, attend(): pl.pallas_call(lambda *refs: attend_kernel(*refs[:5], *refs[5 + len(given...  17.2 us
    pallas_call x1, Pallas kernels, leave(): pl.pallas_call(lambda *refs: leave_kernel(len(weights), *refs), grid=(col...  13.8 us
    ppermute x20, waiting for transfers between devices, swap_cores(): return lax.ppermute(values, 'seq', [(0, 1), (1, 0)])  11.8 us
  transfers between devices with their start and end apart: 42, of which 16 were waited for; matrix products, arithmetic and copies ran while one was open for 5% of the time, Pallas kernels for 48%

profile of v4, /device:TPU:0, one launch (start us, length us, event | category | flops | bytes accessed | tf_op | source)
XLA Modules:
  0.0 280.9 jit_solution(6503759420404807478)
XLA Ops:
  7.3 2.0 cut_weights.1
  9.3 2.9 %collective-permute-start = (bf16[96,1024]{1,0:T(8,128)(2,1)}, bf16[96,1024]{1,0:T(8,128)(2,1)S(1)}, u32[]{:S(2)}, u32[]{:S(2)}) collective-permute-start(bf16[96,1024]{1,0:T(8,128)(2,1)} %get-tuple-element.104), channel_id=1, source_target_pairs={{0,2},{2,0},{4,6},{6,4},{8,10},{10,8},{12,14},{14,12},{16,18},{18,... | collective-permute-start | bytes 589832 | tf_op jit(solution)/shard_map/ppermute | solution.py:1012
  12.2 1.5 collective-permute-start.1
  13.7 2.6 collective-permute-start.5
  16.3 1.3 collective-permute-start.6
  17.7 0.7 collective-permute-start.3
  18.3 1.4 write_notes.1
  19.8 4.7 %all-to-all-start = ((bf16[16,16,128]{2,1,0:T(8,128)(2,1)}), bf16[16,16,128]{2,1,0:T(8,128)(2,1)S(1)}, u32[]{:S(2)}, u32[]{:S(2)}) async-start(bf16[16,16,128]{2,1,0:T(8,128)(2,1)} %write_notes.1), calls=%async_computation | async-start | bytes 131072 | tf_op jit(solution)/shard_map/all_to_all | solution.py:1152
  24.5 0.7 all-gather.8.cloned.1.call-update
  25.2 0.9 constant_dynamic-slice_fusion.1
  26.1 1.0 constant_dynamic-slice_fusion
  27.1 0.7 pad_maximum_fusion.7
  28.0 0.8 concatenate.20.refs_5_
  28.8 0.7 pad_maximum_fusion.6.refs_3_
  29.6 2.0 collective-permute-start.7
  31.6 1.5 collective-permute-start.4
  33.7 1.2 all-to-all-done
  35.3 0.7 copy.39.refs_0_
  36.0 0.6 fusion.10.refs_2_
  36.9 0.7 copy-done.15
  37.6 2.6 prepare.1
  40.5 9.0 %all-to-all-start.1 = ((bf16[16,16,1152]{2,1,0:T(8,128)(2,1)}), bf16[16,16,1152]{2,1,0:T(8,128)(2,1)S(1)}, u32[]{:S(2)}, u32[]{:S(2)}) async-start(bf16[16,16,1152]{2,1,0:T(8,128)(2,1)} %prepare.1), calls=%async_computation.1 | async-start | bytes 1179648 | tf_op jit(solution)/shard_map/all_to_all | solution.py:1152
  49.6 2.0 collective-permute-start.9
  51.6 1.1 pad_maximum_fusion.refs_5_.refs_11_
  52.7 1.5 collective-permute-start.8
  54.8 24.6 %collective-permute-done.10 = bf16[96,1024]{1,0:T(8,128)(2,1)S(1)} collective-permute-done((bf16[96,1024]{1,0:T(8,128)(2,1)S(1)}, bf16[96,1024]{1,0:T(8,128)(2,1)S(1)}, u32[]{:S(2)}, u32[]{:S(2)}) %collective-permute-start.10) | collective-permute-done | bytes 196640 | tf_op jit(solution)/shard_map/ppermute | solution.py:1012
  79.4 2.6 pad_maximum_fusion.2
  83.4 2.6 fusion.14
  86.1 1.3 collective-permute-start.16
  87.3 1.2 collective-permute-start.17
  88.5 0.7 pad_add_fusion.refs_0_
  89.2 2.6 open_block.1
  91.8 9.6 %enter.1 = (bf16[512,1024]{1,0:T(8,128)(2,1)}, bf16[512,2048]{1,0:T(8,128)(2,1)}, bf16[512,16]{1,0:T(8,128)(2,1)}) custom-call(s32[4]{0:T(128)} %pad_add_fusion.refs_0_, bf16[512,1024]{1,0:T(8,128)(2,1)} %bitcast.45, f32[8,1024]{1,0:T(8,128)} %get-tuple-element.109.refs_2_.refs_4_.refs_10_, bf16[16,1024]{1,0:T(8,128)(2,1)} %get-tuple-element.110.refs_3_.refs_7_, ...), custom_call_target="tpu_custom_call" | custom-call | flops 1 | bytes 1 | tf_op jit(solution)/shard_map/enter/pallas_call | solution.py:226
  101.4 5.0 %collective-permute-done.16.refs_12_ = bf16[2,192,1024]{2,1,0:T(8,128)(2,1)} collective-permute-done((bf16[2,192,1024]{2,1,0:T(8,128)(2,1)}, bf16[2,192,1024]{2,1,0:T(8,128)(2,1)}, u32[]{:S(2)}, u32[]{:S(2)}) %collective-permute-start.16) | collective-permute-done | bytes 786464 | tf_op jit(solution)/shard_map/ppermute | solution.py:1012
  106.3 0.9 collective-permute-done.17.refs_15_
  107.8 0.8 collective-permute-start.19
  108.6 1.7 collective-permute-start.20
  110.3 3.9 %collective-permute-done.18.refs_3_.refs_4_.keys_far.values_far = bf16[512,2048]{1,0:T(8,128)(2,1)} collective-permute-done((bf16[512,2048]{1,0:T(8,128)(2,1)}, bf16[512,2048]{1,0:T(8,128)(2,1)}, u32[]{:S(2)}, u32[]{:S(2)}) %collective-permute-start.18) | collective-permute-done | bytes 2097184 | tf_op jit(solution)/shard_map/ppermute | solution.py:716
  114.4 8.6 %attend.2 = (bf16[512,1024]{1,0:T(8,128)(2,1)}, f32[2,512,128]{2,1,0:T(8,128)}) custom-call(bf16[512,1024]{1,0:T(8,128)(2,1)} %get-tuple-element.117.refs_0_.queries, bf16[512,2048]{1,0:T(8,128)(2,1)} %get-tuple-element.118.refs_1_.refs_2_.keys_near.values_near, bf16[512,2048]{1,0:T(8,128)(2,1)} %get-tuple-element.118.refs_1_.refs_2_.keys_near.values_near, ...), custom_call_target="tpu_custom_call" | custom-call | flops 1 | bytes 1 | tf_op jit(solution)/shard_map/attend/pallas_call | solution.py:309
  123.0 4.5 %collective-permute-done.19.refs_13_ = bf16[2,192,1024]{2,1,0:T(8,128)(2,1)} collective-permute-done((bf16[2,192,1024]{2,1,0:T(8,128)(2,1)}, bf16[2,192,1024]{2,1,0:T(8,128)(2,1)}, u32[]{:S(2)}, u32[]{:S(2)}) %collective-permute-start.19) | collective-permute-done | bytes 786464 | tf_op jit(solution)/shard_map/ppermute | solution.py:1012
  128.1 1.2 collective-permute-start.24
  129.3 1.2 collective-permute-start.23
  131.0 8.6 %attend.3 = (bf16[512,1024]{1,0:T(8,128)(2,1)}, f32[2,512,128]{2,1,0:T(8,128)}) custom-call(bf16[512,1024]{1,0:T(8,128)(2,1)} %get-tuple-element.117.refs_0_.queries, bf16[512,2048]{1,0:T(8,128)(2,1)} %get-tuple-element.118.refs_1_.refs_2_.keys_near.values_near, ...), custom_call_target="tpu_custom_call", output_to_operand_aliasing={{0}: (5, {})} | custom-call | flops 1 | bytes 1 | tf_op jit(solution)/shard_map/attend/pallas_call | solution.py:309
  139.6 7.0 %collective-permute-done.24.refs_17_ = bf16[2,192,1024]{2,1,0:T(8,128)(2,1)S(1)} collective-permute-done((bf16[2,192,1024]{2,1,0:T(8,128)(2,1)}, bf16[2,192,1024]{2,1,0:T(8,128)(2,1)S(1)}, u32[]{:S(2)}, u32[]{:S(2)}) %collective-permute-start.24) | collective-permute-done | bytes 786464 | tf_op jit(solution)/shard_map/ppermute | solution.py:1012
  146.6 0.9 collective-permute-done.23.refs_16_
  148.1 2.1 collective-permute-done.28.refs_23_
  150.2 0.9 copy-done.9
  151.2 42.7 %feed.1 = (bf16[512,1024]{1,0:T(8,128)(2,1)}, f32[512,1024]{1,0:T(8,128)}, bf16[512,1024]{1,0:T(8,128)(2,1)}, f32[8,1024]{1,0:T(8,128)}, f32[16,1024]{1,0:T(8,12...) custom-call(s32[4]{0:T(128)} %pad_add_fusion.refs_0_, ...), custom_call_target="tpu_custom_call" | custom-call | flops 1 | bytes 1 | tf_op jit(solution)/shard_map/feed/pallas_call | solution.py:544
  193.9 2.4 pack_late.1
  196.5 15.0 %attend_back.2 = (bf16[512,512]{1,0:T(8,128)(2,1)}, f32[2,512,512]{2,1,0:T(8,128)}, bf16[2,512,512]{2,1,0:T(8,128)(2,1)}) custom-call(bf16[512,1024]{1,0:T(8,128)(2,1)} %get-tuple-element.117.refs_0_.queries, bf16[512,2048]{1,0:T(8,128)(2,1)} %get-tuple-element.118.refs_1_.refs_2_.keys_near.values_near, ...), custom_call_target="tpu_custom_call" | custom-call | flops 1 | bytes 1 | tf_op jit(solution)/shard_map/attend_back/pallas_call | solution.py:402
  211.9 14.8 %attend_back.3 = (bf16[512,512]{1,0:T(8,128)(2,1)}, f32[2,512,512]{2,1,0:T(8,128)}, bf16[2,512,512]{2,1,0:T(8,128)(2,1)}) custom-call(bf16[512,1024]{1,0:T(8,128)(2,1)} %get-tuple-element.117.refs_0_.queries, bf16[512,2048]{1,0:T(8,128)(2,1)} %get-tuple-element.118.refs_1_.refs_2_.keys_near.values_near, ...), custom_call_target="tpu_custom_call" | custom-call | flops 1 | bytes 1 | tf_op jit(solution)/shard_map/attend_back/pallas_call | solution.py:402
  227.3 2.4 collective-permute-done.32.refs_6_
  229.7 13.8 %leave.1 = (f32[512,1024]{1,0:T(8,128)}, f32[8,1024]{1,0:T(8,128)}, f32[16,1024]{1,0:T(8,128)}, f32[16,3072]{1,0:T(8,128)}) custom-call(s32[4]{0:T(128)} %pad_add_fusion.refs_0_, bf16[512,512]{1,0:T(8,128)(2,1)} %get-tuple-element.149.refs_1_, bf16[512,512]{1,0:T(8,128)(2,1)} %get-tuple-element.159.refs_2_, f32[2,512,512]{2,1,0:T(8,128)} %get-tuple-element.160.refs_3_, ...), custom_call_target="tpu_custom_call" | custom-call | flops 1 | bytes 1 | tf_op jit(solution)/shard_map/leave/pallas_call | solution.py:676
  243.9 1.1 collective-permute-done.33.refs_2_
  245.0 0.6 copy-done.17
  245.6 2.9 %pack_early.1 = (f32[16,16,384]{2,1,0:T(8,128)}, f32[16,16,384]{2,1,0:T(8,128)}, bf16[1,6144]{1,0:T(2,128)(2,1)}, bf16[1,16]{1,0:T(2,128)(2,1)}) custom-call(s32[1]{0:T(128)} %bitcast.3.refs_0_.core, f32[8,1024]{1,0:T(8,128)} %get-tuple-element.170.refs_1_, f32[8,1024]{1,0:T(8,128)} %copy-done.17, f32[8,1024]{1,0:T(8,128)} %get-tuple-element.171.refs_3_, ...), custom_call_target="tpu_custom_call" | custom-call | flops 1 | bytes 1 | tf_op jit(solution)/shard_map/pack_early/pallas_call | solution.py:904
  248.6 1.8 collective-permute-done.35
  250.5 1.1 add_convert_fusion
  251.5 0.8 pad_maximum_fusion.5
  252.3 6.0 %all-to-all-start.2 = ((bf16[16,16,768]{2,1,0:T(8,128)(2,1)}), bf16[16,16,768]{2,1,0:T(8,128)(2,1)S(1)}, u32[]{:S(2)}, u32[]{:S(2)}) async-start(bf16[16,16,768]{2,1,0:T(8,128)(2,1)} %pad_maximum_fusion.5), calls=%async_computation.2 | async-start | bytes 786432 | tf_op jit(solution)/shard_map/all_to_all | solution.py:1152
  258.3 9.0 %condition_back.1 = f32[1,1024]{1,0:T(1,128)} custom-call(bf16[1,6144]{1,0:T(2,128)(2,1)} %get-tuple-element.177.grads, bf16[1024,6144]{1,0:T(8,128)(2,1)} %all-gather.6.cloned.1.call-done.weight, bf16[1,16]{1,0:T(2,128)(2,1)} %get-tuple-element.179.back, bf16[16,1024]{1,0:T(8,128)(2,1)} %get-tuple-element.180.down, bf16[1,1024]{1,0:T(2,128)(2,1)} %condition.3), custom_call_target="tpu_custom_call" | custom-call | flops 1 | bytes 1 | tf_op jit(solution)/shard_map/condition_back/pallas_call | solution.py:929
  267.3 3.8 %all-to-all-done.2.refs_1_ = bf16[16,16,768]{2,1,0:T(8,128)(2,1)S(1)} async-done(((bf16[16,16,768]{2,1,0:T(8,128)(2,1)}), bf16[16,16,768]{2,1,0:T(8,128)(2,1)S(1)}, u32[]{:S(2)}, u32[]{:S(2)}) %all-to-all-start.2) | async-done | bytes 393248 | tf_op jit(solution)/shard_map/all_to_all | solution.py:1152
  271.2 0.7 copy-done.5
  271.9 2.3 table_sums.1
  (114 shorter events, 8.0 us)
Async XLA Ops:
  7.2 20.6 %copy-start.19 = (bf16[8,32,16]{1,2,0:T(8,128)(2,1)S(1)}, bf16[8,32,16]{1,2,0:T(8,128)(2,1)}, u32[]{:S(2)}) copy-start(bf16[8,32,16]{1,2,0:T(8,128)(2,1)} %param.30) | copy-start | bytes 24580
  7.2 20.6 %copy-start.20 = (bf16[8,32,16]{1,2,0:T(8,128)(2,1)S(1)}, bf16[8,32,16]{1,2,0:T(8,128)(2,1)}, u32[]{:S(2)}) copy-start(bf16[8,32,16]{1,2,0:T(8,128)(2,1)} %param.28) | copy-start | bytes 24580
  7.2 20.6 %copy-start.16 = (bf16[8,16,192]{2,1,0:T(8,128)(2,1)S(1)}, bf16[8,16,192]{2,1,0:T(8,128)(2,1)}, u32[]{:S(2)}) copy-start(bf16[8,16,192]{2,1,0:T(8,128)(2,1)} %param.29) | copy-start | bytes 147460
  7.2 20.6 %copy-start.18 = (bf16[8,16,96]{2,1,0:T(8,128)(2,1)S(1)}, bf16[8,16,96]{2,1,0:T(8,128)(2,1)}, u32[]{:S(2)}) copy-start(bf16[8,16,96]{2,1,0:T(8,128)(2,1)} %param.31) | copy-start | bytes 73732
  7.2 20.7 %copy-start.21 = (bf16[8,32,16]{1,2,0:T(8,128)(2,1)S(1)}, bf16[8,32,16]{1,2,0:T(8,128)(2,1)}, u32[]{:S(2)}) copy-start(bf16[8,32,16]{1,2,0:T(8,128)(2,1)} %param.32) | copy-start | bytes 24580
  7.2 20.7 %copy-start.23 = (bf16[8,32,16]{1,2,0:T(8,128)(2,1)S(1)}, bf16[8,32,16]{1,2,0:T(8,128)(2,1)}, u32[]{:S(2)}) copy-start(bf16[8,32,16]{1,2,0:T(8,128)(2,1)} %param.34) | copy-start | bytes 24580
  7.2 20.7 %copy-start.25 = (bf16[8,128,16]{1,2,0:T(8,128)(2,1)S(1)}, bf16[8,128,16]{1,2,0:T(8,128)(2,1)}, u32[]{:S(2)}) copy-start(bf16[8,128,16]{1,2,0:T(8,128)(2,1)} %param.36) | copy-start | bytes 98308
  7.3 20.7 %copy-start.22 = (bf16[8,16,32]{2,1,0:T(8,128)(2,1)S(1)}, bf16[8,16,32]{2,1,0:T(8,128)(2,1)}, u32[]{:S(2)}) copy-start(bf16[8,16,32]{2,1,0:T(8,128)(2,1)} %param.33) | copy-start | bytes 24580
  7.3 20.7 %copy-start.24 = (bf16[8,16,128]{2,1,0:T(8,128)(2,1)S(1)}, bf16[8,16,128]{2,1,0:T(8,128)(2,1)}, u32[]{:S(2)}) copy-start(bf16[8,16,128]{2,1,0:T(8,128)(2,1)} %param.35) | copy-start | bytes 98308
  7.3 20.7 %copy-start.26 = (bf16[8,16,32]{2,1,0:T(8,128)(2,1)S(1)}, bf16[8,16,32]{2,1,0:T(8,128)(2,1)}, u32[]{:S(2)}) copy-start(bf16[8,16,32]{2,1,0:T(8,128)(2,1)} %param.37) | copy-start | bytes 24580
  9.3 25.6 %collective-permute-start = (bf16[96,1024]{1,0:T(8,128)(2,1)}, bf16[96,1024]{1,0:T(8,128)(2,1)S(1)}, u32[]{:S(2)}, u32[]{:S(2)}) collective-permute-start(bf16[96,1024]{1,0:T(8,128)(2,1)} %get-tuple-element.104), channel_id=1, source_target_pairs={{0,2},{2,0},{4,6},{6,4},{8,10},{10,8},{12,14},{14,12},{16,18},{18,... | collective-permute-start | bytes 589832 | tf_op jit(solution)/shard_map/ppermute | solution.py:1012
  12.2 22.7 %collective-permute-start.1 = (bf16[96,1024]{1,0:T(8,128)(2,1)}, bf16[96,1024]{1,0:T(8,128)(2,1)}, u32[]{:S(2)}, u32[]{:S(2)}) collective-permute-start(bf16[96,1024]{1,0:T(8,128)(2,1)} %get-tuple-element.104), channel_id=1, source_target_pairs={{0,4},{2,6},{4,0},{6,2},{8,12},{10,14},{12,8},{14,10},{16,20},{18,... | collective-permute-start | bytes 589832 | tf_op jit(solution)/shard_map/ppermute | solution.py:1012
  13.7 15.8 %collective-permute-start.5 = (bf16[32,3072]{1,0:T(8,128)(2,1)}, bf16[32,3072]{1,0:T(8,128)(2,1)S(1)}, u32[]{:S(2)}, u32[]{:S(2)}) collective-permute-start(bf16[32,3072]{1,0:T(8,128)(2,1)} %param.24), channel_id=1, source_target_pairs={{0,16},{2,18},{4,20},{6,22},{8,24},{10,26},{12,28},{14,30},{16,0},... | collective-permute-start | bytes 589832 | tf_op jit(solution)/shard_map/ppermute | solution.py:1015
  16.3 13.2 %collective-permute-start.6 = (bf16[32,3072]{1,0:T(8,128)(2,1)}, bf16[32,3072]{1,0:T(8,128)(2,1)S(1)}, u32[]{:S(2)}, u32[]{:S(2)}) collective-permute-start(bf16[32,3072]{1,0:T(8,128)(2,1)} %param.24), channel_id=1, source_target_pairs={{0,24},{2,26},{4,28},{6,30},{8,0},{10,2},{12,4},{14,6},{16,8},{18,... | collective-permute-start | bytes 589832 | tf_op jit(solution)/shard_map/ppermute | solution.py:1015
  17.7 13.9 %collective-permute-start.3 = (bf16[32,3072]{1,0:T(8,128)(2,1)}, bf16[32,3072]{1,0:T(8,128)(2,1)S(1)}, u32[]{:S(2)}, u32[]{:S(2)}) collective-permute-start(bf16[32,3072]{1,0:T(8,128)(2,1)} %param.24), channel_id=1, source_target_pairs={{0,8},{2,10},{4,12},{6,14},{8,16},{10,18},{12,20},{14,22},{16,24},... | collective-permute-start | bytes 589832 | tf_op jit(solution)/shard_map/ppermute | solution.py:1015
  19.8 11.8 %copy-start.12 = (bf16[32,3072]{1,0:T(8,128)(2,1)S(1)}, bf16[32,3072]{1,0:T(8,128)(2,1)}, u32[]{:S(2)}) copy-start(bf16[32,3072]{1,0:T(8,128)(2,1)} %param.24) | copy-start | bytes 589828
  19.8 15.1 %all-to-all-start = ((bf16[16,16,128]{2,1,0:T(8,128)(2,1)}), bf16[16,16,128]{2,1,0:T(8,128)(2,1)S(1)}, u32[]{:S(2)}, u32[]{:S(2)}) async-start(bf16[16,16,128]{2,1,0:T(8,128)(2,1)} %write_notes.1), calls=%async_computation | async-start | bytes 131072 | tf_op jit(solution)/shard_map/all_to_all | solution.py:1152
  24.4 59.0 %all-gather.8.cloned.1.call-start = ((), (), s32[]{:S(2)}) async-start(), calls=%async_computation.4 | async-start | bytes 1966080 | tf_op jit(solution)/shard_map/all_gather | solution.py:1041
  29.6 10.6 %collective-permute-start.7 = (bf16[2,32,3072]{2,1,0:T(8,128)(2,1)S(1)}, bf16[2,32,3072]{2,1,0:T(8,128)(2,1)S(1)}, u32[]{:S(2)}, u32[]{:S(2)}) collective-permute-start(bf16[2,32,3072]{2,1,0:T(8,128)(2,1)S(1)} %get-tuple-element.198), channel_id=1, source_target_pairs={{0,4},{2,6},{4,0},{6,2},{8,12},{10,14},{12,8},{14,10},{16,20},{18,... | collective-permute-start | bytes 1179656 | tf_op jit(solution)/shard_map/ppermute | solution.py:1012
  31.6 8.9 %collective-permute-start.4 = (bf16[2,32,3072]{2,1,0:T(8,128)(2,1)S(1)}, bf16[2,32,3072]{2,1,0:T(8,128)(2,1)S(1)}, u32[]{:S(2)}, u32[]{:S(2)}) collective-permute-start(bf16[2,32,3072]{2,1,0:T(8,128)(2,1)S(1)} %get-tuple-element.200), channel_id=1, source_target_pairs={{0,2},{2,0},{4,6},{6,4},{8,10},{10,8},{12,14},{14,12},{16,18},{18,... | collective-permute-start | bytes 1179656 | tf_op jit(solution)/shard_map/ppermute | solution.py:1012
  34.9 14.6 %copy-start.13 = (bf16[96,1024]{1,0:T(8,128)(2,1)}, bf16[96,1024]{1,0:T(8,128)(2,1)S(1)}, u32[]{:S(2)}) copy-start(bf16[96,1024]{1,0:T(8,128)(2,1)S(1)} %collective-permute-done) | copy-start | bytes 589828
  35.2 1.7 collective-permute-start.2
  40.5 11.1 %copy-start.10 = (bf16[2,32,3072]{2,1,0:T(8,128)(2,1)}, bf16[2,32,3072]{2,1,0:T(8,128)(2,1)S(1)}, u32[]{:S(2)}) copy-start(bf16[2,32,3072]{2,1,0:T(8,128)(2,1)S(1)} %collective-permute-done.4) | copy-start | bytes 1179652
  40.5 38.9 %all-to-all-start.1 = ((bf16[16,16,1152]{2,1,0:T(8,128)(2,1)}), bf16[16,16,1152]{2,1,0:T(8,128)(2,1)S(1)}, u32[]{:S(2)}, u32[]{:S(2)}) async-start(bf16[16,16,1152]{2,1,0:T(8,128)(2,1)} %prepare.1), calls=%async_computation.1 | async-start | bytes 1179648 | tf_op jit(solution)/shard_map/all_to_all | solution.py:1152
  49.4 98.1 %all-gather.10.cloned.1.call-start = ((), (), s32[]{:S(2)}) async-start(), calls=%async_computation.5 | async-start | bytes 7077888 | tf_op jit(solution)/shard_map/all_gather | solution.py:1055
  49.5 4.7 %copy-start.14 = (bf16[96,1024]{1,0:T(8,128)(2,1)S(1)}, bf16[96,1024]{1,0:T(8,128)(2,1)}, u32[]{:S(2)}) copy-start(bf16[96,1024]{1,0:T(8,128)(2,1)} %copy-done.13) | copy-start | bytes 589828
  49.6 36.4 %copy-start = (bf16[2,2,32,3072]{3,2,1,0:T(8,128)(2,1)}, bf16[2,2,32,3072]{3,2,1,0:T(8,128)(2,1)S(1)}, u32[]{:S(2)}) copy-start(bf16[2,2,32,3072]{3,2,1,0:T(8,128)(2,1)S(1)} %pad_maximum_fusion.1.refs_6_.refs_12_) | copy-start | bytes 2359300
  49.6 29.7 %collective-permute-start.9 = (bf16[2,2,32,3072]{3,2,1,0:T(8,128)(2,1)S(1)}, bf16[2,2,32,3072]{3,2,1,0:T(8,128)(2,1)S(1)}, u32[]{:S(2)}, u32[]{:S(2)}) collective-permute-start(bf16[2,2,32,3072]{3,2,1,0:T(8,128)(2,1)S(1)} %pad_maximum_fusion.1.refs_6_.refs_12_), channel_id=1, source_target_pairs={{0,2},{2,0},{4,6},{6,4},{8,10},{10,8},{12,14},{14,12},{16,18},{18,... | collective-permute-start | bytes 2359304 | tf_op jit(solution)/shard_map/ppermute | solution.py:1012
  52.7 33.4 %copy-start.1 = (bf16[2,2,32,3072]{3,2,1,0:T(8,128)(2,1)}, bf16[2,2,32,3072]{3,2,1,0:T(8,128)(2,1)S(1)}, u32[]{:S(2)}) copy-start(bf16[2,2,32,3072]{3,2,1,0:T(8,128)(2,1)S(1)} %pad_maximum_fusion.refs_5_.refs_11_) | copy-start | bytes 2359300
  52.7 26.7 %collective-permute-start.8 = (bf16[2,2,32,3072]{3,2,1,0:T(8,128)(2,1)S(1)}, bf16[2,2,32,3072]{3,2,1,0:T(8,128)(2,1)}, u32[]{:S(2)}, u32[]{:S(2)}) collective-permute-start(bf16[2,2,32,3072]{3,2,1,0:T(8,128)(2,1)S(1)} %pad_maximum_fusion.refs_5_.refs_11_), channel_id=1, source_target_pairs={{0,4},{2,6},{4,0},{6,2},{8,12},{10,14},{12,8},{14,10},{16,20},{18,... | collective-permute-start | bytes 2359304 | tf_op jit(solution)/shard_map/ppermute | solution.py:1012
  54.2 25.1 %collective-permute-start.10 = (bf16[96,1024]{1,0:T(8,128)(2,1)S(1)}, bf16[96,1024]{1,0:T(8,128)(2,1)S(1)}, u32[]{:S(2)}, u32[]{:S(2)}) collective-permute-start(bf16[96,1024]{1,0:T(8,128)(2,1)S(1)} %copy-done.14), channel_id=1, source_target_pairs={{0,4},{2,6},{4,0},{6,2},{8,12},{10,14},{12,8},{14,10},{16,20},{18,... | collective-permute-start | bytes 589832 | tf_op jit(solution)/shard_map/ppermute | solution.py:1012
  79.3 6.7 %copy-start.3 = (bf16[2,2,32,3072]{3,2,1,0:T(8,128)(2,1)}, bf16[2,2,32,3072]{3,2,1,0:T(8,128)(2,1)S(1)}, u32[]{:S(2)}) copy-start(bf16[2,2,32,3072]{3,2,1,0:T(8,128)(2,1)S(1)} %collective-permute-done.9.refs_8_.refs_14_) | copy-start | bytes 2359300
  79.4 6.7 %copy-start.4 = (bf16[16,16,1152]{2,1,0:T(8,128)(2,1)}, bf16[16,16,1152]{2,1,0:T(8,128)(2,1)S(1)}, u32[]{:S(2)}) copy-start(bf16[16,16,1152]{2,1,0:T(8,128)(2,1)S(1)} %all-to-all-done.1.refs_2_) | copy-start | bytes 1769476
  82.0 176.3 %all-gather.6.cloned.1.call-start = ((), (), s32[]{:S(2)}) async-start(), calls=%async_computation.3 | async-start | bytes 12976128 | tf_op jit(solution)/shard_map/all_gather | solution.py:1210
  82.2 3.8 %collective-permute-start.13 = (bf16[2,2,32,3072]{3,2,1,0:T(8,128)(2,1)S(1)}, bf16[2,2,32,3072]{3,2,1,0:T(8,128)(2,1)}, u32[]{:S(2)}, u32[]{:S(2)}) collective-permute-start(bf16[2,2,32,3072]{3,2,1,0:T(8,128)(2,1)S(1)} %pad_maximum_fusion.1.refs_6_.refs_12_), channel_id=1, source_target_pairs={{0,1},{1,0},{2,3},{3,2},{4,5},{5,4},{6,7},{7,6},{8,9},{9,8},{10,11... | collective-permute-start | bytes 2359304 | tf_op jit(solution)/shard_map/ppermute | solution.py:716
  82.3 5.0 %collective-permute-start.11 = (bf16[16,16,1152]{2,1,0:T(8,128)(2,1)S(1)}, bf16[16,16,1152]{2,1,0:T(8,128)(2,1)}, u32[]{:S(2)}, u32[]{:S(2)}) collective-permute-start(bf16[16,16,1152]{2,1,0:T(8,128)(2,1)S(1)} %all-to-all-done.1.refs_2_), channel_id=1, source_target_pairs={{0,1},{1,0},{2,3},{3,2},{4,5},{5,4},{6,7},{7,6},{8,9},{9,8},{10,11... | collective-permute-start | bytes 1769480 | tf_op jit(solution)/shard_map/ppermute | solution.py:716
  82.8 9.0 %collective-permute-start.12 = (bf16[2,2,32,3072]{3,2,1,0:T(8,128)(2,1)S(1)}, bf16[2,2,32,3072]{3,2,1,0:T(8,128)(2,1)}, u32[]{:S(2)}, u32[]{:S(2)}) collective-permute-start(bf16[2,2,32,3072]{3,2,1,0:T(8,128)(2,1)S(1)} %pad_maximum_fusion.refs_5_.refs_11_), channel_id=1, source_target_pairs={{0,1},{1,0},{2,3},{3,2},{4,5},{5,4},{6,7},{7,6},{8,9},{9,8},{10,11... | collective-permute-start | bytes 2359304 | tf_op jit(solution)/shard_map/ppermute | solution.py:716
  82.9 8.9 %collective-permute-start.14 = (bf16[2,2,32,3072]{3,2,1,0:T(8,128)(2,1)}, bf16[2,2,32,3072]{3,2,1,0:T(8,128)(2,1)}, u32[]{:S(2)}, u32[]{:S(2)}) collective-permute-start(bf16[2,2,32,3072]{3,2,1,0:T(8,128)(2,1)} %collective-permute-done.8.refs_7_.refs_13_), channel_id=1, source_target_pairs={{0,1},{1,0},{2,3},{3,2},{4,5},{5,4},{6,7},{7,6},{8,9},{9,8},{10,11... | collective-permute-start | bytes 2359304 | tf_op jit(solution)/shard_map/ppermute | solution.py:716
  83.3 8.5 %collective-permute-start.15 = (bf16[2,2,32,3072]{3,2,1,0:T(8,128)(2,1)S(1)}, bf16[2,2,32,3072]{3,2,1,0:T(8,128)(2,1)}, u32[]{:S(2)}, u32[]{:S(2)}) collective-permute-start(bf16[2,2,32,3072]{3,2,1,0:T(8,128)(2,1)S(1)} %collective-permute-done.9.refs_8_.refs_14_), channel_id=1, source_target_pairs={{0,1},{1,0},{2,3},{3,2},{4,5},{5,4},{6,7},{7,6},{8,9},{9,8},{10,11... | collective-permute-start | bytes 2359304 | tf_op jit(solution)/shard_map/ppermute | solution.py:716
  86.1 20.3 %collective-permute-start.16 = (bf16[2,192,1024]{2,1,0:T(8,128)(2,1)}, bf16[2,192,1024]{2,1,0:T(8,128)(2,1)}, u32[]{:S(2)}, u32[]{:S(2)}) collective-permute-start(bf16[2,192,1024]{2,1,0:T(8,128)(2,1)} %bitcast.22), channel_id=1, source_target_pairs={{0,2},{2,0},{4,6},{6,4},{8,10},{10,8},{12,14},{14,12},{16,18},{18,... | collective-permute-start | bytes 2359304 | tf_op jit(solution)/shard_map/ppermute | solution.py:1012
  87.3 19.9 %collective-permute-start.17 = (bf16[2,192,1024]{2,1,0:T(8,128)(2,1)}, bf16[2,192,1024]{2,1,0:T(8,128)(2,1)}, u32[]{:S(2)}, u32[]{:S(2)}) collective-permute-start(bf16[2,192,1024]{2,1,0:T(8,128)(2,1)} %bitcast.23), channel_id=1, source_target_pairs={{0,4},{2,6},{4,0},{6,2},{8,12},{10,14},{12,8},{14,10},{16,20},{18,... | collective-permute-start | bytes 2359304 | tf_op jit(solution)/shard_map/ppermute | solution.py:1012
  91.8 15.4 %copy-start.2 = (bf16[768,1024]{1,0:T(8,128)(2,1)S(1)}, bf16[768,1024]{1,0:T(8,128)(2,1)}, u32[]{:S(2)}) copy-start(bf16[768,1024]{1,0:T(8,128)(2,1)} %all-gather.8.cloned.1.call-done) | copy-start | bytes 4718596
  107.2 7.0 %collective-permute-start.18 = (bf16[512,2048]{1,0:T(8,128)(2,1)}, bf16[512,2048]{1,0:T(8,128)(2,1)}, u32[]{:S(2)}, u32[]{:S(2)}) collective-permute-start(bf16[512,2048]{1,0:T(8,128)(2,1)} %get-tuple-element.118.refs_1_.refs_2_.keys_near.values_near), channel_id=1, source_target_pairs={{0,1},{1,0},{2,3},{3,2},{4,5},{5,4},{6,7},{7,6},{8,9},{9,8},{10,11... | collective-permute-start | bytes 6291464 | tf_op jit(solution)/shard_map/ppermute | solution.py:716
  107.3 20.8 %collective-permute-start.21 = (bf16[4,192,1024]{2,1,0:T(8,128)(2,1)S(1)}, bf16[4,192,1024]{2,1,0:T(8,128)(2,1)}, u32[]{:S(2)}, u32[]{:S(2)}) collective-permute-start(bf16[4,192,1024]{2,1,0:T(8,128)(2,1)S(1)} %bitcast.49), channel_id=1, source_target_pairs={{0,1},{1,0},{2,3},{3,2},{4,5},{5,4},{6,7},{7,6},{8,9},{9,8},{10,11... | collective-permute-start | bytes 4718600 | tf_op jit(solution)/shard_map/ppermute | solution.py:716
  107.8 19.8 %collective-permute-start.19 = (bf16[2,192,1024]{2,1,0:T(8,128)(2,1)}, bf16[2,192,1024]{2,1,0:T(8,128)(2,1)}, u32[]{:S(2)}, u32[]{:S(2)}) collective-permute-start(bf16[2,192,1024]{2,1,0:T(8,128)(2,1)} %bitcast.23), channel_id=1, source_target_pairs={{0,2},{2,0},{4,6},{6,4},{8,10},{10,8},{12,14},{14,12},{16,18},{18,... | collective-permute-start | bytes 2359304 | tf_op jit(solution)/shard_map/ppermute | solution.py:1012
  108.6 19.5 %collective-permute-start.20 = (bf16[2,192,1024]{2,1,0:T(8,128)(2,1)}, bf16[2,192,1024]{2,1,0:T(8,128)(2,1)}, u32[]{:S(2)}, u32[]{:S(2)}) collective-permute-start(bf16[2,192,1024]{2,1,0:T(8,128)(2,1)} %bitcast.22), channel_id=1, source_target_pairs={{0,4},{2,6},{4,0},{6,2},{8,12},{10,14},{12,8},{14,10},{16,20},{18,... | collective-permute-start | bytes 2359304 | tf_op jit(solution)/shard_map/ppermute | solution.py:1012
  110.3 17.8 %collective-permute-start.22 = (bf16[2,192,1024]{2,1,0:T(8,128)(2,1)}, bf16[2,192,1024]{2,1,0:T(8,128)(2,1)}, u32[]{:S(2)}, u32[]{:S(2)}) collective-permute-start(bf16[2,192,1024]{2,1,0:T(8,128)(2,1)} %collective-permute-done.16.refs_12_), channel_id=1, source_target_pairs={{0,1},{1,0},{2,3},{3,2},{4,5},{5,4},{6,7},{7,6},{8,9},{9,8},{10,11... | collective-permute-start | bytes 2359304 | tf_op jit(solution)/shard_map/ppermute | solution.py:716
  114.3 25.3 %collective-permute-start.27 = (bf16[2,192,1024]{2,1,0:T(8,128)(2,1)}, bf16[2,192,1024]{2,1,0:T(8,128)(2,1)}, u32[]{:S(2)}, u32[]{:S(2)}) collective-permute-start(bf16[2,192,1024]{2,1,0:T(8,128)(2,1)} %collective-permute-done.17.refs_15_), channel_id=1, source_target_pairs={{0,1},{1,0},{2,3},{3,2},{4,5},{5,4},{6,7},{7,6},{8,9},{9,8},{10,11... | collective-permute-start | bytes 2359304 | tf_op jit(solution)/shard_map/ppermute | solution.py:716
  128.1 18.5 %collective-permute-start.24 = (bf16[2,192,1024]{2,1,0:T(8,128)(2,1)}, bf16[2,192,1024]{2,1,0:T(8,128)(2,1)S(1)}, u32[]{:S(2)}, u32[]{:S(2)}) collective-permute-start(bf16[2,192,1024]{2,1,0:T(8,128)(2,1)} %collective-permute-done.17.refs_15_), channel_id=1, source_target_pairs={{0,2},{2,0},{4,6},{6,4},{8,10},{10,8},{12,14},{14,12},{16,18},{18,... | collective-permute-start | bytes 2359304 | tf_op jit(solution)/shard_map/ppermute | solution.py:1012
  129.3 18.2 %collective-permute-start.23 = (bf16[2,192,1024]{2,1,0:T(8,128)(2,1)}, bf16[2,192,1024]{2,1,0:T(8,128)(2,1)S(1)}, u32[]{:S(2)}, u32[]{:S(2)}) collective-permute-start(bf16[2,192,1024]{2,1,0:T(8,128)(2,1)} %collective-permute-done.16.refs_12_), channel_id=1, source_target_pairs={{0,4},{2,6},{4,0},{6,2},{8,12},{10,14},{12,8},{14,10},{16,20},{18,... | collective-permute-start | bytes 2359304 | tf_op jit(solution)/shard_map/ppermute | solution.py:1012
  130.5 17.0 %collective-permute-start.25 = (bf16[2,192,1024]{2,1,0:T(8,128)(2,1)}, bf16[2,192,1024]{2,1,0:T(8,128)(2,1)}, u32[]{:S(2)}, u32[]{:S(2)}) collective-permute-start(bf16[2,192,1024]{2,1,0:T(8,128)(2,1)} %collective-permute-done.19.refs_13_), channel_id=1, source_target_pairs={{0,1},{1,0},{2,3},{3,2},{4,5},{5,4},{6,7},{7,6},{8,9},{9,8},{10,11... | collective-permute-start | bytes 2359304 | tf_op jit(solution)/shard_map/ppermute | solution.py:716
  130.5 17.0 %collective-permute-start.26 = (bf16[2,192,1024]{2,1,0:T(8,128)(2,1)}, bf16[2,192,1024]{2,1,0:T(8,128)(2,1)}, u32[]{:S(2)}, u32[]{:S(2)}) collective-permute-start(bf16[2,192,1024]{2,1,0:T(8,128)(2,1)} %collective-permute-done.20.refs_14_), channel_id=1, source_target_pairs={{0,1},{1,0},{2,3},{3,2},{4,5},{5,4},{6,7},{7,6},{8,9},{9,8},{10,11... | collective-permute-start | bytes 2359304 | tf_op jit(solution)/shard_map/ppermute | solution.py:716
  146.6 4.6 %copy-start.7 = (bf16[2,192,1024]{2,1,0:T(8,128)(2,1)}, bf16[2,192,1024]{2,1,0:T(8,128)(2,1)S(1)}, u32[]{:S(2)}) copy-start(bf16[2,192,1024]{2,1,0:T(8,128)(2,1)S(1)} %collective-permute-done.24.refs_17_) | copy-start | bytes 2359300
  147.5 3.7 %copy-start.8 = (bf16[2,192,1024]{2,1,0:T(8,128)(2,1)}, bf16[2,192,1024]{2,1,0:T(8,128)(2,1)S(1)}, u32[]{:S(2)}) copy-start(bf16[2,192,1024]{2,1,0:T(8,128)(2,1)S(1)} %collective-permute-done.23.refs_16_) | copy-start | bytes 2359300
  147.5 2.7 collective-permute-start.28
  147.6 3.5 %collective-permute-start.29 = (bf16[2,192,1024]{2,1,0:T(8,128)(2,1)S(1)}, bf16[2,192,1024]{2,1,0:T(8,128)(2,1)}, u32[]{:S(2)}, u32[]{:S(2)}) collective-permute-start(bf16[2,192,1024]{2,1,0:T(8,128)(2,1)S(1)} %collective-permute-done.24.refs_17_), channel_id=1, source_target_pairs={{0,1},{1,0},{2,3},{3,2},{4,5},{5,4},{6,7},{7,6},{8,9},{9,8},{10,11... | collective-permute-start | bytes 2359304 | tf_op jit(solution)/shard_map/ppermute | solution.py:716
  196.4 15.6 %collective-permute-start.30 = (f32[16,16,384]{2,1,0:T(8,128)}, f32[16,16,384]{2,1,0:T(8,128)S(1)}, u32[]{:S(2)}, u32[]{:S(2)}) collective-permute-start(f32[16,16,384]{2,1,0:T(8,128)} %get-tuple-element.156), channel_id=1, source_target_pairs={{0,1},{1,0},{2,3},{3,2},{4,5},{5,4},{6,7},{7,6},{8,9},{9,8},{10,11... | collective-permute-start | bytes 1179656 | tf_op jit(solution)/shard_map/ppermute | solution.py:716
  211.5 15.7 %copy-start.11 = (f32[16,16,384]{2,1,0:T(8,128)S(1)}, f32[16,16,384]{2,1,0:T(8,128)}, u32[]{:S(2)}) copy-start(f32[16,16,384]{2,1,0:T(8,128)} %get-tuple-element.168) | copy-start | bytes 1179652
  211.5 15.8 %collective-permute-start.31 = (bf16[2,512,512]{2,1,0:T(8,128)(2,1)}, bf16[2,512,512]{2,1,0:T(8,128)(2,1)S(1)}, u32[]{:S(2)}, u32[]{:S(2)}) collective-permute-start(bf16[2,512,512]{2,1,0:T(8,128)(2,1)} %get-tuple-element.162), channel_id=1, source_target_pairs={{0,1},{1,0},{2,3},{3,2},{4,5},{5,4},{6,7},{7,6},{8,9},{9,8},{10,11... | collective-permute-start | bytes 3145736 | tf_op jit(solution)/shard_map/ppermute | solution.py:716
  226.7 3.0 %collective-permute-start.32 = (bf16[2,512,512]{2,1,0:T(8,128)(2,1)}, bf16[2,512,512]{2,1,0:T(8,128)(2,1)}, u32[]{:S(2)}, u32[]{:S(2)}) collective-permute-start(bf16[2,512,512]{2,1,0:T(8,128)(2,1)} %get-tuple-element.163), channel_id=1, source_target_pairs={{0,1},{1,0},{2,3},{3,2},{4,5},{5,4},{6,7},{7,6},{8,9},{9,8},{10,11... | collective-permute-start | bytes 3145736 | tf_op jit(solution)/shard_map/ppermute | solution.py:716
  226.9 17.0 %collective-permute-start.34 = (f32[8,1024]{1,0:T(8,128)}, f32[8,1024]{1,0:T(8,128)}, u32[]{:S(2)}, u32[]{:S(2)}) collective-permute-start(f32[8,1024]{1,0:T(8,128)} %get-tuple-element.171.refs_3_), channel_id=1, source_target_pairs={{0,1},{1,0},{2,3},{3,2},{4,5},{5,4},{6,7},{7,6},{8,9},{9,8},{10,11... | collective-permute-start | bytes 98312 | tf_op jit(solution)/shard_map/ppermute | solution.py:716
  243.5 1.5 collective-permute-start.33
  248.5 1.9 collective-permute-start.35
  252.3 18.9 %all-to-all-start.2 = ((bf16[16,16,768]{2,1,0:T(8,128)(2,1)}), bf16[16,16,768]{2,1,0:T(8,128)(2,1)S(1)}, u32[]{:S(2)}, u32[]{:S(2)}) async-start(bf16[16,16,768]{2,1,0:T(8,128)(2,1)} %pad_maximum_fusion.5), calls=%async_computation.2 | async-start | bytes 786432 | tf_op jit(solution)/shard_map/all_to_all | solution.py:1152
  (5 other events, 5.4 us)
Sparse Core Ops, SparseCore 0:
  26.8 50.8 all-gather.7
  82.1 65.0 all-gather.9
  151.3 96.1 all-gather.5

commit v5 on v4

--- a/solution.py
+++ b/solution.py
@@ -19,7 +19,7 @@
 TILE = 512
 WIDE = D + 128
 NADAPT = 8
-CHUNK = 128
+CHUNK = 256
 VMEM_LIMIT = 62 * 1024 * 1024
 FIRST_ROWS = 32
 SHIFT_ATTEND, SCALE_ATTEND, GATE_ATTEND, SHIFT_EXPAND, SCALE_EXPAND, GATE_EXPAND = range(6)
@@ -1213,14 +1213,15 @@
         block_output, grad_middle, grad_attended, sums_feed, *grads_late = feed(
             place, tokens, attended, cotangent[0], modulation, feed_all, chosen_late
         )
-        packed, packed_far = pack_late(late, core_at, grads_late)
-        half_0 = attend_back(queries, near, far, grad_attended, logsum_0, 0)
-        packed_far = swap_cores(packed_far)
-        grad_attended, packed_far = lax.optimization_barrier((grad_attended, packed_far))
-        grads_late = (packed + packed_far).astype(bf16)
-        half_1 = attend_back(queries, near, far, grad_attended, logsum_1, 2)
-        grads_attended = [half_0, half_1]
+        grads_attended = [
+            attend_back(queries, near, far, grad_attended, logsum, 2 * half)
+            for half, logsum in enumerate((logsum_0, logsum_1))
+        ]
         grad_queries, grad_near, grad_far = zip(*grads_attended)
+        packed, packed_far = pack_late(
+            late, core_at, [after(grads_late[0], *grad_far), *grads_late[1:]]
+        )
+        grad_queries = [after(grad_queries[0], packed), grad_queries[1]]
         input_grad, sums_attend, *grads_attend = leave(
             place,
             grad_queries,
@@ -1235,7 +1236,7 @@
             grad_middle,
         )
 
-        sums_attend, grads_late = lax.optimization_barrier((sums_attend, grads_late))
+        grads_late = (packed + swap_cores(packed_far)).astype(bf16)
         packed, packed_far, grad_modulation, grad_middle_modulate = pack_early(
             early,
             core_at,

time: 285 us -> 283 us (level)
  starting transfers between devices: 48.5 us -> 40.3 us
  waiting for transfers between devices: 61.3 us -> 68.7 us
    all_to_all x3, starting transfers between devices: 19.6 us -> 12.9 us  [to_chips(): return lax.all_to_all(values, 'dp', split_axis=0, concat_axis=0, tiled=True)]
    ppermute x3, waiting for transfers between devices: 0.01 us -> 4.89 us  [along(): lax.ppermute(values, 'dp', [(chip, (chip + 4 * step) % self.chips) for ch...]
    ppermute x13, waiting for transfers between devices: 43.7 us -> 47.7 us  [exchange(): lax.ppermute(values, 'dp', [(chip, chip ^ over) for chip in range(self.ch...]
  transfers between devices with their start and end apart: 42 -> 42, of which waited for: 16 -> 17; matrix products, arithmetic and copies ran while one was open for 5% -> 6% of each run, Pallas kernels for 48% -> 48%
where the time goes in v5:
time: 283 us; the launch traced here: 279 us
  Pallas kernels  138 us (49%)
  waiting for transfers between devices  68.7 us (24%)
  starting transfers between devices  40.3 us (14%)
  between operations  14.5 us (5%)
  other arithmetic  9.04 us (3%)
  local copies, waits for them, and re-layouts  8.69 us (3%)
    ppermute x13, waiting for transfers between devices, exchange(): lax.ppermute(values, 'dp', [(chip, chip ^ over) for chip in range(self.ch...  47.7 us
    pallas_call x1, Pallas kernels, feed(): pl.pallas_call(lambda *refs: feed_kernel(len(weights), *refs), grid=(FF /...  42.4 us
    pallas_call x2, Pallas kernels, attend_back(): pl.pallas_call(attend_back_kernel, grid=(groups,), in_specs=[at(0), at(0)...  30 us
    ppermute x13, starting transfers between devices, exchange(): lax.ppermute(values, 'dp', [(chip, chip ^ over) for chip in range(self.ch...  17.6 us
    pallas_call x2, Pallas kernels, attend(): pl.pallas_call(lambda *refs: attend_kernel(*refs[:5], *refs[5 + len(given...  17.2 us
    pallas_call x1, Pallas kernels, leave(): pl.pallas_call(lambda *refs: leave_kernel(len(weights), *refs), grid=(col...  13.4 us
    all_to_all x3, starting transfers between devices, to_chips(): return lax.all_to_all(values, 'dp', split_axis=0, concat_axis=0, tiled=True)  12.9 us
    ppermute x20, waiting for transfers between devices, swap_cores(): return lax.ppermute(values, 'seq', [(0, 1), (1, 0)])  11.5 us
  transfers between devices with their start and end apart: 42, of which 17 were waited for; matrix products, arithmetic and copies ran while one was open for 6% of the time, Pallas kernels for 48%

profile of v5, /device:TPU:0, one launch (start us, length us, event | category | flops | bytes accessed | tf_op | source)
XLA Modules:
  0.0 278.8 jit_solution(7462693446991953234)
XLA Ops:
  7.3 2.0 cut_weights.1
  9.3 2.9 %collective-permute-start = (bf16[96,1024]{1,0:T(8,128)(2,1)}, bf16[96,1024]{1,0:T(8,128)(2,1)S(1)}, u32[]{:S(2)}, u32[]{:S(2)}) collective-permute-start(bf16[96,1024]{1,0:T(8,128)(2,1)} %get-tuple-element.102), channel_id=1, source_target_pairs={{0,2},{2,0},{4,6},{6,4},{8,10},{10,8},{12,14},{14,12},{16,18},{18,... | collective-permute-start | bytes 589832 | tf_op jit(solution)/shard_map/ppermute | solution.py:1012
  12.2 1.5 collective-permute-start.1
  13.8 1.6 collective-permute-start.3
  15.3 2.2 collective-permute-start.6
  17.6 0.8 collective-permute-start.5
  18.4 1.4 write_notes.1
  19.8 3.5 %all-to-all-start = ((bf16[16,16,128]{2,1,0:T(8,128)(2,1)}), bf16[16,16,128]{2,1,0:T(8,128)(2,1)S(1)}, u32[]{:S(2)}, u32[]{:S(2)}) async-start(bf16[16,16,128]{2,1,0:T(8,128)(2,1)} %write_notes.1), calls=%async_computation | async-start | bytes 131072 | tf_op jit(solution)/shard_map/all_to_all | solution.py:1152
  23.4 0.7 all-gather.8.cloned.1.call-update
  24.1 1.0 constant_dynamic-slice_fusion
  25.1 0.9 constant_dynamic-slice_fusion.1
  26.0 0.7 pad_maximum_fusion.6.refs_3_
  26.9 0.8 concatenate.20.refs_5_
  27.7 0.7 pad_maximum_fusion.7
  28.5 2.0 collective-permute-start.4
  30.5 4.9 %collective-permute-done.5 = bf16[32,3072]{1,0:T(8,128)(2,1)S(1)} collective-permute-done((bf16[32,3072]{1,0:T(8,128)(2,1)}, bf16[32,3072]{1,0:T(8,128)(2,1)S(1)}, u32[]{:S(2)}, u32[]{:S(2)}) %collective-permute-start.5) | collective-permute-done | bytes 196640 | tf_op jit(solution)/shard_map/ppermute | solution.py:1015
  35.4 0.6 collective-permute-start.7
  36.0 0.6 pad_add_fusion.1.refs_1_
  37.0 0.7 copy.39.refs_0_
  37.7 0.6 fusion.10.refs_2_
  38.7 2.6 prepare.1
  41.3 5.1 %collective-permute-done.7 = bf16[2,32,3072]{2,1,0:T(8,128)(2,1)S(1)} collective-permute-done((bf16[2,32,3072]{2,1,0:T(8,128)(2,1)S(1)}, bf16[2,32,3072]{2,1,0:T(8,128)(2,1)S(1)}, u32[]{:S(2)}, u32[]{:S(2)}) %collective-permute-start.7) | collective-permute-done | bytes 393248 | tf_op jit(solution)/shard_map/ppermute | solution.py:1012
  46.4 3.6 %all-to-all-start.1 = ((bf16[16,16,1152]{2,1,0:T(8,128)(2,1)}), bf16[16,16,1152]{2,1,0:T(8,128)(2,1)S(1)}, u32[]{:S(2)}, u32[]{:S(2)}) async-start(bf16[16,16,1152]{2,1,0:T(8,128)(2,1)} %prepare.1), calls=%async_computation.1 | async-start | bytes 1179648 | tf_op jit(solution)/shard_map/all_to_all | solution.py:1152
  50.2 1.9 collective-permute-start.8
  52.1 1.1 pad_maximum_fusion.1.refs_6_.refs_12_
  53.1 1.5 collective-permute-start.9
  55.2 23.9 %collective-permute-done.10 = bf16[96,1024]{1,0:T(8,128)(2,1)S(1)} collective-permute-done((bf16[96,1024]{1,0:T(8,128)(2,1)S(1)}, bf16[96,1024]{1,0:T(8,128)(2,1)S(1)}, u32[]{:S(2)}, u32[]{:S(2)}) %collective-permute-start.10) | collective-permute-done | bytes 196640 | tf_op jit(solution)/shard_map/ppermute | solution.py:1012
  79.2 2.6 pad_maximum_fusion.2
  83.2 2.6 fusion.14
  85.9 1.5 collective-permute-start.16
  87.4 1.0 collective-permute-start.17
  88.4 0.6 pad_add_fusion.refs_0_
  89.0 2.6 open_block.1
  91.7 9.4 %enter.1 = (bf16[512,1024]{1,0:T(8,128)(2,1)}, bf16[512,2048]{1,0:T(8,128)(2,1)}, bf16[512,16]{1,0:T(8,128)(2,1)}) custom-call(s32[4]{0:T(128)} %pad_add_fusion.refs_0_, bf16[512,1024]{1,0:T(8,128)(2,1)} %bitcast.45, f32[8,1024]{1,0:T(8,128)} %get-tuple-element.107.refs_2_.refs_4_.refs_10_, bf16[16,1024]{1,0:T(8,128)(2,1)} %get-tuple-element.108.refs_3_.refs_7_, ...), custom_call_target="tpu_custom_call" | custom-call | flops 1 | bytes 1 | tf_op jit(solution)/shard_map/enter/pallas_call | solution.py:226
  101.1 5.1 %collective-permute-done.16.refs_12_ = bf16[2,192,1024]{2,1,0:T(8,128)(2,1)} collective-permute-done((bf16[2,192,1024]{2,1,0:T(8,128)(2,1)}, bf16[2,192,1024]{2,1,0:T(8,128)(2,1)}, u32[]{:S(2)}, u32[]{:S(2)}) %collective-permute-start.16) | collective-permute-done | bytes 786464 | tf_op jit(solution)/shard_map/ppermute | solution.py:1012
  106.1 1.2 collective-permute-done.17.refs_15_
  108.4 1.1 collective-permute-start.20
  109.5 5.0 %collective-permute-done.18.refs_3_.refs_4_.keys_far.values_far = bf16[512,2048]{1,0:T(8,128)(2,1)} collective-permute-done((bf16[512,2048]{1,0:T(8,128)(2,1)}, bf16[512,2048]{1,0:T(8,128)(2,1)}, u32[]{:S(2)}, u32[]{:S(2)}) %collective-permute-start.18) | collective-permute-done | bytes 2097184 | tf_op jit(solution)/shard_map/ppermute | solution.py:716
  114.6 8.6 %attend.2 = (bf16[512,1024]{1,0:T(8,128)(2,1)}, f32[2,512,128]{2,1,0:T(8,128)}) custom-call(bf16[512,1024]{1,0:T(8,128)(2,1)} %get-tuple-element.115.refs_0_.queries, bf16[512,2048]{1,0:T(8,128)(2,1)} %get-tuple-element.116.refs_1_.refs_2_.keys_near.values_near, bf16[512,2048]{1,0:T(8,128)(2,1)} %get-tuple-element.116.refs_1_.refs_2_.keys_near.values_near, ...), custom_call_target="tpu_custom_call" | custom-call | flops 1 | bytes 1 | tf_op jit(solution)/shard_map/attend/pallas_call | solution.py:309
  123.2 4.4 %collective-permute-done.19.refs_13_ = bf16[2,192,1024]{2,1,0:T(8,128)(2,1)} collective-permute-done((bf16[2,192,1024]{2,1,0:T(8,128)(2,1)}, bf16[2,192,1024]{2,1,0:T(8,128)(2,1)}, u32[]{:S(2)}, u32[]{:S(2)}) %collective-permute-start.19) | collective-permute-done | bytes 786464 | tf_op jit(solution)/shard_map/ppermute | solution.py:1012
  127.9 1.1 collective-permute-start.23
  129.0 1.4 collective-permute-start.24
  130.9 8.6 %attend.3 = (bf16[512,1024]{1,0:T(8,128)(2,1)}, f32[2,512,128]{2,1,0:T(8,128)}) custom-call(bf16[512,1024]{1,0:T(8,128)(2,1)} %get-tuple-element.115.refs_0_.queries, bf16[512,2048]{1,0:T(8,128)(2,1)} %get-tuple-element.116.refs_1_.refs_2_.keys_near.values_near, ...), custom_call_target="tpu_custom_call", output_to_operand_aliasing={{0}: (5, {})} | custom-call | flops 1 | bytes 1 | tf_op jit(solution)/shard_map/attend/pallas_call | solution.py:309
  139.5 7.0 %collective-permute-done.23.refs_16_ = bf16[2,192,1024]{2,1,0:T(8,128)(2,1)S(1)} collective-permute-done((bf16[2,192,1024]{2,1,0:T(8,128)(2,1)}, bf16[2,192,1024]{2,1,0:T(8,128)(2,1)S(1)}, u32[]{:S(2)}, u32[]{:S(2)}) %collective-permute-start.23) | collective-permute-done | bytes 786464 | tf_op jit(solution)/shard_map/ppermute | solution.py:1012
  146.5 0.7 collective-permute-done.24.refs_17_
  147.8 1.8 collective-permute-done.28.refs_23_
  149.6 0.9 copy-done.9
  150.9 42.4 %feed.1 = (bf16[512,1024]{1,0:T(8,128)(2,1)}, f32[512,1024]{1,0:T(8,128)}, bf16[512,1024]{1,0:T(8,128)(2,1)}, f32[8,1024]{1,0:T(8,128)}, f32[16,1024]{1,0:T(8,12...) custom-call(s32[4]{0:T(128)} %pad_add_fusion.refs_0_, ...), custom_call_target="tpu_custom_call" | custom-call | flops 1 | bytes 1 | tf_op jit(solution)/shard_map/feed/pallas_call | solution.py:544
  193.3 15.0 %attend_back.2 = (bf16[512,512]{1,0:T(8,128)(2,1)}, f32[2,512,512]{2,1,0:T(8,128)}, bf16[2,512,512]{2,1,0:T(8,128)(2,1)}) custom-call(bf16[512,1024]{1,0:T(8,128)(2,1)} %get-tuple-element.115.refs_0_.queries, bf16[512,2048]{1,0:T(8,128)(2,1)} %get-tuple-element.116.refs_1_.refs_2_.keys_near.values_near, ...), custom_call_target="tpu_custom_call" | custom-call | flops 1 | bytes 1 | tf_op jit(solution)/shard_map/attend_back/pallas_call | solution.py:402
  208.4 14.9 %attend_back.3 = (bf16[512,512]{1,0:T(8,128)(2,1)}, f32[2,512,512]{2,1,0:T(8,128)}, bf16[2,512,512]{2,1,0:T(8,128)(2,1)}) custom-call(bf16[512,1024]{1,0:T(8,128)(2,1)} %get-tuple-element.115.refs_0_.queries, bf16[512,2048]{1,0:T(8,128)(2,1)} %get-tuple-element.116.refs_1_.refs_2_.keys_near.values_near, ...), custom_call_target="tpu_custom_call" | custom-call | flops 1 | bytes 1 | tf_op jit(solution)/shard_map/attend_back/pallas_call | solution.py:402
  223.9 2.4 pack_late.1
  226.8 1.2 collective-permute-done.31.refs_6_
  228.1 13.4 %leave.1 = (f32[512,1024]{1,0:T(8,128)}, f32[8,1024]{1,0:T(8,128)}, f32[16,1024]{1,0:T(8,128)}, f32[16,3072]{1,0:T(8,128)}) custom-call(s32[4]{0:T(128)} %pad_add_fusion.refs_0_, bf16[512,512]{1,0:T(8,128)(2,1)} %get-tuple-element.159.refs_1_, bf16[512,512]{1,0:T(8,128)(2,1)} %get-tuple-element.160.refs_2_, f32[2,512,512]{2,1,0:T(8,128)} %get-tuple-element.161.refs_3_, ...), custom_call_target="tpu_custom_call" | custom-call | flops 1 | bytes 1 | tf_op jit(solution)/shard_map/leave/pallas_call | solution.py:676
  242.0 1.1 collective-permute-done.32.refs_2_
  243.0 0.6 copy-done.19
  243.7 2.9 %pack_early.1 = (f32[16,16,384]{2,1,0:T(8,128)}, f32[16,16,384]{2,1,0:T(8,128)}, bf16[1,6144]{1,0:T(2,128)(2,1)}, bf16[1,16]{1,0:T(2,128)(2,1)}) custom-call(s32[1]{0:T(128)} %bitcast.3.refs_0_.core, f32[8,1024]{1,0:T(8,128)} %get-tuple-element.166.refs_1_, f32[8,1024]{1,0:T(8,128)} %copy-done.19, f32[8,1024]{1,0:T(8,128)} %get-tuple-element.167.refs_3_, ...), custom_call_target="tpu_custom_call" | custom-call | flops 1 | bytes 1 | tf_op jit(solution)/shard_map/pack_early/pallas_call | solution.py:904
  247.0 1.5 collective-permute-done.34
  248.5 1.0 add_convert_fusion.1
  249.5 0.8 pad_maximum_fusion.5
  250.3 5.8 %all-to-all-start.2 = ((bf16[16,16,768]{2,1,0:T(8,128)(2,1)}), bf16[16,16,768]{2,1,0:T(8,128)(2,1)S(1)}, u32[]{:S(2)}, u32[]{:S(2)}) async-start(bf16[16,16,768]{2,1,0:T(8,128)(2,1)} %pad_maximum_fusion.5), calls=%async_computation.2 | async-start | bytes 786432 | tf_op jit(solution)/shard_map/all_to_all | solution.py:1152
  256.2 9.0 %condition_back.1 = f32[1,1024]{1,0:T(1,128)} custom-call(bf16[1,6144]{1,0:T(2,128)(2,1)} %get-tuple-element.173.grads, bf16[1024,6144]{1,0:T(8,128)(2,1)} %all-gather.6.cloned.1.call-done.weight, bf16[1,16]{1,0:T(2,128)(2,1)} %get-tuple-element.175.back, bf16[16,1024]{1,0:T(8,128)(2,1)} %get-tuple-element.176.down, bf16[1,1024]{1,0:T(2,128)(2,1)} %condition.3), custom_call_target="tpu_custom_call" | custom-call | flops 1 | bytes 1 | tf_op jit(solution)/shard_map/condition_back/pallas_call | solution.py:929
  265.2 3.8 %all-to-all-done.2.refs_1_ = bf16[16,16,768]{2,1,0:T(8,128)(2,1)S(1)} async-done(((bf16[16,16,768]{2,1,0:T(8,128)(2,1)}), bf16[16,16,768]{2,1,0:T(8,128)(2,1)S(1)}, u32[]{:S(2)}, u32[]{:S(2)}) %all-to-all-start.2) | async-done | bytes 393248 | tf_op jit(solution)/shard_map/all_to_all | solution.py:1152
  269.1 0.7 copy-done.5
  269.8 2.3 table_sums.1
  (118 shorter events, 8.3 us)
Async XLA Ops:
  7.2 21.2 %copy-start.12 = (bf16[32,3072]{1,0:T(8,128)(2,1)S(1)}, bf16[32,3072]{1,0:T(8,128)(2,1)}, u32[]{:S(2)}) copy-start(bf16[32,3072]{1,0:T(8,128)(2,1)} %param.24) | copy-start | bytes 589828
  7.2 19.5 %copy-start.20 = (bf16[8,16,96]{2,1,0:T(8,128)(2,1)S(1)}, bf16[8,16,96]{2,1,0:T(8,128)(2,1)}, u32[]{:S(2)}) copy-start(bf16[8,16,96]{2,1,0:T(8,128)(2,1)} %param.31) | copy-start | bytes 73732
  7.2 19.5 %copy-start.21 = (bf16[8,32,16]{1,2,0:T(8,128)(2,1)S(1)}, bf16[8,32,16]{1,2,0:T(8,128)(2,1)}, u32[]{:S(2)}) copy-start(bf16[8,32,16]{1,2,0:T(8,128)(2,1)} %param.30) | copy-start | bytes 24580
  7.2 19.5 %copy-start.16 = (bf16[8,16,192]{2,1,0:T(8,128)(2,1)S(1)}, bf16[8,16,192]{2,1,0:T(8,128)(2,1)}, u32[]{:S(2)}) copy-start(bf16[8,16,192]{2,1,0:T(8,128)(2,1)} %param.29) | copy-start | bytes 147460
  7.2 19.5 %copy-start.22 = (bf16[8,32,16]{1,2,0:T(8,128)(2,1)S(1)}, bf16[8,32,16]{1,2,0:T(8,128)(2,1)}, u32[]{:S(2)}) copy-start(bf16[8,32,16]{1,2,0:T(8,128)(2,1)} %param.28) | copy-start | bytes 24580
  7.2 19.6 %copy-start.23 = (bf16[8,32,16]{1,2,0:T(8,128)(2,1)S(1)}, bf16[8,32,16]{1,2,0:T(8,128)(2,1)}, u32[]{:S(2)}) copy-start(bf16[8,32,16]{1,2,0:T(8,128)(2,1)} %param.32) | copy-start | bytes 24580
  7.2 19.6 %copy-start.24 = (bf16[8,16,32]{2,1,0:T(8,128)(2,1)S(1)}, bf16[8,16,32]{2,1,0:T(8,128)(2,1)}, u32[]{:S(2)}) copy-start(bf16[8,16,32]{2,1,0:T(8,128)(2,1)} %param.33) | copy-start | bytes 24580
  7.3 19.6 %copy-start.25 = (bf16[8,32,16]{1,2,0:T(8,128)(2,1)S(1)}, bf16[8,32,16]{1,2,0:T(8,128)(2,1)}, u32[]{:S(2)}) copy-start(bf16[8,32,16]{1,2,0:T(8,128)(2,1)} %param.34) | copy-start | bytes 24580
  7.3 19.6 %copy-start.26 = (bf16[8,16,128]{2,1,0:T(8,128)(2,1)S(1)}, bf16[8,16,128]{2,1,0:T(8,128)(2,1)}, u32[]{:S(2)}) copy-start(bf16[8,16,128]{2,1,0:T(8,128)(2,1)} %param.35) | copy-start | bytes 98308
  7.3 19.6 %copy-start.27 = (bf16[8,128,16]{1,2,0:T(8,128)(2,1)S(1)}, bf16[8,128,16]{1,2,0:T(8,128)(2,1)}, u32[]{:S(2)}) copy-start(bf16[8,128,16]{1,2,0:T(8,128)(2,1)} %param.36) | copy-start | bytes 98308
  7.3 19.6 %copy-start.28 = (bf16[8,16,32]{2,1,0:T(8,128)(2,1)S(1)}, bf16[8,16,32]{2,1,0:T(8,128)(2,1)}, u32[]{:S(2)}) copy-start(bf16[8,16,32]{2,1,0:T(8,128)(2,1)} %param.37) | copy-start | bytes 24580
  9.3 27.3 %collective-permute-start = (bf16[96,1024]{1,0:T(8,128)(2,1)}, bf16[96,1024]{1,0:T(8,128)(2,1)S(1)}, u32[]{:S(2)}, u32[]{:S(2)}) collective-permute-start(bf16[96,1024]{1,0:T(8,128)(2,1)} %get-tuple-element.102), channel_id=1, source_target_pairs={{0,2},{2,0},{4,6},{6,4},{8,10},{10,8},{12,14},{14,12},{16,18},{18,... | collective-permute-start | bytes 589832 | tf_op jit(solution)/shard_map/ppermute | solution.py:1012
  12.2 24.3 %collective-permute-start.1 = (bf16[96,1024]{1,0:T(8,128)(2,1)}, bf16[96,1024]{1,0:T(8,128)(2,1)S(1)}, u32[]{:S(2)}, u32[]{:S(2)}) collective-permute-start(bf16[96,1024]{1,0:T(8,128)(2,1)} %get-tuple-element.102), channel_id=1, source_target_pairs={{0,4},{2,6},{4,0},{6,2},{8,12},{10,14},{12,8},{14,10},{16,20},{18,... | collective-permute-start | bytes 589832 | tf_op jit(solution)/shard_map/ppermute | solution.py:1012
  13.8 14.7 %collective-permute-start.3 = (bf16[32,3072]{1,0:T(8,128)(2,1)}, bf16[32,3072]{1,0:T(8,128)(2,1)S(1)}, u32[]{:S(2)}, u32[]{:S(2)}) collective-permute-start(bf16[32,3072]{1,0:T(8,128)(2,1)} %param.24), channel_id=1, source_target_pairs={{0,8},{2,10},{4,12},{6,14},{8,16},{10,18},{12,20},{14,22},{16,24},... | collective-permute-start | bytes 589832 | tf_op jit(solution)/shard_map/ppermute | solution.py:1015
  15.3 15.1 %collective-permute-start.6 = (bf16[32,3072]{1,0:T(8,128)(2,1)}, bf16[32,3072]{1,0:T(8,128)(2,1)S(1)}, u32[]{:S(2)}, u32[]{:S(2)}) collective-permute-start(bf16[32,3072]{1,0:T(8,128)(2,1)} %param.24), channel_id=1, source_target_pairs={{0,24},{2,26},{4,28},{6,30},{8,0},{10,2},{12,4},{14,6},{16,8},{18,... | collective-permute-start | bytes 589832 | tf_op jit(solution)/shard_map/ppermute | solution.py:1015
  17.6 17.8 %collective-permute-start.5 = (bf16[32,3072]{1,0:T(8,128)(2,1)}, bf16[32,3072]{1,0:T(8,128)(2,1)S(1)}, u32[]{:S(2)}, u32[]{:S(2)}) collective-permute-start(bf16[32,3072]{1,0:T(8,128)(2,1)} %param.24), channel_id=1, source_target_pairs={{0,16},{2,18},{4,20},{6,22},{8,24},{10,26},{12,28},{14,30},{16,0},... | collective-permute-start | bytes 589832 | tf_op jit(solution)/shard_map/ppermute | solution.py:1015
  19.8 16.7 %all-to-all-start = ((bf16[16,16,128]{2,1,0:T(8,128)(2,1)}), bf16[16,16,128]{2,1,0:T(8,128)(2,1)S(1)}, u32[]{:S(2)}, u32[]{:S(2)}) async-start(bf16[16,16,128]{2,1,0:T(8,128)(2,1)} %write_notes.1), calls=%async_computation | async-start | bytes 131072 | tf_op jit(solution)/shard_map/all_to_all | solution.py:1152
  23.3 59.8 %all-gather.8.cloned.1.call-start = ((), (), s32[]{:S(2)}) async-start(), calls=%async_computation.4 | async-start | bytes 1966080 | tf_op jit(solution)/shard_map/all_gather | solution.py:1041
  28.5 12.8 %collective-permute-start.4 = (bf16[2,32,3072]{2,1,0:T(8,128)(2,1)S(1)}, bf16[2,32,3072]{2,1,0:T(8,128)(2,1)S(1)}, u32[]{:S(2)}, u32[]{:S(2)}) collective-permute-start(bf16[2,32,3072]{2,1,0:T(8,128)(2,1)S(1)} %get-tuple-element.196), channel_id=1, source_target_pairs={{0,2},{2,0},{4,6},{6,4},{8,10},{10,8},{12,14},{14,12},{16,18},{18,... | collective-permute-start | bytes 1179656 | tf_op jit(solution)/shard_map/ppermute | solution.py:1012
  35.4 11.0 %collective-permute-start.7 = (bf16[2,32,3072]{2,1,0:T(8,128)(2,1)S(1)}, bf16[2,32,3072]{2,1,0:T(8,128)(2,1)S(1)}, u32[]{:S(2)}, u32[]{:S(2)}) collective-permute-start(bf16[2,32,3072]{2,1,0:T(8,128)(2,1)S(1)} %get-tuple-element.194), channel_id=1, source_target_pairs={{0,4},{2,6},{4,0},{6,2},{8,12},{10,14},{12,8},{14,10},{16,20},{18,... | collective-permute-start | bytes 1179656 | tf_op jit(solution)/shard_map/ppermute | solution.py:1012
  36.6 13.5 %copy-start.13 = (bf16[96,1024]{1,0:T(8,128)(2,1)}, bf16[96,1024]{1,0:T(8,128)(2,1)S(1)}, u32[]{:S(2)}) copy-start(bf16[96,1024]{1,0:T(8,128)(2,1)S(1)} %collective-permute-done) | copy-start | bytes 589828
  36.6 13.5 %copy-start.15 = (bf16[96,1024]{1,0:T(8,128)(2,1)}, bf16[96,1024]{1,0:T(8,128)(2,1)S(1)}, u32[]{:S(2)}) copy-start(bf16[96,1024]{1,0:T(8,128)(2,1)S(1)} %collective-permute-done.1) | copy-start | bytes 589828
  36.9 1.8 collective-permute-start.2
  46.4 5.6 %copy-start.11 = (bf16[2,32,3072]{2,1,0:T(8,128)(2,1)}, bf16[2,32,3072]{2,1,0:T(8,128)(2,1)S(1)}, u32[]{:S(2)}) copy-start(bf16[2,32,3072]{2,1,0:T(8,128)(2,1)S(1)} %collective-permute-done.7) | copy-start | bytes 1179652
  46.4 32.7 %all-to-all-start.1 = ((bf16[16,16,1152]{2,1,0:T(8,128)(2,1)}), bf16[16,16,1152]{2,1,0:T(8,128)(2,1)S(1)}, u32[]{:S(2)}, u32[]{:S(2)}) async-start(bf16[16,16,1152]{2,1,0:T(8,128)(2,1)} %prepare.1), calls=%async_computation.1 | async-start | bytes 1179648 | tf_op jit(solution)/shard_map/all_to_all | solution.py:1152
  50.0 97.2 %all-gather.10.cloned.1.call-start = ((), (), s32[]{:S(2)}) async-start(), calls=%async_computation.5 | async-start | bytes 7077888 | tf_op jit(solution)/shard_map/all_gather | solution.py:1055
  50.1 4.6 %copy-start.14 = (bf16[96,1024]{1,0:T(8,128)(2,1)S(1)}, bf16[96,1024]{1,0:T(8,128)(2,1)}, u32[]{:S(2)}) copy-start(bf16[96,1024]{1,0:T(8,128)(2,1)} %copy-done.13) | copy-start | bytes 589828
  50.2 35.7 %copy-start = (bf16[2,2,32,3072]{3,2,1,0:T(8,128)(2,1)}, bf16[2,2,32,3072]{3,2,1,0:T(8,128)(2,1)S(1)}, u32[]{:S(2)}) copy-start(bf16[2,2,32,3072]{3,2,1,0:T(8,128)(2,1)S(1)} %pad_maximum_fusion.refs_5_.refs_11_) | copy-start | bytes 2359300
  50.2 29.0 %collective-permute-start.8 = (bf16[2,2,32,3072]{3,2,1,0:T(8,128)(2,1)S(1)}, bf16[2,2,32,3072]{3,2,1,0:T(8,128)(2,1)S(1)}, u32[]{:S(2)}, u32[]{:S(2)}) collective-permute-start(bf16[2,2,32,3072]{3,2,1,0:T(8,128)(2,1)S(1)} %pad_maximum_fusion.refs_5_.refs_11_), channel_id=1, source_target_pairs={{0,4},{2,6},{4,0},{6,2},{8,12},{10,14},{12,8},{14,10},{16,20},{18,... | collective-permute-start | bytes 2359304 | tf_op jit(solution)/shard_map/ppermute | solution.py:1012
  53.1 32.7 %copy-start.1 = (bf16[2,2,32,3072]{3,2,1,0:T(8,128)(2,1)}, bf16[2,2,32,3072]{3,2,1,0:T(8,128)(2,1)S(1)}, u32[]{:S(2)}) copy-start(bf16[2,2,32,3072]{3,2,1,0:T(8,128)(2,1)S(1)} %pad_maximum_fusion.1.refs_6_.refs_12_) | copy-start | bytes 2359300
  53.1 26.0 %collective-permute-start.9 = (bf16[2,2,32,3072]{3,2,1,0:T(8,128)(2,1)S(1)}, bf16[2,2,32,3072]{3,2,1,0:T(8,128)(2,1)}, u32[]{:S(2)}, u32[]{:S(2)}) collective-permute-start(bf16[2,2,32,3072]{3,2,1,0:T(8,128)(2,1)S(1)} %pad_maximum_fusion.1.refs_6_.refs_12_), channel_id=1, source_target_pairs={{0,2},{2,0},{4,6},{6,4},{8,10},{10,8},{12,14},{14,12},{16,18},{18,... | collective-permute-start | bytes 2359304 | tf_op jit(solution)/shard_map/ppermute | solution.py:1012
  54.7 24.5 %collective-permute-start.10 = (bf16[96,1024]{1,0:T(8,128)(2,1)S(1)}, bf16[96,1024]{1,0:T(8,128)(2,1)S(1)}, u32[]{:S(2)}, u32[]{:S(2)}) collective-permute-start(bf16[96,1024]{1,0:T(8,128)(2,1)S(1)} %copy-done.14), channel_id=1, source_target_pairs={{0,4},{2,6},{4,0},{6,2},{8,12},{10,14},{12,8},{14,10},{16,20},{18,... | collective-permute-start | bytes 589832 | tf_op jit(solution)/shard_map/ppermute | solution.py:1012
  79.2 6.7 %copy-start.3 = (bf16[2,2,32,3072]{3,2,1,0:T(8,128)(2,1)}, bf16[2,2,32,3072]{3,2,1,0:T(8,128)(2,1)S(1)}, u32[]{:S(2)}) copy-start(bf16[2,2,32,3072]{3,2,1,0:T(8,128)(2,1)S(1)} %collective-permute-done.8.refs_7_.refs_13_) | copy-start | bytes 2359300
  79.2 6.7 %copy-start.4 = (bf16[16,16,1152]{2,1,0:T(8,128)(2,1)}, bf16[16,16,1152]{2,1,0:T(8,128)(2,1)S(1)}, u32[]{:S(2)}) copy-start(bf16[16,16,1152]{2,1,0:T(8,128)(2,1)S(1)} %all-to-all-done.1.refs_2_) | copy-start | bytes 1769476
  81.8 174.4 %all-gather.6.cloned.1.call-start = ((), (), s32[]{:S(2)}) async-start(), calls=%async_computation.3 | async-start | bytes 12976128 | tf_op jit(solution)/shard_map/all_gather | solution.py:1210
  82.0 3.8 %collective-permute-start.12 = (bf16[2,2,32,3072]{3,2,1,0:T(8,128)(2,1)S(1)}, bf16[2,2,32,3072]{3,2,1,0:T(8,128)(2,1)}, u32[]{:S(2)}, u32[]{:S(2)}) collective-permute-start(bf16[2,2,32,3072]{3,2,1,0:T(8,128)(2,1)S(1)} %pad_maximum_fusion.refs_5_.refs_11_), channel_id=1, source_target_pairs={{0,1},{1,0},{2,3},{3,2},{4,5},{5,4},{6,7},{7,6},{8,9},{9,8},{10,11... | collective-permute-start | bytes 2359304 | tf_op jit(solution)/shard_map/ppermute | solution.py:716
  82.1 5.3 %collective-permute-start.11 = (bf16[16,16,1152]{2,1,0:T(8,128)(2,1)S(1)}, bf16[16,16,1152]{2,1,0:T(8,128)(2,1)}, u32[]{:S(2)}, u32[]{:S(2)}) collective-permute-start(bf16[16,16,1152]{2,1,0:T(8,128)(2,1)S(1)} %all-to-all-done.1.refs_2_), channel_id=1, source_target_pairs={{0,1},{1,0},{2,3},{3,2},{4,5},{5,4},{6,7},{7,6},{8,9},{9,8},{10,11... | collective-permute-start | bytes 1769480 | tf_op jit(solution)/shard_map/ppermute | solution.py:716
  82.6 9.0 %collective-permute-start.13 = (bf16[2,2,32,3072]{3,2,1,0:T(8,128)(2,1)S(1)}, bf16[2,2,32,3072]{3,2,1,0:T(8,128)(2,1)}, u32[]{:S(2)}, u32[]{:S(2)}) collective-permute-start(bf16[2,2,32,3072]{3,2,1,0:T(8,128)(2,1)S(1)} %pad_maximum_fusion.1.refs_6_.refs_12_), channel_id=1, source_target_pairs={{0,1},{1,0},{2,3},{3,2},{4,5},{5,4},{6,7},{7,6},{8,9},{9,8},{10,11... | collective-permute-start | bytes 2359304 | tf_op jit(solution)/shard_map/ppermute | solution.py:716
  82.7 9.0 %collective-permute-start.14 = (bf16[2,2,32,3072]{3,2,1,0:T(8,128)(2,1)S(1)}, bf16[2,2,32,3072]{3,2,1,0:T(8,128)(2,1)}, u32[]{:S(2)}, u32[]{:S(2)}) collective-permute-start(bf16[2,2,32,3072]{3,2,1,0:T(8,128)(2,1)S(1)} %collective-permute-done.8.refs_7_.refs_13_), channel_id=1, source_target_pairs={{0,1},{1,0},{2,3},{3,2},{4,5},{5,4},{6,7},{7,6},{8,9},{9,8},{10,11... | collective-permute-start | bytes 2359304 | tf_op jit(solution)/shard_map/ppermute | solution.py:716
  83.1 8.5 %collective-permute-start.15 = (bf16[2,2,32,3072]{3,2,1,0:T(8,128)(2,1)}, bf16[2,2,32,3072]{3,2,1,0:T(8,128)(2,1)}, u32[]{:S(2)}, u32[]{:S(2)}) collective-permute-start(bf16[2,2,32,3072]{3,2,1,0:T(8,128)(2,1)} %collective-permute-done.9.refs_8_.refs_14_), channel_id=1, source_target_pairs={{0,1},{1,0},{2,3},{3,2},{4,5},{5,4},{6,7},{7,6},{8,9},{9,8},{10,11... | collective-permute-start | bytes 2359304 | tf_op jit(solution)/shard_map/ppermute | solution.py:716
  85.9 20.3 %collective-permute-start.16 = (bf16[2,192,1024]{2,1,0:T(8,128)(2,1)}, bf16[2,192,1024]{2,1,0:T(8,128)(2,1)}, u32[]{:S(2)}, u32[]{:S(2)}) collective-permute-start(bf16[2,192,1024]{2,1,0:T(8,128)(2,1)} %bitcast.22), channel_id=1, source_target_pairs={{0,2},{2,0},{4,6},{6,4},{8,10},{10,8},{12,14},{14,12},{16,18},{18,... | collective-permute-start | bytes 2359304 | tf_op jit(solution)/shard_map/ppermute | solution.py:1012
  87.4 19.9 %collective-permute-start.17 = (bf16[2,192,1024]{2,1,0:T(8,128)(2,1)}, bf16[2,192,1024]{2,1,0:T(8,128)(2,1)}, u32[]{:S(2)}, u32[]{:S(2)}) collective-permute-start(bf16[2,192,1024]{2,1,0:T(8,128)(2,1)} %bitcast.23), channel_id=1, source_target_pairs={{0,4},{2,6},{4,0},{6,2},{8,12},{10,14},{12,8},{14,10},{16,20},{18,... | collective-permute-start | bytes 2359304 | tf_op jit(solution)/shard_map/ppermute | solution.py:1012
  91.7 15.7 %copy-start.2 = (bf16[768,1024]{1,0:T(8,128)(2,1)S(1)}, bf16[768,1024]{1,0:T(8,128)(2,1)}, u32[]{:S(2)}) copy-start(bf16[768,1024]{1,0:T(8,128)(2,1)} %all-gather.8.cloned.1.call-done) | copy-start | bytes 4718596
  107.3 7.2 %collective-permute-start.18 = (bf16[512,2048]{1,0:T(8,128)(2,1)}, bf16[512,2048]{1,0:T(8,128)(2,1)}, u32[]{:S(2)}, u32[]{:S(2)}) collective-permute-start(bf16[512,2048]{1,0:T(8,128)(2,1)} %get-tuple-element.116.refs_1_.refs_2_.keys_near.values_near), channel_id=1, source_target_pairs={{0,1},{1,0},{2,3},{3,2},{4,5},{5,4},{6,7},{7,6},{8,9},{9,8},{10,11... | collective-permute-start | bytes 6291464 | tf_op jit(solution)/shard_map/ppermute | solution.py:716
  107.3 20.6 %collective-permute-start.21 = (bf16[4,192,1024]{2,1,0:T(8,128)(2,1)S(1)}, bf16[4,192,1024]{2,1,0:T(8,128)(2,1)}, u32[]{:S(2)}, u32[]{:S(2)}) collective-permute-start(bf16[4,192,1024]{2,1,0:T(8,128)(2,1)S(1)} %bitcast.49), channel_id=1, source_target_pairs={{0,1},{1,0},{2,3},{3,2},{4,5},{5,4},{6,7},{7,6},{8,9},{9,8},{10,11... | collective-permute-start | bytes 4718600 | tf_op jit(solution)/shard_map/ppermute | solution.py:716
  107.8 19.8 %collective-permute-start.19 = (bf16[2,192,1024]{2,1,0:T(8,128)(2,1)}, bf16[2,192,1024]{2,1,0:T(8,128)(2,1)}, u32[]{:S(2)}, u32[]{:S(2)}) collective-permute-start(bf16[2,192,1024]{2,1,0:T(8,128)(2,1)} %bitcast.23), channel_id=1, source_target_pairs={{0,2},{2,0},{4,6},{6,4},{8,10},{10,8},{12,14},{14,12},{16,18},{18,... | collective-permute-start | bytes 2359304 | tf_op jit(solution)/shard_map/ppermute | solution.py:1012
  108.4 19.5 %collective-permute-start.20 = (bf16[2,192,1024]{2,1,0:T(8,128)(2,1)}, bf16[2,192,1024]{2,1,0:T(8,128)(2,1)}, u32[]{:S(2)}, u32[]{:S(2)}) collective-permute-start(bf16[2,192,1024]{2,1,0:T(8,128)(2,1)} %bitcast.22), channel_id=1, source_target_pairs={{0,4},{2,6},{4,0},{6,2},{8,12},{10,14},{12,8},{14,10},{16,20},{18,... | collective-permute-start | bytes 2359304 | tf_op jit(solution)/shard_map/ppermute | solution.py:1012
  109.5 18.4 %collective-permute-start.22 = (bf16[2,192,1024]{2,1,0:T(8,128)(2,1)}, bf16[2,192,1024]{2,1,0:T(8,128)(2,1)}, u32[]{:S(2)}, u32[]{:S(2)}) collective-permute-start(bf16[2,192,1024]{2,1,0:T(8,128)(2,1)} %collective-permute-done.16.refs_12_), channel_id=1, source_target_pairs={{0,1},{1,0},{2,3},{3,2},{4,5},{5,4},{6,7},{7,6},{8,9},{9,8},{10,11... | collective-permute-start | bytes 2359304 | tf_op jit(solution)/shard_map/ppermute | solution.py:716
  114.5 24.9 %collective-permute-start.27 = (bf16[2,192,1024]{2,1,0:T(8,128)(2,1)}, bf16[2,192,1024]{2,1,0:T(8,128)(2,1)}, u32[]{:S(2)}, u32[]{:S(2)}) collective-permute-start(bf16[2,192,1024]{2,1,0:T(8,128)(2,1)} %collective-permute-done.17.refs_15_), channel_id=1, source_target_pairs={{0,1},{1,0},{2,3},{3,2},{4,5},{5,4},{6,7},{7,6},{8,9},{9,8},{10,11... | collective-permute-start | bytes 2359304 | tf_op jit(solution)/shard_map/ppermute | solution.py:716
  127.9 18.6 %collective-permute-start.23 = (bf16[2,192,1024]{2,1,0:T(8,128)(2,1)}, bf16[2,192,1024]{2,1,0:T(8,128)(2,1)S(1)}, u32[]{:S(2)}, u32[]{:S(2)}) collective-permute-start(bf16[2,192,1024]{2,1,0:T(8,128)(2,1)} %collective-permute-done.16.refs_12_), channel_id=1, source_target_pairs={{0,4},{2,6},{4,0},{6,2},{8,12},{10,14},{12,8},{14,10},{16,20},{18,... | collective-permute-start | bytes 2359304 | tf_op jit(solution)/shard_map/ppermute | solution.py:1012
  129.0 18.3 %collective-permute-start.24 = (bf16[2,192,1024]{2,1,0:T(8,128)(2,1)}, bf16[2,192,1024]{2,1,0:T(8,128)(2,1)S(1)}, u32[]{:S(2)}, u32[]{:S(2)}) collective-permute-start(bf16[2,192,1024]{2,1,0:T(8,128)(2,1)} %collective-permute-done.17.refs_15_), channel_id=1, source_target_pairs={{0,2},{2,0},{4,6},{6,4},{8,10},{10,8},{12,14},{14,12},{16,18},{18,... | collective-permute-start | bytes 2359304 | tf_op jit(solution)/shard_map/ppermute | solution.py:1012
  130.3 16.9 %collective-permute-start.25 = (bf16[2,192,1024]{2,1,0:T(8,128)(2,1)}, bf16[2,192,1024]{2,1,0:T(8,128)(2,1)}, u32[]{:S(2)}, u32[]{:S(2)}) collective-permute-start(bf16[2,192,1024]{2,1,0:T(8,128)(2,1)} %collective-permute-done.19.refs_13_), channel_id=1, source_target_pairs={{0,1},{1,0},{2,3},{3,2},{4,5},{5,4},{6,7},{7,6},{8,9},{9,8},{10,11... | collective-permute-start | bytes 2359304 | tf_op jit(solution)/shard_map/ppermute | solution.py:716
  130.4 16.9 %collective-permute-start.26 = (bf16[2,192,1024]{2,1,0:T(8,128)(2,1)}, bf16[2,192,1024]{2,1,0:T(8,128)(2,1)}, u32[]{:S(2)}, u32[]{:S(2)}) collective-permute-start(bf16[2,192,1024]{2,1,0:T(8,128)(2,1)} %collective-permute-done.20.refs_14_), channel_id=1, source_target_pairs={{0,1},{1,0},{2,3},{3,2},{4,5},{5,4},{6,7},{7,6},{8,9},{9,8},{10,11... | collective-permute-start | bytes 2359304 | tf_op jit(solution)/shard_map/ppermute | solution.py:716
  147.3 2.4 collective-permute-start.28
  147.5 3.4 %collective-permute-start.29 = (bf16[2,192,1024]{2,1,0:T(8,128)(2,1)S(1)}, bf16[2,192,1024]{2,1,0:T(8,128)(2,1)}, u32[]{:S(2)}, u32[]{:S(2)}) collective-permute-start(bf16[2,192,1024]{2,1,0:T(8,128)(2,1)S(1)} %collective-permute-done.24.refs_17_), channel_id=1, source_target_pairs={{0,1},{1,0},{2,3},{3,2},{4,5},{5,4},{6,7},{7,6},{8,9},{9,8},{10,11... | collective-permute-start | bytes 2359304 | tf_op jit(solution)/shard_map/ppermute | solution.py:716
  208.4 18.1 %copy-start.17 = (f32[8,1024]{1,0:T(8,128)S(1)}, f32[8,1024]{1,0:T(8,128)}, u32[]{:S(2)}) copy-start(f32[8,1024]{1,0:T(8,128)} %get-tuple-element.167.refs_3_) | copy-start | bytes 98308
  223.3 3.5 %collective-permute-start.30 = (bf16[2,512,512]{2,1,0:T(8,128)(2,1)}, bf16[2,512,512]{2,1,0:T(8,128)(2,1)S(1)}, u32[]{:S(2)}, u32[]{:S(2)}) collective-permute-start(bf16[2,512,512]{2,1,0:T(8,128)(2,1)} %get-tuple-element.149), channel_id=1, source_target_pairs={{0,1},{1,0},{2,3},{3,2},{4,5},{5,4},{6,7},{7,6},{8,9},{9,8},{10,11... | collective-permute-start | bytes 3145736 | tf_op jit(solution)/shard_map/ppermute | solution.py:716
  223.5 4.5 %collective-permute-start.31 = (bf16[2,512,512]{2,1,0:T(8,128)(2,1)}, bf16[2,512,512]{2,1,0:T(8,128)(2,1)}, u32[]{:S(2)}, u32[]{:S(2)}) collective-permute-start(bf16[2,512,512]{2,1,0:T(8,128)(2,1)} %get-tuple-element.151), channel_id=1, source_target_pairs={{0,1},{1,0},{2,3},{3,2},{4,5},{5,4},{6,7},{7,6},{8,9},{9,8},{10,11... | collective-permute-start | bytes 3145736 | tf_op jit(solution)/shard_map/ppermute | solution.py:716
  226.3 20.6 %collective-permute-start.35 = (f32[16,16,384]{2,1,0:T(8,128)}, f32[16,16,384]{2,1,0:T(8,128)S(1)}, u32[]{:S(2)}, u32[]{:S(2)}) collective-permute-start(f32[16,16,384]{2,1,0:T(8,128)} %get-tuple-element.179), channel_id=1, source_target_pairs={{0,1},{1,0},{2,3},{3,2},{4,5},{5,4},{6,7},{7,6},{8,9},{9,8},{10,11... | collective-permute-start | bytes 1179656 | tf_op jit(solution)/shard_map/ppermute | solution.py:716
  226.5 15.5 %collective-permute-start.33 = (f32[8,1024]{1,0:T(8,128)S(1)}, f32[8,1024]{1,0:T(8,128)S(1)}, u32[]{:S(2)}, u32[]{:S(2)}) collective-permute-start(f32[8,1024]{1,0:T(8,128)S(1)} %copy-done.17), channel_id=1, source_target_pairs={{0,1},{1,0},{2,3},{3,2},{4,5},{5,4},{6,7},{7,6},{8,9},{9,8},{10,11... | collective-permute-start | bytes 98312 | tf_op jit(solution)/shard_map/ppermute | solution.py:716
  228.1 18.8 %copy-start.10 = (f32[16,16,384]{2,1,0:T(8,128)S(1)}, f32[16,16,384]{2,1,0:T(8,128)}, u32[]{:S(2)}) copy-start(f32[16,16,384]{2,1,0:T(8,128)} %get-tuple-element.158) | copy-start | bytes 1179652
  241.4 1.6 collective-permute-start.32
  246.6 1.9 collective-permute-start.34
  250.3 18.7 %all-to-all-start.2 = ((bf16[16,16,768]{2,1,0:T(8,128)(2,1)}), bf16[16,16,768]{2,1,0:T(8,128)(2,1)S(1)}, u32[]{:S(2)}, u32[]{:S(2)}) async-start(bf16[16,16,768]{2,1,0:T(8,128)(2,1)} %pad_maximum_fusion.5), calls=%async_computation.2 | async-start | bytes 786432 | tf_op jit(solution)/shard_map/all_to_all | solution.py:1152
  (7 other events, 12.6 us)
Sparse Core Ops, SparseCore 0:
  25.8 50.0 all-gather.7
  81.9 65.2 all-gather.9
  151.0 96.3 all-gather.5

commit v6 on v5

--- a/solution.py
+++ b/solution.py
@@ -384,8 +384,8 @@
             keys_sum[part, rows:] += kf
         if head == heads - 1:
             grad_queries[here] = total.astype(bf16)
-    grad_near[0] = keys_sum[:, :rows].T
-    grad_near[1] = values_sum[:, :rows].T
+    grad_near[0] = keys_sum[:, :rows].T.astype(bf16)
+    grad_near[1] = values_sum[:, :rows].T.astype(bf16)
     grad_far[0] = keys_sum[:, rows:].T.astype(bf16)
     grad_far[1] = values_sum[:, rows:].T.astype(bf16)
 
@@ -407,7 +407,7 @@
         out_specs=[pl.BlockSpec((rows, GROUP), lambda g: (0, g)), pair, pair],
         out_shape=[
             jax.ShapeDtypeStruct((rows, groups * GROUP), bf16),
-            jax.ShapeDtypeStruct((2, rows, groups * GROUP), f32),
+            jax.ShapeDtypeStruct((2, rows, groups * GROUP), bf16),
             jax.ShapeDtypeStruct((2, rows, groups * GROUP), bf16),
         ],
         scratch_shapes=[pltpu.VMEM((GROUP, 2 * rows), f32), pltpu.VMEM((GROUP, 2 * rows), f32)],
@@ -642,8 +642,8 @@
     def _():
         wait_attend(weight, semaphores, step_at)
         total[...] += through(
-            (own_0[0] + other_0[0].astype(f32)).astype(bf16),
-            (own_1[0] + other_1[0].astype(f32)).astype(bf16),
+            (own_0[0].astype(f32) + other_0[0].astype(f32)).astype(bf16),
+            (own_1[0].astype(f32) + other_1[0].astype(f32)).astype(bf16),
         )
 
     @pl.when(step_at == pl.num_programs(0) - 1)

time: 283 us -> 282 us (level)
  no operation moved by 1% of the time
where the time goes in v6:
time: 282 us; the launch traced here: 277 us
  Pallas kernels  136 us (48%)
  waiting for transfers between devices  68.9 us (24%)
  starting transfers between devices  40.1 us (14%)
  between operations  14.5 us (5%)
  other arithmetic  9.04 us (3%)
  local copies, waits for them, and re-layouts  8.69 us (3%)
    ppermute x13, waiting for transfers between devices, exchange(): lax.ppermute(values, 'dp', [(chip, chip ^ over) for chip in range(self.ch...  47.7 us
    pallas_call x1, Pallas kernels, feed(): pl.pallas_call(lambda *refs: feed_kernel(len(weights), *refs), grid=(FF /...  42.4 us
    pallas_call x2, Pallas kernels, attend_back(): pl.pallas_call(attend_back_kernel, grid=(groups,), in_specs=[at(0), at(0)...  29.2 us
    ppermute x13, starting transfers between devices, exchange(): lax.ppermute(values, 'dp', [(chip, chip ^ over) for chip in range(self.ch...  17.6 us
    pallas_call x2, Pallas kernels, attend(): pl.pallas_call(lambda *refs: attend_kernel(*refs[:5], *refs[5 + len(given...  17.2 us
    all_to_all x3, starting transfers between devices, to_chips(): return lax.all_to_all(values, 'dp', split_axis=0, concat_axis=0, tiled=True)  13.2 us
    pallas_call x1, Pallas kernels, leave(): pl.pallas_call(lambda *refs: leave_kernel(len(weights), *refs), grid=(col...  12.9 us
    ppermute x20, waiting for transfers between devices, swap_cores(): return lax.ppermute(values, 'seq', [(0, 1), (1, 0)])  11.7 us
  transfers between devices with their start and end apart: 42, of which 17 were waited for; matrix products, arithmetic and copies ran while one was open for 6% of the time, Pallas kernels for 48%

profile of v6, /device:TPU:0, one launch (start us, length us, event | category | flops | bytes accessed | tf_op | source)
XLA Modules:
  0.0 277.4 jit_solution(6109139755998625864)
XLA Ops:
  7.3 2.0 cut_weights.1
  9.3 2.9 %collective-permute-start = (bf16[96,1024]{1,0:T(8,128)(2,1)}, bf16[96,1024]{1,0:T(8,128)(2,1)S(1)}, u32[]{:S(2)}, u32[]{:S(2)}) collective-permute-start(bf16[96,1024]{1,0:T(8,128)(2,1)} %get-tuple-element.102), channel_id=1, source_target_pairs={{0,2},{2,0},{4,6},{6,4},{8,10},{10,8},{12,14},{14,12},{16,18},{18,... | collective-permute-start | bytes 589832 | tf_op jit(solution)/shard_map/ppermute | solution.py:1012
  12.2 1.5 collective-permute-start.1
  13.8 1.6 collective-permute-start.3
  15.3 2.2 collective-permute-start.6
  17.6 0.8 collective-permute-start.5
  18.4 1.4 write_notes.1
  19.8 3.5 %all-to-all-start = ((bf16[16,16,128]{2,1,0:T(8,128)(2,1)}), bf16[16,16,128]{2,1,0:T(8,128)(2,1)S(1)}, u32[]{:S(2)}, u32[]{:S(2)}) async-start(bf16[16,16,128]{2,1,0:T(8,128)(2,1)} %write_notes.1), calls=%async_computation | async-start | bytes 131072 | tf_op jit(solution)/shard_map/all_to_all | solution.py:1152
  23.4 0.7 all-gather.8.cloned.1.call-update
  24.1 1.0 constant_dynamic-slice_fusion
  25.1 0.9 constant_dynamic-slice_fusion.1
  26.0 0.7 pad_maximum_fusion.6.refs_3_
  26.9 0.8 concatenate.20.refs_5_
  27.7 0.7 pad_maximum_fusion.7
  28.5 2.0 collective-permute-start.4
  30.5 4.9 %collective-permute-done.5 = bf16[32,3072]{1,0:T(8,128)(2,1)S(1)} collective-permute-done((bf16[32,3072]{1,0:T(8,128)(2,1)}, bf16[32,3072]{1,0:T(8,128)(2,1)S(1)}, u32[]{:S(2)}, u32[]{:S(2)}) %collective-permute-start.5) | collective-permute-done | bytes 196640 | tf_op jit(solution)/shard_map/ppermute | solution.py:1015
  35.4 0.6 collective-permute-start.7
  36.0 0.6 pad_add_fusion.1.refs_1_
  37.0 0.7 copy.39.refs_0_
  37.7 0.6 fusion.10.refs_2_
  38.7 2.6 prepare.1
  41.3 5.1 %collective-permute-done.7 = bf16[2,32,3072]{2,1,0:T(8,128)(2,1)S(1)} collective-permute-done((bf16[2,32,3072]{2,1,0:T(8,128)(2,1)S(1)}, bf16[2,32,3072]{2,1,0:T(8,128)(2,1)S(1)}, u32[]{:S(2)}, u32[]{:S(2)}) %collective-permute-start.7) | collective-permute-done | bytes 393248 | tf_op jit(solution)/shard_map/ppermute | solution.py:1012
  46.4 3.6 %all-to-all-start.1 = ((bf16[16,16,1152]{2,1,0:T(8,128)(2,1)}), bf16[16,16,1152]{2,1,0:T(8,128)(2,1)S(1)}, u32[]{:S(2)}, u32[]{:S(2)}) async-start(bf16[16,16,1152]{2,1,0:T(8,128)(2,1)} %prepare.1), calls=%async_computation.1 | async-start | bytes 1179648 | tf_op jit(solution)/shard_map/all_to_all | solution.py:1152
  50.2 1.9 collective-permute-start.8
  52.1 1.1 pad_maximum_fusion.1.refs_6_.refs_12_
  53.1 1.5 collective-permute-start.9
  55.2 23.9 %collective-permute-done.10 = bf16[96,1024]{1,0:T(8,128)(2,1)S(1)} collective-permute-done((bf16[96,1024]{1,0:T(8,128)(2,1)S(1)}, bf16[96,1024]{1,0:T(8,128)(2,1)S(1)}, u32[]{:S(2)}, u32[]{:S(2)}) %collective-permute-start.10) | collective-permute-done | bytes 196640 | tf_op jit(solution)/shard_map/ppermute | solution.py:1012
  79.2 2.6 pad_maximum_fusion.2
  83.2 2.6 fusion.14
  85.9 1.5 collective-permute-start.16
  87.4 1.0 collective-permute-start.17
  88.4 0.6 pad_add_fusion.refs_0_
  89.0 2.6 open_block.1
  91.7 9.4 %enter.1 = (bf16[512,1024]{1,0:T(8,128)(2,1)}, bf16[512,2048]{1,0:T(8,128)(2,1)}, bf16[512,16]{1,0:T(8,128)(2,1)}) custom-call(s32[4]{0:T(128)} %pad_add_fusion.refs_0_, bf16[512,1024]{1,0:T(8,128)(2,1)} %bitcast.45, f32[8,1024]{1,0:T(8,128)} %get-tuple-element.107.refs_2_.refs_4_.refs_10_, bf16[16,1024]{1,0:T(8,128)(2,1)} %get-tuple-element.108.refs_3_.refs_7_, ...), custom_call_target="tpu_custom_call" | custom-call | flops 1 | bytes 1 | tf_op jit(solution)/shard_map/enter/pallas_call | solution.py:226
  101.1 5.1 %collective-permute-done.16.refs_12_ = bf16[2,192,1024]{2,1,0:T(8,128)(2,1)} collective-permute-done((bf16[2,192,1024]{2,1,0:T(8,128)(2,1)}, bf16[2,192,1024]{2,1,0:T(8,128)(2,1)}, u32[]{:S(2)}, u32[]{:S(2)}) %collective-permute-start.16) | collective-permute-done | bytes 786464 | tf_op jit(solution)/shard_map/ppermute | solution.py:1012
  106.1 1.2 collective-permute-done.17.refs_15_
  108.4 1.1 collective-permute-start.20
  109.5 5.0 %collective-permute-done.18.refs_3_.refs_4_.keys_far.values_far = bf16[512,2048]{1,0:T(8,128)(2,1)} collective-permute-done((bf16[512,2048]{1,0:T(8,128)(2,1)}, bf16[512,2048]{1,0:T(8,128)(2,1)}, u32[]{:S(2)}, u32[]{:S(2)}) %collective-permute-start.18) | collective-permute-done | bytes 2097184 | tf_op jit(solution)/shard_map/ppermute | solution.py:716
  114.6 8.6 %attend.2 = (bf16[512,1024]{1,0:T(8,128)(2,1)}, f32[2,512,128]{2,1,0:T(8,128)}) custom-call(bf16[512,1024]{1,0:T(8,128)(2,1)} %get-tuple-element.115.refs_0_.queries, bf16[512,2048]{1,0:T(8,128)(2,1)} %get-tuple-element.116.refs_1_.refs_2_.keys_near.values_near, bf16[512,2048]{1,0:T(8,128)(2,1)} %get-tuple-element.116.refs_1_.refs_2_.keys_near.values_near, ...), custom_call_target="tpu_custom_call" | custom-call | flops 1 | bytes 1 | tf_op jit(solution)/shard_map/attend/pallas_call | solution.py:309
  123.2 4.4 %collective-permute-done.19.refs_13_ = bf16[2,192,1024]{2,1,0:T(8,128)(2,1)} collective-permute-done((bf16[2,192,1024]{2,1,0:T(8,128)(2,1)}, bf16[2,192,1024]{2,1,0:T(8,128)(2,1)}, u32[]{:S(2)}, u32[]{:S(2)}) %collective-permute-start.19) | collective-permute-done | bytes 786464 | tf_op jit(solution)/shard_map/ppermute | solution.py:1012
  127.9 1.1 collective-permute-start.23
  129.0 1.4 collective-permute-start.24
  130.9 8.6 %attend.3 = (bf16[512,1024]{1,0:T(8,128)(2,1)}, f32[2,512,128]{2,1,0:T(8,128)}) custom-call(bf16[512,1024]{1,0:T(8,128)(2,1)} %get-tuple-element.115.refs_0_.queries, bf16[512,2048]{1,0:T(8,128)(2,1)} %get-tuple-element.116.refs_1_.refs_2_.keys_near.values_near, ...), custom_call_target="tpu_custom_call", output_to_operand_aliasing={{0}: (5, {})} | custom-call | flops 1 | bytes 1 | tf_op jit(solution)/shard_map/attend/pallas_call | solution.py:309
  139.5 7.0 %collective-permute-done.23.refs_16_ = bf16[2,192,1024]{2,1,0:T(8,128)(2,1)S(1)} collective-permute-done((bf16[2,192,1024]{2,1,0:T(8,128)(2,1)}, bf16[2,192,1024]{2,1,0:T(8,128)(2,1)S(1)}, u32[]{:S(2)}, u32[]{:S(2)}) %collective-permute-start.23) | collective-permute-done | bytes 786464 | tf_op jit(solution)/shard_map/ppermute | solution.py:1012
  146.5 0.7 collective-permute-done.24.refs_17_
  147.8 1.8 collective-permute-done.28.refs_23_
  149.6 0.9 copy-done.9
  150.9 42.4 %feed.1 = (bf16[512,1024]{1,0:T(8,128)(2,1)}, f32[512,1024]{1,0:T(8,128)}, bf16[512,1024]{1,0:T(8,128)(2,1)}, f32[8,1024]{1,0:T(8,128)}, f32[16,1024]{1,0:T(8,12...) custom-call(s32[4]{0:T(128)} %pad_add_fusion.refs_0_, ...), custom_call_target="tpu_custom_call" | custom-call | flops 1 | bytes 1 | tf_op jit(solution)/shard_map/feed/pallas_call | solution.py:544
  193.3 14.7 %attend_back.2 = (bf16[512,512]{1,0:T(8,128)(2,1)}, bf16[2,512,512]{2,1,0:T(8,128)(2,1)}, bf16[2,512,512]{2,1,0:T(8,128)(2,1)}) custom-call(bf16[512,1024]{1,0:T(8,128)(2,1)} %get-tuple-element.115.refs_0_.queries, bf16[512,2048]{1,0:T(8,128)(2,1)} %get-tuple-element.116.refs_1_.refs_2_.keys_near.values_near, ...), custom_call_target="tpu_custom_call" | custom-call | flops 1 | bytes 1 | tf_op jit(solution)/shard_map/attend_back/pallas_call | solution.py:402
  208.1 14.4 %attend_back.3 = (bf16[512,512]{1,0:T(8,128)(2,1)}, bf16[2,512,512]{2,1,0:T(8,128)(2,1)}, bf16[2,512,512]{2,1,0:T(8,128)(2,1)}) custom-call(bf16[512,1024]{1,0:T(8,128)(2,1)} %get-tuple-element.115.refs_0_.queries, bf16[512,2048]{1,0:T(8,128)(2,1)} %get-tuple-element.116.refs_1_.refs_2_.keys_near.values_near, ...), custom_call_target="tpu_custom_call" | custom-call | flops 1 | bytes 1 | tf_op jit(solution)/shard_map/attend_back/pallas_call | solution.py:402
  223.1 2.4 pack_late.1
  226.0 1.0 collective-permute-done.31.refs_6_
  227.1 12.9 %leave.1 = (f32[512,1024]{1,0:T(8,128)}, f32[8,1024]{1,0:T(8,128)}, f32[16,1024]{1,0:T(8,128)}, f32[16,3072]{1,0:T(8,128)}) custom-call(s32[4]{0:T(128)} %pad_add_fusion.refs_0_, bf16[512,512]{1,0:T(8,128)(2,1)} %get-tuple-element.159.refs_1_, bf16[512,512]{1,0:T(8,128)(2,1)} %get-tuple-element.160.refs_2_, bf16[2,512,512]{2,1,0:T(8,128)(2,1)} %get-tuple-element.161.refs_3_, ...), custom_call_target="tpu_custom_call" | custom-call | flops 1 | bytes 1 | tf_op jit(solution)/shard_map/leave/pallas_call | solution.py:676
  240.2 1.3 collective-permute-done.32.refs_2_
  241.5 0.6 copy-done.19
  242.1 2.7 pack_early.1
  245.0 1.7 collective-permute-done.34
  246.8 1.0 add_convert_fusion.1
  247.8 0.8 pad_maximum_fusion.5
  248.6 6.1 %all-to-all-start.2 = ((bf16[16,16,768]{2,1,0:T(8,128)(2,1)}), bf16[16,16,768]{2,1,0:T(8,128)(2,1)S(1)}, u32[]{:S(2)}, u32[]{:S(2)}) async-start(bf16[16,16,768]{2,1,0:T(8,128)(2,1)} %pad_maximum_fusion.5), calls=%async_computation.2 | async-start | bytes 786432 | tf_op jit(solution)/shard_map/all_to_all | solution.py:1152
  254.8 9.0 %condition_back.1 = f32[1,1024]{1,0:T(1,128)} custom-call(bf16[1,6144]{1,0:T(2,128)(2,1)} %get-tuple-element.173.grads, bf16[1024,6144]{1,0:T(8,128)(2,1)} %all-gather.6.cloned.1.call-done.weight, bf16[1,16]{1,0:T(2,128)(2,1)} %get-tuple-element.175.back, bf16[16,1024]{1,0:T(8,128)(2,1)} %get-tuple-element.176.down, bf16[1,1024]{1,0:T(2,128)(2,1)} %condition.3), custom_call_target="tpu_custom_call" | custom-call | flops 1 | bytes 1 | tf_op jit(solution)/shard_map/condition_back/pallas_call | solution.py:929
  263.8 3.8 %all-to-all-done.2.refs_1_ = bf16[16,16,768]{2,1,0:T(8,128)(2,1)S(1)} async-done(((bf16[16,16,768]{2,1,0:T(8,128)(2,1)}), bf16[16,16,768]{2,1,0:T(8,128)(2,1)S(1)}, u32[]{:S(2)}, u32[]{:S(2)}) %all-to-all-start.2) | async-done | bytes 393248 | tf_op jit(solution)/shard_map/all_to_all | solution.py:1152
  267.7 0.7 copy-done.5
  268.4 2.3 table_sums.1
  (118 shorter events, 7.8 us)
Async XLA Ops:
  7.2 21.2 %copy-start.12 = (bf16[32,3072]{1,0:T(8,128)(2,1)S(1)}, bf16[32,3072]{1,0:T(8,128)(2,1)}, u32[]{:S(2)}) copy-start(bf16[32,3072]{1,0:T(8,128)(2,1)} %param.24) | copy-start | bytes 589828
  7.2 19.5 %copy-start.20 = (bf16[8,16,96]{2,1,0:T(8,128)(2,1)S(1)}, bf16[8,16,96]{2,1,0:T(8,128)(2,1)}, u32[]{:S(2)}) copy-start(bf16[8,16,96]{2,1,0:T(8,128)(2,1)} %param.31) | copy-start | bytes 73732
  7.2 19.5 %copy-start.21 = (bf16[8,32,16]{1,2,0:T(8,128)(2,1)S(1)}, bf16[8,32,16]{1,2,0:T(8,128)(2,1)}, u32[]{:S(2)}) copy-start(bf16[8,32,16]{1,2,0:T(8,128)(2,1)} %param.30) | copy-start | bytes 24580
  7.2 19.5 %copy-start.16 = (bf16[8,16,192]{2,1,0:T(8,128)(2,1)S(1)}, bf16[8,16,192]{2,1,0:T(8,128)(2,1)}, u32[]{:S(2)}) copy-start(bf16[8,16,192]{2,1,0:T(8,128)(2,1)} %param.29) | copy-start | bytes 147460
  7.2 19.5 %copy-start.22 = (bf16[8,32,16]{1,2,0:T(8,128)(2,1)S(1)}, bf16[8,32,16]{1,2,0:T(8,128)(2,1)}, u32[]{:S(2)}) copy-start(bf16[8,32,16]{1,2,0:T(8,128)(2,1)} %param.28) | copy-start | bytes 24580
  7.2 19.6 %copy-start.23 = (bf16[8,32,16]{1,2,0:T(8,128)(2,1)S(1)}, bf16[8,32,16]{1,2,0:T(8,128)(2,1)}, u32[]{:S(2)}) copy-start(bf16[8,32,16]{1,2,0:T(8,128)(2,1)} %param.32) | copy-start | bytes 24580
  7.2 19.6 %copy-start.24 = (bf16[8,16,32]{2,1,0:T(8,128)(2,1)S(1)}, bf16[8,16,32]{2,1,0:T(8,128)(2,1)}, u32[]{:S(2)}) copy-start(bf16[8,16,32]{2,1,0:T(8,128)(2,1)} %param.33) | copy-start | bytes 24580
  7.3 19.6 %copy-start.25 = (bf16[8,32,16]{1,2,0:T(8,128)(2,1)S(1)}, bf16[8,32,16]{1,2,0:T(8,128)(2,1)}, u32[]{:S(2)}) copy-start(bf16[8,32,16]{1,2,0:T(8,128)(2,1)} %param.34) | copy-start | bytes 24580
  7.3 19.6 %copy-start.26 = (bf16[8,16,128]{2,1,0:T(8,128)(2,1)S(1)}, bf16[8,16,128]{2,1,0:T(8,128)(2,1)}, u32[]{:S(2)}) copy-start(bf16[8,16,128]{2,1,0:T(8,128)(2,1)} %param.35) | copy-start | bytes 98308
  7.3 19.6 %copy-start.27 = (bf16[8,128,16]{1,2,0:T(8,128)(2,1)S(1)}, bf16[8,128,16]{1,2,0:T(8,128)(2,1)}, u32[]{:S(2)}) copy-start(bf16[8,128,16]{1,2,0:T(8,128)(2,1)} %param.36) | copy-start | bytes 98308
  7.3 19.6 %copy-start.28 = (bf16[8,16,32]{2,1,0:T(8,128)(2,1)S(1)}, bf16[8,16,32]{2,1,0:T(8,128)(2,1)}, u32[]{:S(2)}) copy-start(bf16[8,16,32]{2,1,0:T(8,128)(2,1)} %param.37) | copy-start | bytes 24580
  9.3 27.3 %collective-permute-start = (bf16[96,1024]{1,0:T(8,128)(2,1)}, bf16[96,1024]{1,0:T(8,128)(2,1)S(1)}, u32[]{:S(2)}, u32[]{:S(2)}) collective-permute-start(bf16[96,1024]{1,0:T(8,128)(2,1)} %get-tuple-element.102), channel_id=1, source_target_pairs={{0,2},{2,0},{4,6},{6,4},{8,10},{10,8},{12,14},{14,12},{16,18},{18,... | collective-permute-start | bytes 589832 | tf_op jit(solution)/shard_map/ppermute | solution.py:1012
  12.2 24.3 %collective-permute-start.1 = (bf16[96,1024]{1,0:T(8,128)(2,1)}, bf16[96,1024]{1,0:T(8,128)(2,1)S(1)}, u32[]{:S(2)}, u32[]{:S(2)}) collective-permute-start(bf16[96,1024]{1,0:T(8,128)(2,1)} %get-tuple-element.102), channel_id=1, source_target_pairs={{0,4},{2,6},{4,0},{6,2},{8,12},{10,14},{12,8},{14,10},{16,20},{18,... | collective-permute-start | bytes 589832 | tf_op jit(solution)/shard_map/ppermute | solution.py:1012
  13.8 14.7 %collective-permute-start.3 = (bf16[32,3072]{1,0:T(8,128)(2,1)}, bf16[32,3072]{1,0:T(8,128)(2,1)S(1)}, u32[]{:S(2)}, u32[]{:S(2)}) collective-permute-start(bf16[32,3072]{1,0:T(8,128)(2,1)} %param.24), channel_id=1, source_target_pairs={{0,8},{2,10},{4,12},{6,14},{8,16},{10,18},{12,20},{14,22},{16,24},... | collective-permute-start | bytes 589832 | tf_op jit(solution)/shard_map/ppermute | solution.py:1015
  15.3 15.1 %collective-permute-start.6 = (bf16[32,3072]{1,0:T(8,128)(2,1)}, bf16[32,3072]{1,0:T(8,128)(2,1)S(1)}, u32[]{:S(2)}, u32[]{:S(2)}) collective-permute-start(bf16[32,3072]{1,0:T(8,128)(2,1)} %param.24), channel_id=1, source_target_pairs={{0,24},{2,26},{4,28},{6,30},{8,0},{10,2},{12,4},{14,6},{16,8},{18,... | collective-permute-start | bytes 589832 | tf_op jit(solution)/shard_map/ppermute | solution.py:1015
  17.6 17.8 %collective-permute-start.5 = (bf16[32,3072]{1,0:T(8,128)(2,1)}, bf16[32,3072]{1,0:T(8,128)(2,1)S(1)}, u32[]{:S(2)}, u32[]{:S(2)}) collective-permute-start(bf16[32,3072]{1,0:T(8,128)(2,1)} %param.24), channel_id=1, source_target_pairs={{0,16},{2,18},{4,20},{6,22},{8,24},{10,26},{12,28},{14,30},{16,0},... | collective-permute-start | bytes 589832 | tf_op jit(solution)/shard_map/ppermute | solution.py:1015
  19.8 16.7 %all-to-all-start = ((bf16[16,16,128]{2,1,0:T(8,128)(2,1)}), bf16[16,16,128]{2,1,0:T(8,128)(2,1)S(1)}, u32[]{:S(2)}, u32[]{:S(2)}) async-start(bf16[16,16,128]{2,1,0:T(8,128)(2,1)} %write_notes.1), calls=%async_computation | async-start | bytes 131072 | tf_op jit(solution)/shard_map/all_to_all | solution.py:1152
  23.3 59.8 %all-gather.8.cloned.1.call-start = ((), (), s32[]{:S(2)}) async-start(), calls=%async_computation.4 | async-start | bytes 1966080 | tf_op jit(solution)/shard_map/all_gather | solution.py:1041
  28.5 12.8 %collective-permute-start.4 = (bf16[2,32,3072]{2,1,0:T(8,128)(2,1)S(1)}, bf16[2,32,3072]{2,1,0:T(8,128)(2,1)S(1)}, u32[]{:S(2)}, u32[]{:S(2)}) collective-permute-start(bf16[2,32,3072]{2,1,0:T(8,128)(2,1)S(1)} %get-tuple-element.196), channel_id=1, source_target_pairs={{0,2},{2,0},{4,6},{6,4},{8,10},{10,8},{12,14},{14,12},{16,18},{18,... | collective-permute-start | bytes 1179656 | tf_op jit(solution)/shard_map/ppermute | solution.py:1012
  35.4 11.0 %collective-permute-start.7 = (bf16[2,32,3072]{2,1,0:T(8,128)(2,1)S(1)}, bf16[2,32,3072]{2,1,0:T(8,128)(2,1)S(1)}, u32[]{:S(2)}, u32[]{:S(2)}) collective-permute-start(bf16[2,32,3072]{2,1,0:T(8,128)(2,1)S(1)} %get-tuple-element.194), channel_id=1, source_target_pairs={{0,4},{2,6},{4,0},{6,2},{8,12},{10,14},{12,8},{14,10},{16,20},{18,... | collective-permute-start | bytes 1179656 | tf_op jit(solution)/shard_map/ppermute | solution.py:1012
  36.6 13.5 %copy-start.13 = (bf16[96,1024]{1,0:T(8,128)(2,1)}, bf16[96,1024]{1,0:T(8,128)(2,1)S(1)}, u32[]{:S(2)}) copy-start(bf16[96,1024]{1,0:T(8,128)(2,1)S(1)} %collective-permute-done) | copy-start | bytes 589828
  36.6 13.5 %copy-start.15 = (bf16[96,1024]{1,0:T(8,128)(2,1)}, bf16[96,1024]{1,0:T(8,128)(2,1)S(1)}, u32[]{:S(2)}) copy-start(bf16[96,1024]{1,0:T(8,128)(2,1)S(1)} %collective-permute-done.1) | copy-start | bytes 589828
  36.9 1.8 collective-permute-start.2
  46.4 5.6 %copy-start.11 = (bf16[2,32,3072]{2,1,0:T(8,128)(2,1)}, bf16[2,32,3072]{2,1,0:T(8,128)(2,1)S(1)}, u32[]{:S(2)}) copy-start(bf16[2,32,3072]{2,1,0:T(8,128)(2,1)S(1)} %collective-permute-done.7) | copy-start | bytes 1179652
  46.4 32.7 %all-to-all-start.1 = ((bf16[16,16,1152]{2,1,0:T(8,128)(2,1)}), bf16[16,16,1152]{2,1,0:T(8,128)(2,1)S(1)}, u32[]{:S(2)}, u32[]{:S(2)}) async-start(bf16[16,16,1152]{2,1,0:T(8,128)(2,1)} %prepare.1), calls=%async_computation.1 | async-start | bytes 1179648 | tf_op jit(solution)/shard_map/all_to_all | solution.py:1152
  50.0 97.2 %all-gather.10.cloned.1.call-start = ((), (), s32[]{:S(2)}) async-start(), calls=%async_computation.5 | async-start | bytes 7077888 | tf_op jit(solution)/shard_map/all_gather | solution.py:1055
  50.1 4.6 %copy-start.14 = (bf16[96,1024]{1,0:T(8,128)(2,1)S(1)}, bf16[96,1024]{1,0:T(8,128)(2,1)}, u32[]{:S(2)}) copy-start(bf16[96,1024]{1,0:T(8,128)(2,1)} %copy-done.13) | copy-start | bytes 589828
  50.2 35.7 %copy-start = (bf16[2,2,32,3072]{3,2,1,0:T(8,128)(2,1)}, bf16[2,2,32,3072]{3,2,1,0:T(8,128)(2,1)S(1)}, u32[]{:S(2)}) copy-start(bf16[2,2,32,3072]{3,2,1,0:T(8,128)(2,1)S(1)} %pad_maximum_fusion.refs_5_.refs_11_) | copy-start | bytes 2359300
  50.2 29.0 %collective-permute-start.8 = (bf16[2,2,32,3072]{3,2,1,0:T(8,128)(2,1)S(1)}, bf16[2,2,32,3072]{3,2,1,0:T(8,128)(2,1)S(1)}, u32[]{:S(2)}, u32[]{:S(2)}) collective-permute-start(bf16[2,2,32,3072]{3,2,1,0:T(8,128)(2,1)S(1)} %pad_maximum_fusion.refs_5_.refs_11_), channel_id=1, source_target_pairs={{0,4},{2,6},{4,0},{6,2},{8,12},{10,14},{12,8},{14,10},{16,20},{18,... | collective-permute-start | bytes 2359304 | tf_op jit(solution)/shard_map/ppermute | solution.py:1012
  53.1 32.7 %copy-start.1 = (bf16[2,2,32,3072]{3,2,1,0:T(8,128)(2,1)}, bf16[2,2,32,3072]{3,2,1,0:T(8,128)(2,1)S(1)}, u32[]{:S(2)}) copy-start(bf16[2,2,32,3072]{3,2,1,0:T(8,128)(2,1)S(1)} %pad_maximum_fusion.1.refs_6_.refs_12_) | copy-start | bytes 2359300
  53.1 26.0 %collective-permute-start.9 = (bf16[2,2,32,3072]{3,2,1,0:T(8,128)(2,1)S(1)}, bf16[2,2,32,3072]{3,2,1,0:T(8,128)(2,1)}, u32[]{:S(2)}, u32[]{:S(2)}) collective-permute-start(bf16[2,2,32,3072]{3,2,1,0:T(8,128)(2,1)S(1)} %pad_maximum_fusion.1.refs_6_.refs_12_), channel_id=1, source_target_pairs={{0,2},{2,0},{4,6},{6,4},{8,10},{10,8},{12,14},{14,12},{16,18},{18,... | collective-permute-start | bytes 2359304 | tf_op jit(solution)/shard_map/ppermute | solution.py:1012
  54.7 24.5 %collective-permute-start.10 = (bf16[96,1024]{1,0:T(8,128)(2,1)S(1)}, bf16[96,1024]{1,0:T(8,128)(2,1)S(1)}, u32[]{:S(2)}, u32[]{:S(2)}) collective-permute-start(bf16[96,1024]{1,0:T(8,128)(2,1)S(1)} %copy-done.14), channel_id=1, source_target_pairs={{0,4},{2,6},{4,0},{6,2},{8,12},{10,14},{12,8},{14,10},{16,20},{18,... | collective-permute-start | bytes 589832 | tf_op jit(solution)/shard_map/ppermute | solution.py:1012
  79.2 6.7 %copy-start.3 = (bf16[2,2,32,3072]{3,2,1,0:T(8,128)(2,1)}, bf16[2,2,32,3072]{3,2,1,0:T(8,128)(2,1)S(1)}, u32[]{:S(2)}) copy-start(bf16[2,2,32,3072]{3,2,1,0:T(8,128)(2,1)S(1)} %collective-permute-done.8.refs_7_.refs_13_) | copy-start | bytes 2359300
  79.2 6.7 %copy-start.4 = (bf16[16,16,1152]{2,1,0:T(8,128)(2,1)}, bf16[16,16,1152]{2,1,0:T(8,128)(2,1)S(1)}, u32[]{:S(2)}) copy-start(bf16[16,16,1152]{2,1,0:T(8,128)(2,1)S(1)} %all-to-all-done.1.refs_2_) | copy-start | bytes 1769476
  81.8 173.0 %all-gather.6.cloned.1.call-start = ((), (), s32[]{:S(2)}) async-start(), calls=%async_computation.3 | async-start | bytes 12976128 | tf_op jit(solution)/shard_map/all_gather | solution.py:1210
  82.0 3.8 %collective-permute-start.12 = (bf16[2,2,32,3072]{3,2,1,0:T(8,128)(2,1)S(1)}, bf16[2,2,32,3072]{3,2,1,0:T(8,128)(2,1)}, u32[]{:S(2)}, u32[]{:S(2)}) collective-permute-start(bf16[2,2,32,3072]{3,2,1,0:T(8,128)(2,1)S(1)} %pad_maximum_fusion.refs_5_.refs_11_), channel_id=1, source_target_pairs={{0,1},{1,0},{2,3},{3,2},{4,5},{5,4},{6,7},{7,6},{8,9},{9,8},{10,11... | collective-permute-start | bytes 2359304 | tf_op jit(solution)/shard_map/ppermute | solution.py:716
  82.1 5.3 %collective-permute-start.11 = (bf16[16,16,1152]{2,1,0:T(8,128)(2,1)S(1)}, bf16[16,16,1152]{2,1,0:T(8,128)(2,1)}, u32[]{:S(2)}, u32[]{:S(2)}) collective-permute-start(bf16[16,16,1152]{2,1,0:T(8,128)(2,1)S(1)} %all-to-all-done.1.refs_2_), channel_id=1, source_target_pairs={{0,1},{1,0},{2,3},{3,2},{4,5},{5,4},{6,7},{7,6},{8,9},{9,8},{10,11... | collective-permute-start | bytes 1769480 | tf_op jit(solution)/shard_map/ppermute | solution.py:716
  82.6 9.0 %collective-permute-start.13 = (bf16[2,2,32,3072]{3,2,1,0:T(8,128)(2,1)S(1)}, bf16[2,2,32,3072]{3,2,1,0:T(8,128)(2,1)}, u32[]{:S(2)}, u32[]{:S(2)}) collective-permute-start(bf16[2,2,32,3072]{3,2,1,0:T(8,128)(2,1)S(1)} %pad_maximum_fusion.1.refs_6_.refs_12_), channel_id=1, source_target_pairs={{0,1},{1,0},{2,3},{3,2},{4,5},{5,4},{6,7},{7,6},{8,9},{9,8},{10,11... | collective-permute-start | bytes 2359304 | tf_op jit(solution)/shard_map/ppermute | solution.py:716
  82.7 9.0 %collective-permute-start.14 = (bf16[2,2,32,3072]{3,2,1,0:T(8,128)(2,1)S(1)}, bf16[2,2,32,3072]{3,2,1,0:T(8,128)(2,1)}, u32[]{:S(2)}, u32[]{:S(2)}) collective-permute-start(bf16[2,2,32,3072]{3,2,1,0:T(8,128)(2,1)S(1)} %collective-permute-done.8.refs_7_.refs_13_), channel_id=1, source_target_pairs={{0,1},{1,0},{2,3},{3,2},{4,5},{5,4},{6,7},{7,6},{8,9},{9,8},{10,11... | collective-permute-start | bytes 2359304 | tf_op jit(solution)/shard_map/ppermute | solution.py:716
  83.1 8.5 %collective-permute-start.15 = (bf16[2,2,32,3072]{3,2,1,0:T(8,128)(2,1)}, bf16[2,2,32,3072]{3,2,1,0:T(8,128)(2,1)}, u32[]{:S(2)}, u32[]{:S(2)}) collective-permute-start(bf16[2,2,32,3072]{3,2,1,0:T(8,128)(2,1)} %collective-permute-done.9.refs_8_.refs_14_), channel_id=1, source_target_pairs={{0,1},{1,0},{2,3},{3,2},{4,5},{5,4},{6,7},{7,6},{8,9},{9,8},{10,11... | collective-permute-start | bytes 2359304 | tf_op jit(solution)/shard_map/ppermute | solution.py:716
  85.9 20.3 %collective-permute-start.16 = (bf16[2,192,1024]{2,1,0:T(8,128)(2,1)}, bf16[2,192,1024]{2,1,0:T(8,128)(2,1)}, u32[]{:S(2)}, u32[]{:S(2)}) collective-permute-start(bf16[2,192,1024]{2,1,0:T(8,128)(2,1)} %bitcast.22), channel_id=1, source_target_pairs={{0,2},{2,0},{4,6},{6,4},{8,10},{10,8},{12,14},{14,12},{16,18},{18,... | collective-permute-start | bytes 2359304 | tf_op jit(solution)/shard_map/ppermute | solution.py:1012
  87.4 19.9 %collective-permute-start.17 = (bf16[2,192,1024]{2,1,0:T(8,128)(2,1)}, bf16[2,192,1024]{2,1,0:T(8,128)(2,1)}, u32[]{:S(2)}, u32[]{:S(2)}) collective-permute-start(bf16[2,192,1024]{2,1,0:T(8,128)(2,1)} %bitcast.23), channel_id=1, source_target_pairs={{0,4},{2,6},{4,0},{6,2},{8,12},{10,14},{12,8},{14,10},{16,20},{18,... | collective-permute-start | bytes 2359304 | tf_op jit(solution)/shard_map/ppermute | solution.py:1012
  91.7 15.7 %copy-start.2 = (bf16[768,1024]{1,0:T(8,128)(2,1)S(1)}, bf16[768,1024]{1,0:T(8,128)(2,1)}, u32[]{:S(2)}) copy-start(bf16[768,1024]{1,0:T(8,128)(2,1)} %all-gather.8.cloned.1.call-done) | copy-start | bytes 4718596
  107.3 7.2 %collective-permute-start.18 = (bf16[512,2048]{1,0:T(8,128)(2,1)}, bf16[512,2048]{1,0:T(8,128)(2,1)}, u32[]{:S(2)}, u32[]{:S(2)}) collective-permute-start(bf16[512,2048]{1,0:T(8,128)(2,1)} %get-tuple-element.116.refs_1_.refs_2_.keys_near.values_near), channel_id=1, source_target_pairs={{0,1},{1,0},{2,3},{3,2},{4,5},{5,4},{6,7},{7,6},{8,9},{9,8},{10,11... | collective-permute-start | bytes 6291464 | tf_op jit(solution)/shard_map/ppermute | solution.py:716
  107.3 20.6 %collective-permute-start.21 = (bf16[4,192,1024]{2,1,0:T(8,128)(2,1)S(1)}, bf16[4,192,1024]{2,1,0:T(8,128)(2,1)}, u32[]{:S(2)}, u32[]{:S(2)}) collective-permute-start(bf16[4,192,1024]{2,1,0:T(8,128)(2,1)S(1)} %bitcast.49), channel_id=1, source_target_pairs={{0,1},{1,0},{2,3},{3,2},{4,5},{5,4},{6,7},{7,6},{8,9},{9,8},{10,11... | collective-permute-start | bytes 4718600 | tf_op jit(solution)/shard_map/ppermute | solution.py:716
  107.8 19.8 %collective-permute-start.19 = (bf16[2,192,1024]{2,1,0:T(8,128)(2,1)}, bf16[2,192,1024]{2,1,0:T(8,128)(2,1)}, u32[]{:S(2)}, u32[]{:S(2)}) collective-permute-start(bf16[2,192,1024]{2,1,0:T(8,128)(2,1)} %bitcast.23), channel_id=1, source_target_pairs={{0,2},{2,0},{4,6},{6,4},{8,10},{10,8},{12,14},{14,12},{16,18},{18,... | collective-permute-start | bytes 2359304 | tf_op jit(solution)/shard_map/ppermute | solution.py:1012
  108.4 19.5 %collective-permute-start.20 = (bf16[2,192,1024]{2,1,0:T(8,128)(2,1)}, bf16[2,192,1024]{2,1,0:T(8,128)(2,1)}, u32[]{:S(2)}, u32[]{:S(2)}) collective-permute-start(bf16[2,192,1024]{2,1,0:T(8,128)(2,1)} %bitcast.22), channel_id=1, source_target_pairs={{0,4},{2,6},{4,0},{6,2},{8,12},{10,14},{12,8},{14,10},{16,20},{18,... | collective-permute-start | bytes 2359304 | tf_op jit(solution)/shard_map/ppermute | solution.py:1012
  109.5 18.4 %collective-permute-start.22 = (bf16[2,192,1024]{2,1,0:T(8,128)(2,1)}, bf16[2,192,1024]{2,1,0:T(8,128)(2,1)}, u32[]{:S(2)}, u32[]{:S(2)}) collective-permute-start(bf16[2,192,1024]{2,1,0:T(8,128)(2,1)} %collective-permute-done.16.refs_12_), channel_id=1, source_target_pairs={{0,1},{1,0},{2,3},{3,2},{4,5},{5,4},{6,7},{7,6},{8,9},{9,8},{10,11... | collective-permute-start | bytes 2359304 | tf_op jit(solution)/shard_map/ppermute | solution.py:716
  114.5 24.9 %collective-permute-start.27 = (bf16[2,192,1024]{2,1,0:T(8,128)(2,1)}, bf16[2,192,1024]{2,1,0:T(8,128)(2,1)}, u32[]{:S(2)}, u32[]{:S(2)}) collective-permute-start(bf16[2,192,1024]{2,1,0:T(8,128)(2,1)} %collective-permute-done.17.refs_15_), channel_id=1, source_target_pairs={{0,1},{1,0},{2,3},{3,2},{4,5},{5,4},{6,7},{7,6},{8,9},{9,8},{10,11... | collective-permute-start | bytes 2359304 | tf_op jit(solution)/shard_map/ppermute | solution.py:716
  127.9 18.6 %collective-permute-start.23 = (bf16[2,192,1024]{2,1,0:T(8,128)(2,1)}, bf16[2,192,1024]{2,1,0:T(8,128)(2,1)S(1)}, u32[]{:S(2)}, u32[]{:S(2)}) collective-permute-start(bf16[2,192,1024]{2,1,0:T(8,128)(2,1)} %collective-permute-done.16.refs_12_), channel_id=1, source_target_pairs={{0,4},{2,6},{4,0},{6,2},{8,12},{10,14},{12,8},{14,10},{16,20},{18,... | collective-permute-start | bytes 2359304 | tf_op jit(solution)/shard_map/ppermute | solution.py:1012
  129.0 18.3 %collective-permute-start.24 = (bf16[2,192,1024]{2,1,0:T(8,128)(2,1)}, bf16[2,192,1024]{2,1,0:T(8,128)(2,1)S(1)}, u32[]{:S(2)}, u32[]{:S(2)}) collective-permute-start(bf16[2,192,1024]{2,1,0:T(8,128)(2,1)} %collective-permute-done.17.refs_15_), channel_id=1, source_target_pairs={{0,2},{2,0},{4,6},{6,4},{8,10},{10,8},{12,14},{14,12},{16,18},{18,... | collective-permute-start | bytes 2359304 | tf_op jit(solution)/shard_map/ppermute | solution.py:1012
  130.3 16.9 %collective-permute-start.25 = (bf16[2,192,1024]{2,1,0:T(8,128)(2,1)}, bf16[2,192,1024]{2,1,0:T(8,128)(2,1)}, u32[]{:S(2)}, u32[]{:S(2)}) collective-permute-start(bf16[2,192,1024]{2,1,0:T(8,128)(2,1)} %collective-permute-done.19.refs_13_), channel_id=1, source_target_pairs={{0,1},{1,0},{2,3},{3,2},{4,5},{5,4},{6,7},{7,6},{8,9},{9,8},{10,11... | collective-permute-start | bytes 2359304 | tf_op jit(solution)/shard_map/ppermute | solution.py:716
  130.4 16.9 %collective-permute-start.26 = (bf16[2,192,1024]{2,1,0:T(8,128)(2,1)}, bf16[2,192,1024]{2,1,0:T(8,128)(2,1)}, u32[]{:S(2)}, u32[]{:S(2)}) collective-permute-start(bf16[2,192,1024]{2,1,0:T(8,128)(2,1)} %collective-permute-done.20.refs_14_), channel_id=1, source_target_pairs={{0,1},{1,0},{2,3},{3,2},{4,5},{5,4},{6,7},{7,6},{8,9},{9,8},{10,11... | collective-permute-start | bytes 2359304 | tf_op jit(solution)/shard_map/ppermute | solution.py:716
  147.3 2.4 collective-permute-start.28
  147.5 3.4 %collective-permute-start.29 = (bf16[2,192,1024]{2,1,0:T(8,128)(2,1)S(1)}, bf16[2,192,1024]{2,1,0:T(8,128)(2,1)}, u32[]{:S(2)}, u32[]{:S(2)}) collective-permute-start(bf16[2,192,1024]{2,1,0:T(8,128)(2,1)S(1)} %collective-permute-done.24.refs_17_), channel_id=1, source_target_pairs={{0,1},{1,0},{2,3},{3,2},{4,5},{5,4},{6,7},{7,6},{8,9},{9,8},{10,11... | collective-permute-start | bytes 2359304 | tf_op jit(solution)/shard_map/ppermute | solution.py:716
  208.1 17.6 %copy-start.17 = (f32[8,1024]{1,0:T(8,128)S(1)}, f32[8,1024]{1,0:T(8,128)}, u32[]{:S(2)}) copy-start(f32[8,1024]{1,0:T(8,128)} %get-tuple-element.167.refs_3_) | copy-start | bytes 98308
  222.5 3.5 %collective-permute-start.30 = (bf16[2,512,512]{2,1,0:T(8,128)(2,1)}, bf16[2,512,512]{2,1,0:T(8,128)(2,1)S(1)}, u32[]{:S(2)}, u32[]{:S(2)}) collective-permute-start(bf16[2,512,512]{2,1,0:T(8,128)(2,1)} %get-tuple-element.149), channel_id=1, source_target_pairs={{0,1},{1,0},{2,3},{3,2},{4,5},{5,4},{6,7},{7,6},{8,9},{9,8},{10,11... | collective-permute-start | bytes 3145736 | tf_op jit(solution)/shard_map/ppermute | solution.py:716
  222.7 4.4 %collective-permute-start.31 = (bf16[2,512,512]{2,1,0:T(8,128)(2,1)}, bf16[2,512,512]{2,1,0:T(8,128)(2,1)}, u32[]{:S(2)}, u32[]{:S(2)}) collective-permute-start(bf16[2,512,512]{2,1,0:T(8,128)(2,1)} %get-tuple-element.151), channel_id=1, source_target_pairs={{0,1},{1,0},{2,3},{3,2},{4,5},{5,4},{6,7},{7,6},{8,9},{9,8},{10,11... | collective-permute-start | bytes 3145736 | tf_op jit(solution)/shard_map/ppermute | solution.py:716
  225.5 19.5 %collective-permute-start.35 = (f32[16,16,384]{2,1,0:T(8,128)}, f32[16,16,384]{2,1,0:T(8,128)S(1)}, u32[]{:S(2)}, u32[]{:S(2)}) collective-permute-start(f32[16,16,384]{2,1,0:T(8,128)} %get-tuple-element.179), channel_id=1, source_target_pairs={{0,1},{1,0},{2,3},{3,2},{4,5},{5,4},{6,7},{7,6},{8,9},{9,8},{10,11... | collective-permute-start | bytes 1179656 | tf_op jit(solution)/shard_map/ppermute | solution.py:716
  225.7 14.5 %collective-permute-start.33 = (f32[8,1024]{1,0:T(8,128)S(1)}, f32[8,1024]{1,0:T(8,128)S(1)}, u32[]{:S(2)}, u32[]{:S(2)}) collective-permute-start(f32[8,1024]{1,0:T(8,128)S(1)} %copy-done.17), channel_id=1, source_target_pairs={{0,1},{1,0},{2,3},{3,2},{4,5},{5,4},{6,7},{7,6},{8,9},{9,8},{10,11... | collective-permute-start | bytes 98312 | tf_op jit(solution)/shard_map/ppermute | solution.py:716
  227.1 17.9 %copy-start.10 = (f32[16,16,384]{2,1,0:T(8,128)S(1)}, f32[16,16,384]{2,1,0:T(8,128)}, u32[]{:S(2)}) copy-start(f32[16,16,384]{2,1,0:T(8,128)} %get-tuple-element.158) | copy-start | bytes 1179652
  240.0 1.5 collective-permute-start.32
  244.8 1.9 collective-permute-start.34
  248.6 19.1 %all-to-all-start.2 = ((bf16[16,16,768]{2,1,0:T(8,128)(2,1)}), bf16[16,16,768]{2,1,0:T(8,128)(2,1)S(1)}, u32[]{:S(2)}, u32[]{:S(2)}) async-start(bf16[16,16,768]{2,1,0:T(8,128)(2,1)} %pad_maximum_fusion.5), calls=%async_computation.2 | async-start | bytes 786432 | tf_op jit(solution)/shard_map/all_to_all | solution.py:1152
  (7 other events, 12.6 us)
Sparse Core Ops, SparseCore 0:
  25.8 50.0 all-gather.7
  81.9 65.2 all-gather.9
  151.0 96.4 all-gather.5
